TPU v7x, 32 devices: a whole 2x2x4 slice. The times are simulated.
32 devices in a mesh: groups: 2 (over y), wide: 4 (over z), layer: 2 (over x), rep: 2 (over core).
Axes of the slice: x: 2, y: 2, z: 4, core: 2. Of those that a mesh axis runs over, the one named last changes fastest.
Arguments:
- acts: bfloat16 [48, 128, 13824], P(('groups', 'wide', 'rep'), None, 'layer'), parts along dimension 0, may hold values from -6 to 6
- grads: bfloat16 [48, 128, 5120], P(('groups', 'wide', 'rep'), None, 'layer'), parts along dimension 0, may hold values from -6 to 6
- counts: int32 [48], P(('groups', 'wide', 'rep')), parts along dimension 0, may hold values from 1 to 128, as said below
- basis_in: bfloat16 [512, 13824], P('wide', 'layer'), may hold values from -0.0546875 to 0.0546875
- basis_out: bfloat16 [512, 5120], P('wide', 'layer'), may hold values from -0.078125 to 0.078125
- query_grads: bfloat16 [64, 512, 512], P(None, ('wide', 'rep'), 'layer'), may hold values from -0.0009765625 to 0.0009765625
- eigenvalues: float32 [512, 512], P(('wide', 'rep'), 'layer'), may hold values from 0.1 to 10
- candidate: int32 [64, 2], P(('layer', 'rep'), 'groups'), parts along dimension 1, may hold values 0 or 1
Outputs:
- scores: float32 [64, 48], P(('layer', 'rep'), ('groups', 'wide')), parts along dimension 1
There are 2 independent parts, one for each index of `groups`. A program takes and returns all parts, laid end to end along the dimension named above; an argument that names none is the same for every part. Nothing has to cross between parts.
Inputs may be any that keep to these rules, and one draw needn't show every extreme that they name: `counts`: some sequence has all 128 tokens. `candidate`: some queries are scored against a block of training sequences and some are not.
All inputs are finite; a program needn't handle non-finite values.
Results may differ from a plain program's by a relative error of at most 0.0058.
Values may be sent and summed in bfloat16 or wider, within the bound.
No kernel may reach another device: no remote copies, remote signals or barrier semaphores. Data moves between devices by JAX's collectives and lax.ppermute only.
A program may use at most 64 MiB of HBM per device.

v0:
```python
import jax
import jax.numpy as jnp
from jax import lax
from jax.sharding import PartitionSpec as P


def local(acts, grads, counts, basis_in, basis_out, query_grads, eigenvalues, candidate):
    seq_dev, seq_len, ff_local = acts.shape
    d_local = grads.shape[2]
    n_wide = lax.axis_size("wide")
    n_layer = lax.axis_size("layer")
    n_rep = lax.axis_size("rep")
    panel_in, panel_out = (
        lax.all_gather(basis_in, "wide", axis=0, tiled=True),
        lax.all_gather(basis_out, "wide", axis=0, tiled=True),
    )
    rank_in = panel_in.shape[0]
    rank_out = panel_out.shape[0]
    quarter = rank_in // n_layer
    tok_in = acts.reshape(seq_dev * seq_len, ff_local)
    tok_out = grads.reshape(seq_dev * seq_len, d_local)
    positions = jnp.arange(seq_len, dtype=jnp.int32)
    alive = (positions[None, :] < counts[:, None]).astype(jnp.float32)
    alive_flat = alive.reshape(seq_dev * seq_len)
    rows = panel_in
    act_turned = lax.psum_scatter(
        lax.dot_general(rows, tok_in, (((1,), (1,)), ((), ())), preferred_element_type=jnp.float32),
        "layer",
        scatter_dimension=0,
        tiled=True,
    )
    act_mine = act_turned.T
    rows = panel_out
    grad_turned = lax.psum_scatter(
        lax.dot_general(
            tok_out, rows, (((1,), (1,)), ((), ())), preferred_element_type=jnp.float32
        ).T,
        "layer",
        scatter_dimension=0,
        tiled=True,
    )
    grad_share = (grad_turned.T * alive_flat[:, None]).astype(jnp.bfloat16)
    grad_rot = lax.all_gather(grad_share, "layer", axis=1, tiled=True)
    grad_rot = grad_rot.reshape(seq_dev, seq_len, rank_out)
    act_rot = act_mine.reshape(seq_dev, seq_len, quarter).astype(jnp.bfloat16)
    per_seq = jnp.einsum("stg,sta->sga", grad_rot, act_rot, preferred_element_type=jnp.float32)
    owners = n_wide * n_rep
    piece = rank_out // owners
    per_seq = per_seq.astype(jnp.bfloat16).reshape(seq_dev, owners, piece, quarter)
    train = lax.all_to_all(per_seq, ("wide", "rep"), split_axis=1, concat_axis=0, tiled=True)
    all_seqs = seq_dev * owners
    train = train.reshape(all_seqs, piece * quarter)
    n_query = query_grads.shape[0]
    weighted = (query_grads.astype(jnp.float32) / eigenvalues[None, :, :]).astype(jnp.bfloat16)
    weighted = weighted.reshape(n_query, piece * quarter)
    partial_value = lax.dot_general(
        weighted, train, (((1,), (1,)), ((), ())), preferred_element_type=jnp.float32
    )
    query_block = n_query // (n_layer * n_rep)
    seq_block = all_seqs // n_wide
    blocks = partial_value.reshape(n_layer * n_rep, query_block, n_wide, seq_block)
    blocks = blocks.transpose(2, 0, 1, 3).reshape(n_wide * n_layer * n_rep * query_block, seq_block)
    mine = lax.psum_scatter(blocks, ("wide", "layer", "rep"), scatter_dimension=0, tiled=True)
    n_blocks = candidate.shape[1]
    block_size = all_seqs // n_blocks
    seq_index = lax.axis_index("wide") * seq_block + jnp.arange(seq_block, dtype=jnp.int32)
    owner_block = seq_index // block_size
    one_hot = (owner_block[None, :] == jnp.arange(n_blocks, dtype=jnp.int32)[:, None]).astype(
        jnp.float32
    )
    keep_mask = jnp.dot(candidate.astype(jnp.float32), one_hot, preferred_element_type=jnp.float32)
    return mine * keep_mask


def solution(mesh):
    in_specs = (
        P(("groups", "wide", "rep"), None, "layer"),
        P(("groups", "wide", "rep"), None, "layer"),
        P(("groups", "wide", "rep")),
        P("wide", "layer"),
        P("wide", "layer"),
        P(None, ("wide", "rep"), "layer"),
        P(("wide", "rep"), "layer"),
        P(("layer", "rep"), "groups"),
    )
    out_specs = P(("layer", "rep"), ("groups", "wide"))
    return jax.shard_map(local, mesh=mesh, in_specs=in_specs, out_specs=out_specs, check_vma=False)
```

profile of v0, /device:TPU:0, one launch (start us, length us, event | category | flops | bytes accessed | tf_op | source)
XLA Modules:
  0.0 329.4 jit_solution(10190746982744180705)
XLA Ops:
  6.5 0.0 copy-start
  6.5 0.0 all-gather.3.cloned.1.call-start
  6.5 0.7 all-gather.3.cloned.1.call-update
  7.3 0.0 all-gather.5.cloned.1.call-start
  7.3 0.7 all-gather.5.cloned.1.call-update
  8.0 0.0 reduce-scatter.6.cloned.1.call-start
  8.1 58.4 %all-gather.3.cloned.1.call-done = bf16[512,2560]{1,0:T(8,128)(2,1)} async-done(((bf16[128,2560]{1,0:T(8,128)(2,1)}), bf16[512,2560]{1,0:T(8,128)(2,1)}) %all-gather.3.cloned.1.call-update) | async-done | bytes 2621456 | tf_op jit(solution)/shard_map/all_gather | solution.py:15
  66.5 0.0 copy-done
  66.5 4.2 %fusion.6 = f32[512,384]{1,0:T(8,128)} fusion(bf16[512,2560]{1,0:T(8,128)(2,1)} %all-gather.3.cloned.1.call-done, bf16[384,2560]{1,0:T(8,128)(2,1)S(1)} %bitcast.38), kind=kOutput, calls=%fused_computation.14 | convolution fusion | flops 1006632960 | bytes 5373952 | tf_op jit(solution)/shard_map/dot_general | solution.py:35
  70.6 0.0 reduce-scatter.6.cloned.1.call-update
  70.7 0.0 reduce-scatter.8.cloned.1.call-start
  70.7 124.3 %all-gather.5.cloned.1.call-done = bf16[512,6912]{1,0:T(8,128)(2,1)} async-done(((bf16[128,6912]{1,0:T(8,128)(2,1)}), bf16[512,6912]{1,0:T(8,128)(2,1)}) %all-gather.5.cloned.1.call-update) | async-done | bytes 7077904 | tf_op jit(solution)/shard_map/all_gather | solution.py:14
  195.1 0.0 copy-start.2
  195.1 9.2 %fusion.7 = f32[512,384]{1,0:T(8,128)} fusion(bf16[512,6912]{1,0:T(8,128)(2,1)} %all-gather.5.cloned.1.call-done, bf16[384,6912]{1,0:T(8,128)(2,1)} %bitcast.44), kind=kOutput, calls=%fused_computation.15 | convolution fusion | flops 2717908992 | bytes 13172736 | tf_op jit(solution)/shard_map/dot_general | solution.py:27
  204.3 0.0 reduce-scatter.8.cloned.1.call-update
  204.3 0.0 copy-done.2
  204.3 0.1 convert_bitcast_fusion.1
  204.4 8.6 %reduce-scatter.6.cloned.1.call-done = f32[256,384]{1,0:T(8,128)} async-done(((f32[512,384]{1,0:T(8,128)}), f32[256,384]{1,0:T(8,128)}) %reduce-scatter.6.cloned.1.call-update) | async-done | bytes 393232 | tf_op jit(solution)/shard_map/reduce_scatter | solution.py:34
  213.0 1.0 fusion.5
  214.0 7.3 %all_gather.10 = bf16[384,512]{0,1:T(8,128)(2,1)S(1)} all-gather(bf16[384,256]{0,1:T(8,128)(2,1)S(1)} %fusion.5), channel_id=1, replica_groups=mesh['groups'=2,'wide'=4,'layer'=2,'rep'=2] {'layer'}, dimensions={1}, use_global_device_ids=true | all-gather | bytes 589824 | tf_op jit(solution)/shard_map/all_gather | solution.py:43
  221.3 0.2 copy.17
  221.5 0.0 copy-start.1
  221.5 11.1 %reduce-scatter.8.cloned.1.call-done = f32[256,384]{1,0:T(8,128)} async-done(((f32[512,384]{1,0:T(8,128)}), f32[256,384]{1,0:T(8,128)}) %reduce-scatter.8.cloned.1.call-update) | async-done | bytes 393232 | tf_op jit(solution)/shard_map/reduce_scatter | solution.py:26
  232.7 1.0 convert_bitcast_fusion
  233.7 0.1 copy.18
  233.8 0.4 convolution_convert_fusion
  234.3 1.0 copy.20
  235.2 4.6 %all-to-all-start = ((bf16[3,8,64,256]{3,2,0,1:T(8,128)(2,1)}), bf16[3,8,64,256]{3,2,0,1:T(8,128)(2,1)S(1)}, u32[]{:S(2)}, u32[]{:S(2)}) async-start(bf16[3,8,64,256]{3,2,0,1:T(8,128)(2,1)} %copy.20), calls=%async_computation.2 | async-start | bytes 1572864 | tf_op jit(solution)/shard_map/all_to_all | solution.py:50
  239.8 0.0 reduce-scatter.10.cloned.1.call-start
  239.9 0.0 copy-done.1
  239.9 3.5 %divide_convert_fusion = bf16[64,64,256]{2,1,0:T(8,128)(2,1)} fusion(bf16[64,64,256]{2,1,0:T(8,128)(2,1)} %param.13, f32[64,256]{1,0:T(8,128)S(1)} %copy-done.1), kind=kLoop, calls=%fused_computation | loop fusion | flops 3145728 | bytes 4259840 | tf_op jit(solution)/shard_map/convert_element_type | solution.py:54
  243.4 0.0 copy-start.3
  243.4 4.2 %reshape.57 = bf16[4,16,16384,1]{2,1,0,3:T(8,128)(2,1)} reshape(bf16[64,64,256]{2,1,0:T(8,128)(2,1)} %divide_convert_fusion) | data formatting | bytes 4194304 | tf_op jit(solution)/shard_map/dot_general | solution.py:56
  247.6 0.0 copy-done.3
  247.6 13.2 %all-to-all-done = bf16[3,8,64,256]{3,2,0,1:T(8,128)(2,1)S(1)} async-done(((bf16[3,8,64,256]{3,2,0,1:T(8,128)(2,1)}), bf16[3,8,64,256]{3,2,0,1:T(8,128)(2,1)S(1)}, u32[]{:S(2)}, u32[]{:S(2)}) %all-to-all-start) | async-done | bytes 786464 | tf_op jit(solution)/shard_map/all_to_all | solution.py:50
  260.8 1.8 reshape.58
  262.6 4.8 %fusion.2 = f32[4,4,16,6]{2,3,0,1:T(8,128)S(1)} fusion(bf16[4,6,16384,1]{2,1,0,3:T(8,128)(2,1)} %reshape.58, bf16[4,16,16384,1]{2,1,0,3:T(8,128)(2,1)} %reshape.57), kind=kOutput, calls=%fused_computation.4 | convolution fusion | flops 50331648 | bytes 2889728 | tf_op jit(solution)/shard_map/dot_general | solution.py:56
  267.4 0.8 copy.26
  268.3 0.0 reduce-scatter.10.cloned.1.call-update
  268.3 53.2 %reduce-scatter.10.cloned.1.call-done = f32[16,6]{1,0:T(8,128)} async-done(((f32[256,6]{1,0:T(8,128)}), f32[16,6]{1,0:T(8,128)}) %reduce-scatter.10.cloned.1.call-update) | async-done | bytes 400
  321.5 0.8 copy.25
  322.3 0.7 bitcast_multiply_fusion
  (2 shorter events, 0.0 us)
Async XLA Ops:
  6.5 59.9 %copy-start = (bf16[3,128,2560]{2,1,0:T(8,128)(2,1)S(1)}, bf16[3,128,2560]{2,1,0:T(8,128)(2,1)}, u32[]{:S(2)}) copy-start(bf16[3,128,2560]{2,1,0:T(8,128)(2,1)} %param.9) | copy-start | bytes 5898244
  6.5 59.9 %all-gather.3.cloned.1.call-start = ((), (), s32[]{:S(2)}) async-start(), calls=%async_computation.4 | async-start | bytes 3276800 | tf_op jit(solution)/shard_map/all_gather | solution.py:15
  7.3 187.8 %all-gather.5.cloned.1.call-start = ((), (), s32[]{:S(2)}) async-start(), calls=%async_computation.6 | async-start | bytes 8847360 | tf_op jit(solution)/shard_map/all_gather | solution.py:14
  8.0 205.0 %reduce-scatter.6.cloned.1.call-start = ((), (), s32[]{:S(2)}) async-start(), calls=%async_computation.5 | async-start | bytes 1179648 | tf_op jit(solution)/shard_map/reduce_scatter | solution.py:34
  70.7 162.0 %reduce-scatter.8.cloned.1.call-start = ((), (), s32[]{:S(2)}) async-start(), calls=%async_computation.7 | async-start | bytes 1179648 | tf_op jit(solution)/shard_map/reduce_scatter | solution.py:26
  195.1 9.3 %copy-start.2 = (s32[3]{0:T(128)S(1)}, s32[3]{0:T(128)}, u32[]{:S(2)}) copy-start(s32[3]{0:T(128)} %param.10) | copy-start | bytes 40
  221.5 18.3 %copy-start.1 = (f32[64,256]{1,0:T(8,128)S(1)}, f32[64,256]{1,0:T(8,128)}, u32[]{:S(2)}) copy-start(f32[64,256]{1,0:T(8,128)} %param.14) | copy-start | bytes 196612
  235.2 25.6 %all-to-all-start = ((bf16[3,8,64,256]{3,2,0,1:T(8,128)(2,1)}), bf16[3,8,64,256]{3,2,0,1:T(8,128)(2,1)S(1)}, u32[]{:S(2)}, u32[]{:S(2)}) async-start(bf16[3,8,64,256]{3,2,0,1:T(8,128)(2,1)} %copy.20), calls=%async_computation.2 | async-start | bytes 1572864 | tf_op jit(solution)/shard_map/all_to_all | solution.py:50
  239.8 81.7 %reduce-scatter.10.cloned.1.call-start = ((), (), s32[]{:S(2)}) async-start(), calls=%async_computation.8 | async-start | bytes 139264
  243.4 4.2 %copy-start.3 = (s32[16,1]{0,1:T(1,128)S(1)}, s32[16,1]{0,1:T(1,128)}, u32[]{:S(2)}) copy-start(s32[16,1]{0,1:T(1,128)} %param.15) | copy-start | bytes 196
Sparse Core Ops, SparseCore 0:
  8.9 57.4 all-gather.2
  68.0 126.9 all-gather.4
  197.3 15.6 reduce-scatter.5
  215.2 17.4 reduce-scatter.7
  268.4 53.0 reduce-scatter.9
where the time goes:
time: 330 us; the launch traced here: 329 us
  waiting for transfers between devices  270 us (82%)
  matrix products  18.7 us (6%)
  between operations  13.2 us (4%)
  local copies, waits for them, and re-layouts  8.95 us (3%)
  blocking collectives  7.31 us (2%)
  other arithmetic  6.32 us (2%)
  starting transfers between devices  4.75 us (1%)
    all_gather x1, waiting for transfers between devices, local(): lax.all_gather(basis_in, 'wide', axis=0, tiled=True)  124 us
    all_gather x1, waiting for transfers between devices, local(): lax.all_gather(basis_out, 'wide', axis=0, tiled=True)  58.4 us
    unnamed x6, waiting for transfers between devices  54.6 us
    all_to_all x1, waiting for transfers between devices, local(): lax.all_to_all(per_seq, ('wide', 'rep'), split_axis=1, concat_axis=0, til...  13.2 us
    reduce_scatter x1, waiting for transfers between devices, local(): lax.psum_scatter(lax.dot_general(rows, tok_in, (((1,), (1,)), ((), ())),...  11.1 us
    dot_general x1, matrix products, local(): lax.dot_general(rows, tok_in, (((1,), (1,)), ((), ())), preferred_element...  9.25 us
    reduce_scatter x1, waiting for transfers between devices, local(): lax.psum_scatter(lax.dot_general(tok_out, rows, (((1,), (1,)), ((), ())),...  8.59 us
    all_gather x1, blocking collectives, local(): grad_rot = lax.all_gather(grad_share, 'layer', axis=1, tiled=True)  7.31 us
  transfers between devices with their start and end apart: 6, of which 6 were waited for; matrix products, arithmetic and copies ran while one was open for 7% of the time, Pallas kernels for 0%

commit v1 on v0

v1 whole, which is shorter than its diff:
```python
import jax
import jax.numpy as jnp
from jax import lax
from jax.sharding import PartitionSpec as P


def swap_pairs(size, valid):
    return [(a * size + k, (1 - a) * size + k) for a in range(2) for k in range(size) if valid(k)]


def gather_rounds(own, n_wide):
    rounds = []
    held = own
    for k in range(1, n_wide):
        pairs = [(2 * w, 2 * w + 2) for w in range(k - 1, n_wide - 1)]
        pairs += [(2 * w + 3, 2 * w + 1) for w in range(0, n_wide - k)]
        held = lax.ppermute(held, ("wide", "rep"), pairs)

        def valid(place, k=k):
            w, r = divmod(place, 2)
            return w >= k if r == 0 else w <= n_wide - 1 - k

        other = lax.ppermute(held, ("groups", "wide", "rep"), swap_pairs(2 * n_wide, valid))
        across = [(p, p ^ 1) for p in range(2 * n_wide) if valid(p)]
        rounds.append(
            (
                held,
                other,
                lax.ppermute(held, ("wide", "rep"), across),
                lax.ppermute(other, ("wide", "rep"), across),
            )
        )
    return rounds


def turn(pieces, tokens):
    return lax.dot_general(
        jnp.concatenate(pieces, axis=0), tokens, (((1,), (1,)), ((), ())), preferred_element_type=jnp.float32
    )


def local(acts, grads, counts, basis_in, basis_out, query_grads, eigenvalues, candidate):
    seq_dev, seq_len, ff_local = acts.shape
    d_local = grads.shape[2]
    n_wide = lax.axis_size("wide")
    n_layer = lax.axis_size("layer")
    group, wide, layer, rep = (lax.axis_index(a) for a in ("groups", "wide", "layer", "rep"))
    n_tok = seq_dev * seq_len
    tok_in = acts.reshape(n_tok, ff_local)
    tok_out = grads.reshape(n_tok, d_local)
    rows_in, rows_out = basis_in.shape[0], basis_out.shape[0]

    def rotate(basis, tokens):
        rows = basis.shape[0]
        half = rows // 2
        own = lax.dynamic_slice_in_dim(basis, group * half, half, axis=0)
        rounds = gather_rounds(own, n_wide)
        slots = [turn([basis], tokens)]
        below, above = {}, {}
        for k, pieces in enumerate(rounds, start=1):
            y = turn(list(pieces), tokens).reshape(2, 2, half, n_tok)
            y = jnp.where(group == 0, y, y[:, ::-1]).reshape(2, rows, n_tok)
            below[k] = jnp.where(rep == 0, y[0], y[1])
            above[k] = jnp.where(rep == 0, y[1], y[0])
        for n in range(1, n_wide):
            slots.append(jnp.where(wide + n <= n_wide - 1, above[n], below[n_wide - n]))
        return jnp.stack(slots)

    grad_part = rotate(basis_out, tok_out).reshape(n_wide * rows_out, n_tok)
    act_part = rotate(basis_in, tok_in).reshape(n_wide * rows_in, n_tok)

    rank_in = n_wide * rows_in
    share = rank_in // n_layer
    doubled = jnp.concatenate([act_part, act_part], axis=0)

    def act_block(owner):
        return lax.dynamic_slice_in_dim(doubled, (owner * share - wide * rows_in) % rank_in, share, axis=0)

    grad_sum = grad_part
    act_sum = act_block(layer)
    grad_sent = grad_part.astype(jnp.bfloat16)
    for m in range(1, n_layer):
        shift = [(i, (i + m) % n_layer) for i in range(n_layer)]
        grad_sum = grad_sum + lax.ppermute(grad_sent, "layer", shift).astype(jnp.float32)
        act_sent = act_block((layer + m) % n_layer).astype(jnp.bfloat16)
        act_sum = act_sum + lax.ppermute(act_sent, "layer", shift).astype(jnp.float32)
    positions = jnp.arange(seq_len, dtype=jnp.int32)
    alive = (positions[None, :] < counts[:, None]).astype(jnp.float32).reshape(n_tok)
    grad_rot = (grad_sum * alive[None, :]).astype(jnp.bfloat16).reshape(n_wide * rows_out, seq_dev, seq_len)
    act_rot = act_sum.astype(jnp.bfloat16).reshape(share, seq_dev, seq_len)
    train = jnp.einsum("gst,ast->sga", grad_rot, act_rot, preferred_element_type=jnp.float32).astype(jnp.bfloat16)

    piece = rows_out // 2
    train = train.reshape(seq_dev, n_wide, 2, piece, share)
    mine = lax.dynamic_index_in_dim(train, rep, axis=2, keepdims=False)
    theirs = lax.ppermute(
        lax.dynamic_index_in_dim(train, 1 - rep, axis=2, keepdims=False), "rep", [(0, 1), (1, 0)]
    )
    both = jnp.stack([jnp.where(rep == 0, mine, theirs), jnp.where(rep == 0, theirs, mine)])
    both = both.reshape(2 * seq_dev, n_wide, piece, share)
    arrived = [both[:, 0]]
    for n in range(1, n_wide):
        shift = [(w, (w + n) % n_wide) for w in range(n_wide)]
        arrived.append(lax.ppermute(both[:, n], "wide", shift))
    chip_seqs = 2 * seq_dev
    train = jnp.stack(arrived).reshape(n_wide * chip_seqs, piece * share)

    n_query = query_grads.shape[0]
    weighted = (query_grads.astype(jnp.float32) / eigenvalues[None, :, :]).astype(jnp.bfloat16)
    weighted = weighted.reshape(n_query, piece * share)
    partial_value = lax.dot_general(weighted, train, (((1,), (1,)), ((), ())), preferred_element_type=jnp.float32)

    block = n_query // (2 * n_layer)
    part = partial_value.reshape(n_layer, 2, block, n_wide, chip_seqs)
    part = lax.dynamic_index_in_dim(part, rep, axis=1, keepdims=False) + lax.ppermute(
        lax.dynamic_index_in_dim(part, 1 - rep, axis=1, keepdims=False), "rep", [(0, 1), (1, 0)]
    )
    total = lax.dynamic_index_in_dim(part, layer, axis=0, keepdims=False)
    for m in range(1, n_layer):
        shift = [(i, (i + m) % n_layer) for i in range(n_layer)]
        total = total + lax.ppermute(
            lax.dynamic_index_in_dim(part, (layer + m) % n_layer, axis=0, keepdims=False), "layer", shift
        )
    scores = total[:, 0]
    for n in range(1, n_wide):
        shift = [(w, (w - n) % n_wide) for w in range(n_wide)]
        scores = scores + lax.ppermute(total[:, n], "wide", shift)

    all_seqs = n_wide * chip_seqs
    n_blocks = candidate.shape[1]
    block_size = all_seqs // n_blocks
    seq_index = wide * chip_seqs + jnp.arange(chip_seqs, dtype=jnp.int32)
    one_hot = (seq_index[None, :] // block_size == jnp.arange(n_blocks, dtype=jnp.int32)[:, None]).astype(jnp.float32)
    keep_mask = jnp.dot(candidate.astype(jnp.float32), one_hot, preferred_element_type=jnp.float32)
    return scores * keep_mask


def solution(mesh):
    in_specs = (
        P(("groups", "wide", "rep"), None, "layer"),
        P(("groups", "wide", "rep"), None, "layer"),
        P(("groups", "wide", "rep")),
        P("wide", "layer"),
        P("wide", "layer"),
        P(None, ("wide", "rep"), "layer"),
        P(("wide", "rep"), "layer"),
        P(("layer", "rep"), "groups"),
    )
    out_specs = P(("layer", "rep"), ("groups", "wide"))
    return jax.shard_map(local, mesh=mesh, in_specs=in_specs, out_specs=out_specs, check_vma=False)
```

time: 330 us -> 151 us (0.46)
  waiting for transfers between devices: 270 us -> 42.8 us
  starting transfers between devices: 4.75 us -> 57.7 us
  between operations: 13.2 us -> 0.63 us
  other arithmetic: 6.32 us -> 15.1 us
  blocking collectives: 7.31 us -> 0 us
    all_gather x2 -> x0, waiting for transfers between devices: 183 us -> none  [the longest x1 124 us: local(): lax.all_gather(basis_in, 'wide', axis=0, tiled=True)]
    ppermute x0 -> x35, starting transfers between devices: none -> 57.7 us  [the longest x6 15.5 us: gather_rounds(): held = lax.ppermute(held, ('wide', 'rep'), pairs)]
    unnamed x6 -> x0, waiting for transfers between devices: 54.6 us -> none
    ppermute x0 -> x35, waiting for transfers between devices: none -> 42.8 us  [the longest x6 13.8 us: gather_rounds(): lax.ppermute(other, ('wide', 'rep'), across)]
    reduce_scatter x2 -> x0, waiting for transfers between devices: 19.7 us -> none  [the longest x1 11.1 us: local(): lax.psum_scatter(lax.dot_general(rows, tok_in, (((1,), (1,)), ((), ())),...]
    all_to_all x1 -> x0, waiting for transfers between devices: 13.2 us -> none  [local(): lax.all_to_all(per_seq, ('wide', 'rep'), split_axis=1, concat_axis=0, til...]
    concatenate x0 -> x6, other arithmetic: none -> 8.52 us  [turn(): jnp.concatenate(pieces, axis=0)]
    all_gather x1 -> x0, blocking collectives: 7.31 us -> none  [local(): grad_rot = lax.all_gather(grad_share, 'layer', axis=1, tiled=True)]
  transfers between devices with their start and end apart: 6 -> 35, of which waited for: 6 -> 13; matrix products, arithmetic and copies ran while one was open for 7% -> 27% of each run, Pallas kernels for 0% -> 0%
where the time goes in v1:
time: 151 us; the launch traced here: 150 us
  starting transfers between devices  57.7 us (38%)
  waiting for transfers between devices  42.8 us (28%)
  matrix products  21.8 us (14%)
  other arithmetic  15.1 us (10%)
  local copies, waits for them, and re-layouts  11.9 us (8%)
    dot_general x8, matrix products, turn(): lax.dot_general(jnp.concatenate(pieces, axis=0), tokens, (((1,), (1,)), (...  16.8 us
    ppermute x6, starting transfers between devices, gather_rounds(): held = lax.ppermute(held, ('wide', 'rep'), pairs)  15.5 us
    ppermute x6, waiting for transfers between devices, gather_rounds(): lax.ppermute(other, ('wide', 'rep'), across)  13.8 us
    ppermute x6, waiting for transfers between devices, gather_rounds(): lax.ppermute(held, ('wide', 'rep'), across)  8.88 us
    ppermute x3, starting transfers between devices, local(): arrived.append(lax.ppermute(both[:, n], 'wide', shift))  8.69 us
    concatenate x6, other arithmetic, turn(): jnp.concatenate(pieces, axis=0)  8.52 us
    ppermute x6, starting transfers between devices, gather_rounds(): lax.ppermute(other, ('wide', 'rep'), across)  7.9 us
    ppermute x6, starting transfers between devices, gather_rounds(): lax.ppermute(held, ('wide', 'rep'), across)  7.73 us
  transfers between devices with their start and end apart: 35, of which 13 were waited for; matrix products, arithmetic and copies ran while one was open for 27% of the time, Pallas kernels for 0%

profile of v1, /device:TPU:0, one launch (start us, length us, event | category | flops | bytes accessed | tf_op | source)
XLA Modules:
  0.0 149.9 jit_solution(9832236462264568525)
XLA Ops:
  0.0 1.1 constant_dynamic-slice_fusion.1
  1.2 5.8 %collective-permute-start = (bf16[64,2560]{1,0:T(8,128)(2,1)S(1)}, bf16[64,2560]{1,0:T(8,128)(2,1)}, u32[]{:S(2)}, u32[]{:S(2)}) collective-permute-start(bf16[64,2560]{1,0:T(8,128)(2,1)S(1)} %constant_dynamic-slice_fusion.1), channel_id=1, source_target_pairs={{0,4},{4,8},{8,12},{5,1},{9,5},{13,9},{2,6},{6,10},{10,14},{7,3},{... | collective-permute-start | bytes 983048 | tf_op jit(solution)/shard_map/ppermute | solution.py:17
  6.9 1.2 constant_dynamic-slice_fusion
  8.2 3.7 %collective-permute-start.13 = (bf16[64,6912]{1,0:T(8,128)(2,1)S(1)}, bf16[64,6912]{1,0:T(8,128)(2,1)}, u32[]{:S(2)}, u32[]{:S(2)}) collective-permute-start(bf16[64,6912]{1,0:T(8,128)(2,1)S(1)} %constant_dynamic-slice_fusion), channel_id=1, source_target_pairs={{0,4},{4,8},{8,12},{5,1},{9,5},{13,9},{2,6},{6,10},{10,14},{7,3},{... | collective-permute-start | bytes 2654216 | tf_op jit(solution)/shard_map/ppermute | solution.py:17
  11.9 1.4 collective-permute-start.4
  13.3 1.4 collective-permute-start.1
  14.7 4.9 %convolution_bitcast_fusion = f32[1,128,384]{2,1,0:T(8,128)} fusion(bf16[128,6912]{1,0:T(8,128)(2,1)S(1)} %copy-done.1, bf16[384,6912]{1,0:T(8,128)(2,1)} %bitcast.123), kind=kOutput, calls=%fused_computation.14 | convolution fusion | flops 679477248 | bytes 7274496 | tf_op jit(solution)/shard_map/dot_general | solution.py:37
  19.6 1.3 collective-permute-start.2
  20.9 1.4 collective-permute-start.5
  22.3 1.4 collective-permute-start.9
  23.7 1.3 collective-permute-start.3
  25.8 1.3 collective-permute-start.10
  27.2 1.6 %collective-permute-start.17 = (bf16[64,6912]{1,0:T(8,128)(2,1)}, bf16[64,6912]{1,0:T(8,128)(2,1)}, u32[]{:S(2)}, u32[]{:S(2)}) collective-permute-start(bf16[64,6912]{1,0:T(8,128)(2,1)} %collective-permute-done.13), channel_id=1, source_target_pairs={{4,8},{8,12},{5,1},{9,5},{6,10},{10,14},{7,3},{11,7},{20,24},{24,2... | collective-permute-start | bytes 2654216 | tf_op jit(solution)/shard_map/ppermute | solution.py:17
  28.8 1.6 %collective-permute-start.14 = (bf16[64,6912]{1,0:T(8,128)(2,1)}, bf16[64,6912]{1,0:T(8,128)(2,1)}, u32[]{:S(2)}, u32[]{:S(2)}) collective-permute-start(bf16[64,6912]{1,0:T(8,128)(2,1)} %collective-permute-done.13), channel_id=1, source_target_pairs={{1,17},{4,20},{5,21},{8,24},{9,25},{12,28},{17,1},{20,4},{21,5},{2... | collective-permute-start | bytes 2654216 | tf_op jit(solution)/shard_map/ppermute | solution.py:23
  31.0 1.3 collective-permute-start.11
  32.3 1.4 pad_maximum_fusion.3
  33.7 0.9 fusion.20
  34.6 1.3 collective-permute-start.15
  35.9 1.3 collective-permute-start.7
  37.2 4.9 %collective-permute-done.11 = bf16[64,2560]{1,0:T(8,128)(2,1)S(1)} collective-permute-done((bf16[64,2560]{1,0:T(8,128)(2,1)}, bf16[64,2560]{1,0:T(8,128)(2,1)S(1)}, u32[]{:S(2)}, u32[]{:S(2)}) %collective-permute-start.11) | collective-permute-done | bytes 327712 | tf_op jit(solution)/shard_map/ppermute | solution.py:30
  42.1 1.3 collective-permute-start.8
  43.4 1.2 pad_maximum_fusion.5
  44.5 0.9 fusion.22
  45.4 8.9 %collective-permute-done.7 = bf16[64,2560]{1,0:T(8,128)(2,1)S(1)} collective-permute-done((bf16[64,2560]{1,0:T(8,128)(2,1)}, bf16[64,2560]{1,0:T(8,128)(2,1)S(1)}, u32[]{:S(2)}, u32[]{:S(2)}) %collective-permute-start.7) | collective-permute-done | bytes 327712 | tf_op jit(solution)/shard_map/ppermute | solution.py:29
  54.3 1.1 collective-permute-done.8
  55.4 1.1 pad_maximum_fusion.4
  56.4 1.6 %collective-permute-start.18 = (bf16[64,6912]{1,0:T(8,128)(2,1)}, bf16[64,6912]{1,0:T(8,128)(2,1)}, u32[]{:S(2)}, u32[]{:S(2)}) collective-permute-start(bf16[64,6912]{1,0:T(8,128)(2,1)} %collective-permute-done.17), channel_id=1, source_target_pairs={{8,12},{5,1},{10,14},{7,3},{24,28},{21,17},{26,30},{23,19}} | collective-permute-start | bytes 2654216 | tf_op jit(solution)/shard_map/ppermute | solution.py:17
  58.0 1.6 %collective-permute-start.22 = (bf16[64,6912]{1,0:T(8,128)(2,1)}, bf16[64,6912]{1,0:T(8,128)(2,1)}, u32[]{:S(2)}, u32[]{:S(2)}) collective-permute-start(bf16[64,6912]{1,0:T(8,128)(2,1)} %collective-permute-done.17), channel_id=1, source_target_pairs={{1,17},{5,21},{8,24},{12,28},{17,1},{21,5},{24,8},{28,12},{3,19},{... | collective-permute-start | bytes 2654216 | tf_op jit(solution)/shard_map/ppermute | solution.py:23
  59.6 1.3 collective-permute-start.16
  60.9 0.9 fusion.21
  63.1 1.5 collective-permute-start.12
  64.6 1.3 collective-permute-start.23
  66.6 1.3 collective-permute-start.20
  67.9 1.3 collective-permute-start.24
  69.2 2.1 %pad_maximum_fusion = bf16[256,6912]{1,0:T(8,128)(2,1)S(1)} fusion(bf16[64,6912]{1,0:T(8,128)(2,1)} %collective-permute-done.16, bf16[64,6912]{1,0:T(8,128)(2,1)} %collective-permute-done.15, bf16[64,6912]{1,0:T(8,128)(2,1)} %collective-permute-done.14, bf16[64,6912]{1,0:T(8,128)(2,1)} %collective-permute-done.13), kind=kLoop, calls=%fused_computation.1 | loop fusion | flops 14155776 | bytes 7077888 | tf_op jit(solution)/shard_map/concatenate | solution.py:38
  71.4 4.7 %fusion.23 = f32[2,2,64,384]{3,2,1,0:T(8,128)S(1)} fusion(bf16[2,2,64,6912]{3,2,1,0:T(8,128)(2,1)S(1)} %bitcast.132, bf16[384,6912,1,1]{1,0,3,2:T(8,128)(2,1)} %bitcast.124), kind=kOutput, calls=%fused_computation.76 | convolution fusion | flops 1358954496 | bytes 9240576 | tf_op jit(solution)/shard_map/dot_general | solution.py:37
  76.1 1.5 collective-permute-start.21
  77.6 1.1 collective-permute-done.24
  78.7 1.6 %pad_maximum_fusion.2 = bf16[256,6912]{1,0:T(8,128)(2,1)S(1)} fusion(bf16[64,6912]{1,0:T(8,128)(2,1)S(1)} %collective-permute-done.24, bf16[64,6912]{1,0:T(8,128)(2,1)S(1)} %collective-permute-done.23, bf16[64,6912]{1,0:T(8,128)(2,1)} %collective-permute-done.22, bf16[64,6912]{1,0:T(8,128)(2,1)} %collective-permute-done.17), kind=kLoop, calls=%fused_computation.3 | loop fusion | flops 14155776 | bytes 7077888 | tf_op jit(solution)/shard_map/concatenate | solution.py:38
  80.3 2.0 %fusion.25 = f32[2,2,64,384]{3,2,1,0:T(8,128)S(1)} fusion(bf16[2,2,64,6912]{3,2,1,0:T(8,128)(2,1)S(1)} %bitcast.133, bf16[384,6912,1,1]{1,0,3,2:T(8,128)(2,1)S(1)} %bitcast.127), kind=kOutput, calls=%fused_computation.78 | convolution fusion | flops 1358954496 | bytes 9240576 | tf_op jit(solution)/shard_map/dot_general | solution.py:37
  82.3 6.6 %collective-permute-done.21 = bf16[64,6912]{1,0:T(8,128)(2,1)S(1)} collective-permute-done((bf16[64,6912]{1,0:T(8,128)(2,1)S(1)}, bf16[64,6912]{1,0:T(8,128)(2,1)S(1)}, u32[]{:S(2)}, u32[]{:S(2)}) %collective-permute-start.21) | collective-permute-done | bytes 884768 | tf_op jit(solution)/shard_map/ppermute | solution.py:30
  89.0 1.3 pad_maximum_fusion.1
  90.3 2.0 %fusion.24 = f32[2,2,64,384]{3,2,1,0:T(8,128)S(1)} fusion(bf16[2,2,64,6912]{3,2,1,0:T(8,128)(2,1)S(1)} %bitcast.134, bf16[384,6912,1,1]{1,0,3,2:T(8,128)(2,1)S(1)} %bitcast.128), kind=kOutput, calls=%fused_computation.77 | convolution fusion | flops 1358954496 | bytes 9240576 | tf_op jit(solution)/shard_map/dot_general | solution.py:37
  93.2 0.9 pad_maximum_fusion.7
  94.2 1.4 copy.12
  95.8 1.6 %collective-permute-start.25 = (bf16[256,384]{0,1:T(8,128)(2,1)S(1)}, bf16[256,384]{0,1:T(8,128)(2,1)S(1)}, u32[]{:S(2)}, u32[]{:S(2)}) collective-permute-start(bf16[256,384]{0,1:T(8,128)(2,1)S(1)} %fusion.9), channel_id=1, source_target_pairs={{0,2},{2,0},{1,3},{3,1},{4,6},{6,4},{5,7},{7,5},{8,10},{10,8},{9,1... | collective-permute-start | bytes 589832 | tf_op jit(solution)/shard_map/ppermute | solution.py:86
  97.3 1.1 multiply_convert_fusion
  98.5 4.1 %collective-permute-done.25 = bf16[256,384]{0,1:T(8,128)(2,1)S(1)} collective-permute-done((bf16[256,384]{0,1:T(8,128)(2,1)S(1)}, bf16[256,384]{0,1:T(8,128)(2,1)S(1)}, u32[]{:S(2)}, u32[]{:S(2)}) %collective-permute-start.25) | collective-permute-done | bytes 196640 | tf_op jit(solution)/shard_map/ppermute | solution.py:86
  103.3 0.9 collective-permute-start.26
  104.2 1.3 collective-permute-done.26
  105.9 8.6 %collective-permute-start.28 = (bf16[6,64,256]{2,1,0:T(8,128)(2,1)S(1)}, bf16[6,64,256]{2,1,0:T(8,128)(2,1)}, u32[]{:S(2)}, u32[]{:S(2)}) collective-permute-start(bf16[6,64,256]{2,1,0:T(8,128)(2,1)S(1)} %get-tuple-element.8), channel_id=1, source_target_pairs={{0,8},{4,12},{8,0},{12,4},{1,9},{5,13},{9,1},{13,5},{2,10},{6,14},... | collective-permute-start | bytes 589832 | tf_op jit(solution)/shard_map/ppermute | solution.py:104
  114.5 1.9 %divide_convert_fusion = bf16[64,64,256]{2,1,0:T(8,128)(2,1)} fusion(bf16[64,64,256]{2,1,0:T(8,128)(2,1)S(1)} %copy-done.2, f32[64,256]{1,0:T(8,128)S(1)} %copy-done.5), kind=kLoop, calls=%fused_computation | loop fusion | flops 3145728 | bytes 4259840 | tf_op jit(solution)/shard_map/convert_element_type | solution.py:109
  116.4 4.2 %reshape.380 = bf16[2,2,16,16384,1]{3,2,1,0,4:T(8,128)(2,1)} reshape(bf16[64,64,256]{2,1,0:T(8,128)(2,1)} %divide_convert_fusion) | data formatting | bytes 4194304 | tf_op jit(solution)/shard_map/dot_general | solution.py:111
  120.9 1.2 stack.49
  122.0 5.8 %collective-permute-done.28 = bf16[6,64,256]{2,1,0:T(8,128)(2,1)} collective-permute-done((bf16[6,64,256]{2,1,0:T(8,128)(2,1)S(1)}, bf16[6,64,256]{2,1,0:T(8,128)(2,1)}, u32[]{:S(2)}, u32[]{:S(2)}) %collective-permute-start.28) | collective-permute-done | bytes 196640 | tf_op jit(solution)/shard_map/ppermute | solution.py:104
  127.8 1.2 stack.50
  129.2 4.6 %fusion = f32[2,2,16,4,6]{2,4,3,1,0:T(8,128)S(1)} fusion(bf16[2,2,16,16384,1]{3,2,1,0,4:T(8,128)(2,1)} %reshape.380, bf16[1,6,16384]{2,1,0:T(8,128)(2,1)S(1)} %stack.51, bf16[1,6,16384]{2,1,0:T(8,128)(2,1)S(1)} %stack.50, bf16[1,6,16384]{2,1,0:T(8,128)(2,1)S(1)} %stack.49, bf16[1,6,16384]{2,1,0:T(8,128)(2,1)S(1)} %stack.48), kind=kOutput, calls=%fused_computation.4 | convolution fusion | flops 53477376 | bytes 2889728 | tf_op jit(solution)/shard_map/dot_general | solution.py:111
  133.9 1.2 collective-permute-done.30
  135.1 1.6 %collective-permute-start.31 = (f32[16,4,6]{0,2,1:T(8,128)S(1)}, f32[16,4,6]{0,2,1:T(8,128)S(1)}, u32[]{:S(2)}, u32[]{:S(2)}) collective-permute-start(f32[16,4,6]{0,2,1:T(8,128)S(1)} %dynamic-slice_bitcast_fusion.2), channel_id=1, source_target_pairs={{0,2},{2,0},{1,3},{3,1},{4,6},{6,4},{5,7},{7,5},{8,10},{10,8},{9,1... | collective-permute-start | bytes 4616 | tf_op jit(solution)/shard_map/ppermute | solution.py:121
  136.7 2.2 %collective-permute-done.31 = f32[16,4,6]{0,2,1:T(8,128)S(1)} collective-permute-done((f32[16,4,6]{0,2,1:T(8,128)S(1)}, f32[16,4,6]{0,2,1:T(8,128)S(1)}, u32[]{:S(2)}, u32[]{:S(2)}) %collective-permute-start.31) | collective-permute-done | bytes 1568 | tf_op jit(solution)/shard_map/ppermute | solution.py:121
  138.9 3.3 %collective-permute-start.32 = (f32[16,6]{0,1:T(8,128)S(1)}, f32[16,6]{0,1:T(8,128)S(1)}, u32[]{:S(2)}, u32[]{:S(2)}) collective-permute-start(f32[16,6]{0,1:T(8,128)S(1)} %get-tuple-element.15), channel_id=1, source_target_pairs={{0,12},{4,0},{8,4},{12,8},{1,13},{5,1},{9,5},{13,9},{2,14},{6,2},{... | collective-permute-start | bytes 1160 | tf_op jit(solution)/shard_map/ppermute | solution.py:127
  142.2 1.6 %collective-permute-start.33 = (f32[16,6]{0,1:T(8,128)S(1)}, f32[16,6]{0,1:T(8,128)S(1)}, u32[]{:S(2)}, u32[]{:S(2)}) collective-permute-start(f32[16,6]{0,1:T(8,128)S(1)} %get-tuple-element.17), channel_id=1, source_target_pairs={{0,8},{4,12},{8,0},{12,4},{1,9},{5,13},{9,1},{13,5},{2,10},{6,14},... | collective-permute-start | bytes 1160 | tf_op jit(solution)/shard_map/ppermute | solution.py:127
  144.0 2.8 %collective-permute-done.33 = f32[16,6]{0,1:T(8,128)S(1)} collective-permute-done((f32[16,6]{0,1:T(8,128)S(1)}, f32[16,6]{0,1:T(8,128)S(1)}, u32[]{:S(2)}, u32[]{:S(2)}) %collective-permute-start.33) | collective-permute-done | bytes 416 | tf_op jit(solution)/shard_map/ppermute | solution.py:127
  146.8 2.5 %collective-permute-done.34 = f32[16,6]{0,1:T(8,128)S(1)} collective-permute-done((f32[16,6]{0,1:T(8,128)S(1)}, f32[16,6]{0,1:T(8,128)S(1)}, u32[]{:S(2)}, u32[]{:S(2)}) %collective-permute-start.34) | collective-permute-done | bytes 416 | tf_op jit(solution)/shard_map/ppermute | solution.py:127
  (80 shorter events, 7.1 us)
Async XLA Ops:
  0.0 25.1 %copy-start = (bf16[3,128,2560]{2,1,0:T(8,128)(2,1)S(1)}, bf16[3,128,2560]{2,1,0:T(8,128)(2,1)}, u32[]{:S(2)}) copy-start(bf16[3,128,2560]{2,1,0:T(8,128)(2,1)} %param.9) | copy-start | bytes 5898244
  0.0 14.7 %copy-start.1 = (bf16[128,6912]{1,0:T(8,128)(2,1)S(1)}, bf16[128,6912]{1,0:T(8,128)(2,1)}, u32[]{:S(2)}) copy-start(bf16[128,6912]{1,0:T(8,128)(2,1)} %param.11) | copy-start | bytes 5308420
  1.2 10.7 %collective-permute-start = (bf16[64,2560]{1,0:T(8,128)(2,1)S(1)}, bf16[64,2560]{1,0:T(8,128)(2,1)}, u32[]{:S(2)}, u32[]{:S(2)}) collective-permute-start(bf16[64,2560]{1,0:T(8,128)(2,1)S(1)} %constant_dynamic-slice_fusion.1), channel_id=1, source_target_pairs={{0,4},{4,8},{8,12},{5,1},{9,5},{13,9},{2,6},{6,10},{10,14},{7,3},{... | collective-permute-start | bytes 983048 | tf_op jit(solution)/shard_map/ppermute | solution.py:17
  8.2 19.0 %collective-permute-start.13 = (bf16[64,6912]{1,0:T(8,128)(2,1)S(1)}, bf16[64,6912]{1,0:T(8,128)(2,1)}, u32[]{:S(2)}, u32[]{:S(2)}) collective-permute-start(bf16[64,6912]{1,0:T(8,128)(2,1)S(1)} %constant_dynamic-slice_fusion), channel_id=1, source_target_pairs={{0,4},{4,8},{8,12},{5,1},{9,5},{13,9},{2,6},{6,10},{10,14},{7,3},{... | collective-permute-start | bytes 2654216 | tf_op jit(solution)/shard_map/ppermute | solution.py:17
  11.9 9.0 %collective-permute-start.4 = (bf16[64,2560]{1,0:T(8,128)(2,1)}, bf16[64,2560]{1,0:T(8,128)(2,1)}, u32[]{:S(2)}, u32[]{:S(2)}) collective-permute-start(bf16[64,2560]{1,0:T(8,128)(2,1)} %collective-permute-done), channel_id=1, source_target_pairs={{4,8},{8,12},{5,1},{9,5},{6,10},{10,14},{7,3},{11,7},{20,24},{24,2... | collective-permute-start | bytes 983048 | tf_op jit(solution)/shard_map/ppermute | solution.py:17
  13.3 10.4 %collective-permute-start.1 = (bf16[64,2560]{1,0:T(8,128)(2,1)}, bf16[64,2560]{1,0:T(8,128)(2,1)}, u32[]{:S(2)}, u32[]{:S(2)}) collective-permute-start(bf16[64,2560]{1,0:T(8,128)(2,1)} %collective-permute-done), channel_id=1, source_target_pairs={{1,17},{4,20},{5,21},{8,24},{9,25},{12,28},{17,1},{20,4},{21,5},{2... | collective-permute-start | bytes 983048 | tf_op jit(solution)/shard_map/ppermute | solution.py:23
  14.7 10.3 %copy-start.6 = (s32[3]{0:T(128)S(1)}, s32[3]{0:T(128)}, u32[]{:S(2)}) copy-start(s32[3]{0:T(128)} %param.10) | copy-start | bytes 40
  14.7 10.4 %copy-start.3 = (bf16[128,2560]{1,0:T(8,128)(2,1)S(1)}, bf16[128,2560]{1,0:T(8,128)(2,1)}, u32[]{:S(2)}) copy-start(bf16[128,2560]{1,0:T(8,128)(2,1)} %param.12) | copy-start | bytes 1966084
  19.6 6.2 %collective-permute-start.2 = (bf16[64,2560]{1,0:T(8,128)(2,1)}, bf16[64,2560]{1,0:T(8,128)(2,1)}, u32[]{:S(2)}, u32[]{:S(2)}) collective-permute-start(bf16[64,2560]{1,0:T(8,128)(2,1)} %collective-permute-done), channel_id=1, source_target_pairs={{1,0},{4,5},{5,4},{8,9},{9,8},{12,13},{3,2},{6,7},{7,6},{10,11},{1... | collective-permute-start | bytes 983048 | tf_op jit(solution)/shard_map/ppermute | solution.py:29
  20.9 7.9 %collective-permute-start.5 = (bf16[64,2560]{1,0:T(8,128)(2,1)}, bf16[64,2560]{1,0:T(8,128)(2,1)}, u32[]{:S(2)}, u32[]{:S(2)}) collective-permute-start(bf16[64,2560]{1,0:T(8,128)(2,1)} %collective-permute-done.4), channel_id=1, source_target_pairs={{8,12},{5,1},{10,14},{7,3},{24,28},{21,17},{26,30},{23,19}} | collective-permute-start | bytes 983048 | tf_op jit(solution)/shard_map/ppermute | solution.py:17
  22.3 8.0 %collective-permute-start.9 = (bf16[64,2560]{1,0:T(8,128)(2,1)}, bf16[64,2560]{1,0:T(8,128)(2,1)}, u32[]{:S(2)}, u32[]{:S(2)}) collective-permute-start(bf16[64,2560]{1,0:T(8,128)(2,1)} %collective-permute-done.4), channel_id=1, source_target_pairs={{1,17},{5,21},{8,24},{12,28},{17,1},{21,5},{24,8},{28,12},{3,19},{... | collective-permute-start | bytes 983048 | tf_op jit(solution)/shard_map/ppermute | solution.py:23
  23.7 7.3 %collective-permute-start.3 = (bf16[64,2560]{1,0:T(8,128)(2,1)}, bf16[64,2560]{1,0:T(8,128)(2,1)}, u32[]{:S(2)}, u32[]{:S(2)}) collective-permute-start(bf16[64,2560]{1,0:T(8,128)(2,1)} %collective-permute-done.1), channel_id=1, source_target_pairs={{1,0},{4,5},{5,4},{8,9},{9,8},{12,13},{3,2},{6,7},{7,6},{10,11},{1... | collective-permute-start | bytes 983048 | tf_op jit(solution)/shard_map/ppermute | solution.py:30
  25.8 8.7 %collective-permute-start.10 = (bf16[64,2560]{1,0:T(8,128)(2,1)}, bf16[64,2560]{1,0:T(8,128)(2,1)S(1)}, u32[]{:S(2)}, u32[]{:S(2)}) collective-permute-start(bf16[64,2560]{1,0:T(8,128)(2,1)} %collective-permute-done.4), channel_id=1, source_target_pairs={{1,0},{5,4},{8,9},{12,13},{3,2},{7,6},{10,11},{14,15},{17,16},{21,... | collective-permute-start | bytes 983048 | tf_op jit(solution)/shard_map/ppermute | solution.py:29
  27.2 29.3 %collective-permute-start.17 = (bf16[64,6912]{1,0:T(8,128)(2,1)}, bf16[64,6912]{1,0:T(8,128)(2,1)}, u32[]{:S(2)}, u32[]{:S(2)}) collective-permute-start(bf16[64,6912]{1,0:T(8,128)(2,1)} %collective-permute-done.13), channel_id=1, source_target_pairs={{4,8},{8,12},{5,1},{9,5},{6,10},{10,14},{7,3},{11,7},{20,24},{24,2... | collective-permute-start | bytes 2654216 | tf_op jit(solution)/shard_map/ppermute | solution.py:17
  28.8 30.9 %collective-permute-start.14 = (bf16[64,6912]{1,0:T(8,128)(2,1)}, bf16[64,6912]{1,0:T(8,128)(2,1)}, u32[]{:S(2)}, u32[]{:S(2)}) collective-permute-start(bf16[64,6912]{1,0:T(8,128)(2,1)} %collective-permute-done.13), channel_id=1, source_target_pairs={{1,17},{4,20},{5,21},{8,24},{9,25},{12,28},{17,1},{20,4},{21,5},{2... | collective-permute-start | bytes 2654216 | tf_op jit(solution)/shard_map/ppermute | solution.py:23
  30.3 5.6 %collective-permute-start.6 = (bf16[64,2560]{1,0:T(8,128)(2,1)}, bf16[64,2560]{1,0:T(8,128)(2,1)S(1)}, u32[]{:S(2)}, u32[]{:S(2)}) collective-permute-start(bf16[64,2560]{1,0:T(8,128)(2,1)} %collective-permute-done.5), channel_id=1, source_target_pairs={{1,17},{12,28},{17,1},{28,12},{3,19},{14,30},{19,3},{30,14}} | collective-permute-start | bytes 983048 | tf_op jit(solution)/shard_map/ppermute | solution.py:23
  31.0 11.0 %collective-permute-start.11 = (bf16[64,2560]{1,0:T(8,128)(2,1)}, bf16[64,2560]{1,0:T(8,128)(2,1)S(1)}, u32[]{:S(2)}, u32[]{:S(2)}) collective-permute-start(bf16[64,2560]{1,0:T(8,128)(2,1)} %collective-permute-done.9), channel_id=1, source_target_pairs={{1,0},{5,4},{8,9},{12,13},{3,2},{7,6},{10,11},{14,15},{17,16},{21,... | collective-permute-start | bytes 983048 | tf_op jit(solution)/shard_map/ppermute | solution.py:30
  34.6 30.0 %collective-permute-start.15 = (bf16[64,6912]{1,0:T(8,128)(2,1)}, bf16[64,6912]{1,0:T(8,128)(2,1)}, u32[]{:S(2)}, u32[]{:S(2)}) collective-permute-start(bf16[64,6912]{1,0:T(8,128)(2,1)} %collective-permute-done.13), channel_id=1, source_target_pairs={{1,0},{4,5},{5,4},{8,9},{9,8},{12,13},{3,2},{6,7},{7,6},{10,11},{1... | collective-permute-start | bytes 2654216 | tf_op jit(solution)/shard_map/ppermute | solution.py:29
  35.9 18.3 %collective-permute-start.7 = (bf16[64,2560]{1,0:T(8,128)(2,1)}, bf16[64,2560]{1,0:T(8,128)(2,1)S(1)}, u32[]{:S(2)}, u32[]{:S(2)}) collective-permute-start(bf16[64,2560]{1,0:T(8,128)(2,1)} %collective-permute-done.5), channel_id=1, source_target_pairs={{1,0},{12,13},{3,2},{14,15},{17,16},{28,29},{19,18},{30,31}} | collective-permute-start | bytes 983048 | tf_op jit(solution)/shard_map/ppermute | solution.py:29
  42.1 13.3 %collective-permute-start.8 = (bf16[64,2560]{1,0:T(8,128)(2,1)S(1)}, bf16[64,2560]{1,0:T(8,128)(2,1)S(1)}, u32[]{:S(2)}, u32[]{:S(2)}) collective-permute-start(bf16[64,2560]{1,0:T(8,128)(2,1)S(1)} %collective-permute-done.6), channel_id=1, source_target_pairs={{1,0},{12,13},{3,2},{14,15},{17,16},{28,29},{19,18},{30,31}} | collective-permute-start | bytes 983048 | tf_op jit(solution)/shard_map/ppermute | solution.py:30
  56.4 9.4 %collective-permute-start.18 = (bf16[64,6912]{1,0:T(8,128)(2,1)}, bf16[64,6912]{1,0:T(8,128)(2,1)}, u32[]{:S(2)}, u32[]{:S(2)}) collective-permute-start(bf16[64,6912]{1,0:T(8,128)(2,1)} %collective-permute-done.17), channel_id=1, source_target_pairs={{8,12},{5,1},{10,14},{7,3},{24,28},{21,17},{26,30},{23,19}} | collective-permute-start | bytes 2654216 | tf_op jit(solution)/shard_map/ppermute | solution.py:17
  58.0 8.6 %collective-permute-start.22 = (bf16[64,6912]{1,0:T(8,128)(2,1)}, bf16[64,6912]{1,0:T(8,128)(2,1)}, u32[]{:S(2)}, u32[]{:S(2)}) collective-permute-start(bf16[64,6912]{1,0:T(8,128)(2,1)} %collective-permute-done.17), channel_id=1, source_target_pairs={{1,17},{5,21},{8,24},{12,28},{17,1},{21,5},{24,8},{28,12},{3,19},{... | collective-permute-start | bytes 2654216 | tf_op jit(solution)/shard_map/ppermute | solution.py:23
  59.6 8.3 %collective-permute-start.16 = (bf16[64,6912]{1,0:T(8,128)(2,1)}, bf16[64,6912]{1,0:T(8,128)(2,1)}, u32[]{:S(2)}, u32[]{:S(2)}) collective-permute-start(bf16[64,6912]{1,0:T(8,128)(2,1)} %collective-permute-done.14), channel_id=1, source_target_pairs={{1,0},{4,5},{5,4},{8,9},{9,8},{12,13},{3,2},{6,7},{7,6},{10,11},{1... | collective-permute-start | bytes 2654216 | tf_op jit(solution)/shard_map/ppermute | solution.py:30
  63.1 34.2 %collective-permute-start.12 = (bf16[512,384]{0,1:T(8,128)(2,1)}, bf16[512,384]{0,1:T(8,128)(2,1)}, u32[]{:S(2)}, u32[]{:S(2)}) collective-permute-start(bf16[512,384]{0,1:T(8,128)(2,1)} %convert_element_type.43), channel_id=1, source_target_pairs={{0,2},{2,0},{1,3},{3,1},{4,6},{6,4},{5,7},{7,5},{8,10},{10,8},{9,1... | collective-permute-start | bytes 1179656 | tf_op jit(solution)/shard_map/ppermute | solution.py:84
  64.6 13.0 %collective-permute-start.23 = (bf16[64,6912]{1,0:T(8,128)(2,1)}, bf16[64,6912]{1,0:T(8,128)(2,1)S(1)}, u32[]{:S(2)}, u32[]{:S(2)}) collective-permute-start(bf16[64,6912]{1,0:T(8,128)(2,1)} %collective-permute-done.17), channel_id=1, source_target_pairs={{1,0},{5,4},{8,9},{12,13},{3,2},{7,6},{10,11},{14,15},{17,16},{21,... | collective-permute-start | bytes 2654216 | tf_op jit(solution)/shard_map/ppermute | solution.py:29
  65.9 10.2 %collective-permute-start.19 = (bf16[64,6912]{1,0:T(8,128)(2,1)}, bf16[64,6912]{1,0:T(8,128)(2,1)S(1)}, u32[]{:S(2)}, u32[]{:S(2)}) collective-permute-start(bf16[64,6912]{1,0:T(8,128)(2,1)} %collective-permute-done.18), channel_id=1, source_target_pairs={{1,17},{12,28},{17,1},{28,12},{3,19},{14,30},{19,3},{30,14}} | collective-permute-start | bytes 2654216 | tf_op jit(solution)/shard_map/ppermute | solution.py:23
  66.6 15.7 %collective-permute-start.20 = (bf16[64,6912]{1,0:T(8,128)(2,1)}, bf16[64,6912]{1,0:T(8,128)(2,1)S(1)}, u32[]{:S(2)}, u32[]{:S(2)}) collective-permute-start(bf16[64,6912]{1,0:T(8,128)(2,1)} %collective-permute-done.18), channel_id=1, source_target_pairs={{1,0},{12,13},{3,2},{14,15},{17,16},{28,29},{19,18},{30,31}} | collective-permute-start | bytes 2654216 | tf_op jit(solution)/shard_map/ppermute | solution.py:29
  67.9 10.8 %collective-permute-start.24 = (bf16[64,6912]{1,0:T(8,128)(2,1)}, bf16[64,6912]{1,0:T(8,128)(2,1)S(1)}, u32[]{:S(2)}, u32[]{:S(2)}) collective-permute-start(bf16[64,6912]{1,0:T(8,128)(2,1)} %collective-permute-done.22), channel_id=1, source_target_pairs={{1,0},{5,4},{8,9},{12,13},{3,2},{7,6},{10,11},{14,15},{17,16},{21,... | collective-permute-start | bytes 2654216 | tf_op jit(solution)/shard_map/ppermute | solution.py:30
  71.4 8.9 %slice-start = ((s8[5308416]{0:T(1024)(128)(4,1)}), s8[4194304]{0:T(1024)(128)(4,1)S(1)}, s32[]{:S(2)}) async-start(s8[5308416]{0:T(1024)(128)(4,1)} %bitcast.125), calls=%async_computation | async-start | bytes 8388608
  71.4 8.9 %slice-start.1 = ((s8[5308416]{0:T(1024)(128)(4,1)}), s8[1114112]{0:T(1024)(128)(4,1)S(1)}, s32[]{:S(2)}) async-start(s8[5308416]{0:T(1024)(128)(4,1)} %bitcast.125), calls=%async_computation.1 | async-start | bytes 2228224
  76.1 12.9 %collective-permute-start.21 = (bf16[64,6912]{1,0:T(8,128)(2,1)S(1)}, bf16[64,6912]{1,0:T(8,128)(2,1)S(1)}, u32[]{:S(2)}, u32[]{:S(2)}) collective-permute-start(bf16[64,6912]{1,0:T(8,128)(2,1)S(1)} %collective-permute-done.19), channel_id=1, source_target_pairs={{1,0},{12,13},{3,2},{14,15},{17,16},{28,29},{19,18},{30,31}} | collective-permute-start | bytes 2654216 | tf_op jit(solution)/shard_map/ppermute | solution.py:30
  92.3 0.9 copy-start.4
  95.8 6.8 %collective-permute-start.25 = (bf16[256,384]{0,1:T(8,128)(2,1)S(1)}, bf16[256,384]{0,1:T(8,128)(2,1)S(1)}, u32[]{:S(2)}, u32[]{:S(2)}) collective-permute-start(bf16[256,384]{0,1:T(8,128)(2,1)S(1)} %fusion.9), channel_id=1, source_target_pairs={{0,2},{2,0},{1,3},{3,1},{4,6},{6,4},{5,7},{7,5},{8,10},{10,8},{9,1... | collective-permute-start | bytes 589832 | tf_op jit(solution)/shard_map/ppermute | solution.py:86
  103.3 2.3 %collective-permute-start.26 = (bf16[3,4,64,256]{3,2,1,0:T(8,128)(2,1)S(1)}, bf16[3,4,64,256]{3,2,1,0:T(8,128)(2,1)S(1)}, u32[]{:S(2)}, u32[]{:S(2)}) collective-permute-start(bf16[3,4,64,256]{3,2,1,0:T(8,128)(2,1)S(1)} %dynamic-slice_bitcast_fusion), channel_id=1, source_target_pairs={{0,1},{1,0},{2,3},{3,2},{4,5},{5,4},{6,7},{7,6},{8,9},{9,8},{10,11... | collective-permute-start | bytes 1179656 | tf_op jit(solution)/shard_map/ppermute | solution.py:96
  104.2 10.3 %copy-start.2 = (bf16[64,64,256]{2,1,0:T(8,128)(2,1)S(1)}, bf16[64,64,256]{2,1,0:T(8,128)(2,1)}, u32[]{:S(2)}) copy-start(bf16[64,64,256]{2,1,0:T(8,128)(2,1)} %param.13) | copy-start | bytes 6291460
  104.2 10.3 %copy-start.5 = (f32[64,256]{1,0:T(8,128)S(1)}, f32[64,256]{1,0:T(8,128)}, u32[]{:S(2)}) copy-start(f32[64,256]{1,0:T(8,128)} %param.14) | copy-start | bytes 196612
  105.8 15.0 %collective-permute-start.27 = (bf16[6,64,256]{2,1,0:T(8,128)(2,1)S(1)}, bf16[6,64,256]{2,1,0:T(8,128)(2,1)}, u32[]{:S(2)}, u32[]{:S(2)}) collective-permute-start(bf16[6,64,256]{2,1,0:T(8,128)(2,1)S(1)} %get-tuple-element.9), channel_id=1, source_target_pairs={{0,4},{4,8},{8,12},{12,0},{1,5},{5,9},{9,13},{13,1},{2,6},{6,10},{... | collective-permute-start | bytes 589832 | tf_op jit(solution)/shard_map/ppermute | solution.py:104
  105.9 21.9 %collective-permute-start.28 = (bf16[6,64,256]{2,1,0:T(8,128)(2,1)S(1)}, bf16[6,64,256]{2,1,0:T(8,128)(2,1)}, u32[]{:S(2)}, u32[]{:S(2)}) collective-permute-start(bf16[6,64,256]{2,1,0:T(8,128)(2,1)S(1)} %get-tuple-element.8), channel_id=1, source_target_pairs={{0,8},{4,12},{8,0},{12,4},{1,9},{5,13},{9,1},{13,5},{2,10},{6,14},... | collective-permute-start | bytes 589832 | tf_op jit(solution)/shard_map/ppermute | solution.py:104
  114.5 14.4 %collective-permute-start.29 = (bf16[6,64,256]{2,1,0:T(8,128)(2,1)S(1)}, bf16[6,64,256]{2,1,0:T(8,128)(2,1)S(1)}, u32[]{:S(2)}, u32[]{:S(2)}) collective-permute-start(bf16[6,64,256]{2,1,0:T(8,128)(2,1)S(1)} %get-tuple-element.10), channel_id=1, source_target_pairs={{0,12},{4,0},{8,4},{12,8},{1,13},{5,1},{9,5},{13,9},{2,14},{6,2},{... | collective-permute-start | bytes 589832 | tf_op jit(solution)/shard_map/ppermute | solution.py:104
  129.2 7.5 %copy-start.7 = (s32[16,1]{0,1:T(1,128)S(1)}, s32[16,1]{0,1:T(1,128)}, u32[]{:S(2)}) copy-start(s32[16,1]{0,1:T(1,128)} %param.15) | copy-start | bytes 196
  133.8 1.3 collective-permute-start.30
  135.1 3.8 %collective-permute-start.31 = (f32[16,4,6]{0,2,1:T(8,128)S(1)}, f32[16,4,6]{0,2,1:T(8,128)S(1)}, u32[]{:S(2)}, u32[]{:S(2)}) collective-permute-start(f32[16,4,6]{0,2,1:T(8,128)S(1)} %dynamic-slice_bitcast_fusion.2), channel_id=1, source_target_pairs={{0,2},{2,0},{1,3},{3,1},{4,6},{6,4},{5,7},{7,5},{8,10},{10,8},{9,1... | collective-permute-start | bytes 4616 | tf_op jit(solution)/shard_map/ppermute | solution.py:121
  138.9 5.1 %collective-permute-start.32 = (f32[16,6]{0,1:T(8,128)S(1)}, f32[16,6]{0,1:T(8,128)S(1)}, u32[]{:S(2)}, u32[]{:S(2)}) collective-permute-start(f32[16,6]{0,1:T(8,128)S(1)} %get-tuple-element.15), channel_id=1, source_target_pairs={{0,12},{4,0},{8,4},{12,8},{1,13},{5,1},{9,5},{13,9},{2,14},{6,2},{... | collective-permute-start | bytes 1160 | tf_op jit(solution)/shard_map/ppermute | solution.py:127
  142.2 4.5 %collective-permute-start.33 = (f32[16,6]{0,1:T(8,128)S(1)}, f32[16,6]{0,1:T(8,128)S(1)}, u32[]{:S(2)}, u32[]{:S(2)}) collective-permute-start(f32[16,6]{0,1:T(8,128)S(1)} %get-tuple-element.17), channel_id=1, source_target_pairs={{0,8},{4,12},{8,0},{12,4},{1,9},{5,13},{9,1},{13,5},{2,10},{6,14},... | collective-permute-start | bytes 1160 | tf_op jit(solution)/shard_map/ppermute | solution.py:127
  143.8 5.4 %collective-permute-start.34 = (f32[16,6]{0,1:T(8,128)S(1)}, f32[16,6]{0,1:T(8,128)S(1)}, u32[]{:S(2)}, u32[]{:S(2)}) collective-permute-start(f32[16,6]{0,1:T(8,128)S(1)} %get-tuple-element.16), channel_id=1, source_target_pairs={{0,4},{4,8},{8,12},{12,0},{1,5},{5,9},{9,13},{13,1},{2,6},{6,10},{... | collective-permute-start | bytes 1160 | tf_op jit(solution)/shard_map/ppermute | solution.py:127

commit v2 on v1

--- a/solution.py
+++ b/solution.py
@@ -1,6 +1,10 @@
+import functools
+
 import jax
 import jax.numpy as jnp
 from jax import lax
+from jax.experimental import pallas as pl
+from jax.experimental.pallas import tpu as pltpu
 from jax.sharding import PartitionSpec as P
 
 
@@ -21,22 +25,46 @@
             return w >= k if r == 0 else w <= n_wide - 1 - k
 
         other = lax.ppermute(held, ("groups", "wide", "rep"), swap_pairs(2 * n_wide, valid))
-        across = [(p, p ^ 1) for p in range(2 * n_wide) if valid(p)]
-        rounds.append(
-            (
-                held,
-                other,
-                lax.ppermute(held, ("wide", "rep"), across),
-                lax.ppermute(other, ("wide", "rep"), across),
-            )
-        )
+        rounds.append((held, other))
     return rounds
 
 
+def tile_of(size, most):
+    return max(t for t in range(128, most + 1, 128) if size % t == 0)
+
+
+def turn_body(n_pieces, *refs):
+    pieces, refs = refs[:n_pieces], refs[n_pieces:]
+    tokens, outs = refs[: len(refs) // 2], refs[len(refs) // 2 :]
+
+    @pl.when(pl.program_id(0) == 0)
+    def _():
+        for out in outs:
+            out[...] = jnp.zeros_like(out)
+
+    panel = jnp.concatenate([p[...] for p in pieces], axis=0)
+    for tok, out in zip(tokens, outs, strict=True):
+        out[...] += lax.dot_general(panel, tok[...], (((1,), (1,)), ((), ())), preferred_element_type=jnp.float32)
+
+
 def turn(pieces, tokens):
-    return lax.dot_general(
-        jnp.concatenate(pieces, axis=0), tokens, (((1,), (1,)), ((), ())), preferred_element_type=jnp.float32
-    )
+    rows = sum(p.shape[0] for p in pieces)
+    depth = pieces[0].shape[1]
+    tile = tile_of(depth, 1408)
+    shapes = [jax.ShapeDtypeStruct((rows, t.shape[0]), jnp.float32) for t in tokens]
+    return pl.pallas_call(
+        functools.partial(turn_body, len(pieces)),
+        grid=(depth // tile,),
+        in_specs=[pl.BlockSpec((x.shape[0], tile), lambda k: (0, k)) for x in (*pieces, *tokens)],
+        out_specs=[pl.BlockSpec(x.shape, lambda k: (0, 0)) for x in shapes],
+        out_shape=shapes,
+        compiler_params=pltpu.CompilerParams(vmem_limit_bytes=32 * 1024 * 1024),
+        cost_estimate=pl.CostEstimate(
+            flops=2 * rows * depth * sum(t.shape[0] for t in tokens),
+            bytes_accessed=2 * depth * (rows + sum(t.shape[0] for t in tokens)),
+            transcendentals=0,
+        ),
+    )(*pieces, *tokens)
 
 
 def local(acts, grads, counts, basis_in, basis_out, query_grads, eigenvalues, candidate):
@@ -50,24 +78,29 @@
     tok_out = grads.reshape(n_tok, d_local)
     rows_in, rows_out = basis_in.shape[0], basis_out.shape[0]
 
+    swap = [(0, 1), (1, 0)]
+    both_in = (tok_in, lax.ppermute(tok_in, "rep", swap))
+    both_out = (tok_out, lax.ppermute(tok_out, "rep", swap))
+
     def rotate(basis, tokens):
         rows = basis.shape[0]
         half = rows // 2
         own = lax.dynamic_slice_in_dim(basis, group * half, half, axis=0)
         rounds = gather_rounds(own, n_wide)
-        slots = [turn([basis], tokens)]
-        below, above = {}, {}
-        for k, pieces in enumerate(rounds, start=1):
-            y = turn(list(pieces), tokens).reshape(2, 2, half, n_tok)
-            y = jnp.where(group == 0, y, y[:, ::-1]).reshape(2, rows, n_tok)
-            below[k] = jnp.where(rep == 0, y[0], y[1])
-            above[k] = jnp.where(rep == 0, y[1], y[0])
+        slots = [turn([basis], tokens[:1])[0]]
+        mine, theirs = zip(*(turn(pieces, tokens) for pieces in rounds), strict=True)
+        mine = jnp.stack(mine)
+        theirs = lax.ppermute(jnp.stack(theirs), "rep", swap)
+        sides = jnp.stack([mine, theirs]).reshape(2, n_wide - 1, 2, half, n_tok)
+        sides = jnp.where(group == 0, sides, sides[:, :, ::-1]).reshape(2, n_wide - 1, rows, n_tok)
+        below = jnp.where(rep == 0, sides[0], sides[1])
+        above = jnp.where(rep == 0, sides[1], sides[0])
         for n in range(1, n_wide):
-            slots.append(jnp.where(wide + n <= n_wide - 1, above[n], below[n_wide - n]))
+            slots.append(jnp.where(wide + n <= n_wide - 1, above[n - 1], below[n_wide - n - 1]))
         return jnp.stack(slots)
 
-    grad_part = rotate(basis_out, tok_out).reshape(n_wide * rows_out, n_tok)
-    act_part = rotate(basis_in, tok_in).reshape(n_wide * rows_in, n_tok)
+    grad_part = rotate(basis_out, both_out).reshape(n_wide * rows_out, n_tok)
+    act_part = rotate(basis_in, both_in).reshape(n_wide * rows_in, n_tok)
 
     rank_in = n_wide * rows_in
     share = rank_in // n_layer

time: 151 us -> 192 us (1.27)
  starting transfers between devices: 57.7 us -> 91 us
  Pallas kernels: 0 us -> 30.4 us
  matrix products: 21.8 us -> 4.99 us
  other arithmetic: 15.1 us -> 3.92 us
  waiting for transfers between devices: 42.8 us -> 46.9 us
    ppermute x12 -> x4, starting transfers between devices: 15.6 us -> 47.4 us  [the longest x2 46.9 us: rotate(): theirs = lax.ppermute(jnp.stack(theirs), 'rep', swap)]
    pallas_call x0 -> x8, Pallas kernels: none -> 30.4 us  [turn(): pl.pallas_call(functools.partial(turn_body, len(pieces)), grid=(depth //...]
    ppermute x12 -> x4, waiting for transfers between devices: 22.7 us -> 1.35 us  [the longest x2 1.35 us: rotate(): theirs = lax.ppermute(jnp.stack(theirs), 'rep', swap)]
    dot_general x8 -> x0, matrix products: 16.8 us -> none  [turn(): lax.dot_general(jnp.concatenate(pieces, axis=0), tokens, (((1,), (1,)), (...]
    ppermute x6, waiting for transfers between devices: 0.02 us -> 13.4 us  [gather_rounds(): held = lax.ppermute(held, ('wide', 'rep'), pairs)]
    concatenate x6 -> x0, other arithmetic: 8.52 us -> none  [turn(): jnp.concatenate(pieces, axis=0)]
    ppermute x1, waiting for transfers between devices: 0.01 us -> 6.56 us  [local(): lax.ppermute(grad_sent, 'layer', shift).astype(jnp.float32)]
    unnamed x21 -> x35, local copies, waits for them, and re-layouts: 0.86 us -> 7.11 us
  transfers between devices with their start and end apart: 35 -> 27, of which waited for: 13 -> 13; matrix products, arithmetic and copies ran while one was open for 27% -> 4% of each run, Pallas kernels for 0% -> 16%
where the time goes in v2:
time: 192 us; the launch traced here: 191 us
  starting transfers between devices  91 us (47%)
  waiting for transfers between devices  46.9 us (24%)
  Pallas kernels  30.4 us (16%)
  local copies, waits for them, and re-layouts  13.3 us (7%)
  matrix products  4.99 us (3%)
  other arithmetic  3.92 us (2%)
    ppermute x2, starting transfers between devices, rotate(): theirs = lax.ppermute(jnp.stack(theirs), 'rep', swap)  46.9 us
    pallas_call x8, Pallas kernels, turn(): pl.pallas_call(functools.partial(turn_body, len(pieces)), grid=(depth //...  30.4 us
    ppermute x6, starting transfers between devices, gather_rounds(): held = lax.ppermute(held, ('wide', 'rep'), pairs)  16.4 us
    ppermute x6, waiting for transfers between devices, gather_rounds(): held = lax.ppermute(held, ('wide', 'rep'), pairs)  13.4 us
    ppermute x3, starting transfers between devices, local(): arrived.append(lax.ppermute(both[:, n], 'wide', shift))  9.87 us
    ppermute x3, waiting for transfers between devices, local(): arrived.append(lax.ppermute(both[:, n], 'wide', shift))  9.79 us
    ppermute x6, starting transfers between devices, gather_rounds(): lax.ppermute(held, ('groups', 'wide', 'rep'), swap_pairs(2 * n_wide, valid))  7.52 us
    unnamed x35, local copies, waits for them, and re-layouts  7.11 us
  transfers between devices with their start and end apart: 27, of which 13 were waited for; matrix products, arithmetic and copies ran while one was open for 4% of the time, Pallas kernels for 16%

profile of v2, /device:TPU:0, one launch (start us, length us, event | category | flops | bytes accessed | tf_op | source)
XLA Modules:
  0.0 191.1 jit_solution(3680301432703895580)
XLA Ops:
  0.0 0.5 collective-permute-start.11
  0.5 1.4 constant_dynamic-slice_fusion
  1.8 4.5 %collective-permute-start.9 = (bf16[64,6912]{1,0:T(8,128)(2,1)S(1)}, bf16[64,6912]{1,0:T(8,128)(2,1)S(1)}, u32[]{:S(2)}, u32[]{:S(2)}) collective-permute-start(bf16[64,6912]{1,0:T(8,128)(2,1)S(1)} %constant_dynamic-slice_fusion), channel_id=1, source_target_pairs={{0,4},{4,8},{8,12},{5,1},{9,5},{13,9},{2,6},{6,10},{10,14},{7,3},{... | collective-permute-start | bytes 2654216 | tf_op jit(solution)/shard_map/ppermute | solution.py:21
  6.4 10.5 %collective-permute-done.9.refs_0_ = bf16[64,6912]{1,0:T(8,128)(2,1)S(1)} collective-permute-done((bf16[64,6912]{1,0:T(8,128)(2,1)S(1)}, bf16[64,6912]{1,0:T(8,128)(2,1)S(1)}, u32[]{:S(2)}, u32[]{:S(2)}) %collective-permute-start.9) | collective-permute-done | bytes 884768 | tf_op jit(solution)/shard_map/ppermute | solution.py:21
  16.9 1.6 collective-permute-start.12
  18.5 1.0 constant_dynamic-slice_fusion.1
  19.5 7.2 %collective-permute-start = (bf16[64,2560]{1,0:T(8,128)(2,1)S(1)}, bf16[64,2560]{1,0:T(8,128)(2,1)S(1)}, u32[]{:S(2)}, u32[]{:S(2)}) collective-permute-start(bf16[64,2560]{1,0:T(8,128)(2,1)S(1)} %constant_dynamic-slice_fusion.1), channel_id=1, source_target_pairs={{0,4},{4,8},{8,12},{5,1},{9,5},{13,9},{2,6},{6,10},{10,14},{7,3},{... | collective-permute-start | bytes 983048 | tf_op jit(solution)/shard_map/ppermute | solution.py:21
  26.7 1.6 collective-permute-start.14
  28.4 2.9 %collective-permute-done.refs_0_ = bf16[64,2560]{1,0:T(8,128)(2,1)S(1)} collective-permute-done((bf16[64,2560]{1,0:T(8,128)(2,1)S(1)}, bf16[64,2560]{1,0:T(8,128)(2,1)S(1)}, u32[]{:S(2)}, u32[]{:S(2)}) %collective-permute-start) | collective-permute-done | bytes 327712 | tf_op jit(solution)/shard_map/ppermute | solution.py:21
  31.3 0.7 collective-permute-start.3
  32.0 0.7 collective-permute-start.5
  32.7 0.7 collective-permute-start.4
  33.4 0.7 collective-permute-start.6
  34.1 0.7 copy-done.7
  34.8 1.6 collective-permute-start.15
  36.4 0.7 copy-done.5
  37.2 1.6 collective-permute-start.13
  38.7 0.7 copy-done.9
  39.5 1.6 collective-permute-start.10
  41.1 1.3 copy-done.1
  42.4 1.4 collective-permute-start.1
  43.7 1.5 copy-done.2
  45.3 1.0 copy-done.8
  46.3 1.0 copy-done.10
  47.2 1.7 shard_map.85
  49.0 1.8 shard_map.84
  50.8 2.4 %shard_map.83 = (f32[128,384]{1,0:T(8,128)S(1)}, f32[128,384]{1,0:T(8,128)S(1)}) custom-call(bf16[64,2560]{1,0:T(8,128)(2,1)S(1)} %collective-permute-done.refs_0_, bf16[64,2560]{1,0:T(8,128)(2,1)} %collective-permute-done.1.refs_1_, bf16[384,2560]{1,0:T(8,128)(2,1)S(1)} %bitcast.111, bf16[384,2560]{1,0:T(8,128)(2,1)S(1)} %copy-done.2), custom_call_target="tpu_custom_call" | custom-call | flops 503316480 | bytes 4587520 | tf_op jit(solution)/shard_map/pallas_call | solution.py:55
  53.3 45.9 %collective-permute-start.7 = (f32[3,128,384]{2,1,0:T(8,128)S(1)}, f32[3,128,384]{2,1,0:T(8,128)S(1)}, u32[]{:S(2)}, u32[]{:S(2)}) collective-permute-start(f32[3,128,384]{2,1,0:T(8,128)S(1)} %pad_maximum_fusion.5), channel_id=1, source_target_pairs={{0,1},{1,0},{2,3},{3,2},{4,5},{5,4},{6,7},{7,6},{8,9},{9,8},{10,11... | collective-permute-start | bytes 1769480 | tf_op jit(solution)/shard_map/ppermute | solution.py:93
  99.3 1.1 shard_map.82
  100.4 3.1 %shard_map.86 = f32[128,384]{1,0:T(8,128)S(1)} custom-call(bf16[128,6912]{1,0:T(8,128)(2,1)S(1)} %copy-done.3, bf16[384,6912]{1,0:T(8,128)(2,1)S(1)} %bitcast.104), custom_call_target="tpu_custom_call" | custom-call | flops 679477248 | bytes 7077888 | tf_op jit(solution)/shard_map/pallas_call | solution.py:55
  103.6 6.8 %shard_map.89 = (f32[128,384]{1,0:T(8,128)S(1)}, f32[128,384]{1,0:T(8,128)S(1)}) custom-call(bf16[64,6912]{1,0:T(8,128)(2,1)} %collective-permute-done.14.refs_0_, bf16[64,6912]{1,0:T(8,128)(2,1)} %collective-permute-done.15.refs_1_, bf16[384,6912]{1,0:T(8,128)(2,1)S(1)} %bitcast.105, bf16[384,6912]{1,0:T(8,128)(2,1)} %collective-permute-done.11.refs_3_), custom_call_target="tpu_custom_call" | custom-call | flops 1358954496 | bytes 12386304 | tf_op jit(solution)/shard_map/pallas_call | solution.py:55
  110.3 6.8 %shard_map.88 = (f32[128,384]{1,0:T(8,128)S(1)}, f32[128,384]{1,0:T(8,128)S(1)}) custom-call(bf16[64,6912]{1,0:T(8,128)(2,1)} %collective-permute-done.12.refs_0_, bf16[64,6912]{1,0:T(8,128)(2,1)} %collective-permute-done.13.refs_1_, bf16[384,6912]{1,0:T(8,128)(2,1)S(1)} %bitcast.106, bf16[384,6912]{1,0:T(8,128)(2,1)} %collective-permute-done.11.refs_3_), custom_call_target="tpu_custom_call" | custom-call | flops 1358954496 | bytes 12386304 | tf_op jit(solution)/shard_map/pallas_call | solution.py:55
  117.1 6.7 %shard_map.87 = (f32[128,384]{1,0:T(8,128)S(1)}, f32[128,384]{1,0:T(8,128)S(1)}) custom-call(bf16[64,6912]{1,0:T(8,128)(2,1)S(1)} %collective-permute-done.9.refs_0_, bf16[64,6912]{1,0:T(8,128)(2,1)} %collective-permute-done.10.refs_1_, bf16[384,6912]{1,0:T(8,128)(2,1)S(1)} %bitcast.107, bf16[384,6912]{1,0:T(8,128)(2,1)} %collective-permute-done.11.refs_3_), custom_call_target="tpu_custom_call" | custom-call | flops 1358954496 | bytes 12386304 | tf_op jit(solution)/shard_map/pallas_call | solution.py:55
  123.9 1.0 collective-permute-start.16
  125.2 1.3 collective-permute-done.16
  126.8 0.2 slice_select_fusion.6
  127.1 0.3 copy.12
  127.3 0.2 fusion.9
  127.5 1.6 collective-permute-start.17
  129.2 0.3 copy.11
  129.5 0.6 collective-permute-start.8
  130.2 5.3 %collective-permute-done.17 = bf16[256,384]{0,1:T(8,128)(2,1)} collective-permute-done((bf16[256,384]{0,1:T(8,128)(2,1)S(1)}, bf16[256,384]{0,1:T(8,128)(2,1)}, u32[]{:S(2)}, u32[]{:S(2)}) %collective-permute-start.17) | collective-permute-done | bytes 196640 | tf_op jit(solution)/shard_map/ppermute | solution.py:119
  135.4 1.2 fusion.12
  136.7 6.6 %collective-permute-done.8 = bf16[512,384]{0,1:T(8,128)(2,1)S(1)} collective-permute-done((bf16[512,384]{0,1:T(8,128)(2,1)S(1)}, bf16[512,384]{0,1:T(8,128)(2,1)S(1)}, u32[]{:S(2)}, u32[]{:S(2)}) %collective-permute-start.8) | collective-permute-done | bytes 393248 | tf_op jit(solution)/shard_map/ppermute | solution.py:117
  143.3 0.4 convolution_convert_fusion
  143.9 1.7 collective-permute-done.18
  145.9 9.8 %collective-permute-start.20 = (bf16[6,64,256]{2,1,0:T(8,128)(2,1)S(1)}, bf16[6,64,256]{2,1,0:T(8,128)(2,1)S(1)}, u32[]{:S(2)}, u32[]{:S(2)}) collective-permute-start(bf16[6,64,256]{2,1,0:T(8,128)(2,1)S(1)} %get-tuple-element.42), channel_id=1, source_target_pairs={{0,8},{4,12},{8,0},{12,4},{1,9},{5,13},{9,1},{13,5},{2,10},{6,14},... | collective-permute-start | bytes 589832 | tf_op jit(solution)/shard_map/ppermute | solution.py:137
  155.7 0.6 divide_convert_fusion
  156.3 2.4 %reshape.146 = bf16[2,2,16,16384,1]{3,2,1,0,4:T(8,128)(2,1)} reshape(bf16[64,64,256]{2,1,0:T(8,128)(2,1)S(1)} %divide_convert_fusion) | data formatting | bytes 4194304 | tf_op jit(solution)/shard_map/dot_general | solution.py:144
  158.6 0.2 stack.130
  158.9 2.1 %collective-permute-done.19 = bf16[6,64,256]{2,1,0:T(8,128)(2,1)S(1)} collective-permute-done((bf16[6,64,256]{2,1,0:T(8,128)(2,1)S(1)}, bf16[6,64,256]{2,1,0:T(8,128)(2,1)S(1)}, u32[]{:S(2)}, u32[]{:S(2)}) %collective-permute-start.19) | collective-permute-done | bytes 196640 | tf_op jit(solution)/shard_map/ppermute | solution.py:137
  161.0 0.2 stack.131
  161.2 7.7 %collective-permute-done.20 = bf16[6,64,256]{2,1,0:T(8,128)(2,1)S(1)} collective-permute-done((bf16[6,64,256]{2,1,0:T(8,128)(2,1)S(1)}, bf16[6,64,256]{2,1,0:T(8,128)(2,1)S(1)}, u32[]{:S(2)}, u32[]{:S(2)}) %collective-permute-start.20) | collective-permute-done | bytes 196640 | tf_op jit(solution)/shard_map/ppermute | solution.py:137
  168.9 0.2 stack.132
  169.1 0.2 stack.133
  169.4 4.6 %fusion = f32[2,2,16,4,6]{2,4,3,1,0:T(8,128)S(1)} fusion(bf16[2,2,16,16384,1]{3,2,1,0,4:T(8,128)(2,1)} %reshape.146, bf16[1,6,16384]{2,1,0:T(8,128)(2,1)S(1)} %stack.133, bf16[1,6,16384]{2,1,0:T(8,128)(2,1)S(1)} %stack.132, bf16[1,6,16384]{2,1,0:T(8,128)(2,1)S(1)} %stack.131, bf16[1,6,16384]{2,1,0:T(8,128)(2,1)S(1)} %stack.130), kind=kOutput, calls=%fused_computation.1 | convolution fusion | flops 53477376 | bytes 2889728 | tf_op jit(solution)/shard_map/dot_general | solution.py:144
  174.1 1.2 collective-permute-done.22
  175.3 1.6 collective-permute-start.23
  176.8 2.2 %collective-permute-done.23 = f32[16,4,6]{0,2,1:T(8,128)S(1)} collective-permute-done((f32[16,4,6]{0,2,1:T(8,128)S(1)}, f32[16,4,6]{0,2,1:T(8,128)S(1)}, u32[]{:S(2)}, u32[]{:S(2)}) %collective-permute-start.23) | collective-permute-done | bytes 1568 | tf_op jit(solution)/shard_map/ppermute | solution.py:154
  179.1 2.7 %collective-permute-start.24 = (f32[16,6]{0,1:T(8,128)S(1)}, f32[16,6]{0,1:T(8,128)S(1)}, u32[]{:S(2)}, u32[]{:S(2)}) collective-permute-start(f32[16,6]{0,1:T(8,128)S(1)} %get-tuple-element.45), channel_id=1, source_target_pairs={{0,12},{4,0},{8,4},{12,8},{1,13},{5,1},{9,5},{13,9},{2,14},{6,2},{... | collective-permute-start | bytes 1160 | tf_op jit(solution)/shard_map/ppermute | solution.py:160
  181.8 3.3 %collective-permute-start.25 = (f32[16,6]{0,1:T(8,128)S(1)}, f32[16,6]{0,1:T(8,128)S(1)}, u32[]{:S(2)}, u32[]{:S(2)}) collective-permute-start(f32[16,6]{0,1:T(8,128)S(1)} %get-tuple-element.47), channel_id=1, source_target_pairs={{0,8},{4,12},{8,0},{12,4},{1,9},{5,13},{9,1},{13,5},{2,10},{6,14},... | collective-permute-start | bytes 1160 | tf_op jit(solution)/shard_map/ppermute | solution.py:160
  185.2 1.5 collective-permute-done.25
  186.7 3.8 %collective-permute-done.26 = f32[16,6]{0,1:T(8,128)S(1)} collective-permute-done((f32[16,6]{0,1:T(8,128)S(1)}, f32[16,6]{0,1:T(8,128)S(1)}, u32[]{:S(2)}, u32[]{:S(2)}) %collective-permute-start.26) | collective-permute-done | bytes 416 | tf_op jit(solution)/shard_map/ppermute | solution.py:160
  190.4 0.7 fusion.18
  (73 shorter events, 1.7 us)
Async XLA Ops:
  0.0 43.7 %copy-start = (bf16[3,128,2560]{2,1,0:T(8,128)(2,1)S(1)}, bf16[3,128,2560]{2,1,0:T(8,128)(2,1)}, u32[]{:S(2)}) copy-start(bf16[3,128,2560]{2,1,0:T(8,128)(2,1)} %param.9) | copy-start | bytes 5898244
  0.0 103.5 %collective-permute-start.11 = (bf16[384,6912]{1,0:T(8,128)(2,1)}, bf16[384,6912]{1,0:T(8,128)(2,1)}, u32[]{:S(2)}, u32[]{:S(2)}) collective-permute-start(bf16[384,6912]{1,0:T(8,128)(2,1)} %bitcast.101), channel_id=1, source_target_pairs={{0,1},{1,0},{2,3},{3,2},{4,5},{5,4},{6,7},{7,6},{8,9},{9,8},{10,11... | collective-permute-start | bytes 15925256 | tf_op jit(solution)/shard_map/ppermute | solution.py:82
  1.8 15.0 %collective-permute-start.9 = (bf16[64,6912]{1,0:T(8,128)(2,1)S(1)}, bf16[64,6912]{1,0:T(8,128)(2,1)S(1)}, u32[]{:S(2)}, u32[]{:S(2)}) collective-permute-start(bf16[64,6912]{1,0:T(8,128)(2,1)S(1)} %constant_dynamic-slice_fusion), channel_id=1, source_target_pairs={{0,4},{4,8},{8,12},{5,1},{9,5},{13,9},{2,6},{6,10},{10,14},{7,3},{... | collective-permute-start | bytes 2654216 | tf_op jit(solution)/shard_map/ppermute | solution.py:21
  16.9 9.9 %collective-permute-start.12 = (bf16[64,6912]{1,0:T(8,128)(2,1)S(1)}, bf16[64,6912]{1,0:T(8,128)(2,1)}, u32[]{:S(2)}, u32[]{:S(2)}) collective-permute-start(bf16[64,6912]{1,0:T(8,128)(2,1)S(1)} %collective-permute-done.9.refs_0_), channel_id=1, source_target_pairs={{4,8},{8,12},{5,1},{9,5},{6,10},{10,14},{7,3},{11,7},{20,24},{24,2... | collective-permute-start | bytes 2654216 | tf_op jit(solution)/shard_map/ppermute | solution.py:21
  18.5 22.6 %collective-permute-start.2 = (bf16[384,2560]{1,0:T(8,128)(2,1)}, bf16[384,2560]{1,0:T(8,128)(2,1)S(1)}, u32[]{:S(2)}, u32[]{:S(2)}) collective-permute-start(bf16[384,2560]{1,0:T(8,128)(2,1)} %bitcast.108), channel_id=1, source_target_pairs={{0,1},{1,0},{2,3},{3,2},{4,5},{5,4},{6,7},{7,6},{8,9},{9,8},{10,11... | collective-permute-start | bytes 5898248 | tf_op jit(solution)/shard_map/ppermute | solution.py:83
  19.5 11.8 %collective-permute-start = (bf16[64,2560]{1,0:T(8,128)(2,1)S(1)}, bf16[64,2560]{1,0:T(8,128)(2,1)S(1)}, u32[]{:S(2)}, u32[]{:S(2)}) collective-permute-start(bf16[64,2560]{1,0:T(8,128)(2,1)S(1)} %constant_dynamic-slice_fusion.1), channel_id=1, source_target_pairs={{0,4},{4,8},{8,12},{5,1},{9,5},{13,9},{2,6},{6,10},{10,14},{7,3},{... | collective-permute-start | bytes 983048 | tf_op jit(solution)/shard_map/ppermute | solution.py:21
  26.7 8.1 %collective-permute-start.14 = (bf16[64,6912]{1,0:T(8,128)(2,1)}, bf16[64,6912]{1,0:T(8,128)(2,1)}, u32[]{:S(2)}, u32[]{:S(2)}) collective-permute-start(bf16[64,6912]{1,0:T(8,128)(2,1)} %collective-permute-done.12.refs_0_), channel_id=1, source_target_pairs={{8,12},{5,1},{10,14},{7,3},{24,28},{21,17},{26,30},{23,19}} | collective-permute-start | bytes 2654216 | tf_op jit(solution)/shard_map/ppermute | solution.py:21
  31.3 0.7 collective-permute-start.3
  32.0 1.4 collective-permute-start.5
  32.7 3.7 %collective-permute-start.4 = (bf16[64,2560]{1,0:T(8,128)(2,1)S(1)}, bf16[64,2560]{1,0:T(8,128)(2,1)S(1)}, u32[]{:S(2)}, u32[]{:S(2)}) collective-permute-start(bf16[64,2560]{1,0:T(8,128)(2,1)S(1)} %collective-permute-done.3.refs_0_), channel_id=1, source_target_pairs={{1,17},{5,21},{8,24},{12,28},{17,1},{21,5},{24,8},{28,12},{3,19},{... | collective-permute-start | bytes 983048 | tf_op jit(solution)/shard_map/ppermute | solution.py:27
  33.4 5.4 %collective-permute-start.6 = (bf16[64,2560]{1,0:T(8,128)(2,1)S(1)}, bf16[64,2560]{1,0:T(8,128)(2,1)S(1)}, u32[]{:S(2)}, u32[]{:S(2)}) collective-permute-start(bf16[64,2560]{1,0:T(8,128)(2,1)S(1)} %collective-permute-done.5.refs_0_), channel_id=1, source_target_pairs={{1,17},{12,28},{17,1},{28,12},{3,19},{14,30},{19,3},{30,14}} | collective-permute-start | bytes 983048 | tf_op jit(solution)/shard_map/ppermute | solution.py:27
  34.1 0.7 copy-start.7
  34.8 68.7 %collective-permute-start.15 = (bf16[64,6912]{1,0:T(8,128)(2,1)}, bf16[64,6912]{1,0:T(8,128)(2,1)}, u32[]{:S(2)}, u32[]{:S(2)}) collective-permute-start(bf16[64,6912]{1,0:T(8,128)(2,1)} %collective-permute-done.14.refs_0_), channel_id=1, source_target_pairs={{1,17},{12,28},{17,1},{28,12},{3,19},{14,30},{19,3},{30,14}} | collective-permute-start | bytes 2654216 | tf_op jit(solution)/shard_map/ppermute | solution.py:27
  36.4 0.7 copy-start.5
  37.2 73.2 %collective-permute-start.13 = (bf16[64,6912]{1,0:T(8,128)(2,1)}, bf16[64,6912]{1,0:T(8,128)(2,1)}, u32[]{:S(2)}, u32[]{:S(2)}) collective-permute-start(bf16[64,6912]{1,0:T(8,128)(2,1)} %collective-permute-done.12.refs_0_), channel_id=1, source_target_pairs={{1,17},{5,21},{8,24},{12,28},{17,1},{21,5},{24,8},{28,12},{3,19},{... | collective-permute-start | bytes 2654216 | tf_op jit(solution)/shard_map/ppermute | solution.py:27
  38.7 0.7 copy-start.9
  39.5 77.6 %collective-permute-start.10 = (bf16[64,6912]{1,0:T(8,128)(2,1)S(1)}, bf16[64,6912]{1,0:T(8,128)(2,1)}, u32[]{:S(2)}, u32[]{:S(2)}) collective-permute-start(bf16[64,6912]{1,0:T(8,128)(2,1)S(1)} %collective-permute-done.9.refs_0_), channel_id=1, source_target_pairs={{1,17},{4,20},{5,21},{8,24},{9,25},{12,28},{17,1},{20,4},{21,5},{2... | collective-permute-start | bytes 2654216 | tf_op jit(solution)/shard_map/ppermute | solution.py:27
  41.1 1.3 copy-start.1
  42.4 8.4 %collective-permute-start.1 = (bf16[64,2560]{1,0:T(8,128)(2,1)S(1)}, bf16[64,2560]{1,0:T(8,128)(2,1)}, u32[]{:S(2)}, u32[]{:S(2)}) collective-permute-start(bf16[64,2560]{1,0:T(8,128)(2,1)S(1)} %collective-permute-done.refs_0_), channel_id=1, source_target_pairs={{1,17},{4,20},{5,21},{8,24},{9,25},{12,28},{17,1},{20,4},{21,5},{2... | collective-permute-start | bytes 983048 | tf_op jit(solution)/shard_map/ppermute | solution.py:27
  43.7 1.5 copy-start.2
  45.3 1.0 copy-start.8
  46.3 1.0 copy-start.10
  47.2 1.8 copy-start.6
  49.0 51.4 %slice-start = ((s8[5308416]{0:T(1024)(128)(4,1)}), s8[4194304]{0:T(1024)(128)(4,1)S(1)}, s32[]{:S(2)}) async-start(s8[5308416]{0:T(1024)(128)(4,1)} %bitcast.102), calls=%async_computation | async-start | bytes 8388608
  50.8 49.6 %slice-start.1 = ((s8[5308416]{0:T(1024)(128)(4,1)}), s8[1114112]{0:T(1024)(128)(4,1)S(1)}, s32[]{:S(2)}) async-start(s8[5308416]{0:T(1024)(128)(4,1)} %bitcast.102), calls=%async_computation.1 | async-start | bytes 2228224
  53.2 46.0 %copy-start.4 = (bf16[128,2560]{1,0:T(8,128)(2,1)S(1)}, bf16[128,2560]{1,0:T(8,128)(2,1)}, u32[]{:S(2)}) copy-start(bf16[128,2560]{1,0:T(8,128)(2,1)} %refs_0_.2) | copy-start | bytes 1966084
  53.3 47.1 %copy-start.3 = (bf16[128,6912]{1,0:T(8,128)(2,1)S(1)}, bf16[128,6912]{1,0:T(8,128)(2,1)}, u32[]{:S(2)}) copy-start(bf16[128,6912]{1,0:T(8,128)(2,1)} %refs_0_.3) | copy-start | bytes 5308420
  53.3 71.6 %collective-permute-start.7 = (f32[3,128,384]{2,1,0:T(8,128)S(1)}, f32[3,128,384]{2,1,0:T(8,128)S(1)}, u32[]{:S(2)}, u32[]{:S(2)}) collective-permute-start(f32[3,128,384]{2,1,0:T(8,128)S(1)} %pad_maximum_fusion.5), channel_id=1, source_target_pairs={{0,1},{1,0},{2,3},{3,2},{4,5},{5,4},{6,7},{7,6},{8,9},{9,8},{10,11... | collective-permute-start | bytes 1769480 | tf_op jit(solution)/shard_map/ppermute | solution.py:93
  123.9 2.6 %collective-permute-start.16 = (f32[3,128,384]{2,1,0:T(8,128)S(1)}, f32[3,128,384]{2,1,0:T(8,128)S(1)}, u32[]{:S(2)}, u32[]{:S(2)}) collective-permute-start(f32[3,128,384]{2,1,0:T(8,128)S(1)} %pad_maximum_fusion.6), channel_id=1, source_target_pairs={{0,1},{1,0},{2,3},{3,2},{4,5},{5,4},{6,7},{7,6},{8,9},{9,8},{10,11... | collective-permute-start | bytes 1769480 | tf_op jit(solution)/shard_map/ppermute | solution.py:93
  127.5 7.9 %collective-permute-start.17 = (bf16[256,384]{0,1:T(8,128)(2,1)S(1)}, bf16[256,384]{0,1:T(8,128)(2,1)}, u32[]{:S(2)}, u32[]{:S(2)}) collective-permute-start(bf16[256,384]{0,1:T(8,128)(2,1)S(1)} %fusion.9), channel_id=1, source_target_pairs={{0,2},{2,0},{1,3},{3,1},{4,6},{6,4},{5,7},{7,5},{8,10},{10,8},{9,1... | collective-permute-start | bytes 589832 | tf_op jit(solution)/shard_map/ppermute | solution.py:119
  129.2 0.9 copy-start.13
  129.5 13.7 %collective-permute-start.8 = (bf16[512,384]{0,1:T(8,128)(2,1)S(1)}, bf16[512,384]{0,1:T(8,128)(2,1)S(1)}, u32[]{:S(2)}, u32[]{:S(2)}) collective-permute-start(bf16[512,384]{0,1:T(8,128)(2,1)S(1)} %convert_element_type.43), channel_id=1, source_target_pairs={{0,2},{2,0},{1,3},{3,1},{4,6},{6,4},{5,7},{7,5},{8,10},{10,8},{9,1... | collective-permute-start | bytes 1179656 | tf_op jit(solution)/shard_map/ppermute | solution.py:117
  143.8 1.8 collective-permute-start.18
  145.7 10.1 %copy-start.11 = (bf16[64,64,256]{2,1,0:T(8,128)(2,1)S(1)}, bf16[64,64,256]{2,1,0:T(8,128)(2,1)}, u32[]{:S(2)}) copy-start(bf16[64,64,256]{2,1,0:T(8,128)(2,1)} %param.13) | copy-start | bytes 6291460
  145.7 10.0 %copy-start.12 = (f32[64,256]{1,0:T(8,128)S(1)}, f32[64,256]{1,0:T(8,128)}, u32[]{:S(2)}) copy-start(f32[64,256]{1,0:T(8,128)} %param.14) | copy-start | bytes 196612
  145.8 15.1 %collective-permute-start.19 = (bf16[6,64,256]{2,1,0:T(8,128)(2,1)S(1)}, bf16[6,64,256]{2,1,0:T(8,128)(2,1)S(1)}, u32[]{:S(2)}, u32[]{:S(2)}) collective-permute-start(bf16[6,64,256]{2,1,0:T(8,128)(2,1)S(1)} %get-tuple-element.43), channel_id=1, source_target_pairs={{0,4},{4,8},{8,12},{12,0},{1,5},{5,9},{9,13},{13,1},{2,6},{6,10},{... | collective-permute-start | bytes 589832 | tf_op jit(solution)/shard_map/ppermute | solution.py:137
  145.9 23.0 %collective-permute-start.20 = (bf16[6,64,256]{2,1,0:T(8,128)(2,1)S(1)}, bf16[6,64,256]{2,1,0:T(8,128)(2,1)S(1)}, u32[]{:S(2)}, u32[]{:S(2)}) collective-permute-start(bf16[6,64,256]{2,1,0:T(8,128)(2,1)S(1)} %get-tuple-element.42), channel_id=1, source_target_pairs={{0,8},{4,12},{8,0},{12,4},{1,9},{5,13},{9,1},{13,5},{2,10},{6,14},... | collective-permute-start | bytes 589832 | tf_op jit(solution)/shard_map/ppermute | solution.py:137
  155.7 13.4 %collective-permute-start.21 = (bf16[6,64,256]{2,1,0:T(8,128)(2,1)S(1)}, bf16[6,64,256]{2,1,0:T(8,128)(2,1)S(1)}, u32[]{:S(2)}, u32[]{:S(2)}) collective-permute-start(bf16[6,64,256]{2,1,0:T(8,128)(2,1)S(1)} %get-tuple-element.44), channel_id=1, source_target_pairs={{0,12},{4,0},{8,4},{12,8},{1,13},{5,1},{9,5},{13,9},{2,14},{6,2},{... | collective-permute-start | bytes 589832 | tf_op jit(solution)/shard_map/ppermute | solution.py:137
  169.4 7.5 %copy-start.14 = (s32[16,1]{0,1:T(1,128)S(1)}, s32[16,1]{0,1:T(1,128)}, u32[]{:S(2)}) copy-start(s32[16,1]{0,1:T(1,128)} %param.15) | copy-start | bytes 196
  174.0 1.3 collective-permute-start.22
  175.3 3.8 %collective-permute-start.23 = (f32[16,4,6]{0,2,1:T(8,128)S(1)}, f32[16,4,6]{0,2,1:T(8,128)S(1)}, u32[]{:S(2)}, u32[]{:S(2)}) collective-permute-start(f32[16,4,6]{0,2,1:T(8,128)S(1)} %dynamic-slice_bitcast_fusion.2), channel_id=1, source_target_pairs={{0,2},{2,0},{1,3},{3,1},{4,6},{6,4},{5,7},{7,5},{8,10},{10,8},{9,1... | collective-permute-start | bytes 4616 | tf_op jit(solution)/shard_map/ppermute | solution.py:154
  179.1 6.1 %collective-permute-start.24 = (f32[16,6]{0,1:T(8,128)S(1)}, f32[16,6]{0,1:T(8,128)S(1)}, u32[]{:S(2)}, u32[]{:S(2)}) collective-permute-start(f32[16,6]{0,1:T(8,128)S(1)} %get-tuple-element.45), channel_id=1, source_target_pairs={{0,12},{4,0},{8,4},{12,8},{1,13},{5,1},{9,5},{13,9},{2,14},{6,2},{... | collective-permute-start | bytes 1160 | tf_op jit(solution)/shard_map/ppermute | solution.py:160
  181.8 4.9 %collective-permute-start.25 = (f32[16,6]{0,1:T(8,128)S(1)}, f32[16,6]{0,1:T(8,128)S(1)}, u32[]{:S(2)}, u32[]{:S(2)}) collective-permute-start(f32[16,6]{0,1:T(8,128)S(1)} %get-tuple-element.47), channel_id=1, source_target_pairs={{0,8},{4,12},{8,0},{12,4},{1,9},{5,13},{9,1},{13,5},{2,10},{6,14},... | collective-permute-start | bytes 1160 | tf_op jit(solution)/shard_map/ppermute | solution.py:160
  185.0 5.4 %collective-permute-start.26 = (f32[16,6]{0,1:T(8,128)S(1)}, f32[16,6]{0,1:T(8,128)S(1)}, u32[]{:S(2)}, u32[]{:S(2)}) collective-permute-start(f32[16,6]{0,1:T(8,128)S(1)} %get-tuple-element.46), channel_id=1, source_target_pairs={{0,4},{4,8},{8,12},{12,0},{1,5},{5,9},{9,13},{13,1},{2,6},{6,10},{... | collective-permute-start | bytes 1160 | tf_op jit(solution)/shard_map/ppermute | solution.py:160

commit v3 on v1

--- a/solution.py
+++ b/solution.py
@@ -1,11 +1,25 @@
+import functools
+
 import jax
 import jax.numpy as jnp
 from jax import lax
+from jax.experimental import pallas as pl
+from jax.experimental.pallas import tpu as pltpu
 from jax.sharding import PartitionSpec as P
 
 
 def swap_pairs(size, valid):
     return [(a * size + k, (1 - a) * size + k) for a in range(2) for k in range(size) if valid(k)]
+
+
+def hop_pairs(k, n_wide):
+    pairs = [(2 * w, 2 * w + 2) for w in range(k - 1, n_wide - 1)]
+    return pairs + [(2 * w + 3, 2 * w + 1) for w in range(0, n_wide - k)]
+
+
+def holds(place, k, n_wide):
+    w, r = divmod(place, 2)
+    return w >= k if r == 0 else w <= n_wide - 1 - k
 
 
 def gather_rounds(own, n_wide):
@@ -37,6 +51,48 @@
     return lax.dot_general(
         jnp.concatenate(pieces, axis=0), tokens, (((1,), (1,)), ((), ())), preferred_element_type=jnp.float32
     )
+
+
+def finish(partial_value, candidate, n_wide, n_layer, chip_seqs):
+    wide, layer, rep = (lax.axis_index(a) for a in ("wide", "layer", "rep"))
+    n_query = partial_value.shape[0]
+    block = n_query // (2 * n_layer)
+    part = partial_value.reshape(n_layer, 2, block, n_wide, chip_seqs)
+    part = lax.dynamic_index_in_dim(part, rep, axis=1, keepdims=False) + lax.ppermute(
+        lax.dynamic_index_in_dim(part, 1 - rep, axis=1, keepdims=False), "rep", [(0, 1), (1, 0)]
+    )
+    total = lax.dynamic_index_in_dim(part, layer, axis=0, keepdims=False)
+    for m in range(1, n_layer):
+        shift = [(i, (i + m) % n_layer) for i in range(n_layer)]
+        total = total + lax.ppermute(
+            lax.dynamic_index_in_dim(part, (layer + m) % n_layer, axis=0, keepdims=False), "layer", shift
+        )
+    if n_wide & (n_wide - 1) == 0:
+        doubled = jnp.concatenate([total[:, :1], total[:, :0:-1]], axis=1)
+        doubled = jnp.concatenate([doubled, doubled], axis=1)
+        scores = lax.dynamic_slice_in_dim(doubled, (n_wide - wide) % n_wide, n_wide, axis=1)
+        bit = n_wide // 2
+        while bit:
+            scores = scores.reshape(block, 2, bit, chip_seqs)
+            upper = (wide // bit) % 2
+            keep = jnp.where(upper == 1, scores[:, 1], scores[:, 0])
+            give = jnp.where(upper == 1, scores[:, 0], scores[:, 1])
+            scores = keep + lax.ppermute(give, "wide", [(w, w ^ bit) for w in range(n_wide)])
+            bit //= 2
+        scores = scores.reshape(block, chip_seqs)
+    else:
+        scores = total[:, 0]
+        for n in range(1, n_wide):
+            shift = [(w, (w - n) % n_wide) for w in range(n_wide)]
+            scores = scores + lax.ppermute(total[:, n], "wide", shift)
+
+    all_seqs = n_wide * chip_seqs
+    n_blocks = candidate.shape[1]
+    block_size = all_seqs // n_blocks
+    seq_index = wide * chip_seqs + jnp.arange(chip_seqs, dtype=jnp.int32)
+    one_hot = (seq_index[None, :] // block_size == jnp.arange(n_blocks, dtype=jnp.int32)[:, None]).astype(jnp.float32)
+    keep_mask = jnp.dot(candidate.astype(jnp.float32), one_hot, preferred_element_type=jnp.float32)
+    return scores * keep_mask
 
 
 def local(acts, grads, counts, basis_in, basis_out, query_grads, eigenvalues, candidate):
@@ -110,32 +166,292 @@
     weighted = weighted.reshape(n_query, piece * share)
     partial_value = lax.dot_general(weighted, train, (((1,), (1,)), ((), ())), preferred_element_type=jnp.float32)
 
-    block = n_query // (2 * n_layer)
-    part = partial_value.reshape(n_layer, 2, block, n_wide, chip_seqs)
-    part = lax.dynamic_index_in_dim(part, rep, axis=1, keepdims=False) + lax.ppermute(
-        lax.dynamic_index_in_dim(part, 1 - rep, axis=1, keepdims=False), "rep", [(0, 1), (1, 0)]
-    )
-    total = lax.dynamic_index_in_dim(part, layer, axis=0, keepdims=False)
-    for m in range(1, n_layer):
-        shift = [(i, (i + m) % n_layer) for i in range(n_layer)]
-        total = total + lax.ppermute(
-            lax.dynamic_index_in_dim(part, (layer + m) % n_layer, axis=0, keepdims=False), "layer", shift
+    return finish(partial_value, candidate, n_wide, n_layer, chip_seqs)
+
+
+VMEM = pl.BlockSpec(memory_space=pltpu.VMEM)
+SMEM = pl.BlockSpec(memory_space=pltpu.SMEM)
+ANY = pl.BlockSpec(memory_space=pl.ANY)
+FLOAT, HALF = jnp.float32, jnp.bfloat16
+
+
+def kernel(body, out_shape, scratch=(), flops=0, grant=6):
+    return lambda **specs: pl.pallas_call(
+        body,
+        **specs,
+        out_shape=out_shape,
+        scratch_shapes=list(scratch),
+        compiler_params=pltpu.CompilerParams(vmem_limit_bytes=grant * 1024 * 1024),
+        cost_estimate=pl.CostEstimate(flops=flops, bytes_accessed=flops // 400 + 1024, transcendentals=0),
+    )
+
+
+def after(value, *earlier):
+    return lax.optimization_barrier((value, *earlier))[0]
+
+
+def run_copies(copies):
+    for copy in copies:
+        copy.start()
+    for copy in copies:
+        copy.wait()
+
+
+def load_body(x_ref, y_ref, x_out, y_out, sems):
+    run_copies(
+        [pltpu.make_async_copy(x_ref, x_out, sems.at[0]), pltpu.make_async_copy(y_ref, y_out, sems.at[1])]
+    )
+
+
+def sum_of(blocks, start, width, tokens, t_start, total, fresh=True):
+    for k in range(0, width, 1024):
+        tile = min(1024, width - k)
+        rows = []
+        for block in blocks:
+            parts = [p[:, o + start + k : o + start + k + tile] for p, o in block]
+            rows.append(parts[0] if len(parts) == 1 else parts[0] + parts[1])
+        part = lax.dot_general(
+            tokens[:, t_start + k : t_start + k + tile],
+            jnp.concatenate(rows, axis=0) if len(rows) > 1 else rows[0],
+            (((1,), (1,)), ((), ())),
+            preferred_element_type=FLOAT,
         )
-    scores = total[:, 0]
-    for n in range(1, n_wide):
-        shift = [(w, (w - n) % n_wide) for w in range(n_wide)]
-        scores = scores + lax.ppermute(total[:, n], "wide", shift)
-
-    all_seqs = n_wide * chip_seqs
-    n_blocks = candidate.shape[1]
-    block_size = all_seqs // n_blocks
-    seq_index = wide * chip_seqs + jnp.arange(chip_seqs, dtype=jnp.int32)
-    one_hot = (seq_index[None, :] // block_size == jnp.arange(n_blocks, dtype=jnp.int32)[:, None]).astype(jnp.float32)
-    keep_mask = jnp.dot(candidate.astype(jnp.float32), one_hot, preferred_element_type=jnp.float32)
-    return scores * keep_mask
+        if fresh and k == 0:
+            total[...] = part
+        else:
+            total[...] += part
+
+
+def put(out, place, rows, value):
+    out[pl.ds(pl.multiple_of(place * rows, rows), rows), :] = value
+
+
+def own_body(b_out, b_in, t_out, t_in, g_own, a_own, total):
+    sum_of([[(b_out, 0)]], 0, b_out.shape[1], t_out, 0, total)
+    g_own[...] = total[...].T
+    sum_of([[(b_in, 0)]], 0, b_in.shape[1], t_in, 0, total)
+    a_own[...] = total[...].T
+
+
+def first_body(at, x, y, x_far, y_far, t_out, t_in, g_first, a_first, total):
+    group, rep = at[0], at[3]
+    blocks = [[(p, 0)] for p in (x, y, x_far, y_far)]
+    half, d = x.shape[0], t_out.shape[1]
+    places = (2 * rep + group, 2 * rep + 1 - group, 2 * (1 - rep) + group, 2 * (1 - rep) + 1 - group)
+    for start, tokens, out in ((0, t_out, g_first), (d, t_in, a_first)):
+        sum_of(blocks, start, tokens.shape[1], tokens, 0, total)
+        turned = total[...].T
+        for r, place in enumerate(places):
+            put(out, place, half, turned[r * half : (r + 1) * half])
+
+
+def late_blocks(second, third, shift):
+    x2, y2, x2_far, y2_far = second
+    x3, y3, x3_far, y3_far = third
+    return [
+        [(x2, shift), (x2_far, shift)],
+        [(y2, shift), (y2_far, shift)],
+        [(x3, 0), (x3_far, 0)],
+        [(y3, 0), (y3_far, 0)],
+    ]
+
+
+def place_all(at, own, first, total, store):
+    group, wide = at[0], at[1]
+    rows = own.shape[0]
+    half = rows // 2
+    store(0, own[...], None)
+    store(1, first[rows:, :], wide <= 2)
+    store(3, first[:rows, :], wide >= 1)
+    turned = total[...].T
+
+    def ordered(k):
+        mine, other = (turned[(2 * k + i) * half : (2 * k + i + 1) * half] for i in range(2))
+        return jnp.concatenate(
+            [jnp.where(group == 0, mine, other), jnp.where(group == 0, other, mine)], axis=0
+        )
+
+    store(2, ordered(0), None)
+    last = ordered(1)
+    store(1, last, wide == 3)
+    store(3, last, wide == 0)
+
+
+def when(condition, do):
+    if condition is None:
+        do()
+    else:
+        pl.when(condition)(do)
+
+
+def out_body(n_second, at, *refs):
+    second, third = refs[:4], refs[4:8]
+    t_out, t_in, own, first, grad, grad_sent, part, total = refs[8:]
+    blocks = late_blocks(second, third, 0)
+    d = t_out.shape[1]
+    sum_of(blocks, 0, d, t_out, 0, total)
+
+    def store(slot, value, condition):
+        rows = value.shape[0]
+
+        def do():
+            grad[slot * rows : (slot + 1) * rows, :] = value
+            grad_sent[slot * rows : (slot + 1) * rows, :] = value.astype(HALF)
+
+        when(condition, do)
+
+    place_all(at, own, first, total, store)
+    sum_of(blocks, d, third[0].shape[1] - d, t_in, 0, part)
+
+
+def in_body(shift, at, *refs):
+    second, third = refs[:4], refs[4:8]
+    t_in, part, own, first, mine, sent, total = refs[8:]
+    total[...] = part[...]
+    width = third[0].shape[1]
+    sum_of(late_blocks(second, third, shift), 0, width, t_in, t_in.shape[1] - width, total, fresh=False)
+    wide, layer = at[1], at[2]
+
+    def store(slot, value, condition):
+        rows = value.shape[0]
+        shard = lax.rem(wide + slot, 4)
+        per_layer = mine.shape[0] // rows
+        place = lax.rem(shard, per_layer)
+        here = lax.div(shard, per_layer) == layer
+
+        def keep():
+            put(mine, place, rows, value)
+
+        def send():
+            put(sent, place, rows, value.astype(HALF))
+
+        both = (here, jnp.logical_not(here)) if condition is None else (condition & here, condition & jnp.logical_not(here))
+        pl.when(both[0])(keep)
+        pl.when(both[1])(send)
+
+    place_all(at, own, first, total, store)
+
+
+def train_body(at, counts, grad, grad_came, act, act_came, *refs):
+    mine, theirs, held = refs[:4], refs[4:8], refs[8]
+    rep = at[3]
+    seqs, half = mine[0].shape[0], mine[0].shape[1]
+    length = grad.shape[1] // seqs
+    spot = lax.broadcasted_iota(jnp.int32, (1, length), 1)
+    for s in range(seqs):
+        cols = slice(s * length, (s + 1) * length)
+        g = grad[:, cols] + grad_came[:, cols].astype(FLOAT)
+        g = jnp.where(spot < counts[s], g, 0.0).astype(HALF)
+        a = (act[:, cols] + act_came[:, cols].astype(FLOAT)).astype(HALF)
+        held[...] = lax.dot_general(g, a, (((1,), (1,)), ((), ())), preferred_element_type=FLOAT).astype(HALF)
+        for n in range(4):
+            for r, outs in ((rep, mine), (1 - rep, theirs)):
+                outs[n][s] = held[pl.ds(pl.multiple_of((2 * n + r) * half, half), half), :]
+
+
+def shaped(*shape, kind=FLOAT):
+    return jax.ShapeDtypeStruct(shape, kind)
+
+
+def local_fast(acts, grads, counts, basis_in, basis_out, query_grads, eigenvalues, candidate):
+    n_wide, n_layer = 4, 2
+    seq_dev, seq_len, ff = acts.shape
+    d = grads.shape[2]
+    n_tok = seq_dev * seq_len
+    rows = basis_in.shape[0]
+    half = rows // 2
+    share = n_wide * rows // n_layer
+    group, wide, layer, rep = (lax.axis_index(a) for a in ("groups", "wide", "layer", "rep"))
+    at = jnp.stack([group, wide, layer, rep]).astype(jnp.int32)
+    swap = [(0, 1), (1, 0)]
+    dma = pltpu.SemaphoreType.DMA((2,))
+
+    held = jnp.concatenate(
+        [lax.dynamic_slice_in_dim(x, group * half, half, axis=0) for x in (basis_out, basis_in)], axis=1
+    )
+    t_out, t_in = kernel(
+        load_body, [pltpu.VMEM((n_tok, d), HALF), pltpu.VMEM((n_tok, ff), HALF)], [dma], grant=4
+    )(in_specs=[ANY, ANY], out_specs=[VMEM, VMEM])(grads.reshape(n_tok, d), acts.reshape(n_tok, ff))
+    g_own, a_own = kernel(
+        own_body, [shaped(rows, n_tok)] * 2, [pltpu.VMEM((n_tok, rows), FLOAT)], 2 * rows * n_tok * (d + ff)
+    )(in_specs=[VMEM] * 4, out_specs=[VMEM] * 2)(basis_out, basis_in, t_out, t_in)
+
+    def to_group(x, k):
+        pairs = swap_pairs(2 * n_wide, functools.partial(holds, k=k, n_wide=n_wide))
+        return lax.ppermute(x, ("groups", "wide", "rep"), pairs)
+
+    def to_core(x, k):
+        return lax.ppermute(x, ("wide", "rep"), [(p, p ^ 1) for p in range(2 * n_wide) if holds(p, k, n_wide)])
+
+    def hop(x, k):
+        return lax.ppermute(x, ("wide", "rep"), hop_pairs(k, n_wide))
+
+    x1 = hop(held, 1)
+    y1 = to_group(x1, 1)
+    x2 = hop(after(x1, g_own, a_own), 2)
+    y2 = to_group(x2, 2)
+    cut = (ff - d) // 256 * 128
+    x3 = [hop(x2[:, : d + cut], 3), hop(x2[:, d + cut :], 3)]
+    y3 = [to_group(x, 3) for x in x3]
+
+    def on_both(x, y, k, *earlier):
+        return x, y, to_core(after(x, *earlier), k), to_core(after(y, *earlier), k)
+
+    first = on_both(x1, y1, 1, *x3)
+    g_first, a_first = kernel(
+        first_body, [shaped(2 * rows, n_tok)] * 2, [pltpu.VMEM((n_tok, 2 * rows), FLOAT)], 4 * rows * n_tok * (d + ff)
+    )(in_specs=[SMEM] + [VMEM] * 6, out_specs=[VMEM] * 2)(at, *first, t_out, t_in)
+    second = on_both(x2, y2, 2, *x3)
+    thirds = [on_both(x3[0], y3[0], 3), on_both(x3[1], y3[1], 3)]
+
+    wide_sum = pltpu.VMEM((n_tok, 2 * rows), FLOAT)
+    grad, grad_sent, part = kernel(
+        functools.partial(out_body, 4),
+        [shaped(n_wide * rows, n_tok), shaped(n_wide * rows, n_tok, kind=HALF), shaped(n_tok, 2 * rows)],
+        [wide_sum],
+        4 * rows * n_tok * (d + cut),
+    )(in_specs=[SMEM] + [VMEM] * 12, out_specs=[VMEM] * 3)(
+        at, *second, *thirds[0], t_out, t_in, g_own, g_first
+    )
+    grad_came = lax.ppermute(grad_sent, "layer", swap)
+    act, act_sent = kernel(
+        functools.partial(in_body, d + cut),
+        [shaped(share, n_tok), shaped(share, n_tok, kind=HALF)],
+        [wide_sum],
+        4 * rows * n_tok * (ff - cut),
+    )(in_specs=[SMEM] + [VMEM] * 12, out_specs=[VMEM] * 2)(
+        at, *second, *thirds[1], t_in, part, a_own, a_first
+    )
+    act_came = lax.ppermute(after(act_sent, grad_came), "layer", swap)
+
+    pieces = kernel(
+        train_body,
+        [shaped(seq_dev, half, share, kind=HALF)] * 8,
+        [pltpu.VMEM((n_wide * rows, share), HALF)],
+        2 * n_wide * rows * share * n_tok,
+    )(in_specs=[SMEM, SMEM] + [VMEM] * 4, out_specs=[VMEM] * 8)(at, counts, grad, grad_came, act, act_came)
+    mine, theirs = pieces[:4], pieces[4:]
+
+    def send(x, n, cross):
+        pairs = [(2 * w + r, 2 * ((w + n) % n_wide) + (r ^ cross)) for w in range(n_wide) for r in range(2)]
+        return lax.ppermute(x, ("wide", "rep"), pairs)
+
+    same = [mine[0]] + [send(mine[n], n, 0) for n in range(1, n_wide)]
+    cross = [send(theirs[n], n, 1) for n in range(n_wide)]
+    chip_seqs = 2 * seq_dev
+    train = jnp.stack([jnp.stack([a, b]) for a, b in zip(same, cross, strict=True)])
+    train = train.reshape(n_wide * chip_seqs, half * share)
+    n_query = query_grads.shape[0]
+    weighted = (query_grads.astype(FLOAT) / eigenvalues[None, :, :]).astype(HALF).reshape(n_query, half * share)
+    scored = lax.dot_general(weighted, train, (((1,), (1,)), ((), ())), preferred_element_type=FLOAT)
+    scored = scored.reshape(n_query, n_wide, 2, seq_dev)
+    scored = jnp.where(rep == 0, scored, scored[:, :, ::-1]).reshape(n_query, n_wide * chip_seqs)
+    return finish(scored, candidate, n_wide, n_layer, chip_seqs)
 
 
 def solution(mesh):
+    sizes = tuple(mesh.shape[a] for a in ("groups", "wide", "layer", "rep"))
+    body = local_fast if sizes == (2, 4, 2, 2) else local
     in_specs = (
         P(("groups", "wide", "rep"), None, "layer"),
         P(("groups", "wide", "rep"), None, "layer"),
@@ -147,4 +463,4 @@
         P(("layer", "rep"), "groups"),
     )
     out_specs = P(("layer", "rep"), ("groups", "wide"))
-    return jax.shard_map(local, mesh=mesh, in_specs=in_specs, out_specs=out_specs, check_vma=False)
+    return jax.shard_map(body, mesh=mesh, in_specs=in_specs, out_specs=out_specs, check_vma=False)

time: 151 us -> 153 us (1.013)
  waiting for transfers between devices: 42.8 us -> 62.4 us
  matrix products: 21.8 us -> 3.1 us
  Pallas kernels: 0 us -> 17.1 us
  other arithmetic: 15.1 us -> 1.71 us
    ppermute x35 -> x29, waiting for transfers between devices: 42.8 us -> 62.4 us  [the longest x8 31.6 us: to_core(): lax.ppermute(x, ('wide', 'rep'), [(p, p ^ 1) for p in range(2 * n_wide) i...]
    dot_general x10 -> x1, matrix products: 21.8 us -> 3.1 us  [local_fast(): lax.dot_general(weighted, train, (((1,), (1,)), ((), ())), preferred_elem...]
    pallas_call x0 -> x6, Pallas kernels: none -> 17.1 us  [the longest x1 4.97 us: local_fast(): kernel(functools.partial(out_body, 4), [shaped(n_wide * rows, n_tok), sha...]
    concatenate x6 -> x2, other arithmetic: 8.52 us -> 0.13 us  [the longest x1 0.08 us: local_fast(): jnp.concatenate([lax.dynamic_slice_in_dim(x, group * half, half, axis=0)...]
    unnamed x21 -> x45, local copies, waits for them, and re-layouts: 0.86 us -> 9.03 us
    dot_general x1 -> x0, local copies, waits for them, and re-layouts: 4.18 us -> none  [local(): lax.dot_general(weighted, train, (((1,), (1,)), ((), ())), preferred_elem...]
    convert_element_type x6 -> x1, other arithmetic: 4.39 us -> 0.58 us  [local_fast(): (query_grads.astype(FLOAT) / eigenvalues[None, :, :]).astype(HALF)]
    another operation x4 -> x1, local copies, waits for them, and re-layouts: 2.76 us -> 0.1 us  [finish(): part = partial_value.reshape(n_layer, 2, block, n_wide, chip_seqs)]
  transfers between devices with their start and end apart: 35 -> 29, of which waited for: 13 -> 15; matrix products, arithmetic and copies ran while one was open for 27% -> 1% of each run, Pallas kernels for 0% -> 11%
where the time goes in v3:
time: 153 us; the launch traced here: 152 us
  waiting for transfers between devices  62.4 us (41%)
  starting transfers between devices  56.8 us (37%)
  Pallas kernels  17.1 us (11%)
  local copies, waits for them, and re-layouts  10.6 us (7%)
  matrix products  3.1 us (2%)
  other arithmetic  1.71 us (1%)
    ppermute x8, waiting for transfers between devices, to_core(): lax.ppermute(x, ('wide', 'rep'), [(p, p ^ 1) for p in range(2 * n_wide) i...  31.6 us
    ppermute x7, starting transfers between devices, send(): return lax.ppermute(x, ('wide', 'rep'), pairs)  20.2 us
    ppermute x8, starting transfers between devices, to_core(): lax.ppermute(x, ('wide', 'rep'), [(p, p ^ 1) for p in range(2 * n_wide) i...  10.3 us
    ppermute x7, waiting for transfers between devices, send(): return lax.ppermute(x, ('wide', 'rep'), pairs)  9.49 us
    unnamed x45, local copies, waits for them, and re-layouts  9.03 us
    ppermute x4, starting transfers between devices, hop(): return lax.ppermute(x, ('wide', 'rep'), hop_pairs(k, n_wide))  8.23 us
    ppermute x2, starting transfers between devices, finish(): lax.ppermute(give, 'wide', [(w, w ^ bit) for w in range(n_wide)])  7.78 us
    ppermute x4, waiting for transfers between devices, hop(): return lax.ppermute(x, ('wide', 'rep'), hop_pairs(k, n_wide))  6.23 us
  transfers between devices with their start and end apart: 29, of which 15 were waited for; matrix products, arithmetic and copies ran while one was open for 1% of the time, Pallas kernels for 11%

profile of v3, /device:TPU:0, one launch (start us, length us, event | category | flops | bytes accessed | tf_op | source)
XLA Modules:
  0.0 152.4 jit_solution(11266946007357933515)
XLA Ops:
  0.0 1.3 constant_dynamic-slice_fusion.2
  1.4 0.1 pad_maximum_fusion
  1.5 6.1 %collective-permute-start = (bf16[64,9472]{1,0:T(8,128)(2,1)S(1)}, bf16[64,9472]{1,0:T(8,128)(2,1)}, u32[]{:S(2)}, u32[]{:S(2)}) collective-permute-start(bf16[64,9472]{1,0:T(8,128)(2,1)S(1)} %pad_maximum_fusion), channel_id=1, source_target_pairs={{0,4},{4,8},{8,12},{5,1},{9,5},{13,9},{2,6},{6,10},{10,14},{7,3},{... | collective-permute-start | bytes 3637256 | tf_op jit(solution)/shard_map/ppermute | solution.py:387
  7.6 2.5 %copy-done.2 = bf16[3,128,6912]{2,1,0:T(8,128)(2,1)S(1)} copy-done((bf16[3,128,6912]{2,1,0:T(8,128)(2,1)S(1)}, bf16[3,128,6912]{2,1,0:T(8,128)(2,1)}, u32[]{:S(2)}) %copy-start.2) | copy-done | bytes 5308440
  10.1 0.8 shard_map.82
  10.9 0.7 copy-done.3
  11.6 2.1 %shard_map.83 = (f32[128,384]{1,0:T(8,128)S(1)}, f32[128,384]{1,0:T(8,128)S(1)}) custom-call(bf16[128,2560]{1,0:T(8,128)(2,1)S(1)} %copy-done.5, bf16[128,6912]{1,0:T(8,128)(2,1)S(1)} %copy-done.3, bf16[384,2560]{1,0:T(8,128)(2,1)S(1)} %get-tuple-element.30.t_out.refs_8_, bf16[384,6912]{1,0:T(8,128)(2,1)S(1)} %get-tuple-element.31.t_in.refs_9_.refs_8_), custom_call_target="tpu_custom_call" | custom-call | flops 931135488 | bytes 2328862 | tf_op jit(solution)/shard_map/pallas_call | solution.py:375
  13.7 0.7 copy-done.14
  14.4 6.2 %collective-permute-done.x = bf16[64,9472]{1,0:T(8,128)(2,1)} collective-permute-done((bf16[64,9472]{1,0:T(8,128)(2,1)S(1)}, bf16[64,9472]{1,0:T(8,128)(2,1)}, u32[]{:S(2)}, u32[]{:S(2)}) %collective-permute-start) | collective-permute-done | bytes 1212448 | tf_op jit(solution)/shard_map/ppermute | solution.py:387
  20.6 0.7 collective-permute-start.1
  21.3 1.7 %collective-permute-start.10 = (bf16[64,9472]{1,0:T(8,128)(2,1)}, bf16[64,9472]{1,0:T(8,128)(2,1)}, u32[]{:S(2)}, u32[]{:S(2)}) collective-permute-start(bf16[64,9472]{1,0:T(8,128)(2,1)} %collective-permute-done.x), channel_id=1, source_target_pairs={{1,17},{4,20},{5,21},{8,24},{9,25},{12,28},{17,1},{20,4},{21,5},{2... | collective-permute-start | bytes 3637256 | tf_op jit(solution)/shard_map/ppermute | solution.py:381
  23.0 1.7 %collective-permute-start.2 = (bf16[64,9472]{1,0:T(8,128)(2,1)S(1)}, bf16[64,9472]{1,0:T(8,128)(2,1)}, u32[]{:S(2)}, u32[]{:S(2)}) collective-permute-start(bf16[64,9472]{1,0:T(8,128)(2,1)S(1)} %collective-permute-done.1.refs_0_), channel_id=1, source_target_pairs={{1,17},{5,21},{8,24},{12,28},{17,1},{21,5},{24,8},{28,12},{3,19},{... | collective-permute-start | bytes 3637256 | tf_op jit(solution)/shard_map/ppermute | solution.py:381
  24.7 0.1 fusion.18
  24.8 0.7 collective-permute-start.3
  25.5 0.7 collective-permute-start.4
  26.2 1.5 collective-permute-start.7
  27.7 1.3 collective-permute-start.8
  29.0 0.8 copy-done.10
  29.9 1.3 collective-permute-start.12
  31.2 1.3 collective-permute-start.11
  32.5 1.3 collective-permute-start.5
  33.8 0.7 collective-permute-start.14
  34.5 22.4 %collective-permute-done.8.refs_6_ = bf16[64,4736]{1,0:T(8,128)(2,1)S(1)} collective-permute-done((bf16[64,4736]{1,0:T(8,128)(2,1)S(1)}, bf16[64,4736]{1,0:T(8,128)(2,1)S(1)}, u32[]{:S(2)}, u32[]{:S(2)}) %collective-permute-start.8) | collective-permute-done | bytes 606240 | tf_op jit(solution)/shard_map/ppermute | solution.py:384
  56.9 0.8 copy-done.12
  57.7 1.3 collective-permute-start.6
  59.1 0.8 copy-done.8
  59.9 1.3 collective-permute-start.9
  61.2 1.3 collective-permute-done.12.y_far
  62.5 1.3 collective-permute-start.15
  63.7 1.0 collective-permute-done.11.x_far
  64.8 1.3 collective-permute-start.16
  66.1 0.1 pad_add_fusion.at
  66.1 2.5 %copy-done.1 = bf16[384,6912]{1,0:T(8,128)(2,1)S(1)} copy-done((bf16[384,6912]{1,0:T(8,128)(2,1)S(1)}, bf16[384,6912]{1,0:T(8,128)(2,1)}, u32[]{:S(2)}) %copy-start.1) | copy-done | bytes 5308440
  68.7 4.7 %shard_map.84 = (f32[256,384]{1,0:T(8,128)S(1)}, f32[256,384]{1,0:T(8,128)S(1)}) custom-call(s32[4]{0:T(128)S(1)} %pad_add_fusion.at, bf16[64,9472]{1,0:T(8,128)(2,1)} %collective-permute-done.x, bf16[64,9472]{1,0:T(8,128)(2,1)} %collective-permute-done.10.y, bf16[64,9472]{1,0:T(8,128)(2,1)} %collective-permute-done.11.x_far, ...), custom_call_target="tpu_custom_call" | custom-call | flops 1862270976 | bytes 4656701 | tf_op jit(solution)/shard_map/pallas_call | solution.py:401
  73.4 7.0 %collective-permute-done.9.refs_7_ = bf16[64,4736]{1,0:T(8,128)(2,1)} collective-permute-done((bf16[64,4736]{1,0:T(8,128)(2,1)}, bf16[64,4736]{1,0:T(8,128)(2,1)}, u32[]{:S(2)}, u32[]{:S(2)}) %collective-permute-start.9) | collective-permute-done | bytes 606240 | tf_op jit(solution)/shard_map/ppermute | solution.py:384
  80.4 5.0 %shard_map.85 = (f32[512,384]{1,0:T(8,128)S(1)}, bf16[512,384]{1,0:T(8,128)(2,1)S(1)}, f32[384,256]{1,0:T(8,128)S(1)}) custom-call(s32[4]{0:T(128)S(1)} %pad_add_fusion.at, bf16[64,9472]{1,0:T(8,128)(2,1)S(1)} %collective-permute-done.1.refs_0_, bf16[64,9472]{1,0:T(8,128)(2,1)} %collective-permute-done.2.refs_1_, ...), custom_call_target="tpu_custom_call" | custom-call | flops 931135488 | bytes 2328862 | tf_op jit(solution)/shard_map/pallas_call | solution.py:408
  85.4 1.6 %collective-permute-start.13 = (bf16[512,384]{1,0:T(8,128)(2,1)S(1)}, bf16[512,384]{1,0:T(8,128)(2,1)S(1)}, u32[]{:S(2)}, u32[]{:S(2)}) collective-permute-start(bf16[512,384]{1,0:T(8,128)(2,1)S(1)} %get-tuple-element.41), channel_id=1, source_target_pairs={{0,2},{2,0},{1,3},{3,1},{4,6},{6,4},{5,7},{7,5},{8,10},{10,8},{9,1... | collective-permute-start | bytes 1179656 | tf_op jit(solution)/shard_map/ppermute | solution.py:416
  87.0 3.6 %shard_map.86 = (f32[256,384]{1,0:T(8,128)S(1)}, bf16[256,384]{1,0:T(8,128)(2,1)S(1)}) custom-call(s32[4]{0:T(128)S(1)} %pad_add_fusion.at, bf16[64,9472]{1,0:T(8,128)(2,1)S(1)} %collective-permute-done.1.refs_0_, bf16[64,9472]{1,0:T(8,128)(2,1)} %collective-permute-done.2.refs_1_, bf16[64,9472]{1,0:T(8,128)(2,1)} %collective-permute-done.5.refs_2_, ...), custom_call_target="tpu_custom_call" | custom-call | flops 931135488 | bytes 2328862 | tf_op jit(solution)/shard_map/pallas_call | solution.py:417
  90.6 2.5 %collective-permute-done.13.grad_came = bf16[512,384]{1,0:T(8,128)(2,1)S(1)} collective-permute-done((bf16[512,384]{1,0:T(8,128)(2,1)S(1)}, bf16[512,384]{1,0:T(8,128)(2,1)S(1)}, u32[]{:S(2)}, u32[]{:S(2)}) %collective-permute-start.13) | collective-permute-done | bytes 393248 | tf_op jit(solution)/shard_map/ppermute | solution.py:416
  93.2 1.5 collective-permute-start.17
  94.7 6.0 %collective-permute-done.17.act_came = bf16[256,384]{1,0:T(8,128)(2,1)S(1)} collective-permute-done((bf16[256,384]{1,0:T(8,128)(2,1)S(1)}, bf16[256,384]{1,0:T(8,128)(2,1)S(1)}, u32[]{:S(2)}, u32[]{:S(2)}) %collective-permute-start.17) | collective-permute-done | bytes 196640 | tf_op jit(solution)/shard_map/ppermute | solution.py:425
  100.7 1.0 shard_map.87
  101.7 6.8 %collective-permute-start.18 = (bf16[3,64,256]{2,1,0:T(8,128)(2,1)S(1)}, bf16[3,64,256]{2,1,0:T(8,128)(2,1)S(1)}, u32[]{:S(2)}, u32[]{:S(2)}) collective-permute-start(bf16[3,64,256]{2,1,0:T(8,128)(2,1)S(1)} %get-tuple-element.48), channel_id=1, source_target_pairs={{0,1},{1,0},{4,5},{5,4},{8,9},{9,8},{12,13},{13,12},{2,3},{3,2},{6... | collective-permute-start | bytes 294920 | tf_op jit(solution)/shard_map/ppermute | solution.py:437
  108.5 0.6 fusion
  109.1 0.1 collective-permute-start.19
  109.2 9.6 %collective-permute-start.21 = (bf16[3,64,256]{2,1,0:T(8,128)(2,1)S(1)}, bf16[3,64,256]{2,1,0:T(8,128)(2,1)S(1)}, u32[]{:S(2)}, u32[]{:S(2)}) collective-permute-start(bf16[3,64,256]{2,1,0:T(8,128)(2,1)S(1)} %get-tuple-element.51), channel_id=1, source_target_pairs={{0,8},{1,9},{4,12},{5,13},{8,0},{9,1},{12,4},{13,5},{2,10},{3,11},... | collective-permute-start | bytes 294920 | tf_op jit(solution)/shard_map/ppermute | solution.py:437
  118.8 2.6 %collective-permute-start.23 = (bf16[3,64,256]{2,1,0:T(8,128)(2,1)S(1)}, bf16[3,64,256]{2,1,0:T(8,128)(2,1)S(1)}, u32[]{:S(2)}, u32[]{:S(2)}) collective-permute-start(bf16[3,64,256]{2,1,0:T(8,128)(2,1)S(1)} %get-tuple-element.53), channel_id=1, source_target_pairs={{0,12},{1,13},{4,0},{5,1},{8,4},{9,5},{12,8},{13,9},{2,14},{3,15},... | collective-permute-start | bytes 294920 | tf_op jit(solution)/shard_map/ppermute | solution.py:437
  121.4 0.4 collective-permute-done.19
  121.9 1.1 collective-permute-start.24
  122.9 0.7 collective-permute-done.20
  123.6 6.4 %collective-permute-done.21 = bf16[3,64,256]{2,1,0:T(8,128)(2,1)S(1)} collective-permute-done((bf16[3,64,256]{2,1,0:T(8,128)(2,1)S(1)}, bf16[3,64,256]{2,1,0:T(8,128)(2,1)S(1)}, u32[]{:S(2)}, u32[]{:S(2)}) %collective-permute-start.21) | collective-permute-done | bytes 98336 | tf_op jit(solution)/shard_map/ppermute | solution.py:437
  130.0 2.0 %collective-permute-done.22 = bf16[3,64,256]{2,1,0:T(8,128)(2,1)S(1)} collective-permute-done((bf16[3,64,256]{2,1,0:T(8,128)(2,1)S(1)}, bf16[3,64,256]{2,1,0:T(8,128)(2,1)S(1)}, u32[]{:S(2)}, u32[]{:S(2)}) %collective-permute-start.22) | collective-permute-done | bytes 98336 | tf_op jit(solution)/shard_map/ppermute | solution.py:437
  132.1 0.1 pad_maximum_fusion.1
  132.2 3.1 %fusion.3 = f32[64,4,2,3]{0,1,3,2:T(4,128)S(1)} fusion(bf16[64,64,256,1,1]{2,1,0,4,3:T(8,128)(2,1)S(1)} %fusion, bf16[4,2,3,64,256]{4,3,2,1,0:T(8,128)(2,1)S(1)} %pad_maximum_fusion.1), kind=kOutput, calls=%fused_computation.5 | convolution fusion | flops 50331648 | bytes 2889728 | tf_op jit(solution)/shard_map/dot_general | solution.py:446
  135.3 0.1 reshape_reshape.3
  135.5 0.2 collective-permute-start.25
  135.7 1.1 collective-permute-done.25
  136.8 1.6 %collective-permute-start.26 = (f32[16,4,6]{0,1,2:T(4,128)S(1)}, f32[16,4,6]{0,1,2:T(4,128)S(1)}, u32[]{:S(2)}, u32[]{:S(2)}) collective-permute-start(f32[16,4,6]{0,1,2:T(4,128)S(1)} %dynamic-slice_bitcast_fusion), channel_id=1, source_target_pairs={{0,2},{2,0},{1,3},{3,1},{4,6},{6,4},{5,7},{7,5},{8,10},{10,8},{9,1... | collective-permute-start | bytes 4616 | tf_op jit(solution)/shard_map/ppermute | solution.py:67
  138.4 2.2 %collective-permute-done.26 = f32[16,4,6]{0,1,2:T(4,128)S(1)} collective-permute-done((f32[16,4,6]{0,1,2:T(4,128)S(1)}, f32[16,4,6]{0,1,2:T(4,128)S(1)}, u32[]{:S(2)}, u32[]{:S(2)}) %collective-permute-start.26) | collective-permute-done | bytes 1568 | tf_op jit(solution)/shard_map/ppermute | solution.py:67
  140.7 3.9 %collective-permute-start.27 = (f32[16,2,6]{0,1,2:T(2,128)S(1)}, f32[16,2,6]{0,1,2:T(2,128)S(1)}, u32[]{:S(2)}, u32[]{:S(2)}) collective-permute-start(f32[16,2,6]{0,1,2:T(2,128)S(1)} %fusion.11), channel_id=1, source_target_pairs={{0,8},{4,12},{8,0},{12,4},{1,9},{5,13},{9,1},{13,5},{2,10},{6,14},... | collective-permute-start | bytes 2312 | tf_op jit(solution)/shard_map/ppermute | solution.py:80
  144.6 1.6 %collective-permute-done.27 = f32[16,2,6]{0,1,2:T(2,128)S(1)} collective-permute-done((f32[16,2,6]{0,1,2:T(2,128)S(1)}, f32[16,2,6]{0,1,2:T(2,128)S(1)}, u32[]{:S(2)}, u32[]{:S(2)}) %collective-permute-start.27) | collective-permute-done | bytes 800 | tf_op jit(solution)/shard_map/ppermute | solution.py:80
  146.2 3.9 %collective-permute-start.28 = (f32[16,1,6]{0,1,2:T(1,128)S(1)}, f32[16,1,6]{0,1,2:T(1,128)S(1)}, u32[]{:S(2)}, u32[]{:S(2)}) collective-permute-start(f32[16,1,6]{0,1,2:T(1,128)S(1)} %fusion.17), channel_id=1, source_target_pairs={{0,4},{4,0},{8,12},{12,8},{1,5},{5,1},{9,13},{13,9},{2,6},{6,2},{1... | collective-permute-start | bytes 1160 | tf_op jit(solution)/shard_map/ppermute | solution.py:80
  150.1 1.6 %collective-permute-done.28 = f32[16,1,6]{0,1,2:T(1,128)S(1)} collective-permute-done((f32[16,1,6]{0,1,2:T(1,128)S(1)}, f32[16,1,6]{0,1,2:T(1,128)S(1)}, u32[]{:S(2)}, u32[]{:S(2)}) %collective-permute-start.28) | collective-permute-done | bytes 416 | tf_op jit(solution)/shard_map/ppermute | solution.py:80
  151.7 0.7 bitcast_multiply_fusion
  (75 shorter events, 0.6 us)
Async XLA Ops:
  0.0 1.4 copy-start.5
  1.4 6.2 %copy-start.4 = (bf16[3,128,2560]{2,1,0:T(8,128)(2,1)S(1)}, bf16[3,128,2560]{2,1,0:T(8,128)(2,1)}, u32[]{:S(2)}) copy-start(bf16[3,128,2560]{2,1,0:T(8,128)(2,1)} %param.9) | copy-start | bytes 5898244
  1.5 19.1 %collective-permute-start = (bf16[64,9472]{1,0:T(8,128)(2,1)S(1)}, bf16[64,9472]{1,0:T(8,128)(2,1)}, u32[]{:S(2)}, u32[]{:S(2)}) collective-permute-start(bf16[64,9472]{1,0:T(8,128)(2,1)S(1)} %pad_maximum_fusion), channel_id=1, source_target_pairs={{0,4},{4,8},{8,12},{5,1},{9,5},{13,9},{2,6},{6,10},{10,14},{7,3},{... | collective-permute-start | bytes 3637256 | tf_op jit(solution)/shard_map/ppermute | solution.py:387
  7.6 2.5 %copy-start.2 = (bf16[3,128,6912]{2,1,0:T(8,128)(2,1)S(1)}, bf16[3,128,6912]{2,1,0:T(8,128)(2,1)}, u32[]{:S(2)}) copy-start(bf16[3,128,6912]{2,1,0:T(8,128)(2,1)} %param.8) | copy-start | bytes 15925252
  10.1 1.5 copy-start.3
  10.8 2.8 %copy-start = (bf16[384,6912]{1,0:T(8,128)(2,1)}, bf16[384,6912]{1,0:T(8,128)(2,1)S(1)}, u32[]{:S(2)}) copy-start(bf16[384,6912]{1,0:T(8,128)(2,1)S(1)} %get-tuple-element.31.t_in.refs_9_.refs_8_) | copy-start | bytes 15925252
  13.7 0.7 copy-start.14
  20.6 2.4 %collective-permute-start.1 = (bf16[64,9472]{1,0:T(8,128)(2,1)}, bf16[64,9472]{1,0:T(8,128)(2,1)S(1)}, u32[]{:S(2)}, u32[]{:S(2)}) collective-permute-start(bf16[64,9472]{1,0:T(8,128)(2,1)} %collective-permute-done.x), channel_id=1, source_target_pairs={{4,8},{8,12},{5,1},{9,5},{6,10},{10,14},{7,3},{11,7},{20,24},{24,2... | collective-permute-start | bytes 3637256 | tf_op jit(solution)/shard_map/ppermute | solution.py:387
  21.3 8.5 %collective-permute-start.10 = (bf16[64,9472]{1,0:T(8,128)(2,1)}, bf16[64,9472]{1,0:T(8,128)(2,1)}, u32[]{:S(2)}, u32[]{:S(2)}) collective-permute-start(bf16[64,9472]{1,0:T(8,128)(2,1)} %collective-permute-done.x), channel_id=1, source_target_pairs={{1,17},{4,20},{5,21},{8,24},{9,25},{12,28},{17,1},{20,4},{21,5},{2... | collective-permute-start | bytes 3637256 | tf_op jit(solution)/shard_map/ppermute | solution.py:381
  23.0 9.5 %collective-permute-start.2 = (bf16[64,9472]{1,0:T(8,128)(2,1)S(1)}, bf16[64,9472]{1,0:T(8,128)(2,1)}, u32[]{:S(2)}, u32[]{:S(2)}) collective-permute-start(bf16[64,9472]{1,0:T(8,128)(2,1)S(1)} %collective-permute-done.1.refs_0_), channel_id=1, source_target_pairs={{1,17},{5,21},{8,24},{12,28},{17,1},{21,5},{24,8},{28,12},{3,19},{... | collective-permute-start | bytes 3637256 | tf_op jit(solution)/shard_map/ppermute | solution.py:381
  24.8 1.4 collective-permute-start.3
  25.5 4.4 %collective-permute-start.4 = (bf16[64,4736]{1,0:T(8,128)(2,1)S(1)}, bf16[64,4736]{1,0:T(8,128)(2,1)S(1)}, u32[]{:S(2)}, u32[]{:S(2)}) collective-permute-start(bf16[64,4736]{1,0:T(8,128)(2,1)S(1)} %get-tuple-element.55), channel_id=1, source_target_pairs={{8,12},{5,1},{10,14},{7,3},{24,28},{21,17},{26,30},{23,19}} | collective-permute-start | bytes 1818632 | tf_op jit(solution)/shard_map/ppermute | solution.py:387
  26.2 7.6 %collective-permute-start.7 = (bf16[64,4736]{1,0:T(8,128)(2,1)S(1)}, bf16[64,4736]{1,0:T(8,128)(2,1)}, u32[]{:S(2)}, u32[]{:S(2)}) collective-permute-start(bf16[64,4736]{1,0:T(8,128)(2,1)S(1)} %collective-permute-done.3.refs_4_), channel_id=1, source_target_pairs={{1,17},{12,28},{17,1},{28,12},{3,19},{14,30},{19,3},{30,14}} | collective-permute-start | bytes 1818632 | tf_op jit(solution)/shard_map/ppermute | solution.py:381
  27.7 29.1 %collective-permute-start.8 = (bf16[64,4736]{1,0:T(8,128)(2,1)S(1)}, bf16[64,4736]{1,0:T(8,128)(2,1)S(1)}, u32[]{:S(2)}, u32[]{:S(2)}) collective-permute-start(bf16[64,4736]{1,0:T(8,128)(2,1)S(1)} %collective-permute-done.3.refs_4_), channel_id=1, source_target_pairs={{1,0},{12,13},{3,2},{14,15},{17,16},{28,29},{19,18},{30,31}} | collective-permute-start | bytes 1818632 | tf_op jit(solution)/shard_map/ppermute | solution.py:384
  29.0 0.8 copy-start.10
  29.9 3.9 %copy-start.6 = (bf16[64,4736]{1,0:T(8,128)(2,1)}, bf16[64,4736]{1,0:T(8,128)(2,1)S(1)}, u32[]{:S(2)}) copy-start(bf16[64,4736]{1,0:T(8,128)(2,1)S(1)} %collective-permute-done.4.refs_4_) | copy-start | bytes 1818628
  29.9 32.6 %collective-permute-start.12 = (bf16[64,9472]{1,0:T(8,128)(2,1)}, bf16[64,9472]{1,0:T(8,128)(2,1)}, u32[]{:S(2)}, u32[]{:S(2)}) collective-permute-start(bf16[64,9472]{1,0:T(8,128)(2,1)} %collective-permute-done.10.y), channel_id=1, source_target_pairs={{1,0},{4,5},{5,4},{8,9},{9,8},{12,13},{3,2},{6,7},{7,6},{10,11},{1... | collective-permute-start | bytes 3637256 | tf_op jit(solution)/shard_map/ppermute | solution.py:384
  31.2 33.6 %collective-permute-start.11 = (bf16[64,9472]{1,0:T(8,128)(2,1)}, bf16[64,9472]{1,0:T(8,128)(2,1)}, u32[]{:S(2)}, u32[]{:S(2)}) collective-permute-start(bf16[64,9472]{1,0:T(8,128)(2,1)} %collective-permute-done.x), channel_id=1, source_target_pairs={{1,0},{4,5},{5,4},{8,9},{9,8},{12,13},{3,2},{6,7},{7,6},{10,11},{1... | collective-permute-start | bytes 3637256 | tf_op jit(solution)/shard_map/ppermute | solution.py:384
  32.5 40.9 %collective-permute-start.5 = (bf16[64,9472]{1,0:T(8,128)(2,1)S(1)}, bf16[64,9472]{1,0:T(8,128)(2,1)}, u32[]{:S(2)}, u32[]{:S(2)}) collective-permute-start(bf16[64,9472]{1,0:T(8,128)(2,1)S(1)} %collective-permute-done.1.refs_0_), channel_id=1, source_target_pairs={{1,0},{5,4},{8,9},{12,13},{3,2},{7,6},{10,11},{14,15},{17,16},{21,... | collective-permute-start | bytes 3637256 | tf_op jit(solution)/shard_map/ppermute | solution.py:384
  33.8 25.2 %collective-permute-start.14 = (bf16[64,4736]{1,0:T(8,128)(2,1)S(1)}, bf16[64,4736]{1,0:T(8,128)(2,1)S(1)}, u32[]{:S(2)}, u32[]{:S(2)}) collective-permute-start(bf16[64,4736]{1,0:T(8,128)(2,1)S(1)} %collective-permute-done.4.refs_4_), channel_id=1, source_target_pairs={{1,17},{12,28},{17,1},{28,12},{3,19},{14,30},{19,3},{30,14}} | collective-permute-start | bytes 1818632 | tf_op jit(solution)/shard_map/ppermute | solution.py:381
  56.9 0.8 copy-start.12
  57.7 22.6 %collective-permute-start.6 = (bf16[64,9472]{1,0:T(8,128)(2,1)}, bf16[64,9472]{1,0:T(8,128)(2,1)}, u32[]{:S(2)}, u32[]{:S(2)}) collective-permute-start(bf16[64,9472]{1,0:T(8,128)(2,1)} %collective-permute-done.2.refs_1_), channel_id=1, source_target_pairs={{1,0},{5,4},{8,9},{12,13},{3,2},{7,6},{10,11},{14,15},{17,16},{21,... | collective-permute-start | bytes 3637256 | tf_op jit(solution)/shard_map/ppermute | solution.py:384
  59.0 0.8 copy-start.8
  59.9 20.4 %collective-permute-start.9 = (bf16[64,4736]{1,0:T(8,128)(2,1)}, bf16[64,4736]{1,0:T(8,128)(2,1)}, u32[]{:S(2)}, u32[]{:S(2)}) collective-permute-start(bf16[64,4736]{1,0:T(8,128)(2,1)} %collective-permute-done.7.refs_5_), channel_id=1, source_target_pairs={{1,0},{12,13},{3,2},{14,15},{17,16},{28,29},{19,18},{30,31}} | collective-permute-start | bytes 1818632 | tf_op jit(solution)/shard_map/ppermute | solution.py:384
  62.5 24.5 %collective-permute-start.15 = (bf16[64,4736]{1,0:T(8,128)(2,1)}, bf16[64,4736]{1,0:T(8,128)(2,1)S(1)}, u32[]{:S(2)}, u32[]{:S(2)}) collective-permute-start(bf16[64,4736]{1,0:T(8,128)(2,1)} %copy-done.6), channel_id=1, source_target_pairs={{1,0},{12,13},{3,2},{14,15},{17,16},{28,29},{19,18},{30,31}} | collective-permute-start | bytes 1818632 | tf_op jit(solution)/shard_map/ppermute | solution.py:384
  64.8 22.1 %collective-permute-start.16 = (bf16[64,4736]{1,0:T(8,128)(2,1)}, bf16[64,4736]{1,0:T(8,128)(2,1)S(1)}, u32[]{:S(2)}, u32[]{:S(2)}) collective-permute-start(bf16[64,4736]{1,0:T(8,128)(2,1)} %copy-done.8), channel_id=1, source_target_pairs={{1,0},{12,13},{3,2},{14,15},{17,16},{28,29},{19,18},{30,31}} | collective-permute-start | bytes 1818632 | tf_op jit(solution)/shard_map/ppermute | solution.py:384
  66.1 2.5 %copy-start.1 = (bf16[384,6912]{1,0:T(8,128)(2,1)S(1)}, bf16[384,6912]{1,0:T(8,128)(2,1)}, u32[]{:S(2)}) copy-start(bf16[384,6912]{1,0:T(8,128)(2,1)} %copy-done) | copy-start | bytes 15925252
  68.6 11.7 %copy-start.11 = (bf16[64,4736]{1,0:T(8,128)(2,1)S(1)}, bf16[64,4736]{1,0:T(8,128)(2,1)}, u32[]{:S(2)}) copy-start(bf16[64,4736]{1,0:T(8,128)(2,1)} %copy-done.10) | copy-start | bytes 1818628
  68.7 11.7 %copy-start.13 = (bf16[64,4736]{1,0:T(8,128)(2,1)S(1)}, bf16[64,4736]{1,0:T(8,128)(2,1)}, u32[]{:S(2)}) copy-start(bf16[64,4736]{1,0:T(8,128)(2,1)} %copy-done.12) | copy-start | bytes 1818628
  80.3 6.6 %slice-start = ((s8[5308416]{0:T(1024)(128)(4,1)}), s8[4194304]{0:T(1024)(128)(4,1)S(1)}, s32[]{:S(2)}) async-start(s8[5308416]{0:T(1024)(128)(4,1)} %bitcast.79), calls=%async_computation | async-start | bytes 8388608
  80.3 6.6 %slice-start.1 = ((s8[5308416]{0:T(1024)(128)(4,1)}), s8[1114112]{0:T(1024)(128)(4,1)S(1)}, s32[]{:S(2)}) async-start(s8[5308416]{0:T(1024)(128)(4,1)} %bitcast.79), calls=%async_computation.1 | async-start | bytes 2228224
  80.3 6.6 %copy-start.7 = (bf16[64,4736]{1,0:T(8,128)(2,1)S(1)}, bf16[64,4736]{1,0:T(8,128)(2,1)}, u32[]{:S(2)}) copy-start(bf16[64,4736]{1,0:T(8,128)(2,1)} %copy-done.6) | copy-start | bytes 1818628
  80.4 6.6 %copy-start.9 = (bf16[64,4736]{1,0:T(8,128)(2,1)S(1)}, bf16[64,4736]{1,0:T(8,128)(2,1)}, u32[]{:S(2)}) copy-start(bf16[64,4736]{1,0:T(8,128)(2,1)} %copy-done.8) | copy-start | bytes 1818628
  80.4 6.6 %copy-start.15 = (f32[128,384]{1,0:T(8,128)S(1)}, f32[128,384]{1,0:T(8,128)}, u32[]{:S(2)}) copy-start(f32[128,384]{1,0:T(8,128)} %copy-done.14) | copy-start | bytes 589828
  85.4 7.8 %collective-permute-start.13 = (bf16[512,384]{1,0:T(8,128)(2,1)S(1)}, bf16[512,384]{1,0:T(8,128)(2,1)S(1)}, u32[]{:S(2)}, u32[]{:S(2)}) collective-permute-start(bf16[512,384]{1,0:T(8,128)(2,1)S(1)} %get-tuple-element.41), channel_id=1, source_target_pairs={{0,2},{2,0},{1,3},{3,1},{4,6},{6,4},{5,7},{7,5},{8,10},{10,8},{9,1... | collective-permute-start | bytes 1179656 | tf_op jit(solution)/shard_map/ppermute | solution.py:416
  87.0 13.7 %copy-start.16 = (s32[3]{0:T(128)S(1)}, s32[3]{0:T(128)}, u32[]{:S(2)}) copy-start(s32[3]{0:T(128)} %counts.1) | copy-start | bytes 40
  87.0 21.5 %copy-start.17 = (bf16[64,64,256]{2,1,0:T(8,128)(2,1)S(1)}, bf16[64,64,256]{2,1,0:T(8,128)(2,1)}, u32[]{:S(2)}) copy-start(bf16[64,64,256]{2,1,0:T(8,128)(2,1)} %param.13) | copy-start | bytes 6291460
  87.0 21.5 %copy-start.18 = (f32[64,256]{1,0:T(8,128)S(1)}, f32[64,256]{1,0:T(8,128)}, u32[]{:S(2)}) copy-start(f32[64,256]{1,0:T(8,128)} %param.14) | copy-start | bytes 196612
  93.2 7.5 %collective-permute-start.17 = (bf16[256,384]{1,0:T(8,128)(2,1)S(1)}, bf16[256,384]{1,0:T(8,128)(2,1)S(1)}, u32[]{:S(2)}, u32[]{:S(2)}) collective-permute-start(bf16[256,384]{1,0:T(8,128)(2,1)S(1)} %get-tuple-element.46), channel_id=1, source_target_pairs={{0,2},{2,0},{1,3},{3,1},{4,6},{6,4},{5,7},{7,5},{8,10},{10,8},{9,1... | collective-permute-start | bytes 589832 | tf_op jit(solution)/shard_map/ppermute | solution.py:425
  101.7 17.1 %collective-permute-start.18 = (bf16[3,64,256]{2,1,0:T(8,128)(2,1)S(1)}, bf16[3,64,256]{2,1,0:T(8,128)(2,1)S(1)}, u32[]{:S(2)}, u32[]{:S(2)}) collective-permute-start(bf16[3,64,256]{2,1,0:T(8,128)(2,1)S(1)} %get-tuple-element.48), channel_id=1, source_target_pairs={{0,1},{1,0},{4,5},{5,4},{8,9},{9,8},{12,13},{13,12},{2,3},{3,2},{6... | collective-permute-start | bytes 294920 | tf_op jit(solution)/shard_map/ppermute | solution.py:437
  109.1 12.8 %collective-permute-start.19 = (bf16[3,64,256]{2,1,0:T(8,128)(2,1)S(1)}, bf16[3,64,256]{2,1,0:T(8,128)(2,1)S(1)}, u32[]{:S(2)}, u32[]{:S(2)}) collective-permute-start(bf16[3,64,256]{2,1,0:T(8,128)(2,1)S(1)} %get-tuple-element.49), channel_id=1, source_target_pairs={{0,4},{1,5},{4,8},{5,9},{8,12},{9,13},{12,0},{13,1},{2,6},{3,7},{6... | collective-permute-start | bytes 294920 | tf_op jit(solution)/shard_map/ppermute | solution.py:437
  109.1 14.5 %collective-permute-start.20 = (bf16[3,64,256]{2,1,0:T(8,128)(2,1)S(1)}, bf16[3,64,256]{2,1,0:T(8,128)(2,1)S(1)}, u32[]{:S(2)}, u32[]{:S(2)}) collective-permute-start(bf16[3,64,256]{2,1,0:T(8,128)(2,1)S(1)} %get-tuple-element.50), channel_id=1, source_target_pairs={{0,5},{1,4},{4,9},{5,8},{8,13},{9,12},{12,1},{13,0},{2,7},{3,6},{6... | collective-permute-start | bytes 294920 | tf_op jit(solution)/shard_map/ppermute | solution.py:437
  109.2 20.8 %collective-permute-start.21 = (bf16[3,64,256]{2,1,0:T(8,128)(2,1)S(1)}, bf16[3,64,256]{2,1,0:T(8,128)(2,1)S(1)}, u32[]{:S(2)}, u32[]{:S(2)}) collective-permute-start(bf16[3,64,256]{2,1,0:T(8,128)(2,1)S(1)} %get-tuple-element.51), channel_id=1, source_target_pairs={{0,8},{1,9},{4,12},{5,13},{8,0},{9,1},{12,4},{13,5},{2,10},{3,11},... | collective-permute-start | bytes 294920 | tf_op jit(solution)/shard_map/ppermute | solution.py:437
  118.8 13.2 %collective-permute-start.22 = (bf16[3,64,256]{2,1,0:T(8,128)(2,1)S(1)}, bf16[3,64,256]{2,1,0:T(8,128)(2,1)S(1)}, u32[]{:S(2)}, u32[]{:S(2)}) collective-permute-start(bf16[3,64,256]{2,1,0:T(8,128)(2,1)S(1)} %get-tuple-element.52), channel_id=1, source_target_pairs={{0,9},{1,8},{4,13},{5,12},{8,1},{9,0},{12,5},{13,4},{2,11},{3,10},... | collective-permute-start | bytes 294920 | tf_op jit(solution)/shard_map/ppermute | solution.py:437
  118.8 13.2 %collective-permute-start.23 = (bf16[3,64,256]{2,1,0:T(8,128)(2,1)S(1)}, bf16[3,64,256]{2,1,0:T(8,128)(2,1)S(1)}, u32[]{:S(2)}, u32[]{:S(2)}) collective-permute-start(bf16[3,64,256]{2,1,0:T(8,128)(2,1)S(1)} %get-tuple-element.53), channel_id=1, source_target_pairs={{0,12},{1,13},{4,0},{5,1},{8,4},{9,5},{12,8},{13,9},{2,14},{3,15},... | collective-permute-start | bytes 294920 | tf_op jit(solution)/shard_map/ppermute | solution.py:437
  121.9 10.2 %collective-permute-start.24 = (bf16[3,64,256]{2,1,0:T(8,128)(2,1)S(1)}, bf16[3,64,256]{2,1,0:T(8,128)(2,1)S(1)}, u32[]{:S(2)}, u32[]{:S(2)}) collective-permute-start(bf16[3,64,256]{2,1,0:T(8,128)(2,1)S(1)} %get-tuple-element.54), channel_id=1, source_target_pairs={{0,13},{1,12},{4,1},{5,0},{8,5},{9,4},{12,9},{13,8},{2,15},{3,14},... | collective-permute-start | bytes 294920 | tf_op jit(solution)/shard_map/ppermute | solution.py:437
  132.2 12.4 %copy-start.19 = (s32[16,1]{0,1:T(1,128)S(1)}, s32[16,1]{0,1:T(1,128)}, u32[]{:S(2)}) copy-start(s32[16,1]{0,1:T(1,128)} %param.15) | copy-start | bytes 196
  135.5 1.3 collective-permute-start.25
  136.8 3.8 %collective-permute-start.26 = (f32[16,4,6]{0,1,2:T(4,128)S(1)}, f32[16,4,6]{0,1,2:T(4,128)S(1)}, u32[]{:S(2)}, u32[]{:S(2)}) collective-permute-start(f32[16,4,6]{0,1,2:T(4,128)S(1)} %dynamic-slice_bitcast_fusion), channel_id=1, source_target_pairs={{0,2},{2,0},{1,3},{3,1},{4,6},{6,4},{5,7},{7,5},{8,10},{10,8},{9,1... | collective-permute-start | bytes 4616 | tf_op jit(solution)/shard_map/ppermute | solution.py:67
  140.7 5.5 %collective-permute-start.27 = (f32[16,2,6]{0,1,2:T(2,128)S(1)}, f32[16,2,6]{0,1,2:T(2,128)S(1)}, u32[]{:S(2)}, u32[]{:S(2)}) collective-permute-start(f32[16,2,6]{0,1,2:T(2,128)S(1)} %fusion.11), channel_id=1, source_target_pairs={{0,8},{4,12},{8,0},{12,4},{1,9},{5,13},{9,1},{13,5},{2,10},{6,14},... | collective-permute-start | bytes 2312 | tf_op jit(solution)/shard_map/ppermute | solution.py:80
  146.2 5.5 %collective-permute-start.28 = (f32[16,1,6]{0,1,2:T(1,128)S(1)}, f32[16,1,6]{0,1,2:T(1,128)S(1)}, u32[]{:S(2)}, u32[]{:S(2)}) collective-permute-start(f32[16,1,6]{0,1,2:T(1,128)S(1)} %fusion.17), channel_id=1, source_target_pairs={{0,4},{4,0},{8,12},{12,8},{1,5},{5,1},{9,13},{13,9},{2,6},{6,2},{1... | collective-permute-start | bytes 1160 | tf_op jit(solution)/shard_map/ppermute | solution.py:80

commit v4 on v3

--- a/solution.py
+++ b/solution.py
@@ -15,11 +15,6 @@
 def hop_pairs(k, n_wide):
     pairs = [(2 * w, 2 * w + 2) for w in range(k - 1, n_wide - 1)]
     return pairs + [(2 * w + 3, 2 * w + 1) for w in range(0, n_wide - k)]
-
-
-def holds(place, k, n_wide):
-    w, r = divmod(place, 2)
-    return w >= k if r == 0 else w <= n_wide - 1 - k
 
 
 def gather_rounds(own, n_wide):
@@ -175,14 +170,14 @@
 FLOAT, HALF = jnp.float32, jnp.bfloat16
 
 
-def kernel(body, out_shape, scratch=(), flops=0, grant=6):
+def kernel(body, out_shape, scratch=(), flops=0, grant=12):
     return lambda **specs: pl.pallas_call(
         body,
         **specs,
         out_shape=out_shape,
         scratch_shapes=list(scratch),
         compiler_params=pltpu.CompilerParams(vmem_limit_bytes=grant * 1024 * 1024),
-        cost_estimate=pl.CostEstimate(flops=flops, bytes_accessed=flops // 400 + 1024, transcendentals=0),
+        cost_estimate=pl.CostEstimate(flops=flops // 1000, bytes_accessed=1024, transcendentals=0),
     )
 
 
@@ -203,13 +198,10 @@
     )
 
 
-def sum_of(blocks, start, width, tokens, t_start, total, fresh=True):
+def sum_of(pieces, start, width, tokens, t_start, total, fresh=True):
     for k in range(0, width, 1024):
         tile = min(1024, width - k)
-        rows = []
-        for block in blocks:
-            parts = [p[:, o + start + k : o + start + k + tile] for p, o in block]
-            rows.append(parts[0] if len(parts) == 1 else parts[0] + parts[1])
+        rows = [p[:, start + k : start + k + tile] for p in pieces]
         part = lax.dot_general(
             tokens[:, t_start + k : t_start + k + tile],
             jnp.concatenate(rows, axis=0) if len(rows) > 1 else rows[0],
@@ -227,54 +219,48 @@
 
 
 def own_body(b_out, b_in, t_out, t_in, g_own, a_own, total):
-    sum_of([[(b_out, 0)]], 0, b_out.shape[1], t_out, 0, total)
+    sum_of([b_out], 0, b_out.shape[1], t_out, 0, total)
     g_own[...] = total[...].T
-    sum_of([[(b_in, 0)]], 0, b_in.shape[1], t_in, 0, total)
+    sum_of([b_in], 0, b_in.shape[1], t_in, 0, total)
     a_own[...] = total[...].T
 
 
-def first_body(at, x, y, x_far, y_far, t_out, t_in, g_first, a_first, total):
-    group, rep = at[0], at[3]
-    blocks = [[(p, 0)] for p in (x, y, x_far, y_far)]
-    half, d = x.shape[0], t_out.shape[1]
-    places = (2 * rep + group, 2 * rep + 1 - group, 2 * (1 - rep) + group, 2 * (1 - rep) + 1 - group)
-    for start, tokens, out in ((0, t_out, g_first), (d, t_in, a_first)):
-        sum_of(blocks, start, tokens.shape[1], tokens, 0, total)
-        turned = total[...].T
-        for r, place in enumerate(places):
-            put(out, place, half, turned[r * half : (r + 1) * half])
-
-
-def late_blocks(second, third, shift):
-    x2, y2, x2_far, y2_far = second
-    x3, y3, x3_far, y3_far = third
-    return [
-        [(x2, shift), (x2_far, shift)],
-        [(y2, shift), (y2_far, shift)],
-        [(x3, 0), (x3_far, 0)],
-        [(y3, 0), (y3_far, 0)],
-    ]
-
-
-def place_all(at, own, first, total, store):
-    group, wide = at[0], at[1]
-    rows = own.shape[0]
-    half = rows // 2
-    store(0, own[...], None)
-    store(1, first[rows:, :], wide <= 2)
-    store(3, first[:rows, :], wide >= 1)
-    turned = total[...].T
-
-    def ordered(k):
-        mine, other = (turned[(2 * k + i) * half : (2 * k + i + 1) * half] for i in range(2))
-        return jnp.concatenate(
-            [jnp.where(group == 0, mine, other), jnp.where(group == 0, other, mine)], axis=0
-        )
-
-    store(2, ordered(0), None)
-    last = ordered(1)
-    store(1, last, wide == 3)
-    store(3, last, wide == 0)
+def in_order(group, turned):
+    half = turned.shape[0] // 2
+    mine, other = turned[:half], turned[half:]
+    return jnp.concatenate([jnp.where(group == 0, mine, other), jnp.where(group == 0, other, mine)], axis=0)
+
+
+def shard_body(flag, at, x, y, t_out, t_in, o_out, o_in, mine, theirs, held, total, sems):
+    d, ff = t_out.shape[1], t_in.shape[1]
+    rows = mine.shape[0] // 2
+    cuts = [(0, d)] + [(d + k, min(ff // 2 // 128 * 128 + 128, ff - k)) for k in range(0, ff, ff // 2 // 128 * 128 + 128)]
+    cuts = [(start, width) for start, width in cuts if width > 0]
+
+    @pl.when(at[flag] == 1)
+    def _():
+        copies = []
+        for i, (start, width) in enumerate(cuts):
+            columns = pl.ds(start, width)
+            copies.append(
+                [
+                    pltpu.make_async_copy(p.at[:, columns], held.at[j, :, columns], sems.at[i, j])
+                    for j, p in enumerate((x, y))
+                ]
+            )
+        for pair in copies:
+            for copy in pair:
+                copy.start()
+        for i, (start, width) in enumerate(cuts):
+            for copy in copies[i]:
+                copy.wait()
+            for j, tokens in enumerate((t_out, o_out) if start < d else (t_in, o_in)):
+                first = start if start < d else start - d
+                sum_of([held.at[0], held.at[1]], start, width, tokens, first, total.at[j], first == 0)
+            if i == 0 or i == len(cuts) - 1:
+                put_rows = slice(0, rows) if i == 0 else slice(rows, 2 * rows)
+                for j, out in enumerate((mine, theirs)):
+                    out[put_rows, :] = in_order(at[0], total[j].T)
 
 
 def when(condition, do):
@@ -284,52 +270,47 @@
         pl.when(condition)(do)
 
 
-def out_body(n_second, at, *refs):
-    second, third = refs[:4], refs[4:8]
-    t_out, t_in, own, first, grad, grad_sent, part, total = refs[8:]
-    blocks = late_blocks(second, third, 0)
-    d = t_out.shape[1]
-    sum_of(blocks, 0, d, t_out, 0, total)
-
-    def store(slot, value, condition):
-        rows = value.shape[0]
-
-        def do():
-            grad[slot * rows : (slot + 1) * rows, :] = value
-            grad_sent[slot * rows : (slot + 1) * rows, :] = value.astype(HALF)
-
-        when(condition, do)
-
-    place_all(at, own, first, total, store)
-    sum_of(blocks, d, third[0].shape[1] - d, t_in, 0, part)
-
-
-def in_body(shift, at, *refs):
-    second, third = refs[:4], refs[4:8]
-    t_in, part, own, first, mine, sent, total = refs[8:]
-    total[...] = part[...]
-    width = third[0].shape[1]
-    sum_of(late_blocks(second, third, shift), 0, width, t_in, t_in.shape[1] - width, total, fresh=False)
-    wide, layer = at[1], at[2]
-
-    def store(slot, value, condition):
-        rows = value.shape[0]
+def slots_body(at, g_own, a_own, near, near_far, middle, middle_far, inner, inner_far, outer, outer_far, *outs):
+    grad, grad_sent, act, act_sent = outs
+    wide, layer, holds = at[1], at[2], at[4] == 1
+    rows = g_own.shape[0]
+
+    def store(slot, value, condition, is_out):
+        if is_out:
+
+            def do():
+                grad[slot * rows : (slot + 1) * rows, :] = value()
+                grad_sent[slot * rows : (slot + 1) * rows, :] = value().astype(HALF)
+
+            when(condition, do)
+            return
         shard = lax.rem(wide + slot, 4)
-        per_layer = mine.shape[0] // rows
+        per_layer = act.shape[0] // rows
         place = lax.rem(shard, per_layer)
         here = lax.div(shard, per_layer) == layer
-
-        def keep():
-            put(mine, place, rows, value)
-
-        def send():
-            put(sent, place, rows, value.astype(HALF))
-
-        both = (here, jnp.logical_not(here)) if condition is None else (condition & here, condition & jnp.logical_not(here))
-        pl.when(both[0])(keep)
-        pl.when(both[1])(send)
-
-    place_all(at, own, first, total, store)
+        away = jnp.logical_not(here)
+        pl.when(here if condition is None else condition & here)(lambda: put(act, place, rows, value()))
+        pl.when(away if condition is None else condition & away)(
+            lambda: put(act_sent, place, rows, value().astype(HALF))
+        )
+
+    for is_out in (True, False):
+        part = slice(0, rows) if is_out else slice(rows, 2 * rows)
+        other = jnp.logical_not(holds)
+        own = g_own if is_out else a_own
+        store(0, lambda own=own: own[...], None, is_out)
+        for slot, here, away, condition, at_holder in (
+            (1, near, near_far, wide <= 1, holds),
+            (3, near, near_far, wide >= 2, holds),
+            (2, middle, middle_far, None, holds),
+            (3, inner, inner_far, wide == 1, other),
+            (1, inner, inner_far, wide == 2, other),
+            (3, outer, outer_far, wide == 0, holds),
+            (1, outer, outer_far, wide == 3, holds),
+        ):
+            for source, at_this in ((here, at_holder), (away, jnp.logical_not(at_holder))):
+                both = at_this if condition is None else condition & at_this
+                store(slot, lambda source=source, part=part: source[part, :], both, is_out)
 
 
 def train_body(at, counts, grad, grad_came, act, act_came, *refs):
@@ -362,67 +343,73 @@
     half = rows // 2
     share = n_wide * rows // n_layer
     group, wide, layer, rep = (lax.axis_index(a) for a in ("groups", "wide", "layer", "rep"))
-    at = jnp.stack([group, wide, layer, rep]).astype(jnp.int32)
+    holds = (rep == 1) == (wide <= 1)
+    outside = (wide == 0) | (wide == 3)
+    at = jnp.stack([group, wide, layer, rep, holds, ~holds & ~outside, holds & outside]).astype(jnp.int32)
     swap = [(0, 1), (1, 0)]
+    n_query = query_grads.shape[0]
+    weighted = (query_grads.astype(FLOAT) / eigenvalues[None, :, :]).astype(HALF).reshape(n_query, half * share)
     dma = pltpu.SemaphoreType.DMA((2,))
 
     held = jnp.concatenate(
         [lax.dynamic_slice_in_dim(x, group * half, half, axis=0) for x in (basis_out, basis_in)], axis=1
     )
-    t_out, t_in = kernel(
-        load_body, [pltpu.VMEM((n_tok, d), HALF), pltpu.VMEM((n_tok, ff), HALF)], [dma], grant=4
-    )(in_specs=[ANY, ANY], out_specs=[VMEM, VMEM])(grads.reshape(n_tok, d), acts.reshape(n_tok, ff))
+
+    def load(x, y):
+        return kernel(
+            load_body, [pltpu.VMEM((n_tok, d), HALF), pltpu.VMEM((n_tok, ff), HALF)], [dma], grant=4
+        )(in_specs=[ANY, ANY], out_specs=[VMEM, VMEM])(x.reshape(n_tok, d), y.reshape(n_tok, ff))
+
+    t_out, t_in = load(grads, acts)
     g_own, a_own = kernel(
         own_body, [shaped(rows, n_tok)] * 2, [pltpu.VMEM((n_tok, rows), FLOAT)], 2 * rows * n_tok * (d + ff)
     )(in_specs=[VMEM] * 4, out_specs=[VMEM] * 2)(basis_out, basis_in, t_out, t_in)
 
-    def to_group(x, k):
-        pairs = swap_pairs(2 * n_wide, functools.partial(holds, k=k, n_wide=n_wide))
-        return lax.ppermute(x, ("groups", "wide", "rep"), pairs)
-
-    def to_core(x, k):
-        return lax.ppermute(x, ("wide", "rep"), [(p, p ^ 1) for p in range(2 * n_wide) if holds(p, k, n_wide)])
+    near = [(0, 1), (1, 1), (2, 0), (3, 0)]
+    inner = [(1, 0), (2, 1)]
+    outer = [(0, 1), (3, 0)]
+
+    def to_group(x, places):
+        numbers = {2 * w + r for w, r in places}
+        return lax.ppermute(x, ("groups", "wide", "rep"), swap_pairs(2 * n_wide, numbers.__contains__))
 
     def hop(x, k):
         return lax.ppermute(x, ("wide", "rep"), hop_pairs(k, n_wide))
 
+    o_out, o_in = load(lax.ppermute(grads, "rep", swap), lax.ppermute(acts, "rep", swap))
+
+    def rotate(flag, x, y):
+        both = 2 * rows
+        mine, theirs = kernel(
+            functools.partial(shard_body, flag),
+            [shaped(both, n_tok)] * 2,
+            [pltpu.VMEM((2, half, d + ff), HALF), pltpu.VMEM((2, n_tok, rows), FLOAT), pltpu.SemaphoreType.DMA((4, 2))],
+            4 * rows * n_tok * (d + ff),
+        )(in_specs=[SMEM, ANY, ANY] + [VMEM] * 4, out_specs=[VMEM] * 2)(at, x, y, t_out, t_in, o_out, o_in)
+        return mine, lax.ppermute(theirs, "rep", swap)
+
     x1 = hop(held, 1)
-    y1 = to_group(x1, 1)
-    x2 = hop(after(x1, g_own, a_own), 2)
-    y2 = to_group(x2, 2)
-    cut = (ff - d) // 256 * 128
-    x3 = [hop(x2[:, : d + cut], 3), hop(x2[:, d + cut :], 3)]
-    y3 = [to_group(x, 3) for x in x3]
-
-    def on_both(x, y, k, *earlier):
-        return x, y, to_core(after(x, *earlier), k), to_core(after(y, *earlier), k)
-
-    first = on_both(x1, y1, 1, *x3)
-    g_first, a_first = kernel(
-        first_body, [shaped(2 * rows, n_tok)] * 2, [pltpu.VMEM((n_tok, 2 * rows), FLOAT)], 4 * rows * n_tok * (d + ff)
-    )(in_specs=[SMEM] + [VMEM] * 6, out_specs=[VMEM] * 2)(at, *first, t_out, t_in)
-    second = on_both(x2, y2, 2, *x3)
-    thirds = [on_both(x3[0], y3[0], 3), on_both(x3[1], y3[1], 3)]
-
-    wide_sum = pltpu.VMEM((n_tok, 2 * rows), FLOAT)
-    grad, grad_sent, part = kernel(
-        functools.partial(out_body, 4),
-        [shaped(n_wide * rows, n_tok), shaped(n_wide * rows, n_tok, kind=HALF), shaped(n_tok, 2 * rows)],
-        [wide_sum],
-        4 * rows * n_tok * (d + cut),
-    )(in_specs=[SMEM] + [VMEM] * 12, out_specs=[VMEM] * 3)(
-        at, *second, *thirds[0], t_out, t_in, g_own, g_first
+    y1 = to_group(x1, near)
+    x1_sent, weighted, _, _ = lax.optimization_barrier((x1, weighted, g_own, a_own))
+    x2 = hop(x1_sent, 2)
+    x3 = hop(after(x2, y1), 3)
+    y2 = to_group(x2, near)
+    near_done = rotate(4, x1, y1)
+    y3 = to_group(after(x3, y2, near_done[0]), outer)
+    y1_inner = to_group(after(x1, y1), inner)
+    middle_done = rotate(4, x2, y2)
+    inner_done = rotate(5, x1, y1_inner)
+    outer_done = rotate(6, x3, after(y3, middle_done[0], inner_done[0]))
+
+    all_rows = n_wide * rows
+    grad, grad_sent, act, act_sent = kernel(
+        slots_body,
+        [shaped(r, n_tok, kind=kind) for r in (all_rows, share) for kind in (FLOAT, HALF)],
+    )(in_specs=[SMEM] + [VMEM] * 10, out_specs=[VMEM] * 4)(
+        at, g_own, a_own, *near_done, *middle_done, *inner_done, *outer_done
     )
     grad_came = lax.ppermute(grad_sent, "layer", swap)
-    act, act_sent = kernel(
-        functools.partial(in_body, d + cut),
-        [shaped(share, n_tok), shaped(share, n_tok, kind=HALF)],
-        [wide_sum],
-        4 * rows * n_tok * (ff - cut),
-    )(in_specs=[SMEM] + [VMEM] * 12, out_specs=[VMEM] * 2)(
-        at, *second, *thirds[1], t_in, part, a_own, a_first
-    )
-    act_came = lax.ppermute(after(act_sent, grad_came), "layer", swap)
+    act_came = lax.ppermute(act_sent, "layer", swap)
 
     pieces = kernel(
         train_body,
@@ -441,8 +428,6 @@
     chip_seqs = 2 * seq_dev
     train = jnp.stack([jnp.stack([a, b]) for a, b in zip(same, cross, strict=True)])
     train = train.reshape(n_wide * chip_seqs, half * share)
-    n_query = query_grads.shape[0]
-    weighted = (query_grads.astype(FLOAT) / eigenvalues[None, :, :]).astype(HALF).reshape(n_query, half * share)
     scored = lax.dot_general(weighted, train, (((1,), (1,)), ((), ())), preferred_element_type=FLOAT)
     scored = scored.reshape(n_query, n_wide, 2, seq_dev)
     scored = jnp.where(rep == 0, scored, scored[:, :, ::-1]).reshape(n_query, n_wide * chip_seqs)

time: 153 us -> 147 us (0.961)
  waiting for transfers between devices: 62.4 us -> 37.1 us
  starting transfers between devices: 56.8 us -> 80.3 us
  Pallas kernels: 17.1 us -> 11.7 us
  local copies, waits for them, and re-layouts: 10.6 us -> 12.7 us
    ppermute x13 -> x11, starting transfers between devices: 17.4 us -> 52.3 us  [the longest x4 45 us: rotate(): return (mine, lax.ppermute(theirs, 'rep', swap))]
    ppermute x13 -> x11, waiting for transfers between devices: 37.7 us -> 14.9 us  [the longest x1 13.6 us: local_fast(): act_came = lax.ppermute(act_sent, 'layer', swap)]
    ppermute x7, starting transfers between devices: 20.2 us -> 12.5 us  [send(): return lax.ppermute(x, ('wide', 'rep'), pairs)]
    pallas_call x4 -> x7, Pallas kernels: 14 us -> 8.59 us  [the longest x2 4.98 us: load(): kernel(load_body, [pltpu.VMEM((n_tok, d), HALF), pltpu.VMEM((n_tok, ff),...]
    another operation x0 -> x9, local copies, waits for them, and re-layouts: none -> 4.64 us  [the longest x8 4.56 us: local_fast(): jnp.stack([a, b])]
    ppermute x2, starting transfers between devices: 7.78 us -> 3.93 us  [finish(): lax.ppermute(give, 'wide', [(w, w ^ bit) for w in range(n_wide)])]
    ppermute x1, waiting for transfers between devices: 2.55 us -> 0.01 us  [local_fast(): grad_came = lax.ppermute(grad_sent, 'layer', swap)]
    unnamed x45 -> x34, local copies, waits for them, and re-layouts: 9.03 us -> 6.63 us
  transfers between devices with their start and end apart: 29 -> 26, of which waited for: 15 -> 10; matrix products, arithmetic and copies ran while one was open for 1% -> 6% of each run, Pallas kernels for 11% -> 7%
where the time goes in v4:
time: 147 us
  starting transfers between devices  80.3 us (55%)
  waiting for transfers between devices  37.1 us (25%)
  local copies, waits for them, and re-layouts  12.7 us (9%)
  Pallas kernels  11.7 us (8%)
  matrix products  2.85 us (2%)
  other arithmetic  1.48 us (1%)
    ppermute x4, starting transfers between devices, rotate(): return (mine, lax.ppermute(theirs, 'rep', swap))  45 us
    ppermute x1, waiting for transfers between devices, local_fast(): act_came = lax.ppermute(act_sent, 'layer', swap)  13.6 us
    ppermute x7, starting transfers between devices, send(): return lax.ppermute(x, ('wide', 'rep'), pairs)  12.5 us
    ppermute x7, waiting for transfers between devices, send(): return lax.ppermute(x, ('wide', 'rep'), pairs)  8.39 us
    ppermute x3, starting transfers between devices, hop(): return lax.ppermute(x, ('wide', 'rep'), hop_pairs(k, n_wide))  8.31 us
    unnamed x34, local copies, waits for them, and re-layouts  6.63 us
    ppermute x3, waiting for transfers between devices, hop(): return lax.ppermute(x, ('wide', 'rep'), hop_pairs(k, n_wide))  5.61 us
    pallas_call x2, Pallas kernels, load(): kernel(load_body, [pltpu.VMEM((n_tok, d), HALF), pltpu.VMEM((n_tok, ff),...  4.98 us
  transfers between devices with their start and end apart: 26, of which 10 were waited for; matrix products, arithmetic and copies ran while one was open for 6% of the time, Pallas kernels for 7%

profile of v4, /device:TPU:0, one launch (start us, length us, event | category | flops | bytes accessed | tf_op | source)
XLA Modules:
  0.0 146.6 jit_solution(902888963767559887)
XLA Ops:
  0.0 0.5 collective-permute-start.3
  0.5 1.2 constant_dynamic-slice_fusion.2
  1.8 0.1 pad_maximum_fusion
  1.9 0.0 slice-start.1
  1.9 4.9 %collective-permute-start = (bf16[64,9472]{1,0:T(8,128)(2,1)S(1)}, bf16[64,9472]{1,0:T(8,128)(2,1)S(1)}, u32[]{:S(2)}, u32[]{:S(2)}) collective-permute-start(bf16[64,9472]{1,0:T(8,128)(2,1)S(1)} %pad_maximum_fusion), channel_id=1, source_target_pairs={{0,4},{4,8},{8,12},{5,1},{9,5},{13,9},{2,6},{6,10},{10,14},{7,3},{... | collective-permute-start | bytes 3637256 | tf_op jit(solution)/shard_map/ppermute | solution.py:377
  6.8 0.6 divide_convert_fusion
  7.4 2.7 %copy.48 = bf16[8,8,64,256]{3,1,2,0:T(8,128)(2,1)} copy(bf16[8,8,64,256]{3,2,1,0:T(8,128)(2,1)S(1)} %bitcast.73) | data formatting | bytes 4194304
  10.1 1.7 %shard_map.82 = (bf16[384,2560]{1,0:T(8,128)(2,1)S(1)}, bf16[384,6912]{1,0:T(8,128)(2,1)S(1)}) custom-call(bf16[384,2560]{1,0:T(8,128)(2,1)} %bitcast.x_ref, bf16[384,6912]{1,0:T(8,128)(2,1)S(1)} %bitcast.72), custom_call_target="tpu_custom_call" | custom-call | bytes 1024 | tf_op jit(solution)/shard_map/pallas_call | solution.py:359
  11.9 0.3 copy-done.2
  12.2 0.1 copy-done.4
  12.3 2.1 %shard_map.83 = (f32[128,384]{1,0:T(8,128)S(1)}, f32[128,384]{1,0:T(8,128)S(1)}) custom-call(bf16[128,2560]{1,0:T(8,128)(2,1)S(1)} %copy-done.4, bf16[128,6912]{1,0:T(8,128)(2,1)S(1)} %copy-done.2, bf16[384,2560]{1,0:T(8,128)(2,1)S(1)} %get-tuple-element.37.t_out, bf16[384,6912]{1,0:T(8,128)(2,1)S(1)} %get-tuple-element.38.t_in), custom_call_target="tpu_custom_call" | custom-call | flops 931135 | bytes 1024 | tf_op jit(solution)/shard_map/pallas_call | solution.py:364
  14.5 0.7 copy-done.7
  15.1 5.6 %collective-permute-done.x = bf16[64,9472]{1,0:T(8,128)(2,1)S(1)} collective-permute-done((bf16[64,9472]{1,0:T(8,128)(2,1)S(1)}, bf16[64,9472]{1,0:T(8,128)(2,1)S(1)}, u32[]{:S(2)}, u32[]{:S(2)}) %collective-permute-start) | collective-permute-done | bytes 1212448 | tf_op jit(solution)/shard_map/ppermute | solution.py:377
  20.8 0.7 collective-permute-start.1
  21.5 1.7 %collective-permute-start.5 = (bf16[64,9472]{1,0:T(8,128)(2,1)S(1)}, bf16[64,9472]{1,0:T(8,128)(2,1)}, u32[]{:S(2)}, u32[]{:S(2)}) collective-permute-start(bf16[64,9472]{1,0:T(8,128)(2,1)S(1)} %collective-permute-done.x), channel_id=1, source_target_pairs={{4,8},{8,12},{5,1},{9,5},{6,10},{10,14},{7,3},{11,7},{20,24},{24,2... | collective-permute-start | bytes 3637256 | tf_op jit(solution)/shard_map/ppermute | solution.py:377
  23.2 2.4 %collective-permute-start.2 = (bf16[3,128,2560]{2,1,0:T(8,128)(2,1)}, bf16[3,128,2560]{2,1,0:T(8,128)(2,1)}, u32[]{:S(2)}, u32[]{:S(2)}) collective-permute-start(bf16[3,128,2560]{2,1,0:T(8,128)(2,1)} %param.9), channel_id=1, source_target_pairs={{0,1},{1,0},{2,3},{3,2},{4,5},{5,4},{6,7},{7,6},{8,9},{9,8},{10,11... | collective-permute-start | bytes 5898248 | tf_op jit(solution)/shard_map/ppermute | solution.py:379
  25.6 1.1 copy-done.5
  26.6 1.7 %collective-permute-start.10 = (bf16[64,9472]{1,0:T(8,128)(2,1)}, bf16[64,9472]{1,0:T(8,128)(2,1)}, u32[]{:S(2)}, u32[]{:S(2)}) collective-permute-start(bf16[64,9472]{1,0:T(8,128)(2,1)} %collective-permute-done.5.x), channel_id=1, source_target_pairs={{8,12},{5,1},{10,14},{7,3},{24,28},{21,17},{26,30},{23,19}} | collective-permute-start | bytes 3637256 | tf_op jit(solution)/shard_map/ppermute | solution.py:377
  28.3 1.7 %collective-permute-start.6 = (bf16[64,9472]{1,0:T(8,128)(2,1)}, bf16[64,9472]{1,0:T(8,128)(2,1)}, u32[]{:S(2)}, u32[]{:S(2)}) collective-permute-start(bf16[64,9472]{1,0:T(8,128)(2,1)} %collective-permute-done.5.x), channel_id=1, source_target_pairs={{1,17},{5,21},{8,24},{12,28},{17,1},{21,5},{24,8},{28,12},{3,19},{... | collective-permute-start | bytes 3637256 | tf_op jit(solution)/shard_map/ppermute | solution.py:374
  30.0 0.1 stack.86.at
  30.1 0.7 collective-permute-start.8
  30.9 3.3 %shard_map.84 = (bf16[384,2560]{1,0:T(8,128)(2,1)S(1)}, bf16[384,6912]{1,0:T(8,128)(2,1)S(1)}) custom-call(bf16[384,2560]{1,0:T(8,128)(2,1)} %bitcast.11.x_ref, bf16[384,6912]{1,0:T(8,128)(2,1)} %bitcast.12.y_ref), custom_call_target="tpu_custom_call" | custom-call | bytes 1024 | tf_op jit(solution)/shard_map/pallas_call | solution.py:359
  34.2 1.3 copy-done.1
  35.5 0.4 copy-done.6
  35.8 0.6 shard_map.85
  36.5 0.7 collective-permute-start.11
  37.2 0.6 shard_map.87
  37.9 25.6 %collective-permute-start.9 = (f32[256,384]{1,0:T(8,128)S(1)}, f32[256,384]{1,0:T(8,128)S(1)}, u32[]{:S(2)}, u32[]{:S(2)}) collective-permute-start(f32[256,384]{1,0:T(8,128)S(1)} %get-tuple-element.51), channel_id=1, source_target_pairs={{0,1},{1,0},{2,3},{3,2},{4,5},{5,4},{6,7},{7,6},{8,9},{9,8},{10,11... | collective-permute-start | bytes 1179656 | tf_op jit(solution)/shard_map/ppermute | solution.py:389
  63.5 0.1 collective-permute-start.4
  63.6 0.6 shard_map.86
  64.2 5.9 %collective-permute-start.7 = (f32[256,384]{1,0:T(8,128)S(1)}, f32[256,384]{1,0:T(8,128)S(1)}, u32[]{:S(2)}, u32[]{:S(2)}) collective-permute-start(f32[256,384]{1,0:T(8,128)S(1)} %get-tuple-element.48), channel_id=1, source_target_pairs={{0,1},{1,0},{2,3},{3,2},{4,5},{5,4},{6,7},{7,6},{8,9},{9,8},{10,11... | collective-permute-start | bytes 1179656 | tf_op jit(solution)/shard_map/ppermute | solution.py:389
  70.1 0.8 shard_map.88
  70.9 13.4 %collective-permute-start.12 = (f32[256,384]{1,0:T(8,128)S(1)}, f32[256,384]{1,0:T(8,128)S(1)}, u32[]{:S(2)}, u32[]{:S(2)}) collective-permute-start(f32[256,384]{1,0:T(8,128)S(1)} %get-tuple-element.56), channel_id=1, source_target_pairs={{0,1},{1,0},{2,3},{3,2},{4,5},{5,4},{6,7},{7,6},{8,9},{9,8},{10,11... | collective-permute-start | bytes 1179656 | tf_op jit(solution)/shard_map/ppermute | solution.py:389
  84.3 1.3 collective-permute-done.12.outer_far
  85.7 0.9 shard_map.89
  86.6 1.6 %collective-permute-start.13 = (bf16[512,384]{1,0:T(8,128)(2,1)S(1)}, bf16[512,384]{1,0:T(8,128)(2,1)S(1)}, u32[]{:S(2)}, u32[]{:S(2)}) collective-permute-start(bf16[512,384]{1,0:T(8,128)(2,1)S(1)} %get-tuple-element.58), channel_id=1, source_target_pairs={{0,2},{2,0},{1,3},{3,1},{4,6},{6,4},{5,7},{7,5},{8,10},{10,8},{9,1... | collective-permute-start | bytes 1179656 | tf_op jit(solution)/shard_map/ppermute | solution.py:411
  88.2 0.5 collective-permute-start.14
  88.7 13.6 %collective-permute-done.14.act_came = bf16[256,384]{1,0:T(8,128)(2,1)S(1)} collective-permute-done((bf16[256,384]{1,0:T(8,128)(2,1)S(1)}, bf16[256,384]{1,0:T(8,128)(2,1)S(1)}, u32[]{:S(2)}, u32[]{:S(2)}) %collective-permute-start.14) | collective-permute-done | bytes 196640 | tf_op jit(solution)/shard_map/ppermute | solution.py:412
  102.3 1.0 shard_map.90
  103.3 0.1 collective-permute-start.15
  103.4 5.8 %collective-permute-start.16 = (bf16[3,64,256]{2,1,0:T(8,128)(2,1)S(1)}, bf16[3,64,256]{2,1,0:T(8,128)(2,1)S(1)}, u32[]{:S(2)}, u32[]{:S(2)}) collective-permute-start(bf16[3,64,256]{2,1,0:T(8,128)(2,1)S(1)} %get-tuple-element.63), channel_id=1, source_target_pairs={{0,4},{1,5},{4,8},{5,9},{8,12},{9,13},{12,0},{13,1},{2,6},{3,7},{6... | collective-permute-start | bytes 294920 | tf_op jit(solution)/shard_map/ppermute | solution.py:424
  109.2 0.1 collective-permute-start.17
  109.2 2.8 %collective-permute-start.18 = (bf16[3,64,256]{2,1,0:T(8,128)(2,1)S(1)}, bf16[3,64,256]{2,1,0:T(8,128)(2,1)}, u32[]{:S(2)}, u32[]{:S(2)}) collective-permute-start(bf16[3,64,256]{2,1,0:T(8,128)(2,1)S(1)} %get-tuple-element.65), channel_id=1, source_target_pairs={{0,8},{1,9},{4,12},{5,13},{8,0},{9,1},{12,4},{13,5},{2,10},{3,11},... | collective-permute-start | bytes 294920 | tf_op jit(solution)/shard_map/ppermute | solution.py:424
  112.0 3.3 %collective-permute-start.20 = (bf16[3,64,256]{2,1,0:T(8,128)(2,1)S(1)}, bf16[3,64,256]{2,1,0:T(8,128)(2,1)}, u32[]{:S(2)}, u32[]{:S(2)}) collective-permute-start(bf16[3,64,256]{2,1,0:T(8,128)(2,1)S(1)} %get-tuple-element.67), channel_id=1, source_target_pairs={{0,12},{1,13},{4,0},{5,1},{8,4},{9,5},{12,8},{13,9},{2,14},{3,15},... | collective-permute-start | bytes 294920 | tf_op jit(solution)/shard_map/ppermute | solution.py:424
  115.4 0.5 collective-permute-start.21
  116.0 0.8 collective-permute-done.17
  116.8 6.5 %collective-permute-done.18 = bf16[3,64,256]{2,1,0:T(8,128)(2,1)} collective-permute-done((bf16[3,64,256]{2,1,0:T(8,128)(2,1)S(1)}, bf16[3,64,256]{2,1,0:T(8,128)(2,1)}, u32[]{:S(2)}, u32[]{:S(2)}) %collective-permute-start.18) | collective-permute-done | bytes 98336 | tf_op jit(solution)/shard_map/ppermute | solution.py:424
  123.4 0.9 stack.107
  124.3 1.0 collective-permute-done.19
  125.3 0.9 stack.108
  126.3 1.6 %stack.109 = bf16[1,1,3,16384]{3,0,2,1:T(2,128)(2,1)} reshape(bf16[3,64,256]{2,1,0:T(8,128)(2,1)} %collective-permute-done.20) | data formatting | bytes 196608 | tf_op jit(solution)/shard_map/stack | solution.py:429
  127.9 0.9 stack.110
  128.8 2.8 %fusion = f32[64,4,2,3]{0,1,3,2:T(4,128)S(1)} fusion(bf16[64,16384]{1,0:T(8,128)(2,1)S(1)} %bitcast.74, bf16[1,1,3,16384]{3,0,2,1:T(2,128)(2,1)S(1)} %stack.110, bf16[1,1,3,16384]{3,0,2,1:T(2,128)(2,1)} %stack.109, bf16[1,1,3,16384]{3,0,2,1:T(2,128)(2,1)S(1)} %stack.108, bf16[1,1,3,16384]{3,0,2,1:T(2,128)(2,1)S(1)} %stack.107, ...), kind=kOutput, calls=%fused_computation.1 | convolution fusion | flops 56623104 | bytes 2889728 | tf_op jit(solution)/shard_map/dot_general | solution.py:431
  131.7 0.1 reshape_reshape.3
  131.8 0.1 constant_dynamic-slice_fusion.1
  131.9 0.2 collective-permute-start.22
  132.1 1.1 collective-permute-done.22
  133.2 1.5 %collective-permute-start.23 = (f32[16,4,6]{0,1,2:T(4,128)S(1)}, f32[16,4,6]{0,1,2:T(4,128)S(1)}, u32[]{:S(2)}, u32[]{:S(2)}) collective-permute-start(f32[16,4,6]{0,1,2:T(4,128)S(1)} %dynamic-slice_bitcast_fusion), channel_id=1, source_target_pairs={{0,2},{2,0},{1,3},{3,1},{4,6},{6,4},{5,7},{7,5},{8,10},{10,8},{9,1... | collective-permute-start | bytes 4616 | tf_op jit(solution)/shard_map/ppermute | solution.py:62
  134.7 2.2 %collective-permute-done.23 = f32[16,4,6]{0,1,2:T(4,128)S(1)} collective-permute-done((f32[16,4,6]{0,1,2:T(4,128)S(1)}, f32[16,4,6]{0,1,2:T(4,128)S(1)}, u32[]{:S(2)}, u32[]{:S(2)}) %collective-permute-start.23) | collective-permute-done | bytes 1568 | tf_op jit(solution)/shard_map/ppermute | solution.py:62
  137.1 1.2 collective-permute-start.24
  138.3 3.3 %collective-permute-done.24 = f32[16,2,6]{0,1,2:T(2,128)S(1)} collective-permute-done((f32[16,2,6]{0,1,2:T(2,128)S(1)}, f32[16,2,6]{0,1,2:T(2,128)S(1)}, u32[]{:S(2)}, u32[]{:S(2)}) %collective-permute-start.24) | collective-permute-done | bytes 800 | tf_op jit(solution)/shard_map/ppermute | solution.py:75
  141.7 2.7 %collective-permute-start.25 = (f32[16,1,6]{0,1,2:T(1,128)S(1)}, f32[16,1,6]{0,1,2:T(1,128)S(1)}, u32[]{:S(2)}, u32[]{:S(2)}) collective-permute-start(f32[16,1,6]{0,1,2:T(1,128)S(1)} %fusion.27), channel_id=1, source_target_pairs={{0,4},{4,0},{8,12},{12,8},{1,5},{5,1},{9,13},{13,9},{2,6},{6,2},{1... | collective-permute-start | bytes 1160 | tf_op jit(solution)/shard_map/ppermute | solution.py:75
  144.4 1.6 %collective-permute-done.25 = f32[16,1,6]{0,1,2:T(1,128)S(1)} collective-permute-done((f32[16,1,6]{0,1,2:T(1,128)S(1)}, f32[16,1,6]{0,1,2:T(1,128)S(1)}, u32[]{:S(2)}, u32[]{:S(2)}) %collective-permute-start.25) | collective-permute-done | bytes 416 | tf_op jit(solution)/shard_map/ppermute | solution.py:75
  146.0 0.7 bitcast_multiply_fusion
  (63 shorter events, 0.5 us)
Async XLA Ops:
  0.0 1.7 %copy-start.3 = (bf16[128,2560]{1,0:T(8,128)(2,1)S(1)}, bf16[128,2560]{1,0:T(8,128)(2,1)}, u32[]{:S(2)}) copy-start(bf16[128,2560]{1,0:T(8,128)(2,1)} %b_out.1) | copy-start | bytes 1966084
  0.0 30.9 %collective-permute-start.3 = (bf16[3,128,6912]{2,1,0:T(8,128)(2,1)}, bf16[3,128,6912]{2,1,0:T(8,128)(2,1)}, u32[]{:S(2)}, u32[]{:S(2)}) collective-permute-start(bf16[3,128,6912]{2,1,0:T(8,128)(2,1)} %param.8), channel_id=1, source_target_pairs={{0,1},{1,0},{2,3},{3,2},{4,5},{5,4},{6,7},{7,6},{8,9},{9,8},{10,11... | collective-permute-start | bytes 15925256 | tf_op jit(solution)/shard_map/ppermute | solution.py:379
  1.7 5.1 %copy-start.10 = (bf16[64,64,256]{2,1,0:T(8,128)(2,1)S(1)}, bf16[64,64,256]{2,1,0:T(8,128)(2,1)}, u32[]{:S(2)}) copy-start(bf16[64,64,256]{2,1,0:T(8,128)(2,1)} %param.13) | copy-start | bytes 6291460
  1.7 5.1 %copy-start.12 = (f32[64,256]{1,0:T(8,128)S(1)}, f32[64,256]{1,0:T(8,128)}, u32[]{:S(2)}) copy-start(f32[64,256]{1,0:T(8,128)} %param.14) | copy-start | bytes 196612
  1.8 8.4 %slice-start = ((s8[5308416]{0:T(1024)(128)(4,1)}), s8[4194304]{0:T(1024)(128)(4,1)S(1)}, s32[]{:S(2)}) async-start(s8[5308416]{0:T(1024)(128)(4,1)} %bitcast.70), calls=%async_computation | async-start | bytes 8388608
  1.9 8.3 %slice-start.1 = ((s8[5308416]{0:T(1024)(128)(4,1)}), s8[1114112]{0:T(1024)(128)(4,1)S(1)}, s32[]{:S(2)}) async-start(s8[5308416]{0:T(1024)(128)(4,1)} %bitcast.70), calls=%async_computation.1 | async-start | bytes 2228224
  1.9 18.9 %collective-permute-start = (bf16[64,9472]{1,0:T(8,128)(2,1)S(1)}, bf16[64,9472]{1,0:T(8,128)(2,1)S(1)}, u32[]{:S(2)}, u32[]{:S(2)}) collective-permute-start(bf16[64,9472]{1,0:T(8,128)(2,1)S(1)} %pad_maximum_fusion), channel_id=1, source_target_pairs={{0,4},{4,8},{8,12},{5,1},{9,5},{13,9},{2,6},{6,10},{10,14},{7,3},{... | collective-permute-start | bytes 3637256 | tf_op jit(solution)/shard_map/ppermute | solution.py:377
  10.1 2.1 %copy-start.2 = (bf16[128,6912]{1,0:T(8,128)(2,1)S(1)}, bf16[128,6912]{1,0:T(8,128)(2,1)}, u32[]{:S(2)}) copy-start(bf16[128,6912]{1,0:T(8,128)(2,1)} %b_in.1) | copy-start | bytes 5308420
  10.1 2.2 %copy-start.4 = (bf16[128,2560]{1,0:T(8,128)(2,1)S(1)}, bf16[128,2560]{1,0:T(8,128)(2,1)}, u32[]{:S(2)}) copy-start(bf16[128,2560]{1,0:T(8,128)(2,1)} %b_out.1) | copy-start | bytes 1966084
  11.9 2.6 %copy-start = (bf16[384,6912]{1,0:T(8,128)(2,1)}, bf16[384,6912]{1,0:T(8,128)(2,1)S(1)}, u32[]{:S(2)}) copy-start(bf16[384,6912]{1,0:T(8,128)(2,1)S(1)} %get-tuple-element.38.t_in) | copy-start | bytes 15925252
  14.5 0.7 copy-start.7
  20.8 4.8 %collective-permute-start.1 = (bf16[64,9472]{1,0:T(8,128)(2,1)S(1)}, bf16[64,9472]{1,0:T(8,128)(2,1)S(1)}, u32[]{:S(2)}, u32[]{:S(2)}) collective-permute-start(bf16[64,9472]{1,0:T(8,128)(2,1)S(1)} %collective-permute-done.x), channel_id=1, source_target_pairs={{1,17},{5,21},{8,24},{12,28},{17,1},{21,5},{24,8},{28,12},{3,19},{... | collective-permute-start | bytes 3637256 | tf_op jit(solution)/shard_map/ppermute | solution.py:374
  21.5 5.2 %collective-permute-start.5 = (bf16[64,9472]{1,0:T(8,128)(2,1)S(1)}, bf16[64,9472]{1,0:T(8,128)(2,1)}, u32[]{:S(2)}, u32[]{:S(2)}) collective-permute-start(bf16[64,9472]{1,0:T(8,128)(2,1)S(1)} %collective-permute-done.x), channel_id=1, source_target_pairs={{4,8},{8,12},{5,1},{9,5},{6,10},{10,14},{7,3},{11,7},{20,24},{24,2... | collective-permute-start | bytes 3637256 | tf_op jit(solution)/shard_map/ppermute | solution.py:377
  23.2 7.6 %collective-permute-start.2 = (bf16[3,128,2560]{2,1,0:T(8,128)(2,1)}, bf16[3,128,2560]{2,1,0:T(8,128)(2,1)}, u32[]{:S(2)}, u32[]{:S(2)}) collective-permute-start(bf16[3,128,2560]{2,1,0:T(8,128)(2,1)} %param.9), channel_id=1, source_target_pairs={{0,1},{1,0},{2,3},{3,2},{4,5},{5,4},{6,7},{7,6},{8,9},{9,8},{10,11... | collective-permute-start | bytes 5898248 | tf_op jit(solution)/shard_map/ppermute | solution.py:379
  25.6 1.1 copy-start.5
  26.6 9.8 %collective-permute-start.10 = (bf16[64,9472]{1,0:T(8,128)(2,1)}, bf16[64,9472]{1,0:T(8,128)(2,1)}, u32[]{:S(2)}, u32[]{:S(2)}) collective-permute-start(bf16[64,9472]{1,0:T(8,128)(2,1)} %collective-permute-done.5.x), channel_id=1, source_target_pairs={{8,12},{5,1},{10,14},{7,3},{24,28},{21,17},{26,30},{23,19}} | collective-permute-start | bytes 3637256 | tf_op jit(solution)/shard_map/ppermute | solution.py:377
  28.3 8.1 %collective-permute-start.6 = (bf16[64,9472]{1,0:T(8,128)(2,1)}, bf16[64,9472]{1,0:T(8,128)(2,1)}, u32[]{:S(2)}, u32[]{:S(2)}) collective-permute-start(bf16[64,9472]{1,0:T(8,128)(2,1)} %collective-permute-done.5.x), channel_id=1, source_target_pairs={{1,17},{5,21},{8,24},{12,28},{17,1},{21,5},{24,8},{28,12},{3,19},{... | collective-permute-start | bytes 3637256 | tf_op jit(solution)/shard_map/ppermute | solution.py:374
  30.1 7.1 %collective-permute-start.8 = (bf16[64,9472]{1,0:T(8,128)(2,1)S(1)}, bf16[64,9472]{1,0:T(8,128)(2,1)S(1)}, u32[]{:S(2)}, u32[]{:S(2)}) collective-permute-start(bf16[64,9472]{1,0:T(8,128)(2,1)S(1)} %collective-permute-done.x), channel_id=1, source_target_pairs={{4,20},{9,25},{20,4},{25,9},{6,22},{11,27},{22,6},{27,11}} | collective-permute-start | bytes 3637256 | tf_op jit(solution)/shard_map/ppermute | solution.py:374
  30.9 4.6 %copy-start.1 = (bf16[384,6912]{1,0:T(8,128)(2,1)S(1)}, bf16[384,6912]{1,0:T(8,128)(2,1)}, u32[]{:S(2)}) copy-start(bf16[384,6912]{1,0:T(8,128)(2,1)} %copy-done) | copy-start | bytes 15925252
  30.9 4.9 %copy-start.6 = (bf16[64,9472]{1,0:T(8,128)(2,1)S(1)}, bf16[64,9472]{1,0:T(8,128)(2,1)}, u32[]{:S(2)}) copy-start(bf16[64,9472]{1,0:T(8,128)(2,1)} %copy-done.5) | copy-start | bytes 3637252
  36.5 33.6 %collective-permute-start.11 = (bf16[64,9472]{1,0:T(8,128)(2,1)}, bf16[64,9472]{1,0:T(8,128)(2,1)S(1)}, u32[]{:S(2)}, u32[]{:S(2)}) collective-permute-start(bf16[64,9472]{1,0:T(8,128)(2,1)} %collective-permute-done.10.x), channel_id=1, source_target_pairs={{1,17},{12,28},{17,1},{28,12},{3,19},{14,30},{19,3},{30,14}} | collective-permute-start | bytes 3637256 | tf_op jit(solution)/shard_map/ppermute | solution.py:374
  37.9 46.5 %collective-permute-start.9 = (f32[256,384]{1,0:T(8,128)S(1)}, f32[256,384]{1,0:T(8,128)S(1)}, u32[]{:S(2)}, u32[]{:S(2)}) collective-permute-start(f32[256,384]{1,0:T(8,128)S(1)} %get-tuple-element.51), channel_id=1, source_target_pairs={{0,1},{1,0},{2,3},{3,2},{4,5},{5,4},{6,7},{7,6},{8,9},{9,8},{10,11... | collective-permute-start | bytes 1179656 | tf_op jit(solution)/shard_map/ppermute | solution.py:389
  63.5 20.8 %collective-permute-start.4 = (f32[256,384]{1,0:T(8,128)S(1)}, f32[256,384]{1,0:T(8,128)S(1)}, u32[]{:S(2)}, u32[]{:S(2)}) collective-permute-start(f32[256,384]{1,0:T(8,128)S(1)} %get-tuple-element.45), channel_id=1, source_target_pairs={{0,1},{1,0},{2,3},{3,2},{4,5},{5,4},{6,7},{7,6},{8,9},{9,8},{10,11... | collective-permute-start | bytes 1179656 | tf_op jit(solution)/shard_map/ppermute | solution.py:389
  64.2 20.1 %collective-permute-start.7 = (f32[256,384]{1,0:T(8,128)S(1)}, f32[256,384]{1,0:T(8,128)S(1)}, u32[]{:S(2)}, u32[]{:S(2)}) collective-permute-start(f32[256,384]{1,0:T(8,128)S(1)} %get-tuple-element.48), channel_id=1, source_target_pairs={{0,1},{1,0},{2,3},{3,2},{4,5},{5,4},{6,7},{7,6},{8,9},{9,8},{10,11... | collective-permute-start | bytes 1179656 | tf_op jit(solution)/shard_map/ppermute | solution.py:389
  70.1 15.6 %copy-start.8 = (f32[128,384]{1,0:T(8,128)S(1)}, f32[128,384]{1,0:T(8,128)}, u32[]{:S(2)}) copy-start(f32[128,384]{1,0:T(8,128)} %copy-done.7) | copy-start | bytes 589828
  70.9 14.8 %collective-permute-start.12 = (f32[256,384]{1,0:T(8,128)S(1)}, f32[256,384]{1,0:T(8,128)S(1)}, u32[]{:S(2)}, u32[]{:S(2)}) collective-permute-start(f32[256,384]{1,0:T(8,128)S(1)} %get-tuple-element.56), channel_id=1, source_target_pairs={{0,1},{1,0},{2,3},{3,2},{4,5},{5,4},{6,7},{7,6},{8,9},{9,8},{10,11... | collective-permute-start | bytes 1179656 | tf_op jit(solution)/shard_map/ppermute | solution.py:389
  85.7 16.6 %copy-start.9 = (s32[3]{0:T(128)S(1)}, s32[3]{0:T(128)}, u32[]{:S(2)}) copy-start(s32[3]{0:T(128)} %counts.1) | copy-start | bytes 40
  86.6 15.7 %collective-permute-start.13 = (bf16[512,384]{1,0:T(8,128)(2,1)S(1)}, bf16[512,384]{1,0:T(8,128)(2,1)S(1)}, u32[]{:S(2)}, u32[]{:S(2)}) collective-permute-start(bf16[512,384]{1,0:T(8,128)(2,1)S(1)} %get-tuple-element.58), channel_id=1, source_target_pairs={{0,2},{2,0},{1,3},{3,1},{4,6},{6,4},{5,7},{7,5},{8,10},{10,8},{9,1... | collective-permute-start | bytes 1179656 | tf_op jit(solution)/shard_map/ppermute | solution.py:411
  88.2 14.1 %collective-permute-start.14 = (bf16[256,384]{1,0:T(8,128)(2,1)S(1)}, bf16[256,384]{1,0:T(8,128)(2,1)S(1)}, u32[]{:S(2)}, u32[]{:S(2)}) collective-permute-start(bf16[256,384]{1,0:T(8,128)(2,1)S(1)} %get-tuple-element.60), channel_id=1, source_target_pairs={{0,2},{2,0},{1,3},{3,1},{4,6},{6,4},{5,7},{7,5},{8,10},{10,8},{9,1... | collective-permute-start | bytes 589832 | tf_op jit(solution)/shard_map/ppermute | solution.py:412
  103.3 25.5 %copy-start.11 = (bf16[8,8,64,256]{3,1,2,0:T(8,128)(2,1)S(1)}, bf16[8,8,64,256]{3,1,2,0:T(8,128)(2,1)}, u32[]{:S(2)}) copy-start(bf16[8,8,64,256]{3,1,2,0:T(8,128)(2,1)} %copy.48) | copy-start | bytes 6291460
  103.3 8.7 %collective-permute-start.15 = (bf16[3,64,256]{2,1,0:T(8,128)(2,1)S(1)}, bf16[3,64,256]{2,1,0:T(8,128)(2,1)S(1)}, u32[]{:S(2)}, u32[]{:S(2)}) collective-permute-start(bf16[3,64,256]{2,1,0:T(8,128)(2,1)S(1)} %get-tuple-element.62), channel_id=1, source_target_pairs={{0,1},{1,0},{4,5},{5,4},{8,9},{9,8},{12,13},{13,12},{2,3},{3,2},{6... | collective-permute-start | bytes 294920 | tf_op jit(solution)/shard_map/ppermute | solution.py:424
  103.4 12.0 %collective-permute-start.16 = (bf16[3,64,256]{2,1,0:T(8,128)(2,1)S(1)}, bf16[3,64,256]{2,1,0:T(8,128)(2,1)S(1)}, u32[]{:S(2)}, u32[]{:S(2)}) collective-permute-start(bf16[3,64,256]{2,1,0:T(8,128)(2,1)S(1)} %get-tuple-element.63), channel_id=1, source_target_pairs={{0,4},{1,5},{4,8},{5,9},{8,12},{9,13},{12,0},{13,1},{2,6},{3,7},{6... | collective-permute-start | bytes 294920 | tf_op jit(solution)/shard_map/ppermute | solution.py:424
  109.2 7.6 %collective-permute-start.17 = (bf16[3,64,256]{2,1,0:T(8,128)(2,1)S(1)}, bf16[3,64,256]{2,1,0:T(8,128)(2,1)S(1)}, u32[]{:S(2)}, u32[]{:S(2)}) collective-permute-start(bf16[3,64,256]{2,1,0:T(8,128)(2,1)S(1)} %get-tuple-element.64), channel_id=1, source_target_pairs={{0,5},{1,4},{4,9},{5,8},{8,13},{9,12},{12,1},{13,0},{2,7},{3,6},{6... | collective-permute-start | bytes 294920 | tf_op jit(solution)/shard_map/ppermute | solution.py:424
  109.2 14.1 %collective-permute-start.18 = (bf16[3,64,256]{2,1,0:T(8,128)(2,1)S(1)}, bf16[3,64,256]{2,1,0:T(8,128)(2,1)}, u32[]{:S(2)}, u32[]{:S(2)}) collective-permute-start(bf16[3,64,256]{2,1,0:T(8,128)(2,1)S(1)} %get-tuple-element.65), channel_id=1, source_target_pairs={{0,8},{1,9},{4,12},{5,13},{8,0},{9,1},{12,4},{13,5},{2,10},{3,11},... | collective-permute-start | bytes 294920 | tf_op jit(solution)/shard_map/ppermute | solution.py:424
  112.0 13.3 %collective-permute-start.19 = (bf16[3,64,256]{2,1,0:T(8,128)(2,1)S(1)}, bf16[3,64,256]{2,1,0:T(8,128)(2,1)}, u32[]{:S(2)}, u32[]{:S(2)}) collective-permute-start(bf16[3,64,256]{2,1,0:T(8,128)(2,1)S(1)} %get-tuple-element.66), channel_id=1, source_target_pairs={{0,9},{1,8},{4,13},{5,12},{8,1},{9,0},{12,5},{13,4},{2,11},{3,10},... | collective-permute-start | bytes 294920 | tf_op jit(solution)/shard_map/ppermute | solution.py:424
  112.0 14.3 %collective-permute-start.20 = (bf16[3,64,256]{2,1,0:T(8,128)(2,1)S(1)}, bf16[3,64,256]{2,1,0:T(8,128)(2,1)}, u32[]{:S(2)}, u32[]{:S(2)}) collective-permute-start(bf16[3,64,256]{2,1,0:T(8,128)(2,1)S(1)} %get-tuple-element.67), channel_id=1, source_target_pairs={{0,12},{1,13},{4,0},{5,1},{8,4},{9,5},{12,8},{13,9},{2,14},{3,15},... | collective-permute-start | bytes 294920 | tf_op jit(solution)/shard_map/ppermute | solution.py:424
  115.4 12.5 %collective-permute-start.21 = (bf16[3,64,256]{2,1,0:T(8,128)(2,1)S(1)}, bf16[3,64,256]{2,1,0:T(8,128)(2,1)}, u32[]{:S(2)}, u32[]{:S(2)}) collective-permute-start(bf16[3,64,256]{2,1,0:T(8,128)(2,1)S(1)} %get-tuple-element.68), channel_id=1, source_target_pairs={{0,13},{1,12},{4,1},{5,0},{8,5},{9,4},{12,9},{13,8},{2,15},{3,14},... | collective-permute-start | bytes 294920 | tf_op jit(solution)/shard_map/ppermute | solution.py:424
  128.8 9.5 %copy-start.13 = (s32[16,1]{0,1:T(1,128)S(1)}, s32[16,1]{0,1:T(1,128)}, u32[]{:S(2)}) copy-start(s32[16,1]{0,1:T(1,128)} %param.15) | copy-start | bytes 196
  131.9 1.3 collective-permute-start.22
  133.2 3.8 %collective-permute-start.23 = (f32[16,4,6]{0,1,2:T(4,128)S(1)}, f32[16,4,6]{0,1,2:T(4,128)S(1)}, u32[]{:S(2)}, u32[]{:S(2)}) collective-permute-start(f32[16,4,6]{0,1,2:T(4,128)S(1)} %dynamic-slice_bitcast_fusion), channel_id=1, source_target_pairs={{0,2},{2,0},{1,3},{3,1},{4,6},{6,4},{5,7},{7,5},{8,10},{10,8},{9,1... | collective-permute-start | bytes 4616 | tf_op jit(solution)/shard_map/ppermute | solution.py:62
  137.1 4.6 %collective-permute-start.24 = (f32[16,2,6]{0,1,2:T(2,128)S(1)}, f32[16,2,6]{0,1,2:T(2,128)S(1)}, u32[]{:S(2)}, u32[]{:S(2)}) collective-permute-start(f32[16,2,6]{0,1,2:T(2,128)S(1)} %fusion.21), channel_id=1, source_target_pairs={{0,8},{4,12},{8,0},{12,4},{1,9},{5,13},{9,1},{13,5},{2,10},{6,14},... | collective-permute-start | bytes 2312 | tf_op jit(solution)/shard_map/ppermute | solution.py:75
  141.7 4.3 %collective-permute-start.25 = (f32[16,1,6]{0,1,2:T(1,128)S(1)}, f32[16,1,6]{0,1,2:T(1,128)S(1)}, u32[]{:S(2)}, u32[]{:S(2)}) collective-permute-start(f32[16,1,6]{0,1,2:T(1,128)S(1)} %fusion.27), channel_id=1, source_target_pairs={{0,4},{4,0},{8,12},{12,8},{1,5},{5,1},{9,13},{13,9},{2,6},{6,2},{1... | collective-permute-start | bytes 1160 | tf_op jit(solution)/shard_map/ppermute | solution.py:75

commit v5 on v4

--- a/solution.py
+++ b/solution.py
@@ -53,15 +53,14 @@
     n_query = partial_value.shape[0]
     block = n_query // (2 * n_layer)
     part = partial_value.reshape(n_layer, 2, block, n_wide, chip_seqs)
-    part = lax.dynamic_index_in_dim(part, rep, axis=1, keepdims=False) + lax.ppermute(
-        lax.dynamic_index_in_dim(part, 1 - rep, axis=1, keepdims=False), "rep", [(0, 1), (1, 0)]
-    )
-    total = lax.dynamic_index_in_dim(part, layer, axis=0, keepdims=False)
-    for m in range(1, n_layer):
-        shift = [(i, (i + m) % n_layer) for i in range(n_layer)]
-        total = total + lax.ppermute(
-            lax.dynamic_index_in_dim(part, (layer + m) % n_layer, axis=0, keepdims=False), "layer", shift
-        )
+    part = part.reshape(2 * n_layer, block, n_wide, chip_seqs)
+    here = 2 * layer + rep
+    total = lax.dynamic_index_in_dim(part, here, axis=0, keepdims=False)
+    places = 2 * n_layer
+    for m in range(1, places):
+        shift = [(p, (p + m) % places) for p in range(places)]
+        given = lax.dynamic_index_in_dim(part, (here + m) % places, axis=0, keepdims=False)
+        total = total + lax.ppermute(given, ("layer", "rep"), shift)
     if n_wide & (n_wide - 1) == 0:
         doubled = jnp.concatenate([total[:, :1], total[:, :0:-1]], axis=1)
         doubled = jnp.concatenate([doubled, doubled], axis=1)
@@ -231,28 +230,38 @@
     return jnp.concatenate([jnp.where(group == 0, mine, other), jnp.where(group == 0, other, mine)], axis=0)
 
 
-def shard_body(flag, at, x, y, t_out, t_in, o_out, o_in, mine, theirs, held, total, sems):
+def shard_body(flags, at, *refs):
+    sources = [refs[2 * i : 2 * i + 2] for i in range(len(flags))]
+    t_out, t_in, o_out, o_in, mine, theirs, held, total, sems = refs[2 * len(flags) :]
     d, ff = t_out.shape[1], t_in.shape[1]
     rows = mine.shape[0] // 2
-    cuts = [(0, d)] + [(d + k, min(ff // 2 // 128 * 128 + 128, ff - k)) for k in range(0, ff, ff // 2 // 128 * 128 + 128)]
-    cuts = [(start, width) for start, width in cuts if width > 0]
-
-    @pl.when(at[flag] == 1)
+    step = ff // 2 // 128 * 128 + 128
+    cuts = [(0, d)] + [(d + k, min(step, ff - k)) for k in range(0, ff, step)]
+
+    def copies(source):
+        return [
+            [
+                pltpu.make_async_copy(p.at[:, pl.ds(*cut)], held.at[j, :, pl.ds(*cut)], sems.at[i, j])
+                for j, p in enumerate(source)
+            ]
+            for i, cut in enumerate(cuts)
+        ]
+
+    chosen = at[flags[0]] == 1
+    for flag, source in zip(flags, sources, strict=True):
+        chosen = chosen | (at[flag] == 1)
+
+        @pl.when(at[flag] == 1)
+        def _(source=source):
+            for pair in copies(source):
+                for copy in pair:
+                    copy.start()
+
+    @pl.when(chosen)
     def _():
-        copies = []
+        waits = copies(sources[0])
         for i, (start, width) in enumerate(cuts):
-            columns = pl.ds(start, width)
-            copies.append(
-                [
-                    pltpu.make_async_copy(p.at[:, columns], held.at[j, :, columns], sems.at[i, j])
-                    for j, p in enumerate((x, y))
-                ]
-            )
-        for pair in copies:
-            for copy in pair:
-                copy.start()
-        for i, (start, width) in enumerate(cuts):
-            for copy in copies[i]:
+            for copy in waits[i]:
                 copy.wait()
             for j, tokens in enumerate((t_out, o_out) if start < d else (t_in, o_in)):
                 first = start if start < d else start - d
@@ -263,71 +272,95 @@
                     out[put_rows, :] = in_order(at[0], total[j].T)
 
 
-def when(condition, do):
-    if condition is None:
-        do()
-    else:
-        pl.when(condition)(do)
-
-
-def slots_body(at, g_own, a_own, near, near_far, middle, middle_far, inner, inner_far, outer, outer_far, *outs):
-    grad, grad_sent, act, act_sent = outs
-    wide, layer, holds = at[1], at[2], at[4] == 1
+def sources_of(at, near, near_far, both, both_far, last, last_far):
+    holds, outside = at[4] == 1, at[6] + at[7] == 1
+    other, inside = jnp.logical_not(holds), jnp.logical_not(outside)
+    return (
+        ((near, holds), (near_far, other)),
+        ((both, holds), (both_far, other)),
+        ((both_far, holds & inside), (both, other & inside), (last, holds & outside), (last_far, other & outside)),
+    )
+
+
+def early_body(at, g_own, a_own, near, near_far, sent):
     rows = g_own.shape[0]
-
-    def store(slot, value, condition, is_out):
-        if is_out:
-
-            def do():
-                grad[slot * rows : (slot + 1) * rows, :] = value()
-                grad_sent[slot * rows : (slot + 1) * rows, :] = value().astype(HALF)
-
-            when(condition, do)
-            return
+    sent[:rows, :] = g_own[...].astype(HALF)
+    sent[rows : 2 * rows, :] = a_own[...].astype(HALF)
+    choices = sources_of(at, near, near_far, near, near, near, near)
+    for source, condition in choices[0]:
+
+        @pl.when(condition)
+        def _(source=source):
+            sent[2 * rows :, :] = source[...].astype(HALF)
+
+
+def late_body(at, both, both_far, last, last_far, sent):
+    size = both.shape[0]
+    choices = sources_of(at, both, both_far, both, both_far, last, last_far)
+    for i, sources in enumerate(choices[1:]):
+        for source, condition in sources:
+
+            @pl.when(condition)
+            def _(source=source, i=i):
+                sent[i * size : (i + 1) * size, :] = source[...].astype(HALF)
+
+
+def train_body(at, counts, g_own, a_own, near, near_far, both, both_far, last, last_far, early, late, *refs):
+    mine, theirs, (grad, act, held) = refs[:4], refs[4:8], refs[8:]
+    wide, layer, rep = at[1], at[2], at[3]
+    rows, half = g_own.shape[0], mine[0].shape[1]
+    near_slot = jnp.where(wide <= 1, 1, 3)
+
+    def place(slot, g, a):
+        put(grad, slot, rows, g.astype(HALF))
         shard = lax.rem(wide + slot, 4)
-        per_layer = act.shape[0] // rows
-        place = lax.rem(shard, per_layer)
-        here = lax.div(shard, per_layer) == layer
-        away = jnp.logical_not(here)
-        pl.when(here if condition is None else condition & here)(lambda: put(act, place, rows, value()))
-        pl.when(away if condition is None else condition & away)(
-            lambda: put(act_sent, place, rows, value().astype(HALF))
-        )
-
-    for is_out in (True, False):
-        part = slice(0, rows) if is_out else slice(rows, 2 * rows)
-        other = jnp.logical_not(holds)
-        own = g_own if is_out else a_own
-        store(0, lambda own=own: own[...], None, is_out)
-        for slot, here, away, condition, at_holder in (
-            (1, near, near_far, wide <= 1, holds),
-            (3, near, near_far, wide >= 2, holds),
-            (2, middle, middle_far, None, holds),
-            (3, inner, inner_far, wide == 1, other),
-            (1, inner, inner_far, wide == 2, other),
-            (3, outer, outer_far, wide == 0, holds),
-            (1, outer, outer_far, wide == 3, holds),
-        ):
-            for source, at_this in ((here, at_holder), (away, jnp.logical_not(at_holder))):
-                both = at_this if condition is None else condition & at_this
-                store(slot, lambda source=source, part=part: source[part, :], both, is_out)
-
-
-def train_body(at, counts, grad, grad_came, act, act_came, *refs):
-    mine, theirs, held = refs[:4], refs[4:8], refs[8]
-    rep = at[3]
-    seqs, half = mine[0].shape[0], mine[0].shape[1]
+        here = lax.div(shard, 2) == layer
+
+        @pl.when(here)
+        def _():
+            put(act, lax.rem(shard, 2), rows, a.astype(HALF))
+
+    def came(ref, block):
+        return ref[block * rows : (block + 1) * rows, :].astype(FLOAT)
+
+    place(0, g_own[...] + came(early, 0), a_own[...] + came(early, 1))
+    choices = sources_of(at, near, near_far, both, both_far, last, last_far)
+    for sources, slot, ref, block in zip(choices, (near_slot, 2, 4 - near_slot), (early, late, late), (2, 0, 2), strict=True):
+        for source, condition in sources:
+
+            @pl.when(condition)
+            def _(source=source, slot=slot, ref=ref, block=block):
+                place(slot, source[:rows, :] + came(ref, block), source[rows:, :] + came(ref, block + 1))
+
+    seqs = mine[0].shape[0]
     length = grad.shape[1] // seqs
     spot = lax.broadcasted_iota(jnp.int32, (1, length), 1)
     for s in range(seqs):
         cols = slice(s * length, (s + 1) * length)
-        g = grad[:, cols] + grad_came[:, cols].astype(FLOAT)
-        g = jnp.where(spot < counts[s], g, 0.0).astype(HALF)
-        a = (act[:, cols] + act_came[:, cols].astype(FLOAT)).astype(HALF)
-        held[...] = lax.dot_general(g, a, (((1,), (1,)), ((), ())), preferred_element_type=FLOAT).astype(HALF)
+        g = jnp.where(spot < counts[s], grad[:, cols].astype(FLOAT), 0.0).astype(HALF)
+        held[...] = lax.dot_general(g, act[:, cols], (((1,), (1,)), ((), ())), preferred_element_type=FLOAT).astype(HALF)
         for n in range(4):
             for r, outs in ((rep, mine), (1 - rep, theirs)):
                 outs[n][s] = held[pl.ds(pl.multiple_of((2 * n + r) * half, half), half), :]
+
+
+def score_body(at, weights, *refs):
+    same, cross, (out, held, total) = refs[:4], refs[4:8], refs[8:]
+    rep = at[3]
+    seqs, half = same[0].shape[0], same[0].shape[1]
+    for n in range(4):
+        for core, pieces in ((rep, same), (1 - rep, cross)):
+            for s in range(seqs):
+                where = pl.ds(pl.multiple_of(((2 * n + core) * seqs + s) * half, half), half)
+                for c in range(held.shape[0]):
+                    held[c, where, :] = pieces[n][s][:, c * 128 : (c + 1) * 128].astype(FLOAT)
+    count = 8 * seqs
+    total[...] = jnp.zeros_like(total)
+    for i in range(half):
+        block = jnp.concatenate([held[c, pl.ds(i, count, stride=half), :] for c in range(held.shape[0])], axis=1)
+        block = block.astype(HALF)
+        total[...] += lax.dot_general(weights[i], block, (((1,), (1,)), ((), ())), preferred_element_type=FLOAT)
+    out[...] = total[...]
 
 
 def shaped(*shape, kind=FLOAT):
@@ -345,10 +378,11 @@
     group, wide, layer, rep = (lax.axis_index(a) for a in ("groups", "wide", "layer", "rep"))
     holds = (rep == 1) == (wide <= 1)
     outside = (wide == 0) | (wide == 3)
-    at = jnp.stack([group, wide, layer, rep, holds, ~holds & ~outside, holds & outside]).astype(jnp.int32)
+    flags = [group, wide, layer, rep, holds, ~holds & ~outside, holds & outside, ~holds & outside]
+    at = jnp.stack(flags).astype(jnp.int32)
     swap = [(0, 1), (1, 0)]
     n_query = query_grads.shape[0]
-    weighted = (query_grads.astype(FLOAT) / eigenvalues[None, :, :]).astype(HALF).reshape(n_query, half * share)
+    weighted = (query_grads.astype(FLOAT) / eigenvalues[None, :, :]).astype(HALF).transpose(1, 0, 2)
     dma = pltpu.SemaphoreType.DMA((2,))
 
     held = jnp.concatenate(
@@ -378,14 +412,14 @@
 
     o_out, o_in = load(lax.ppermute(grads, "rep", swap), lax.ppermute(acts, "rep", swap))
 
-    def rotate(flag, x, y):
+    def rotate(flags, *pieces):
         both = 2 * rows
         mine, theirs = kernel(
-            functools.partial(shard_body, flag),
+            functools.partial(shard_body, flags),
             [shaped(both, n_tok)] * 2,
             [pltpu.VMEM((2, half, d + ff), HALF), pltpu.VMEM((2, n_tok, rows), FLOAT), pltpu.SemaphoreType.DMA((4, 2))],
             4 * rows * n_tok * (d + ff),
-        )(in_specs=[SMEM, ANY, ANY] + [VMEM] * 4, out_specs=[VMEM] * 2)(at, x, y, t_out, t_in, o_out, o_in)
+        )(in_specs=[SMEM] + [ANY] * len(pieces) + [VMEM] * 4, out_specs=[VMEM] * 2)(at, *pieces, t_out, t_in, o_out, o_in)
         return mine, lax.ppermute(theirs, "rep", swap)
 
     x1 = hop(held, 1)
@@ -394,29 +428,25 @@
     x2 = hop(x1_sent, 2)
     x3 = hop(after(x2, y1), 3)
     y2 = to_group(x2, near)
-    near_done = rotate(4, x1, y1)
+    near_done = rotate([4], x1, y1)
     y3 = to_group(after(x3, y2, near_done[0]), outer)
     y1_inner = to_group(after(x1, y1), inner)
-    middle_done = rotate(4, x2, y2)
-    inner_done = rotate(5, x1, y1_inner)
-    outer_done = rotate(6, x3, after(y3, middle_done[0], inner_done[0]))
-
-    all_rows = n_wide * rows
-    grad, grad_sent, act, act_sent = kernel(
-        slots_body,
-        [shaped(r, n_tok, kind=kind) for r in (all_rows, share) for kind in (FLOAT, HALF)],
-    )(in_specs=[SMEM] + [VMEM] * 10, out_specs=[VMEM] * 4)(
-        at, g_own, a_own, *near_done, *middle_done, *inner_done, *outer_done
-    )
-    grad_came = lax.ppermute(grad_sent, "layer", swap)
-    act_came = lax.ppermute(act_sent, "layer", swap)
+    packed = shaped(4 * rows, n_tok, kind=HALF)
+    early = kernel(early_body, packed)(in_specs=[SMEM] + [VMEM] * 4, out_specs=VMEM)(at, g_own, a_own, *near_done)
+    early = lax.ppermute(early, "layer", swap)
+    both_done = rotate([4, 5], x2, y2, x1, y1_inner)
+    last_done = rotate([6], x3, after(y3, both_done[0], early))
+    late = kernel(late_body, packed)(in_specs=[SMEM] + [VMEM] * 4, out_specs=VMEM)(at, *both_done, *last_done)
+    late = lax.ppermute(late, "layer", swap)
 
     pieces = kernel(
         train_body,
         [shaped(seq_dev, half, share, kind=HALF)] * 8,
-        [pltpu.VMEM((n_wide * rows, share), HALF)],
+        [pltpu.VMEM((n_wide * rows, n_tok), HALF), pltpu.VMEM((share, n_tok), HALF), pltpu.VMEM((n_wide * rows, share), HALF)],
         2 * n_wide * rows * share * n_tok,
-    )(in_specs=[SMEM, SMEM] + [VMEM] * 4, out_specs=[VMEM] * 8)(at, counts, grad, grad_came, act, act_came)
+    )(in_specs=[SMEM, SMEM] + [VMEM] * 10, out_specs=[VMEM] * 8)(
+        at, counts, g_own, a_own, *near_done, *both_done, *last_done, early, late
+    )
     mine, theirs = pieces[:4], pieces[4:]
 
     def send(x, n, cross):
@@ -426,11 +456,12 @@
     same = [mine[0]] + [send(mine[n], n, 0) for n in range(1, n_wide)]
     cross = [send(theirs[n], n, 1) for n in range(n_wide)]
     chip_seqs = 2 * seq_dev
-    train = jnp.stack([jnp.stack([a, b]) for a, b in zip(same, cross, strict=True)])
-    train = train.reshape(n_wide * chip_seqs, half * share)
-    scored = lax.dot_general(weighted, train, (((1,), (1,)), ((), ())), preferred_element_type=FLOAT)
-    scored = scored.reshape(n_query, n_wide, 2, seq_dev)
-    scored = jnp.where(rep == 0, scored, scored[:, :, ::-1]).reshape(n_query, n_wide * chip_seqs)
+    scored = kernel(
+        score_body,
+        shaped(n_query, n_wide * chip_seqs),
+        [pltpu.VMEM((share // 128, n_wide * chip_seqs * half, 128), FLOAT), pltpu.VMEM((n_query, n_wide * chip_seqs), FLOAT)],
+        2 * n_query * n_wide * chip_seqs * half * share,
+    )(in_specs=[SMEM] + [VMEM] * 9, out_specs=VMEM)(at, weighted, *same, *cross)
     return finish(scored, candidate, n_wide, n_layer, chip_seqs)
 
 

time: 147 us -> 139 us (0.946)
  waiting for transfers between devices: 37.1 us -> 33 us
  starting transfers between devices: 80.3 us -> 76.6 us
  matrix products: 2.85 us -> 0 us
  Pallas kernels: 11.7 us -> 14.2 us
  local copies, waits for them, and re-layouts: 12.7 us -> 10.4 us
  other arithmetic: 1.48 us -> 3.77 us
    ppermute x4 -> x3, starting transfers between devices: 45 us -> 38.4 us  [rotate(): return (mine, lax.ppermute(theirs, 'rep', swap))]
    another operation x10 -> x2, local copies, waits for them, and re-layouts: 4.75 us -> 0.18 us  [the longest x1 0.1 us: finish(): part = part.reshape(2 * n_layer, block, n_wide, chip_seqs)]
    ppermute x3, waiting for transfers between devices: 5.61 us -> 1.17 us  [hop(): return lax.ppermute(x, ('wide', 'rep'), hop_pairs(k, n_wide))]
    transpose x0 -> x1, other arithmetic: none -> 2.92 us  [local_fast(): (query_grads.astype(FLOAT) / eigenvalues[None, :, :]).astype(HALF)]
    dot_general x1 -> x0, matrix products: 2.85 us -> none  [local_fast(): lax.dot_general(weighted, train, (((1,), (1,)), ((), ())), preferred_elem...]
    ppermute x4 -> x5, starting transfers between devices: 3.83 us -> 6.17 us  [the longest x3 3.02 us: finish(): total = total + lax.ppermute(given, ('layer', 'rep'), shift)]
    unnamed x34 -> x30, local copies, waits for them, and re-layouts: 6.63 us -> 8.78 us
    ppermute x4 -> x5, waiting for transfers between devices: 16.9 us -> 15.3 us  [the longest x1 9.88 us: local_fast(): late = lax.ppermute(late, 'layer', swap)]
  transfers between devices with their start and end apart: 26 -> 26, of which waited for: 10 -> 12; matrix products, arithmetic and copies ran while one was open for 6% -> 3% of each run, Pallas kernels for 7% -> 7%
where the time goes in v5:
time: 139 us; the launch traced here: 138 us
  starting transfers between devices  76.6 us (55%)
  waiting for transfers between devices  33 us (24%)
  Pallas kernels  14.2 us (10%)
  local copies, waits for them, and re-layouts  10.4 us (7%)
  other arithmetic  3.77 us (3%)
    ppermute x3, starting transfers between devices, rotate(): return (mine, lax.ppermute(theirs, 'rep', swap))  38.4 us
    ppermute x7, starting transfers between devices, send(): return lax.ppermute(x, ('wide', 'rep'), pairs)  13.4 us
    ppermute x1, waiting for transfers between devices, local_fast(): late = lax.ppermute(late, 'layer', swap)  9.88 us
    ppermute x7, waiting for transfers between devices, send(): return lax.ppermute(x, ('wide', 'rep'), pairs)  9.39 us
    unnamed x30, local copies, waits for them, and re-layouts  8.78 us
    ppermute x3, starting transfers between devices, hop(): return lax.ppermute(x, ('wide', 'rep'), hop_pairs(k, n_wide))  8.07 us
    pallas_call x2, Pallas kernels, load(): kernel(load_body, [pltpu.VMEM((n_tok, d), HALF), pltpu.VMEM((n_tok, ff),...  4.98 us
    ppermute x2, waiting for transfers between devices, finish(): lax.ppermute(give, 'wide', [(w, w ^ bit) for w in range(n_wide)])  4.45 us
  transfers between devices with their start and end apart: 26, of which 12 were waited for; matrix products, arithmetic and copies ran while one was open for 3% of the time, Pallas kernels for 7%

profile of v5, /device:TPU:0, one launch (start us, length us, event | category | flops | bytes accessed | tf_op | source)
XLA Modules:
  0.0 138.3 jit_solution(16021114820126523243)
XLA Ops:
  0.0 0.5 collective-permute-start.3
  0.5 1.2 constant_dynamic-slice_fusion.4
  1.7 0.1 pad_maximum_fusion
  1.8 4.7 %collective-permute-start = (bf16[64,9472]{1,0:T(8,128)(2,1)S(1)}, bf16[64,9472]{1,0:T(8,128)(2,1)S(1)}, u32[]{:S(2)}, u32[]{:S(2)}) collective-permute-start(bf16[64,9472]{1,0:T(8,128)(2,1)S(1)} %pad_maximum_fusion), channel_id=1, source_target_pairs={{0,4},{4,8},{8,12},{5,1},{9,5},{13,9},{2,6},{6,10},{10,14},{7,3},{... | collective-permute-start | bytes 3637256 | tf_op jit(solution)/shard_map/ppermute | solution.py:411
  6.5 0.0 copy-start.3
  6.5 2.5 %copy-done.3 = bf16[3,128,6912]{2,1,0:T(8,128)(2,1)S(1)} copy-done((bf16[3,128,6912]{2,1,0:T(8,128)(2,1)S(1)}, bf16[3,128,6912]{2,1,0:T(8,128)(2,1)}, u32[]{:S(2)}) %copy-start.3) | copy-done | bytes 5308440
  9.0 1.7 %shard_map.82 = (bf16[384,2560]{1,0:T(8,128)(2,1)S(1)}, bf16[384,6912]{1,0:T(8,128)(2,1)S(1)}) custom-call(bf16[384,2560]{1,0:T(8,128)(2,1)} %bitcast.9.x_ref, bf16[384,6912]{1,0:T(8,128)(2,1)S(1)} %bitcast.70), custom_call_target="tpu_custom_call" | custom-call | bytes 1024 | tf_op jit(solution)/shard_map/pallas_call | solution.py:393
  10.7 0.3 copy-done.4
  11.1 0.1 copy-done.6
  11.2 2.1 %shard_map.83 = (f32[128,384]{1,0:T(8,128)S(1)}, f32[128,384]{1,0:T(8,128)S(1)}) custom-call(bf16[128,2560]{1,0:T(8,128)(2,1)S(1)} %copy-done.6, bf16[128,6912]{1,0:T(8,128)(2,1)S(1)} %copy-done.4, bf16[384,2560]{1,0:T(8,128)(2,1)S(1)} %get-tuple-element.31.t_out.refs_2_.refs_4_, bf16[384,6912]{1,0:T(8,128)(2,1)S(1)} %get-tuple-element.32.t_in.refs_3_.refs_5_), custom_call_target="tpu_custom_call" | custom-call | flops 931135 | bytes 1024 | tf_op jit(solution)/shard_map/pallas_call | solution.py:398
  13.3 2.4 %copy-done = bf16[384,6912]{1,0:T(8,128)(2,1)} copy-done((bf16[384,6912]{1,0:T(8,128)(2,1)}, bf16[384,6912]{1,0:T(8,128)(2,1)S(1)}, u32[]{:S(2)}) %copy-start) | copy-done | bytes 5308440
  15.7 0.7 copy-done.9
  16.4 2.9 %fusion.weights = bf16[64,64,256]{2,1,0:T(8,128)(2,1)} fusion(bf16[64,64,256]{2,1,0:T(8,128)(2,1)S(1)} %copy-done.12, f32[64,256]{1,0:T(8,128)S(1)} %copy-done.13), kind=kLoop, calls=%fused_computation.1 | loop fusion | flops 3145728 | bytes 4259840 | tf_op jit(solution)/shard_map/transpose | solution.py:385
  19.3 1.2 collective-permute-done.refs_0_.refs_2_
  20.5 0.7 collective-permute-start.1
  21.2 1.7 %collective-permute-start.5 = (bf16[64,9472]{1,0:T(8,128)(2,1)S(1)}, bf16[64,9472]{1,0:T(8,128)(2,1)}, u32[]{:S(2)}, u32[]{:S(2)}) collective-permute-start(bf16[64,9472]{1,0:T(8,128)(2,1)S(1)} %collective-permute-done.refs_0_.refs_2_), channel_id=1, source_target_pairs={{4,8},{8,12},{5,1},{9,5},{6,10},{10,14},{7,3},{11,7},{20,24},{24,2... | collective-permute-start | bytes 3637256 | tf_op jit(solution)/shard_map/ppermute | solution.py:411
  22.9 2.2 %collective-permute-start.2 = (bf16[3,128,2560]{2,1,0:T(8,128)(2,1)}, bf16[3,128,2560]{2,1,0:T(8,128)(2,1)}, u32[]{:S(2)}, u32[]{:S(2)}) collective-permute-start(bf16[3,128,2560]{2,1,0:T(8,128)(2,1)} %param.9), channel_id=1, source_target_pairs={{0,1},{1,0},{2,3},{3,2},{4,5},{5,4},{6,7},{7,6},{8,9},{9,8},{10,11... | collective-permute-start | bytes 5898248 | tf_op jit(solution)/shard_map/ppermute | solution.py:413
  25.1 1.0 copy-done.7
  26.2 1.7 %collective-permute-start.9 = (bf16[64,9472]{1,0:T(8,128)(2,1)}, bf16[64,9472]{1,0:T(8,128)(2,1)}, u32[]{:S(2)}, u32[]{:S(2)}) collective-permute-start(bf16[64,9472]{1,0:T(8,128)(2,1)} %collective-permute-done.5.refs_0_), channel_id=1, source_target_pairs={{8,12},{5,1},{10,14},{7,3},{24,28},{21,17},{26,30},{23,19}} | collective-permute-start | bytes 3637256 | tf_op jit(solution)/shard_map/ppermute | solution.py:411
  27.9 1.7 %collective-permute-start.6 = (bf16[64,9472]{1,0:T(8,128)(2,1)}, bf16[64,9472]{1,0:T(8,128)(2,1)}, u32[]{:S(2)}, u32[]{:S(2)}) collective-permute-start(bf16[64,9472]{1,0:T(8,128)(2,1)} %collective-permute-done.5.refs_0_), channel_id=1, source_target_pairs={{1,17},{5,21},{8,24},{12,28},{17,1},{21,5},{24,8},{28,12},{3,19},{... | collective-permute-start | bytes 3637256 | tf_op jit(solution)/shard_map/ppermute | solution.py:408
  29.6 0.1 stack.51.at
  29.7 0.7 collective-permute-start.7
  30.5 3.3 %shard_map.84 = (bf16[384,2560]{1,0:T(8,128)(2,1)S(1)}, bf16[384,6912]{1,0:T(8,128)(2,1)S(1)}) custom-call(bf16[384,2560]{1,0:T(8,128)(2,1)} %bitcast.11.x_ref, bf16[384,6912]{1,0:T(8,128)(2,1)} %bitcast.12.y_ref), custom_call_target="tpu_custom_call" | custom-call | bytes 1024 | tf_op jit(solution)/shard_map/pallas_call | solution.py:393
  33.7 1.3 copy-done.1
  35.1 0.4 copy-done.8
  35.4 0.6 shard_map.85
  36.1 0.7 collective-permute-start.10
  36.8 25.6 %collective-permute-start.4 = (f32[256,384]{1,0:T(8,128)S(1)}, f32[256,384]{1,0:T(8,128)S(1)}, u32[]{:S(2)}, u32[]{:S(2)}) collective-permute-start(f32[256,384]{1,0:T(8,128)S(1)} %get-tuple-element.39), channel_id=1, source_target_pairs={{0,1},{1,0},{2,3},{3,2},{4,5},{5,4},{6,7},{7,6},{8,9},{9,8},{10,11... | collective-permute-start | bytes 1179656 | tf_op jit(solution)/shard_map/ppermute | solution.py:423
  62.4 1.3 collective-permute-done.4.near_far
  63.8 0.6 shard_map.87
  64.4 1.6 %collective-permute-start.11 = (bf16[512,384]{1,0:T(8,128)(2,1)S(1)}, bf16[512,384]{1,0:T(8,128)(2,1)S(1)}, u32[]{:S(2)}, u32[]{:S(2)}) collective-permute-start(bf16[512,384]{1,0:T(8,128)(2,1)S(1)} %shard_map.87), channel_id=1, source_target_pairs={{0,2},{2,0},{1,3},{3,1},{4,6},{6,4},{5,7},{7,5},{8,10},{10,8},{9,1... | collective-permute-start | bytes 1179656 | tf_op jit(solution)/shard_map/ppermute | solution.py:436
  65.9 0.6 shard_map.86
  66.6 5.5 %collective-permute-start.8 = (f32[256,384]{1,0:T(8,128)S(1)}, f32[256,384]{1,0:T(8,128)S(1)}, u32[]{:S(2)}, u32[]{:S(2)}) collective-permute-start(f32[256,384]{1,0:T(8,128)S(1)} %get-tuple-element.43), channel_id=1, source_target_pairs={{0,1},{1,0},{2,3},{3,2},{4,5},{5,4},{6,7},{7,6},{8,9},{9,8},{10,11... | collective-permute-start | bytes 1179656 | tf_op jit(solution)/shard_map/ppermute | solution.py:423
  72.1 3.7 %collective-permute-done.11.early = bf16[512,384]{1,0:T(8,128)(2,1)S(1)} collective-permute-done((bf16[512,384]{1,0:T(8,128)(2,1)S(1)}, bf16[512,384]{1,0:T(8,128)(2,1)S(1)}, u32[]{:S(2)}, u32[]{:S(2)}) %collective-permute-start.11) | collective-permute-done | bytes 393248 | tf_op jit(solution)/shard_map/ppermute | solution.py:436
  75.8 0.6 shard_map.88
  76.5 0.0 copy-start.11
  76.5 7.3 %collective-permute-start.12 = (f32[256,384]{1,0:T(8,128)S(1)}, f32[256,384]{1,0:T(8,128)S(1)}, u32[]{:S(2)}, u32[]{:S(2)}) collective-permute-start(f32[256,384]{1,0:T(8,128)S(1)} %get-tuple-element.48), channel_id=1, source_target_pairs={{0,1},{1,0},{2,3},{3,2},{4,5},{5,4},{6,7},{7,6},{8,9},{9,8},{10,11... | collective-permute-start | bytes 1179656 | tf_op jit(solution)/shard_map/ppermute | solution.py:423
  83.7 1.3 collective-permute-done.12.last_far
  85.1 0.6 shard_map.89
  85.7 1.6 %collective-permute-start.13 = (bf16[512,384]{1,0:T(8,128)(2,1)S(1)}, bf16[512,384]{1,0:T(8,128)(2,1)S(1)}, u32[]{:S(2)}, u32[]{:S(2)}) collective-permute-start(bf16[512,384]{1,0:T(8,128)(2,1)S(1)} %shard_map.89), channel_id=1, source_target_pairs={{0,2},{2,0},{1,3},{3,1},{4,6},{6,4},{5,7},{7,5},{8,10},{10,8},{9,1... | collective-permute-start | bytes 1179656 | tf_op jit(solution)/shard_map/ppermute | solution.py:440
  87.3 9.9 %collective-permute-done.13.late = bf16[512,384]{1,0:T(8,128)(2,1)S(1)} collective-permute-done((bf16[512,384]{1,0:T(8,128)(2,1)S(1)}, bf16[512,384]{1,0:T(8,128)(2,1)S(1)}, u32[]{:S(2)}, u32[]{:S(2)}) %collective-permute-start.13) | collective-permute-done | bytes 393248 | tf_op jit(solution)/shard_map/ppermute | solution.py:440
  97.2 2.0 %shard_map.90 = (bf16[3,64,256]{2,1,0:T(8,128)(2,1)S(1)}, bf16[3,64,256]{2,1,0:T(8,128)(2,1)S(1)}, bf16[3,64,256]{2,1,0:T(8,128)(2,1)S(1)}, bf16[3,64,256]{2,1,0...) custom-call(s32[8]{0:T(128)S(1)} %stack.51.at, ...), custom_call_target="tpu_custom_call" | custom-call | flops 100663 | bytes 1024 | tf_op jit(solution)/shard_map/pallas_call | solution.py:442
  99.2 5.9 %collective-permute-start.14 = (bf16[3,64,256]{2,1,0:T(8,128)(2,1)S(1)}, bf16[3,64,256]{2,1,0:T(8,128)(2,1)S(1)}, u32[]{:S(2)}, u32[]{:S(2)}) collective-permute-start(bf16[3,64,256]{2,1,0:T(8,128)(2,1)S(1)} %get-tuple-element.50), channel_id=1, source_target_pairs={{0,4},{1,5},{4,8},{5,9},{8,12},{9,13},{12,0},{13,1},{2,6},{3,7},{6... | collective-permute-start | bytes 294920 | tf_op jit(solution)/shard_map/ppermute | solution.py:454
  105.0 2.8 %collective-permute-start.15 = (bf16[3,64,256]{2,1,0:T(8,128)(2,1)S(1)}, bf16[3,64,256]{2,1,0:T(8,128)(2,1)S(1)}, u32[]{:S(2)}, u32[]{:S(2)}) collective-permute-start(bf16[3,64,256]{2,1,0:T(8,128)(2,1)S(1)} %get-tuple-element.51), channel_id=1, source_target_pairs={{0,8},{1,9},{4,12},{5,13},{8,0},{9,1},{12,4},{13,5},{2,10},{3,11},... | collective-permute-start | bytes 294920 | tf_op jit(solution)/shard_map/ppermute | solution.py:454
  107.8 2.0 %collective-permute-start.16 = (bf16[3,64,256]{2,1,0:T(8,128)(2,1)}, bf16[3,64,256]{2,1,0:T(8,128)(2,1)S(1)}, u32[]{:S(2)}, u32[]{:S(2)}) collective-permute-start(bf16[3,64,256]{2,1,0:T(8,128)(2,1)} %get-tuple-element.52), channel_id=1, source_target_pairs={{0,12},{1,13},{4,0},{5,1},{8,4},{9,5},{12,8},{13,9},{2,14},{3,15},... | collective-permute-start | bytes 294920 | tf_op jit(solution)/shard_map/ppermute | solution.py:454
  109.8 0.1 collective-permute-start.18
  109.9 0.3 collective-permute-done.14.refs_1_
  110.3 3.7 %collective-permute-done.15.refs_2_ = bf16[3,64,256]{2,1,0:T(8,128)(2,1)S(1)} collective-permute-done((bf16[3,64,256]{2,1,0:T(8,128)(2,1)S(1)}, bf16[3,64,256]{2,1,0:T(8,128)(2,1)S(1)}, u32[]{:S(2)}, u32[]{:S(2)}) %collective-permute-start.15) | collective-permute-done | bytes 98336 | tf_op jit(solution)/shard_map/ppermute | solution.py:454
  114.0 2.6 %collective-permute-start.20 = (bf16[3,64,256]{2,1,0:T(8,128)(2,1)S(1)}, bf16[3,64,256]{2,1,0:T(8,128)(2,1)S(1)}, u32[]{:S(2)}, u32[]{:S(2)}) collective-permute-start(bf16[3,64,256]{2,1,0:T(8,128)(2,1)S(1)} %get-tuple-element.56), channel_id=1, source_target_pairs={{0,13},{1,12},{4,1},{5,0},{8,5},{9,4},{12,9},{13,8},{2,15},{3,14},... | collective-permute-start | bytes 294920 | tf_op jit(solution)/shard_map/ppermute | solution.py:454
  116.6 5.3 %collective-permute-done.19.refs_6_ = bf16[3,64,256]{2,1,0:T(8,128)(2,1)S(1)} collective-permute-done((bf16[3,64,256]{2,1,0:T(8,128)(2,1)S(1)}, bf16[3,64,256]{2,1,0:T(8,128)(2,1)S(1)}, u32[]{:S(2)}, u32[]{:S(2)}) %collective-permute-start.19) | collective-permute-done | bytes 98336 | tf_op jit(solution)/shard_map/ppermute | solution.py:454
  121.9 2.0 %shard_map.91 = f32[64,24]{1,0:T(8,128)S(1)} custom-call(s32[8]{0:T(128)S(1)} %stack.51.at, bf16[64,64,256]{2,1,0:T(8,128)(2,1)S(1)} %copy-done.2, bf16[3,64,256]{2,1,0:T(8,128)(2,1)S(1)} %get-tuple-element.49.refs_0_, bf16[3,64,256]{2,1,0:T(8,128)(2,1)S(1)} %collective-permute-done.14.refs_1_, bf16[3,64,256]{2,1,0:T(8,128)(2,1)S(1)} %collective-permute-done.15.refs_2_, ...), custom_call_target="tpu_custom_call" | custom-call | flops 50331 | bytes 1024 | tf_op jit(solution)/shard_map/pallas_call | solution.py:459
  123.9 0.1 copy.17
  124.0 0.1 reshape_reshape.3
  124.1 0.1 constant_dynamic-slice_fusion.3
  124.2 1.0 collective-permute-start.21
  125.2 1.5 %collective-permute-start.22 = (f32[16,4,6]{0,1,2:T(4,128)S(1)}, f32[16,4,6]{0,1,2:T(4,128)S(1)}, u32[]{:S(2)}, u32[]{:S(2)}) collective-permute-start(f32[16,4,6]{0,1,2:T(4,128)S(1)} %bitcast.74), channel_id=1, source_target_pairs={{0,2},{1,3},{2,0},{3,1},{4,6},{5,7},{6,4},{7,5},{8,10},{9,11},{10,... | collective-permute-start | bytes 4616 | tf_op jit(solution)/shard_map/ppermute | solution.py:63
  126.7 0.5 collective-permute-start.23
  127.2 0.5 collective-permute-done.21
  127.7 1.2 collective-permute-done.22
  129.0 1.7 %collective-permute-start.24 = (f32[16,2,6]{0,1,2:T(2,128)S(1)}, f32[16,2,6]{0,1,2:T(2,128)S(1)}, u32[]{:S(2)}, u32[]{:S(2)}) collective-permute-start(f32[16,2,6]{0,1,2:T(2,128)S(1)} %fusion.6), channel_id=1, source_target_pairs={{0,8},{4,12},{8,0},{12,4},{1,9},{5,13},{9,1},{13,5},{2,10},{6,14},... | collective-permute-start | bytes 2312 | tf_op jit(solution)/shard_map/ppermute | solution.py:74
  130.7 2.9 %collective-permute-done.24 = f32[16,2,6]{0,1,2:T(2,128)S(1)} collective-permute-done((f32[16,2,6]{0,1,2:T(2,128)S(1)}, f32[16,2,6]{0,1,2:T(2,128)S(1)}, u32[]{:S(2)}, u32[]{:S(2)}) %collective-permute-start.24) | collective-permute-done | bytes 800 | tf_op jit(solution)/shard_map/ppermute | solution.py:74
  133.7 2.4 %collective-permute-start.25 = (f32[16,1,6]{0,1,2:T(1,128)S(1)}, f32[16,1,6]{0,1,2:T(1,128)S(1)}, u32[]{:S(2)}, u32[]{:S(2)}) collective-permute-start(f32[16,1,6]{0,1,2:T(1,128)S(1)} %fusion.12), channel_id=1, source_target_pairs={{0,4},{4,0},{8,12},{12,8},{1,5},{5,1},{9,13},{13,9},{2,6},{6,2},{1... | collective-permute-start | bytes 1160 | tf_op jit(solution)/shard_map/ppermute | solution.py:74
  136.1 1.6 %collective-permute-done.25 = f32[16,1,6]{0,1,2:T(1,128)S(1)} collective-permute-done((f32[16,1,6]{0,1,2:T(1,128)S(1)}, f32[16,1,6]{0,1,2:T(1,128)S(1)}, u32[]{:S(2)}, u32[]{:S(2)}) %collective-permute-start.25) | collective-permute-done | bytes 416 | tf_op jit(solution)/shard_map/ppermute | solution.py:74
  137.6 0.7 bitcast_multiply_fusion
  (51 shorter events, 0.3 us)
Async XLA Ops:
  0.0 1.7 %copy-start.5 = (bf16[128,2560]{1,0:T(8,128)(2,1)S(1)}, bf16[128,2560]{1,0:T(8,128)(2,1)}, u32[]{:S(2)}) copy-start(bf16[128,2560]{1,0:T(8,128)(2,1)} %b_out.1) | copy-start | bytes 1966084
  0.0 30.4 %collective-permute-start.3 = (bf16[3,128,6912]{2,1,0:T(8,128)(2,1)}, bf16[3,128,6912]{2,1,0:T(8,128)(2,1)}, u32[]{:S(2)}, u32[]{:S(2)}) collective-permute-start(bf16[3,128,6912]{2,1,0:T(8,128)(2,1)} %param.8), channel_id=1, source_target_pairs={{0,1},{1,0},{2,3},{3,2},{4,5},{5,4},{6,7},{7,6},{8,9},{9,8},{10,11... | collective-permute-start | bytes 15925256 | tf_op jit(solution)/shard_map/ppermute | solution.py:413
  1.8 18.6 %collective-permute-start = (bf16[64,9472]{1,0:T(8,128)(2,1)S(1)}, bf16[64,9472]{1,0:T(8,128)(2,1)S(1)}, u32[]{:S(2)}, u32[]{:S(2)}) collective-permute-start(bf16[64,9472]{1,0:T(8,128)(2,1)S(1)} %pad_maximum_fusion), channel_id=1, source_target_pairs={{0,4},{4,8},{8,12},{5,1},{9,5},{13,9},{2,6},{6,10},{10,14},{7,3},{... | collective-permute-start | bytes 3637256 | tf_op jit(solution)/shard_map/ppermute | solution.py:411
  6.5 2.5 %copy-start.3 = (bf16[3,128,6912]{2,1,0:T(8,128)(2,1)S(1)}, bf16[3,128,6912]{2,1,0:T(8,128)(2,1)}, u32[]{:S(2)}) copy-start(bf16[3,128,6912]{2,1,0:T(8,128)(2,1)} %param.8) | copy-start | bytes 15925252
  9.0 2.1 %copy-start.4 = (bf16[128,6912]{1,0:T(8,128)(2,1)S(1)}, bf16[128,6912]{1,0:T(8,128)(2,1)}, u32[]{:S(2)}) copy-start(bf16[128,6912]{1,0:T(8,128)(2,1)} %b_in.1) | copy-start | bytes 5308420
  9.0 2.2 %copy-start.6 = (bf16[128,2560]{1,0:T(8,128)(2,1)S(1)}, bf16[128,2560]{1,0:T(8,128)(2,1)}, u32[]{:S(2)}) copy-start(bf16[128,2560]{1,0:T(8,128)(2,1)} %b_out.1) | copy-start | bytes 1966084
  11.2 5.2 %copy-start.12 = (bf16[64,64,256]{2,1,0:T(8,128)(2,1)S(1)}, bf16[64,64,256]{2,1,0:T(8,128)(2,1)}, u32[]{:S(2)}) copy-start(bf16[64,64,256]{2,1,0:T(8,128)(2,1)} %param.13) | copy-start | bytes 6291460
  11.2 5.2 %copy-start.13 = (f32[64,256]{1,0:T(8,128)S(1)}, f32[64,256]{1,0:T(8,128)}, u32[]{:S(2)}) copy-start(f32[64,256]{1,0:T(8,128)} %param.14) | copy-start | bytes 196612
  13.3 2.4 %copy-start = (bf16[384,6912]{1,0:T(8,128)(2,1)}, bf16[384,6912]{1,0:T(8,128)(2,1)S(1)}, u32[]{:S(2)}) copy-start(bf16[384,6912]{1,0:T(8,128)(2,1)S(1)} %get-tuple-element.32.t_in.refs_3_.refs_5_) | copy-start | bytes 15925252
  15.7 0.7 copy-start.9
  20.5 4.7 %collective-permute-start.1 = (bf16[64,9472]{1,0:T(8,128)(2,1)S(1)}, bf16[64,9472]{1,0:T(8,128)(2,1)S(1)}, u32[]{:S(2)}, u32[]{:S(2)}) collective-permute-start(bf16[64,9472]{1,0:T(8,128)(2,1)S(1)} %collective-permute-done.refs_0_.refs_2_), channel_id=1, source_target_pairs={{1,17},{5,21},{8,24},{12,28},{17,1},{21,5},{24,8},{28,12},{3,19},{... | collective-permute-start | bytes 3637256 | tf_op jit(solution)/shard_map/ppermute | solution.py:408
  21.2 5.0 %collective-permute-start.5 = (bf16[64,9472]{1,0:T(8,128)(2,1)S(1)}, bf16[64,9472]{1,0:T(8,128)(2,1)}, u32[]{:S(2)}, u32[]{:S(2)}) collective-permute-start(bf16[64,9472]{1,0:T(8,128)(2,1)S(1)} %collective-permute-done.refs_0_.refs_2_), channel_id=1, source_target_pairs={{4,8},{8,12},{5,1},{9,5},{6,10},{10,14},{7,3},{11,7},{20,24},{24,2... | collective-permute-start | bytes 3637256 | tf_op jit(solution)/shard_map/ppermute | solution.py:411
  22.9 7.5 %collective-permute-start.2 = (bf16[3,128,2560]{2,1,0:T(8,128)(2,1)}, bf16[3,128,2560]{2,1,0:T(8,128)(2,1)}, u32[]{:S(2)}, u32[]{:S(2)}) collective-permute-start(bf16[3,128,2560]{2,1,0:T(8,128)(2,1)} %param.9), channel_id=1, source_target_pairs={{0,1},{1,0},{2,3},{3,2},{4,5},{5,4},{6,7},{7,6},{8,9},{9,8},{10,11... | collective-permute-start | bytes 5898248 | tf_op jit(solution)/shard_map/ppermute | solution.py:413
  25.1 1.1 copy-start.7
  26.2 9.8 %collective-permute-start.9 = (bf16[64,9472]{1,0:T(8,128)(2,1)}, bf16[64,9472]{1,0:T(8,128)(2,1)}, u32[]{:S(2)}, u32[]{:S(2)}) collective-permute-start(bf16[64,9472]{1,0:T(8,128)(2,1)} %collective-permute-done.5.refs_0_), channel_id=1, source_target_pairs={{8,12},{5,1},{10,14},{7,3},{24,28},{21,17},{26,30},{23,19}} | collective-permute-start | bytes 3637256 | tf_op jit(solution)/shard_map/ppermute | solution.py:411
  27.9 8.2 %collective-permute-start.6 = (bf16[64,9472]{1,0:T(8,128)(2,1)}, bf16[64,9472]{1,0:T(8,128)(2,1)}, u32[]{:S(2)}, u32[]{:S(2)}) collective-permute-start(bf16[64,9472]{1,0:T(8,128)(2,1)} %collective-permute-done.5.refs_0_), channel_id=1, source_target_pairs={{1,17},{5,21},{8,24},{12,28},{17,1},{21,5},{24,8},{28,12},{3,19},{... | collective-permute-start | bytes 3637256 | tf_op jit(solution)/shard_map/ppermute | solution.py:408
  29.7 36.2 %collective-permute-start.7 = (bf16[64,9472]{1,0:T(8,128)(2,1)S(1)}, bf16[64,9472]{1,0:T(8,128)(2,1)S(1)}, u32[]{:S(2)}, u32[]{:S(2)}) collective-permute-start(bf16[64,9472]{1,0:T(8,128)(2,1)S(1)} %collective-permute-done.refs_0_.refs_2_), channel_id=1, source_target_pairs={{4,20},{9,25},{20,4},{25,9},{6,22},{11,27},{22,6},{27,11}} | collective-permute-start | bytes 3637256 | tf_op jit(solution)/shard_map/ppermute | solution.py:408
  30.4 4.6 %copy-start.1 = (bf16[384,6912]{1,0:T(8,128)(2,1)S(1)}, bf16[384,6912]{1,0:T(8,128)(2,1)}, u32[]{:S(2)}) copy-start(bf16[384,6912]{1,0:T(8,128)(2,1)} %copy-done) | copy-start | bytes 15925252
  30.5 4.9 %copy-start.8 = (bf16[64,9472]{1,0:T(8,128)(2,1)S(1)}, bf16[64,9472]{1,0:T(8,128)(2,1)}, u32[]{:S(2)}) copy-start(bf16[64,9472]{1,0:T(8,128)(2,1)} %copy-done.7) | copy-start | bytes 3637252
  35.4 28.4 %copy-start.10 = (f32[128,384]{1,0:T(8,128)S(1)}, f32[128,384]{1,0:T(8,128)}, u32[]{:S(2)}) copy-start(f32[128,384]{1,0:T(8,128)} %copy-done.9) | copy-start | bytes 589828
  36.1 39.8 %collective-permute-start.10 = (bf16[64,9472]{1,0:T(8,128)(2,1)}, bf16[64,9472]{1,0:T(8,128)(2,1)S(1)}, u32[]{:S(2)}, u32[]{:S(2)}) collective-permute-start(bf16[64,9472]{1,0:T(8,128)(2,1)} %collective-permute-done.9.refs_0_), channel_id=1, source_target_pairs={{1,17},{12,28},{17,1},{28,12},{3,19},{14,30},{19,3},{30,14}} | collective-permute-start | bytes 3637256 | tf_op jit(solution)/shard_map/ppermute | solution.py:408
  36.8 27.0 %collective-permute-start.4 = (f32[256,384]{1,0:T(8,128)S(1)}, f32[256,384]{1,0:T(8,128)S(1)}, u32[]{:S(2)}, u32[]{:S(2)}) collective-permute-start(f32[256,384]{1,0:T(8,128)S(1)} %get-tuple-element.39), channel_id=1, source_target_pairs={{0,1},{1,0},{2,3},{3,2},{4,5},{5,4},{6,7},{7,6},{8,9},{9,8},{10,11... | collective-permute-start | bytes 1179656 | tf_op jit(solution)/shard_map/ppermute | solution.py:423
  64.4 11.5 %collective-permute-start.11 = (bf16[512,384]{1,0:T(8,128)(2,1)S(1)}, bf16[512,384]{1,0:T(8,128)(2,1)S(1)}, u32[]{:S(2)}, u32[]{:S(2)}) collective-permute-start(bf16[512,384]{1,0:T(8,128)(2,1)S(1)} %shard_map.87), channel_id=1, source_target_pairs={{0,2},{2,0},{1,3},{3,1},{4,6},{6,4},{5,7},{7,5},{8,10},{10,8},{9,1... | collective-permute-start | bytes 1179656 | tf_op jit(solution)/shard_map/ppermute | solution.py:436
  66.6 17.2 %collective-permute-start.8 = (f32[256,384]{1,0:T(8,128)S(1)}, f32[256,384]{1,0:T(8,128)S(1)}, u32[]{:S(2)}, u32[]{:S(2)}) collective-permute-start(f32[256,384]{1,0:T(8,128)S(1)} %get-tuple-element.43), channel_id=1, source_target_pairs={{0,1},{1,0},{2,3},{3,2},{4,5},{5,4},{6,7},{7,6},{8,9},{9,8},{10,11... | collective-permute-start | bytes 1179656 | tf_op jit(solution)/shard_map/ppermute | solution.py:423
  76.5 20.7 %copy-start.11 = (s32[3]{0:T(128)S(1)}, s32[3]{0:T(128)}, u32[]{:S(2)}) copy-start(s32[3]{0:T(128)} %counts.1) | copy-start | bytes 40
  76.5 8.6 %collective-permute-start.12 = (f32[256,384]{1,0:T(8,128)S(1)}, f32[256,384]{1,0:T(8,128)S(1)}, u32[]{:S(2)}, u32[]{:S(2)}) collective-permute-start(f32[256,384]{1,0:T(8,128)S(1)} %get-tuple-element.48), channel_id=1, source_target_pairs={{0,1},{1,0},{2,3},{3,2},{4,5},{5,4},{6,7},{7,6},{8,9},{9,8},{10,11... | collective-permute-start | bytes 1179656 | tf_op jit(solution)/shard_map/ppermute | solution.py:423
  85.7 36.2 %copy-start.2 = (bf16[64,64,256]{2,1,0:T(8,128)(2,1)S(1)}, bf16[64,64,256]{2,1,0:T(8,128)(2,1)}, u32[]{:S(2)}) copy-start(bf16[64,64,256]{2,1,0:T(8,128)(2,1)} %fusion.weights) | copy-start | bytes 6291460
  85.7 11.5 %collective-permute-start.13 = (bf16[512,384]{1,0:T(8,128)(2,1)S(1)}, bf16[512,384]{1,0:T(8,128)(2,1)S(1)}, u32[]{:S(2)}, u32[]{:S(2)}) collective-permute-start(bf16[512,384]{1,0:T(8,128)(2,1)S(1)} %shard_map.89), channel_id=1, source_target_pairs={{0,2},{2,0},{1,3},{3,1},{4,6},{6,4},{5,7},{7,5},{8,10},{10,8},{9,1... | collective-permute-start | bytes 1179656 | tf_op jit(solution)/shard_map/ppermute | solution.py:440
  99.2 31.6 %copy-start.14 = (s32[16,1]{0,1:T(1,128)S(1)}, s32[16,1]{0,1:T(1,128)}, u32[]{:S(2)}) copy-start(s32[16,1]{0,1:T(1,128)} %param.15) | copy-start | bytes 196
  99.2 11.1 %collective-permute-start.14 = (bf16[3,64,256]{2,1,0:T(8,128)(2,1)S(1)}, bf16[3,64,256]{2,1,0:T(8,128)(2,1)S(1)}, u32[]{:S(2)}, u32[]{:S(2)}) collective-permute-start(bf16[3,64,256]{2,1,0:T(8,128)(2,1)S(1)} %get-tuple-element.50), channel_id=1, source_target_pairs={{0,4},{1,5},{4,8},{5,9},{8,12},{9,13},{12,0},{13,1},{2,6},{3,7},{6... | collective-permute-start | bytes 294920 | tf_op jit(solution)/shard_map/ppermute | solution.py:454
  105.0 9.0 %collective-permute-start.15 = (bf16[3,64,256]{2,1,0:T(8,128)(2,1)S(1)}, bf16[3,64,256]{2,1,0:T(8,128)(2,1)S(1)}, u32[]{:S(2)}, u32[]{:S(2)}) collective-permute-start(bf16[3,64,256]{2,1,0:T(8,128)(2,1)S(1)} %get-tuple-element.51), channel_id=1, source_target_pairs={{0,8},{1,9},{4,12},{5,13},{8,0},{9,1},{12,4},{13,5},{2,10},{3,11},... | collective-permute-start | bytes 294920 | tf_op jit(solution)/shard_map/ppermute | solution.py:454
  107.8 8.8 %collective-permute-start.16 = (bf16[3,64,256]{2,1,0:T(8,128)(2,1)}, bf16[3,64,256]{2,1,0:T(8,128)(2,1)S(1)}, u32[]{:S(2)}, u32[]{:S(2)}) collective-permute-start(bf16[3,64,256]{2,1,0:T(8,128)(2,1)} %get-tuple-element.52), channel_id=1, source_target_pairs={{0,12},{1,13},{4,0},{5,1},{8,4},{9,5},{12,8},{13,9},{2,14},{3,15},... | collective-permute-start | bytes 294920 | tf_op jit(solution)/shard_map/ppermute | solution.py:454
  109.8 6.8 %collective-permute-start.17 = (bf16[3,64,256]{2,1,0:T(8,128)(2,1)}, bf16[3,64,256]{2,1,0:T(8,128)(2,1)S(1)}, u32[]{:S(2)}, u32[]{:S(2)}) collective-permute-start(bf16[3,64,256]{2,1,0:T(8,128)(2,1)} %get-tuple-element.53), channel_id=1, source_target_pairs={{0,1},{1,0},{4,5},{5,4},{8,9},{9,8},{12,13},{13,12},{2,3},{3,2},{6... | collective-permute-start | bytes 294920 | tf_op jit(solution)/shard_map/ppermute | solution.py:454
  109.8 6.8 %collective-permute-start.18 = (bf16[3,64,256]{2,1,0:T(8,128)(2,1)S(1)}, bf16[3,64,256]{2,1,0:T(8,128)(2,1)S(1)}, u32[]{:S(2)}, u32[]{:S(2)}) collective-permute-start(bf16[3,64,256]{2,1,0:T(8,128)(2,1)S(1)} %get-tuple-element.54), channel_id=1, source_target_pairs={{0,5},{1,4},{4,9},{5,8},{8,13},{9,12},{12,1},{13,0},{2,7},{3,6},{6... | collective-permute-start | bytes 294920 | tf_op jit(solution)/shard_map/ppermute | solution.py:454
  110.3 11.6 %collective-permute-start.19 = (bf16[3,64,256]{2,1,0:T(8,128)(2,1)S(1)}, bf16[3,64,256]{2,1,0:T(8,128)(2,1)S(1)}, u32[]{:S(2)}, u32[]{:S(2)}) collective-permute-start(bf16[3,64,256]{2,1,0:T(8,128)(2,1)S(1)} %get-tuple-element.55), channel_id=1, source_target_pairs={{0,9},{1,8},{4,13},{5,12},{8,1},{9,0},{12,5},{13,4},{2,11},{3,10},... | collective-permute-start | bytes 294920 | tf_op jit(solution)/shard_map/ppermute | solution.py:454
  114.0 7.9 %collective-permute-start.20 = (bf16[3,64,256]{2,1,0:T(8,128)(2,1)S(1)}, bf16[3,64,256]{2,1,0:T(8,128)(2,1)S(1)}, u32[]{:S(2)}, u32[]{:S(2)}) collective-permute-start(bf16[3,64,256]{2,1,0:T(8,128)(2,1)S(1)} %get-tuple-element.56), channel_id=1, source_target_pairs={{0,13},{1,12},{4,1},{5,0},{8,5},{9,4},{12,9},{13,8},{2,15},{3,14},... | collective-permute-start | bytes 294920 | tf_op jit(solution)/shard_map/ppermute | solution.py:454
  124.2 3.5 %collective-permute-start.21 = (f32[16,4,6]{0,1,2:T(4,128)S(1)}, f32[16,4,6]{0,1,2:T(4,128)S(1)}, u32[]{:S(2)}, u32[]{:S(2)}) collective-permute-start(f32[16,4,6]{0,1,2:T(4,128)S(1)} %bitcast.75), channel_id=1, source_target_pairs={{0,1},{1,2},{2,3},{3,0},{4,5},{5,6},{6,7},{7,4},{8,9},{9,10},{10,1... | collective-permute-start | bytes 4616 | tf_op jit(solution)/shard_map/ppermute | solution.py:63
  125.2 3.7 %collective-permute-start.22 = (f32[16,4,6]{0,1,2:T(4,128)S(1)}, f32[16,4,6]{0,1,2:T(4,128)S(1)}, u32[]{:S(2)}, u32[]{:S(2)}) collective-permute-start(f32[16,4,6]{0,1,2:T(4,128)S(1)} %bitcast.74), channel_id=1, source_target_pairs={{0,2},{1,3},{2,0},{3,1},{4,6},{5,7},{6,4},{7,5},{8,10},{9,11},{10,... | collective-permute-start | bytes 4616 | tf_op jit(solution)/shard_map/ppermute | solution.py:63
  126.7 2.2 %collective-permute-start.23 = (f32[16,4,6]{0,1,2:T(4,128)S(1)}, f32[16,4,6]{0,1,2:T(4,128)S(1)}, u32[]{:S(2)}, u32[]{:S(2)}) collective-permute-start(f32[16,4,6]{0,1,2:T(4,128)S(1)} %bitcast.73), channel_id=1, source_target_pairs={{0,3},{1,0},{2,1},{3,2},{4,7},{5,4},{6,5},{7,6},{8,11},{9,8},{10,9... | collective-permute-start | bytes 4616 | tf_op jit(solution)/shard_map/ppermute | solution.py:63
  129.0 4.6 %collective-permute-start.24 = (f32[16,2,6]{0,1,2:T(2,128)S(1)}, f32[16,2,6]{0,1,2:T(2,128)S(1)}, u32[]{:S(2)}, u32[]{:S(2)}) collective-permute-start(f32[16,2,6]{0,1,2:T(2,128)S(1)} %fusion.6), channel_id=1, source_target_pairs={{0,8},{4,12},{8,0},{12,4},{1,9},{5,13},{9,1},{13,5},{2,10},{6,14},... | collective-permute-start | bytes 2312 | tf_op jit(solution)/shard_map/ppermute | solution.py:74
  133.7 4.0 %collective-permute-start.25 = (f32[16,1,6]{0,1,2:T(1,128)S(1)}, f32[16,1,6]{0,1,2:T(1,128)S(1)}, u32[]{:S(2)}, u32[]{:S(2)}) collective-permute-start(f32[16,1,6]{0,1,2:T(1,128)S(1)} %fusion.12), channel_id=1, source_target_pairs={{0,4},{4,0},{8,12},{12,8},{1,5},{5,1},{9,13},{13,9},{2,6},{6,2},{1... | collective-permute-start | bytes 1160 | tf_op jit(solution)/shard_map/ppermute | solution.py:74

commit v6 on v5

--- a/solution.py
+++ b/solution.py
@@ -231,21 +231,27 @@
 
 
 def shard_body(flags, at, *refs):
-    sources = [refs[2 * i : 2 * i + 2] for i in range(len(flags))]
-    t_out, t_in, o_out, o_in, mine, theirs, held, total, sems = refs[2 * len(flags) :]
+    sources = [refs[4 * i : 4 * i + 4] for i in range(len(flags))]
+    t_out, t_in, o_out, o_in, mine, theirs, held, total, sems = refs[4 * len(flags) :]
     d, ff = t_out.shape[1], t_in.shape[1]
     rows = mine.shape[0] // 2
-    step = ff // 2 // 128 * 128 + 128
-    cuts = [(0, d)] + [(d + k, min(step, ff - k)) for k in range(0, ff, step)]
+    bound = sources[0][0].shape[1]
+    middle = (d + ff - bound) // 256 * 128
+    cuts = [(0, d), (d, bound - d), (bound, middle), (bound + middle, d + ff - bound - middle)]
 
     def copies(source):
-        return [
-            [
-                pltpu.make_async_copy(p.at[:, pl.ds(*cut)], held.at[j, :, pl.ds(*cut)], sems.at[i, j])
-                for j, p in enumerate(source)
-            ]
-            for i, cut in enumerate(cuts)
-        ]
+        pairs = []
+        for i, (start, width) in enumerate(cuts):
+            part, first = (0, start) if start < bound else (1, start - bound)
+            pairs.append(
+                [
+                    pltpu.make_async_copy(
+                        source[2 * j + part].at[:, pl.ds(first, width)], held.at[j, :, pl.ds(start, width)], sems.at[i, j]
+                    )
+                    for j in range(2)
+                ]
+            )
+        return pairs
 
     chosen = at[flags[0]] == 1
     for flag, source in zip(flags, sources, strict=True):
@@ -294,18 +300,23 @@
             sent[2 * rows :, :] = source[...].astype(HALF)
 
 
-def late_body(at, both, both_far, last, last_far, sent):
-    size = both.shape[0]
-    choices = sources_of(at, both, both_far, both, both_far, last, last_far)
-    for i, sources in enumerate(choices[1:]):
-        for source, condition in sources:
-
-            @pl.when(condition)
-            def _(source=source, i=i):
-                sent[i * size : (i + 1) * size, :] = source[...].astype(HALF)
-
-
-def train_body(at, counts, g_own, a_own, near, near_far, both, both_far, last, last_far, early, late, *refs):
+def middle_body(at, both, both_far, sent):
+    for source, condition in sources_of(at, both, both_far, both, both_far, both, both)[1]:
+
+        @pl.when(condition)
+        def _(source=source):
+            sent[...] = source[...].astype(HALF)
+
+
+def last_body(at, both, both_far, last, last_far, sent):
+    for source, condition in sources_of(at, both, both_far, both, both_far, last, last_far)[2]:
+
+        @pl.when(condition)
+        def _(source=source):
+            sent[...] = source[...].astype(HALF)
+
+
+def train_body(at, counts, g_own, a_own, near, near_far, both, both_far, last, last_far, early, middle, late, *refs):
     mine, theirs, (grad, act, held) = refs[:4], refs[4:8], refs[8:]
     wide, layer, rep = at[1], at[2], at[3]
     rows, half = g_own.shape[0], mine[0].shape[1]
@@ -325,7 +336,7 @@
 
     place(0, g_own[...] + came(early, 0), a_own[...] + came(early, 1))
     choices = sources_of(at, near, near_far, both, both_far, last, last_far)
-    for sources, slot, ref, block in zip(choices, (near_slot, 2, 4 - near_slot), (early, late, late), (2, 0, 2), strict=True):
+    for sources, slot, ref, block in zip(choices, (near_slot, 2, 4 - near_slot), (early, middle, late), (2, 0, 0), strict=True):
         for source, condition in sources:
 
             @pl.when(condition)
@@ -385,34 +396,41 @@
     weighted = (query_grads.astype(FLOAT) / eigenvalues[None, :, :]).astype(HALF).transpose(1, 0, 2)
     dma = pltpu.SemaphoreType.DMA((2,))
 
-    held = jnp.concatenate(
-        [lax.dynamic_slice_in_dim(x, group * half, half, axis=0) for x in (basis_out, basis_in)], axis=1
-    )
+    cut = (ff - d) // 256 * 128
+    half_out, half_in = (lax.dynamic_slice_in_dim(x, group * half, half, axis=0) for x in (basis_out, basis_in))
+    held = [jnp.concatenate([half_out, half_in[:, :cut]], axis=1), half_in[:, cut:]]
 
     def load(x, y):
         return kernel(
             load_body, [pltpu.VMEM((n_tok, d), HALF), pltpu.VMEM((n_tok, ff), HALF)], [dma], grant=4
         )(in_specs=[ANY, ANY], out_specs=[VMEM, VMEM])(x.reshape(n_tok, d), y.reshape(n_tok, ff))
 
-    t_out, t_in = load(grads, acts)
+    near = [(0, 1), (1, 1), (2, 0), (3, 0)]
+    inner = [(1, 0), (2, 1)]
+    outer = [(0, 1), (3, 0)]
+
+    def to_group(x, places):
+        numbers = {2 * w + r for w, r in places}
+        return lax.ppermute(x, ("groups", "wide", "rep"), swap_pairs(2 * n_wide, numbers.__contains__))
+
+    def hop(x, k):
+        return lax.ppermute(x, ("wide", "rep"), hop_pairs(k, n_wide))
+
+
+    x1 = [hop(x, 1) for x in held]
+    x2 = [hop(x, 2) for x in x1]
+    y1 = [to_group(x, near) for x in x1]
+    x3 = [hop(after(x, y), 3) for x, y in zip(x2, y1, strict=True)]
+
+    g_other, a_other = lax.ppermute(grads, "rep", swap), lax.ppermute(acts, "rep", swap)
+    own_tokens = [after(x, *x2) for x in (grads, acts)]
+    t_out, t_in = load(*own_tokens)
     g_own, a_own = kernel(
         own_body, [shaped(rows, n_tok)] * 2, [pltpu.VMEM((n_tok, rows), FLOAT)], 2 * rows * n_tok * (d + ff)
     )(in_specs=[VMEM] * 4, out_specs=[VMEM] * 2)(basis_out, basis_in, t_out, t_in)
 
-    near = [(0, 1), (1, 1), (2, 0), (3, 0)]
-    inner = [(1, 0), (2, 1)]
-    outer = [(0, 1), (3, 0)]
-
-    def to_group(x, places):
-        numbers = {2 * w + r for w, r in places}
-        return lax.ppermute(x, ("groups", "wide", "rep"), swap_pairs(2 * n_wide, numbers.__contains__))
-
-    def hop(x, k):
-        return lax.ppermute(x, ("wide", "rep"), hop_pairs(k, n_wide))
-
-    o_out, o_in = load(lax.ppermute(grads, "rep", swap), lax.ppermute(acts, "rep", swap))
-
-    def rotate(flags, *pieces):
+    o_out, o_in = load(g_other, a_other)
+    def rotate(flags, *pieces, before=()):
         both = 2 * rows
         mine, theirs = kernel(
             functools.partial(shard_body, flags),
@@ -420,23 +438,23 @@
             [pltpu.VMEM((2, half, d + ff), HALF), pltpu.VMEM((2, n_tok, rows), FLOAT), pltpu.SemaphoreType.DMA((4, 2))],
             4 * rows * n_tok * (d + ff),
         )(in_specs=[SMEM] + [ANY] * len(pieces) + [VMEM] * 4, out_specs=[VMEM] * 2)(at, *pieces, t_out, t_in, o_out, o_in)
-        return mine, lax.ppermute(theirs, "rep", swap)
-
-    x1 = hop(held, 1)
-    y1 = to_group(x1, near)
-    x1_sent, weighted, _, _ = lax.optimization_barrier((x1, weighted, g_own, a_own))
-    x2 = hop(x1_sent, 2)
-    x3 = hop(after(x2, y1), 3)
-    y2 = to_group(x2, near)
-    near_done = rotate([4], x1, y1)
-    y3 = to_group(after(x3, y2, near_done[0]), outer)
-    y1_inner = to_group(after(x1, y1), inner)
-    packed = shaped(4 * rows, n_tok, kind=HALF)
-    early = kernel(early_body, packed)(in_specs=[SMEM] + [VMEM] * 4, out_specs=VMEM)(at, g_own, a_own, *near_done)
+        return mine, lax.ppermute(after(theirs, *before), "rep", swap)
+
+    near_done = rotate([4], *x1, *y1)
+    y2 = [to_group(x, near) for x in x2]
+    y3 = [to_group(x, outer) for x in x3]
+    y1_inner = [to_group(after(x, y), inner) for x, y in zip(x1, y1, strict=True)]
+    weighted = after(weighted, x3[1])
+    early = kernel(early_body, shaped(4 * rows, n_tok, kind=HALF))(in_specs=[SMEM] + [VMEM] * 4, out_specs=VMEM)(
+        at, g_own, a_own, *near_done
+    )
     early = lax.ppermute(early, "layer", swap)
-    both_done = rotate([4, 5], x2, y2, x1, y1_inner)
-    last_done = rotate([6], x3, after(y3, both_done[0], early))
-    late = kernel(late_body, packed)(in_specs=[SMEM] + [VMEM] * 4, out_specs=VMEM)(at, *both_done, *last_done)
+    both_done = rotate([4, 5], *x2, y2[0], after(y2[1], early), *x1, *y1_inner)
+    pair = shaped(2 * rows, n_tok, kind=HALF)
+    middle = kernel(middle_body, pair)(in_specs=[SMEM] + [VMEM] * 2, out_specs=VMEM)(at, *both_done)
+    middle_came = lax.ppermute(middle, "layer", swap)
+    last_done = rotate([6], *x3, y3[0], after(y3[1], middle), before=(middle_came,))
+    late = kernel(last_body, pair)(in_specs=[SMEM] + [VMEM] * 4, out_specs=VMEM)(at, *both_done, *last_done)
     late = lax.ppermute(late, "layer", swap)
 
     pieces = kernel(
@@ -444,8 +462,8 @@
         [shaped(seq_dev, half, share, kind=HALF)] * 8,
         [pltpu.VMEM((n_wide * rows, n_tok), HALF), pltpu.VMEM((share, n_tok), HALF), pltpu.VMEM((n_wide * rows, share), HALF)],
         2 * n_wide * rows * share * n_tok,
-    )(in_specs=[SMEM, SMEM] + [VMEM] * 10, out_specs=[VMEM] * 8)(
-        at, counts, g_own, a_own, *near_done, *both_done, *last_done, early, late
+    )(in_specs=[SMEM, SMEM] + [VMEM] * 11, out_specs=[VMEM] * 8)(
+        at, counts, g_own, a_own, *near_done, *both_done, *last_done, early, middle_came, late
     )
     mine, theirs = pieces[:4], pieces[4:]
 

time: 139 us -> 137 us (0.986)
  waiting for transfers between devices: 33 us -> 36.7 us
  local copies, waits for them, and re-layouts: 10.4 us -> 7.79 us
  other arithmetic: 3.77 us -> 2.31 us
    ppermute x3 -> x4, starting transfers between devices: 38.4 us -> 25.4 us  [the longest x3 23.8 us: rotate(): return (mine, lax.ppermute(after(theirs, *before), 'rep', swap))]
    ppermute x7, waiting for transfers between devices: 9.39 us -> 2.84 us  [send(): return lax.ppermute(x, ('wide', 'rep'), pairs)]
    ppermute x7, starting transfers between devices: 13.4 us -> 18.9 us  [send(): return lax.ppermute(x, ('wide', 'rep'), pairs)]
    ppermute x3 -> x4, waiting for transfers between devices: 2.7 us -> 7.85 us  [the longest x1 4.85 us: local_fast(): middle_came = lax.ppermute(middle, 'layer', swap)]
    ppermute x3 -> x6, waiting for transfers between devices: 1.17 us -> 6.19 us  [hop(): return lax.ppermute(x, ('wide', 'rep'), hop_pairs(k, n_wide))]
    unnamed x30 -> x24, local copies, waits for them, and re-layouts: 8.78 us -> 4.21 us
    ppermute x1, waiting for transfers between devices: 9.88 us -> 5.45 us  [local_fast(): late = lax.ppermute(late, 'layer', swap)]
    ppermute x3 -> x6, starting transfers between devices: 8.07 us -> 12.4 us  [hop(): return lax.ppermute(x, ('wide', 'rep'), hop_pairs(k, n_wide))]
  transfers between devices with their start and end apart: 26 -> 34, of which waited for: 12 -> 13; matrix products, arithmetic and copies ran while one was open for 3% -> 4% of each run, Pallas kernels for 7% -> 7%
where the time goes in v6:
time: 137 us; the launch traced here: 136 us
  starting transfers between devices  76.1 us (56%)
  waiting for transfers between devices  36.7 us (27%)
  Pallas kernels  13 us (9%)
  local copies, waits for them, and re-layouts  7.79 us (6%)
  other arithmetic  2.31 us (2%)
    ppermute x3, starting transfers between devices, rotate(): return (mine, lax.ppermute(after(theirs, *before), 'rep', swap))  23.8 us
    ppermute x7, starting transfers between devices, send(): return lax.ppermute(x, ('wide', 'rep'), pairs)  18.9 us
    ppermute x6, starting transfers between devices, hop(): return lax.ppermute(x, ('wide', 'rep'), hop_pairs(k, n_wide))  12.4 us
    ppermute x1, waiting for transfers between devices, local_fast(): early = lax.ppermute(early, 'layer', swap)  7.33 us
    ppermute x8, starting transfers between devices, to_group(): lax.ppermute(x, ('groups', 'wide', 'rep'), swap_pairs(2 * n_wide, numbers...  7.21 us
    ppermute x6, waiting for transfers between devices, hop(): return lax.ppermute(x, ('wide', 'rep'), hop_pairs(k, n_wide))  6.19 us
    ppermute x1, waiting for transfers between devices, local_fast(): late = lax.ppermute(late, 'layer', swap)  5.45 us
    ppermute x1, waiting for transfers between devices, local_fast(): middle_came = lax.ppermute(middle, 'layer', swap)  4.85 us
  transfers between devices with their start and end apart: 34, of which 13 were waited for; matrix products, arithmetic and copies ran while one was open for 4% of the time, Pallas kernels for 7%

profile of v6, /device:TPU:0, one launch (start us, length us, event | category | flops | bytes accessed | tf_op | source)
XLA Modules:
  0.0 136.4 jit_solution(897366831203039449)
XLA Ops:
  0.0 0.5 collective-permute-start.8
  0.5 1.2 dynamic-slice
  1.7 4.5 %collective-permute-start = (bf16[64,4736]{1,0:T(8,128)(2,1)S(1)}, bf16[64,4736]{1,0:T(8,128)(2,1)S(1)}, u32[]{:S(2)}, u32[]{:S(2)}) collective-permute-start(bf16[64,4736]{1,0:T(8,128)(2,1)S(1)} %dynamic-slice), channel_id=1, source_target_pairs={{0,4},{4,8},{8,12},{5,1},{9,5},{13,9},{2,6},{6,10},{10,14},{7,3},{... | collective-permute-start | bytes 1818632 | tf_op jit(solution)/shard_map/ppermute | solution.py:417
  6.2 0.1 collective-permute-start.7
  6.3 1.0 constant_dynamic-slice_fusion.5
  7.3 1.0 constant_dynamic-slice_fusion.4
  8.4 3.5 %collective-permute-start.4 = (bf16[64,4736]{1,0:T(8,128)(2,1)S(1)}, bf16[64,4736]{1,0:T(8,128)(2,1)S(1)}, u32[]{:S(2)}, u32[]{:S(2)}) collective-permute-start(bf16[64,4736]{1,0:T(8,128)(2,1)S(1)} %pad_maximum_fusion), channel_id=1, source_target_pairs={{0,4},{4,8},{8,12},{5,1},{9,5},{13,9},{2,6},{6,10},{10,14},{7,3},{... | collective-permute-start | bytes 1818632 | tf_op jit(solution)/shard_map/ppermute | solution.py:417
  11.9 1.9 %collective-permute-done.refs_1_.refs_5_ = bf16[64,4736]{1,0:T(8,128)(2,1)S(1)} collective-permute-done((bf16[64,4736]{1,0:T(8,128)(2,1)S(1)}, bf16[64,4736]{1,0:T(8,128)(2,1)S(1)}, u32[]{:S(2)}, u32[]{:S(2)}) %collective-permute-start) | collective-permute-done | bytes 606240 | tf_op jit(solution)/shard_map/ppermute | solution.py:417
  13.8 1.5 %collective-permute-start.1 = (bf16[64,4736]{1,0:T(8,128)(2,1)S(1)}, bf16[64,4736]{1,0:T(8,128)(2,1)}, u32[]{:S(2)}, u32[]{:S(2)}) collective-permute-start(bf16[64,4736]{1,0:T(8,128)(2,1)S(1)} %collective-permute-done.refs_1_.refs_5_), channel_id=1, source_target_pairs={{4,8},{8,12},{5,1},{9,5},{6,10},{10,14},{7,3},{11,7},{20,24},{24,2... | collective-permute-start | bytes 1818632 | tf_op jit(solution)/shard_map/ppermute | solution.py:417
  15.3 0.7 collective-permute-start.2
  16.0 4.3 %collective-permute-done.4.refs_0_.refs_4_ = bf16[64,4736]{1,0:T(8,128)(2,1)S(1)} collective-permute-done((bf16[64,4736]{1,0:T(8,128)(2,1)S(1)}, bf16[64,4736]{1,0:T(8,128)(2,1)S(1)}, u32[]{:S(2)}, u32[]{:S(2)}) %collective-permute-start.4) | collective-permute-done | bytes 606240 | tf_op jit(solution)/shard_map/ppermute | solution.py:417
  20.3 0.7 collective-permute-start.5
  21.0 1.5 %collective-permute-start.6 = (bf16[64,4736]{1,0:T(8,128)(2,1)S(1)}, bf16[64,4736]{1,0:T(8,128)(2,1)}, u32[]{:S(2)}, u32[]{:S(2)}) collective-permute-start(bf16[64,4736]{1,0:T(8,128)(2,1)S(1)} %collective-permute-done.4.refs_0_.refs_4_), channel_id=1, source_target_pairs={{1,17},{5,21},{8,24},{12,28},{17,1},{21,5},{24,8},{28,12},{3,19},{... | collective-permute-start | bytes 1818632 | tf_op jit(solution)/shard_map/ppermute | solution.py:414
  22.5 0.8 copy-done.4
  23.3 1.6 %collective-permute-start.11 = (bf16[64,4736]{1,0:T(8,128)(2,1)}, bf16[64,4736]{1,0:T(8,128)(2,1)}, u32[]{:S(2)}, u32[]{:S(2)}) collective-permute-start(bf16[64,4736]{1,0:T(8,128)(2,1)} %collective-permute-done.1.refs_1_), channel_id=1, source_target_pairs={{1,17},{5,21},{8,24},{12,28},{17,1},{21,5},{24,8},{28,12},{3,19},{... | collective-permute-start | bytes 1818632 | tf_op jit(solution)/shard_map/ppermute | solution.py:414
  24.9 0.8 copy-done.6
  25.7 1.5 %collective-permute-start.3 = (bf16[64,4736]{1,0:T(8,128)(2,1)}, bf16[64,4736]{1,0:T(8,128)(2,1)}, u32[]{:S(2)}, u32[]{:S(2)}) collective-permute-start(bf16[64,4736]{1,0:T(8,128)(2,1)} %collective-permute-done.1.refs_1_), channel_id=1, source_target_pairs={{8,12},{5,1},{10,14},{7,3},{24,28},{21,17},{26,30},{23,19}} | collective-permute-start | bytes 1818632 | tf_op jit(solution)/shard_map/ppermute | solution.py:417
  27.1 0.1 stack.51.at
  27.2 2.5 %copy-done = bf16[3,128,6912]{2,1,0:T(8,128)(2,1)S(1)} copy-done((bf16[3,128,6912]{2,1,0:T(8,128)(2,1)S(1)}, bf16[3,128,6912]{2,1,0:T(8,128)(2,1)}, u32[]{:S(2)}) %copy-start) | copy-done | bytes 5308440
  29.7 0.8 shard_map.82
  30.5 3.2 %shard_map.84 = (bf16[384,2560]{1,0:T(8,128)(2,1)S(1)}, bf16[384,6912]{1,0:T(8,128)(2,1)S(1)}) custom-call(bf16[384,2560]{1,0:T(8,128)(2,1)} %bitcast.11.x_ref, bf16[384,6912]{1,0:T(8,128)(2,1)} %bitcast.12.y_ref), custom_call_target="tpu_custom_call" | custom-call | bytes 1024 | tf_op jit(solution)/shard_map/pallas_call | solution.py:404
  33.8 0.6 shard_map.85
  34.4 14.2 %collective-permute-start.9 = (f32[256,384]{1,0:T(8,128)S(1)}, f32[256,384]{1,0:T(8,128)S(1)}, u32[]{:S(2)}, u32[]{:S(2)}) collective-permute-start(f32[256,384]{1,0:T(8,128)S(1)} %get-tuple-element.46), channel_id=1, source_target_pairs={{0,1},{1,0},{2,3},{3,2},{4,5},{5,4},{6,7},{7,6},{8,9},{9,8},{10,11... | collective-permute-start | bytes 1179656 | tf_op jit(solution)/shard_map/ppermute | solution.py:441
  48.6 0.7 collective-permute-start.16
  49.3 0.7 collective-permute-start.13
  50.0 0.7 collective-permute-start.14
  50.7 0.7 collective-permute-start.10
  51.4 2.1 %shard_map.83 = (f32[128,384]{1,0:T(8,128)S(1)}, f32[128,384]{1,0:T(8,128)S(1)}) custom-call(bf16[128,2560]{1,0:T(8,128)(2,1)S(1)} %copy-done.3, bf16[128,6912]{1,0:T(8,128)(2,1)S(1)} %copy-done.1, bf16[384,2560]{1,0:T(8,128)(2,1)S(1)} %get-tuple-element.39.t_out.refs_4_.refs_8_, bf16[384,6912]{1,0:T(8,128)(2,1)S(1)} %get-tuple-element.40.t_in.refs_5_.refs_9_), custom_call_target="tpu_custom_call" | custom-call | flops 931135 | bytes 1024 | tf_op jit(solution)/shard_map/pallas_call | solution.py:428
  53.6 0.6 shard_map.86
  54.2 1.7 %collective-permute-start.12 = (bf16[512,384]{1,0:T(8,128)(2,1)S(1)}, bf16[512,384]{1,0:T(8,128)(2,1)S(1)}, u32[]{:S(2)}, u32[]{:S(2)}) collective-permute-start(bf16[512,384]{1,0:T(8,128)(2,1)S(1)} %shard_map.86), channel_id=1, source_target_pairs={{0,2},{2,0},{1,3},{3,1},{4,6},{6,4},{5,7},{7,5},{8,10},{10,8},{9,1... | collective-permute-start | bytes 1179656 | tf_op jit(solution)/shard_map/ppermute | solution.py:451
  55.9 0.7 collective-permute-start.18
  56.6 7.3 %collective-permute-done.12.early = bf16[512,384]{1,0:T(8,128)(2,1)S(1)} collective-permute-done((bf16[512,384]{1,0:T(8,128)(2,1)S(1)}, bf16[512,384]{1,0:T(8,128)(2,1)S(1)}, u32[]{:S(2)}, u32[]{:S(2)}) %collective-permute-start.12) | collective-permute-done | bytes 393248 | tf_op jit(solution)/shard_map/ppermute | solution.py:451
  63.9 0.7 collective-permute-start.17
  64.6 0.6 shard_map.87
  65.3 9.5 %collective-permute-start.15 = (f32[256,384]{1,0:T(8,128)S(1)}, f32[256,384]{1,0:T(8,128)S(1)}, u32[]{:S(2)}, u32[]{:S(2)}) collective-permute-start(f32[256,384]{1,0:T(8,128)S(1)} %get-tuple-element.51), channel_id=1, source_target_pairs={{0,1},{1,0},{2,3},{3,2},{4,5},{5,4},{6,7},{7,6},{8,9},{9,8},{10,11... | collective-permute-start | bytes 1179656 | tf_op jit(solution)/shard_map/ppermute | solution.py:441
  74.8 1.3 collective-permute-done.15.both_far
  76.2 0.6 shard_map.88
  76.7 1.6 %collective-permute-start.19 = (bf16[256,384]{1,0:T(8,128)(2,1)S(1)}, bf16[256,384]{1,0:T(8,128)(2,1)S(1)}, u32[]{:S(2)}, u32[]{:S(2)}) collective-permute-start(bf16[256,384]{1,0:T(8,128)(2,1)S(1)} %shard_map.88), channel_id=1, source_target_pairs={{0,2},{2,0},{1,3},{3,1},{4,6},{6,4},{5,7},{7,5},{8,10},{10,8},{9,1... | collective-permute-start | bytes 589832 | tf_op jit(solution)/shard_map/ppermute | solution.py:455
  78.3 0.8 shard_map.89
  79.1 4.9 %collective-permute-done.19.middle = bf16[256,384]{1,0:T(8,128)(2,1)S(1)} collective-permute-done((bf16[256,384]{1,0:T(8,128)(2,1)S(1)}, bf16[256,384]{1,0:T(8,128)(2,1)S(1)}, u32[]{:S(2)}, u32[]{:S(2)}) %collective-permute-start.19) | collective-permute-done | bytes 196640 | tf_op jit(solution)/shard_map/ppermute | solution.py:455
  84.1 1.6 %collective-permute-done.20.last_far = f32[256,384]{1,0:T(8,128)S(1)} collective-permute-done((f32[256,384]{1,0:T(8,128)S(1)}, f32[256,384]{1,0:T(8,128)S(1)}, u32[]{:S(2)}, u32[]{:S(2)}) %collective-permute-start.20) | collective-permute-done | bytes 393248 | tf_op jit(solution)/shard_map/ppermute | solution.py:441
  85.7 0.6 shard_map.90
  86.3 1.6 %collective-permute-start.21 = (bf16[256,384]{1,0:T(8,128)(2,1)S(1)}, bf16[256,384]{1,0:T(8,128)(2,1)S(1)}, u32[]{:S(2)}, u32[]{:S(2)}) collective-permute-start(bf16[256,384]{1,0:T(8,128)(2,1)S(1)} %shard_map.90), channel_id=1, source_target_pairs={{0,2},{2,0},{1,3},{3,1},{4,6},{6,4},{5,7},{7,5},{8,10},{10,8},{9,1... | collective-permute-start | bytes 589832 | tf_op jit(solution)/shard_map/ppermute | solution.py:458
  87.9 5.4 %collective-permute-done.21.late = bf16[256,384]{1,0:T(8,128)(2,1)S(1)} collective-permute-done((bf16[256,384]{1,0:T(8,128)(2,1)S(1)}, bf16[256,384]{1,0:T(8,128)(2,1)S(1)}, u32[]{:S(2)}, u32[]{:S(2)}) %collective-permute-start.21) | collective-permute-done | bytes 196640 | tf_op jit(solution)/shard_map/ppermute | solution.py:458
  93.3 1.2 shard_map.91
  94.5 8.2 %collective-permute-start.22 = (bf16[3,64,256]{2,1,0:T(8,128)(2,1)S(1)}, bf16[3,64,256]{2,1,0:T(8,128)(2,1)S(1)}, u32[]{:S(2)}, u32[]{:S(2)}) collective-permute-start(bf16[3,64,256]{2,1,0:T(8,128)(2,1)S(1)} %get-tuple-element.58), channel_id=1, source_target_pairs={{0,4},{1,5},{4,8},{5,9},{8,12},{9,13},{12,0},{13,1},{2,6},{3,7},{6... | collective-permute-start | bytes 294920 | tf_op jit(solution)/shard_map/ppermute | solution.py:472
  102.8 3.0 %collective-permute-start.23 = (bf16[3,64,256]{2,1,0:T(8,128)(2,1)S(1)}, bf16[3,64,256]{2,1,0:T(8,128)(2,1)S(1)}, u32[]{:S(2)}, u32[]{:S(2)}) collective-permute-start(bf16[3,64,256]{2,1,0:T(8,128)(2,1)S(1)} %get-tuple-element.59), channel_id=1, source_target_pairs={{0,8},{1,9},{4,12},{5,13},{8,0},{9,1},{12,4},{13,5},{2,10},{3,11},... | collective-permute-start | bytes 294920 | tf_op jit(solution)/shard_map/ppermute | solution.py:472
  105.7 2.8 %collective-permute-start.24 = (bf16[3,64,256]{2,1,0:T(8,128)(2,1)S(1)}, bf16[3,64,256]{2,1,0:T(8,128)(2,1)S(1)}, u32[]{:S(2)}, u32[]{:S(2)}) collective-permute-start(bf16[3,64,256]{2,1,0:T(8,128)(2,1)S(1)} %get-tuple-element.60), channel_id=1, source_target_pairs={{0,12},{1,13},{4,0},{5,1},{8,4},{9,5},{12,8},{13,9},{2,14},{3,15},... | collective-permute-start | bytes 294920 | tf_op jit(solution)/shard_map/ppermute | solution.py:472
  108.6 0.3 collective-permute-start.27
  108.9 1.7 %collective-permute-done.23.refs_2_ = bf16[3,64,256]{2,1,0:T(8,128)(2,1)S(1)} collective-permute-done((bf16[3,64,256]{2,1,0:T(8,128)(2,1)S(1)}, bf16[3,64,256]{2,1,0:T(8,128)(2,1)S(1)}, u32[]{:S(2)}, u32[]{:S(2)}) %collective-permute-start.23) | collective-permute-done | bytes 98336 | tf_op jit(solution)/shard_map/ppermute | solution.py:472
  110.6 4.6 %collective-permute-start.28 = (bf16[3,64,256]{2,1,0:T(8,128)(2,1)S(1)}, bf16[3,64,256]{2,1,0:T(8,128)(2,1)S(1)}, u32[]{:S(2)}, u32[]{:S(2)}) collective-permute-start(bf16[3,64,256]{2,1,0:T(8,128)(2,1)S(1)} %get-tuple-element.64), channel_id=1, source_target_pairs={{0,13},{1,12},{4,1},{5,0},{8,5},{9,4},{12,9},{13,8},{2,15},{3,14},... | collective-permute-start | bytes 294920 | tf_op jit(solution)/shard_map/ppermute | solution.py:472
  115.2 1.5 %fusion.weights = bf16[64,64,256]{2,1,0:T(8,128)(2,1)S(1)} fusion(bf16[64,64,256]{2,1,0:T(8,128)(2,1)S(1)} %copy-done.9, f32[64,256]{1,0:T(8,128)S(1)} %copy-done.10), kind=kLoop, calls=%fused_computation.1 | loop fusion | flops 3145728 | bytes 4259840 | tf_op jit(solution)/shard_map/transpose | solution.py:396
  116.8 1.1 collective-permute-done.27.refs_6_
  117.9 2.0 %shard_map.92 = f32[64,24]{1,0:T(8,128)S(1)} custom-call(s32[8]{0:T(128)S(1)} %stack.51.at, bf16[64,64,256]{2,1,0:T(8,128)(2,1)S(1)} %fusion.weights, bf16[3,64,256]{2,1,0:T(8,128)(2,1)S(1)} %get-tuple-element.57.refs_0_, bf16[3,64,256]{2,1,0:T(8,128)(2,1)S(1)} %collective-permute-done.22.refs_1_, bf16[3,64,256]{2,1,0:T(8,128)(2,1)S(1)} %collective-permute-done.23.refs_2_, ...), custom_call_target="tpu_custom_call" | custom-call | flops 50331 | bytes 1024 | tf_op jit(solution)/shard_map/pallas_call | solution.py:477
  120.0 0.1 reshape_reshape.3
  120.1 3.0 %collective-permute-start.29 = (f32[16,4,6]{0,1,2:T(4,128)S(1)}, f32[16,4,6]{0,1,2:T(4,128)S(1)}, u32[]{:S(2)}, u32[]{:S(2)}) collective-permute-start(f32[16,4,6]{0,1,2:T(4,128)S(1)} %bitcast.74), channel_id=1, source_target_pairs={{0,1},{1,2},{2,3},{3,0},{4,5},{5,6},{6,7},{7,4},{8,9},{9,10},{10,1... | collective-permute-start | bytes 4616 | tf_op jit(solution)/shard_map/ppermute | solution.py:63
  123.1 1.5 %collective-permute-start.30 = (f32[16,4,6]{0,1,2:T(4,128)S(1)}, f32[16,4,6]{0,1,2:T(4,128)S(1)}, u32[]{:S(2)}, u32[]{:S(2)}) collective-permute-start(f32[16,4,6]{0,1,2:T(4,128)S(1)} %bitcast.75), channel_id=1, source_target_pairs={{0,2},{1,3},{2,0},{3,1},{4,6},{5,7},{6,4},{7,5},{8,10},{9,11},{10,... | collective-permute-start | bytes 4616 | tf_op jit(solution)/shard_map/ppermute | solution.py:63
  124.6 1.0 collective-permute-done.29
  125.6 1.2 collective-permute-done.30
  127.0 1.4 %collective-permute-start.32 = (f32[16,2,6]{0,1,2:T(2,128)S(1)}, f32[16,2,6]{0,1,2:T(2,128)S(1)}, u32[]{:S(2)}, u32[]{:S(2)}) collective-permute-start(f32[16,2,6]{0,1,2:T(2,128)S(1)} %fusion.6), channel_id=1, source_target_pairs={{0,8},{4,12},{8,0},{12,4},{1,9},{5,13},{9,1},{13,5},{2,10},{6,14},... | collective-permute-start | bytes 2312 | tf_op jit(solution)/shard_map/ppermute | solution.py:74
  128.4 3.2 %collective-permute-done.32 = f32[16,2,6]{0,1,2:T(2,128)S(1)} collective-permute-done((f32[16,2,6]{0,1,2:T(2,128)S(1)}, f32[16,2,6]{0,1,2:T(2,128)S(1)}, u32[]{:S(2)}, u32[]{:S(2)}) %collective-permute-start.32) | collective-permute-done | bytes 800 | tf_op jit(solution)/shard_map/ppermute | solution.py:74
  131.6 2.6 %collective-permute-start.33 = (f32[16,1,6]{0,1,2:T(1,128)S(1)}, f32[16,1,6]{0,1,2:T(1,128)S(1)}, u32[]{:S(2)}, u32[]{:S(2)}) collective-permute-start(f32[16,1,6]{0,1,2:T(1,128)S(1)} %fusion.12), channel_id=1, source_target_pairs={{0,4},{4,0},{8,12},{12,8},{1,5},{5,1},{9,13},{13,9},{2,6},{6,2},{1... | collective-permute-start | bytes 1160 | tf_op jit(solution)/shard_map/ppermute | solution.py:74
  134.2 1.6 %collective-permute-done.33 = f32[16,1,6]{0,1,2:T(1,128)S(1)} collective-permute-done((f32[16,1,6]{0,1,2:T(1,128)S(1)}, f32[16,1,6]{0,1,2:T(1,128)S(1)}, u32[]{:S(2)}, u32[]{:S(2)}) %collective-permute-start.33) | collective-permute-done | bytes 416 | tf_op jit(solution)/shard_map/ppermute | solution.py:74
  135.7 0.7 bitcast_multiply_fusion
  (63 shorter events, 0.5 us)
Async XLA Ops:
  0.0 27.2 %copy-start.2 = (bf16[3,128,2560]{2,1,0:T(8,128)(2,1)S(1)}, bf16[3,128,2560]{2,1,0:T(8,128)(2,1)}, u32[]{:S(2)}) copy-start(bf16[3,128,2560]{2,1,0:T(8,128)(2,1)} %param.9) | copy-start | bytes 5898244
  0.0 30.5 %collective-permute-start.8 = (bf16[3,128,6912]{2,1,0:T(8,128)(2,1)}, bf16[3,128,6912]{2,1,0:T(8,128)(2,1)}, u32[]{:S(2)}, u32[]{:S(2)}) collective-permute-start(bf16[3,128,6912]{2,1,0:T(8,128)(2,1)} %param.8), channel_id=1, source_target_pairs={{0,1},{1,0},{2,3},{3,2},{4,5},{5,4},{6,7},{7,6},{8,9},{9,8},{10,11... | collective-permute-start | bytes 15925256 | tf_op jit(solution)/shard_map/ppermute | solution.py:425
  1.7 12.1 %collective-permute-start = (bf16[64,4736]{1,0:T(8,128)(2,1)S(1)}, bf16[64,4736]{1,0:T(8,128)(2,1)S(1)}, u32[]{:S(2)}, u32[]{:S(2)}) collective-permute-start(bf16[64,4736]{1,0:T(8,128)(2,1)S(1)} %dynamic-slice), channel_id=1, source_target_pairs={{0,4},{4,8},{8,12},{5,1},{9,5},{13,9},{2,6},{6,10},{10,14},{7,3},{... | collective-permute-start | bytes 1818632 | tf_op jit(solution)/shard_map/ppermute | solution.py:417
  6.2 24.3 %collective-permute-start.7 = (bf16[3,128,2560]{2,1,0:T(8,128)(2,1)}, bf16[3,128,2560]{2,1,0:T(8,128)(2,1)}, u32[]{:S(2)}, u32[]{:S(2)}) collective-permute-start(bf16[3,128,2560]{2,1,0:T(8,128)(2,1)} %param.9), channel_id=1, source_target_pairs={{0,1},{1,0},{2,3},{3,2},{4,5},{5,4},{6,7},{7,6},{8,9},{9,8},{10,11... | collective-permute-start | bytes 5898248 | tf_op jit(solution)/shard_map/ppermute | solution.py:425
  8.4 11.9 %collective-permute-start.4 = (bf16[64,4736]{1,0:T(8,128)(2,1)S(1)}, bf16[64,4736]{1,0:T(8,128)(2,1)S(1)}, u32[]{:S(2)}, u32[]{:S(2)}) collective-permute-start(bf16[64,4736]{1,0:T(8,128)(2,1)S(1)} %pad_maximum_fusion), channel_id=1, source_target_pairs={{0,4},{4,8},{8,12},{5,1},{9,5},{13,9},{2,6},{6,10},{10,14},{7,3},{... | collective-permute-start | bytes 1818632 | tf_op jit(solution)/shard_map/ppermute | solution.py:417
  13.8 7.2 %collective-permute-start.1 = (bf16[64,4736]{1,0:T(8,128)(2,1)S(1)}, bf16[64,4736]{1,0:T(8,128)(2,1)}, u32[]{:S(2)}, u32[]{:S(2)}) collective-permute-start(bf16[64,4736]{1,0:T(8,128)(2,1)S(1)} %collective-permute-done.refs_1_.refs_5_), channel_id=1, source_target_pairs={{4,8},{8,12},{5,1},{9,5},{6,10},{10,14},{7,3},{11,7},{20,24},{24,2... | collective-permute-start | bytes 1818632 | tf_op jit(solution)/shard_map/ppermute | solution.py:417
  15.3 7.2 %collective-permute-start.2 = (bf16[64,4736]{1,0:T(8,128)(2,1)S(1)}, bf16[64,4736]{1,0:T(8,128)(2,1)S(1)}, u32[]{:S(2)}, u32[]{:S(2)}) collective-permute-start(bf16[64,4736]{1,0:T(8,128)(2,1)S(1)} %collective-permute-done.refs_1_.refs_5_), channel_id=1, source_target_pairs={{1,17},{5,21},{8,24},{12,28},{17,1},{21,5},{24,8},{28,12},{3,19},{... | collective-permute-start | bytes 1818632 | tf_op jit(solution)/shard_map/ppermute | solution.py:414
  20.3 4.6 %collective-permute-start.5 = (bf16[64,4736]{1,0:T(8,128)(2,1)S(1)}, bf16[64,4736]{1,0:T(8,128)(2,1)S(1)}, u32[]{:S(2)}, u32[]{:S(2)}) collective-permute-start(bf16[64,4736]{1,0:T(8,128)(2,1)S(1)} %collective-permute-done.4.refs_0_.refs_4_), channel_id=1, source_target_pairs={{4,8},{8,12},{5,1},{9,5},{6,10},{10,14},{7,3},{11,7},{20,24},{24,2... | collective-permute-start | bytes 1818632 | tf_op jit(solution)/shard_map/ppermute | solution.py:417
  21.0 12.7 %collective-permute-start.6 = (bf16[64,4736]{1,0:T(8,128)(2,1)S(1)}, bf16[64,4736]{1,0:T(8,128)(2,1)}, u32[]{:S(2)}, u32[]{:S(2)}) collective-permute-start(bf16[64,4736]{1,0:T(8,128)(2,1)S(1)} %collective-permute-done.4.refs_0_.refs_4_), channel_id=1, source_target_pairs={{1,17},{5,21},{8,24},{12,28},{17,1},{21,5},{24,8},{28,12},{3,19},{... | collective-permute-start | bytes 1818632 | tf_op jit(solution)/shard_map/ppermute | solution.py:414
  22.5 0.8 copy-start.4
  23.3 26.7 %collective-permute-start.11 = (bf16[64,4736]{1,0:T(8,128)(2,1)}, bf16[64,4736]{1,0:T(8,128)(2,1)}, u32[]{:S(2)}, u32[]{:S(2)}) collective-permute-start(bf16[64,4736]{1,0:T(8,128)(2,1)} %collective-permute-done.1.refs_1_), channel_id=1, source_target_pairs={{1,17},{5,21},{8,24},{12,28},{17,1},{21,5},{24,8},{28,12},{3,19},{... | collective-permute-start | bytes 1818632 | tf_op jit(solution)/shard_map/ppermute | solution.py:414
  24.9 0.8 copy-start.6
  25.7 28.5 %collective-permute-start.3 = (bf16[64,4736]{1,0:T(8,128)(2,1)}, bf16[64,4736]{1,0:T(8,128)(2,1)}, u32[]{:S(2)}, u32[]{:S(2)}) collective-permute-start(bf16[64,4736]{1,0:T(8,128)(2,1)} %collective-permute-done.1.refs_1_), channel_id=1, source_target_pairs={{8,12},{5,1},{10,14},{7,3},{24,28},{21,17},{26,30},{23,19}} | collective-permute-start | bytes 1818632 | tf_op jit(solution)/shard_map/ppermute | solution.py:417
  27.2 2.5 %copy-start = (bf16[3,128,6912]{2,1,0:T(8,128)(2,1)S(1)}, bf16[3,128,6912]{2,1,0:T(8,128)(2,1)}, u32[]{:S(2)}) copy-start(bf16[3,128,6912]{2,1,0:T(8,128)(2,1)} %param.8) | copy-start | bytes 15925252
  30.5 3.2 %copy-start.5 = (bf16[64,4736]{1,0:T(8,128)(2,1)S(1)}, bf16[64,4736]{1,0:T(8,128)(2,1)}, u32[]{:S(2)}) copy-start(bf16[64,4736]{1,0:T(8,128)(2,1)} %copy-done.4) | copy-start | bytes 1818628
  33.7 14.9 %copy-start.7 = (bf16[64,4736]{1,0:T(8,128)(2,1)S(1)}, bf16[64,4736]{1,0:T(8,128)(2,1)}, u32[]{:S(2)}) copy-start(bf16[64,4736]{1,0:T(8,128)(2,1)} %copy-done.6) | copy-start | bytes 1818628
  33.7 17.7 %copy-start.1 = (bf16[128,6912]{1,0:T(8,128)(2,1)S(1)}, bf16[128,6912]{1,0:T(8,128)(2,1)}, u32[]{:S(2)}) copy-start(bf16[128,6912]{1,0:T(8,128)(2,1)} %b_in.1) | copy-start | bytes 5308420
  33.7 17.7 %copy-start.3 = (bf16[128,2560]{1,0:T(8,128)(2,1)S(1)}, bf16[128,2560]{1,0:T(8,128)(2,1)}, u32[]{:S(2)}) copy-start(bf16[128,2560]{1,0:T(8,128)(2,1)} %b_out.1) | copy-start | bytes 1966084
  34.4 16.3 %collective-permute-start.9 = (f32[256,384]{1,0:T(8,128)S(1)}, f32[256,384]{1,0:T(8,128)S(1)}, u32[]{:S(2)}, u32[]{:S(2)}) collective-permute-start(f32[256,384]{1,0:T(8,128)S(1)} %get-tuple-element.46), channel_id=1, source_target_pairs={{0,1},{1,0},{2,3},{3,2},{4,5},{5,4},{6,7},{7,6},{8,9},{9,8},{10,11... | collective-permute-start | bytes 1179656 | tf_op jit(solution)/shard_map/ppermute | solution.py:441
  48.6 7.3 %collective-permute-start.16 = (bf16[64,4736]{1,0:T(8,128)(2,1)S(1)}, bf16[64,4736]{1,0:T(8,128)(2,1)S(1)}, u32[]{:S(2)}, u32[]{:S(2)}) collective-permute-start(bf16[64,4736]{1,0:T(8,128)(2,1)S(1)} %copy-done.7), channel_id=1, source_target_pairs={{8,12},{5,1},{10,14},{7,3},{24,28},{21,17},{26,30},{23,19}} | collective-permute-start | bytes 1818632 | tf_op jit(solution)/shard_map/ppermute | solution.py:417
  49.3 15.3 %collective-permute-start.13 = (bf16[64,4736]{1,0:T(8,128)(2,1)S(1)}, bf16[64,4736]{1,0:T(8,128)(2,1)S(1)}, u32[]{:S(2)}, u32[]{:S(2)}) collective-permute-start(bf16[64,4736]{1,0:T(8,128)(2,1)S(1)} %collective-permute-done.4.refs_0_.refs_4_), channel_id=1, source_target_pairs={{4,20},{9,25},{20,4},{25,9},{6,22},{11,27},{22,6},{27,11}} | collective-permute-start | bytes 1818632 | tf_op jit(solution)/shard_map/ppermute | solution.py:414
  50.0 14.6 %collective-permute-start.14 = (bf16[64,4736]{1,0:T(8,128)(2,1)S(1)}, bf16[64,4736]{1,0:T(8,128)(2,1)S(1)}, u32[]{:S(2)}, u32[]{:S(2)}) collective-permute-start(bf16[64,4736]{1,0:T(8,128)(2,1)S(1)} %collective-permute-done.refs_1_.refs_5_), channel_id=1, source_target_pairs={{4,20},{9,25},{20,4},{25,9},{6,22},{11,27},{22,6},{27,11}} | collective-permute-start | bytes 1818632 | tf_op jit(solution)/shard_map/ppermute | solution.py:414
  50.7 13.9 %collective-permute-start.10 = (bf16[64,4736]{1,0:T(8,128)(2,1)S(1)}, bf16[64,4736]{1,0:T(8,128)(2,1)S(1)}, u32[]{:S(2)}, u32[]{:S(2)}) collective-permute-start(bf16[64,4736]{1,0:T(8,128)(2,1)S(1)} %copy-done.7), channel_id=1, source_target_pairs={{1,17},{5,21},{8,24},{12,28},{17,1},{21,5},{24,8},{28,12},{3,19},{... | collective-permute-start | bytes 1818632 | tf_op jit(solution)/shard_map/ppermute | solution.py:414
  54.2 9.7 %collective-permute-start.12 = (bf16[512,384]{1,0:T(8,128)(2,1)S(1)}, bf16[512,384]{1,0:T(8,128)(2,1)S(1)}, u32[]{:S(2)}, u32[]{:S(2)}) collective-permute-start(bf16[512,384]{1,0:T(8,128)(2,1)S(1)} %shard_map.86), channel_id=1, source_target_pairs={{0,2},{2,0},{1,3},{3,1},{4,6},{6,4},{5,7},{7,5},{8,10},{10,8},{9,1... | collective-permute-start | bytes 1179656 | tf_op jit(solution)/shard_map/ppermute | solution.py:451
  55.9 22.4 %collective-permute-start.18 = (bf16[64,4736]{1,0:T(8,128)(2,1)}, bf16[64,4736]{1,0:T(8,128)(2,1)S(1)}, u32[]{:S(2)}, u32[]{:S(2)}) collective-permute-start(bf16[64,4736]{1,0:T(8,128)(2,1)} %collective-permute-done.3.refs_1_), channel_id=1, source_target_pairs={{1,17},{12,28},{17,1},{28,12},{3,19},{14,30},{19,3},{30,14}} | collective-permute-start | bytes 1818632 | tf_op jit(solution)/shard_map/ppermute | solution.py:414
  63.9 14.4 %collective-permute-start.17 = (bf16[64,4736]{1,0:T(8,128)(2,1)S(1)}, bf16[64,4736]{1,0:T(8,128)(2,1)S(1)}, u32[]{:S(2)}, u32[]{:S(2)}) collective-permute-start(bf16[64,4736]{1,0:T(8,128)(2,1)S(1)} %collective-permute-done.16.refs_0_), channel_id=1, source_target_pairs={{1,17},{12,28},{17,1},{28,12},{3,19},{14,30},{19,3},{30,14}} | collective-permute-start | bytes 1818632 | tf_op jit(solution)/shard_map/ppermute | solution.py:414
  65.3 10.9 %collective-permute-start.15 = (f32[256,384]{1,0:T(8,128)S(1)}, f32[256,384]{1,0:T(8,128)S(1)}, u32[]{:S(2)}, u32[]{:S(2)}) collective-permute-start(f32[256,384]{1,0:T(8,128)S(1)} %get-tuple-element.51), channel_id=1, source_target_pairs={{0,1},{1,0},{2,3},{3,2},{4,5},{5,4},{6,7},{7,6},{8,9},{9,8},{10,11... | collective-permute-start | bytes 1179656 | tf_op jit(solution)/shard_map/ppermute | solution.py:441
  76.7 16.6 %copy-start.8 = (s32[3]{0:T(128)S(1)}, s32[3]{0:T(128)}, u32[]{:S(2)}) copy-start(s32[3]{0:T(128)} %counts.1) | copy-start | bytes 40
  76.7 7.2 %collective-permute-start.19 = (bf16[256,384]{1,0:T(8,128)(2,1)S(1)}, bf16[256,384]{1,0:T(8,128)(2,1)S(1)}, u32[]{:S(2)}, u32[]{:S(2)}) collective-permute-start(bf16[256,384]{1,0:T(8,128)(2,1)S(1)} %shard_map.88), channel_id=1, source_target_pairs={{0,2},{2,0},{1,3},{3,1},{4,6},{6,4},{5,7},{7,5},{8,10},{10,8},{9,1... | collective-permute-start | bytes 589832 | tf_op jit(solution)/shard_map/ppermute | solution.py:455
  84.0 1.7 %collective-permute-start.20 = (f32[256,384]{1,0:T(8,128)S(1)}, f32[256,384]{1,0:T(8,128)S(1)}, u32[]{:S(2)}, u32[]{:S(2)}) collective-permute-start(f32[256,384]{1,0:T(8,128)S(1)} %get-tuple-element.56), channel_id=1, source_target_pairs={{0,1},{1,0},{2,3},{3,2},{4,5},{5,4},{6,7},{7,6},{8,9},{9,8},{10,11... | collective-permute-start | bytes 1179656 | tf_op jit(solution)/shard_map/ppermute | solution.py:441
  86.3 28.8 %copy-start.9 = (bf16[64,64,256]{2,1,0:T(8,128)(2,1)S(1)}, bf16[64,64,256]{2,1,0:T(8,128)(2,1)}, u32[]{:S(2)}) copy-start(bf16[64,64,256]{2,1,0:T(8,128)(2,1)} %param.13) | copy-start | bytes 6291460
  86.3 28.8 %copy-start.10 = (f32[64,256]{1,0:T(8,128)S(1)}, f32[64,256]{1,0:T(8,128)}, u32[]{:S(2)}) copy-start(f32[64,256]{1,0:T(8,128)} %param.14) | copy-start | bytes 196612
  86.3 7.0 %collective-permute-start.21 = (bf16[256,384]{1,0:T(8,128)(2,1)S(1)}, bf16[256,384]{1,0:T(8,128)(2,1)S(1)}, u32[]{:S(2)}, u32[]{:S(2)}) collective-permute-start(bf16[256,384]{1,0:T(8,128)(2,1)S(1)} %shard_map.90), channel_id=1, source_target_pairs={{0,2},{2,0},{1,3},{3,1},{4,6},{6,4},{5,7},{7,5},{8,10},{10,8},{9,1... | collective-permute-start | bytes 589832 | tf_op jit(solution)/shard_map/ppermute | solution.py:458
  94.5 14.1 %collective-permute-start.22 = (bf16[3,64,256]{2,1,0:T(8,128)(2,1)S(1)}, bf16[3,64,256]{2,1,0:T(8,128)(2,1)S(1)}, u32[]{:S(2)}, u32[]{:S(2)}) collective-permute-start(bf16[3,64,256]{2,1,0:T(8,128)(2,1)S(1)} %get-tuple-element.58), channel_id=1, source_target_pairs={{0,4},{1,5},{4,8},{5,9},{8,12},{9,13},{12,0},{13,1},{2,6},{3,7},{6... | collective-permute-start | bytes 294920 | tf_op jit(solution)/shard_map/ppermute | solution.py:472
  102.8 7.8 %collective-permute-start.23 = (bf16[3,64,256]{2,1,0:T(8,128)(2,1)S(1)}, bf16[3,64,256]{2,1,0:T(8,128)(2,1)S(1)}, u32[]{:S(2)}, u32[]{:S(2)}) collective-permute-start(bf16[3,64,256]{2,1,0:T(8,128)(2,1)S(1)} %get-tuple-element.59), channel_id=1, source_target_pairs={{0,8},{1,9},{4,12},{5,13},{8,0},{9,1},{12,4},{13,5},{2,10},{3,11},... | collective-permute-start | bytes 294920 | tf_op jit(solution)/shard_map/ppermute | solution.py:472
  105.7 11.0 %collective-permute-start.24 = (bf16[3,64,256]{2,1,0:T(8,128)(2,1)S(1)}, bf16[3,64,256]{2,1,0:T(8,128)(2,1)S(1)}, u32[]{:S(2)}, u32[]{:S(2)}) collective-permute-start(bf16[3,64,256]{2,1,0:T(8,128)(2,1)S(1)} %get-tuple-element.60), channel_id=1, source_target_pairs={{0,12},{1,13},{4,0},{5,1},{8,4},{9,5},{12,8},{13,9},{2,14},{3,15},... | collective-permute-start | bytes 294920 | tf_op jit(solution)/shard_map/ppermute | solution.py:472
  108.6 8.2 %collective-permute-start.25 = (bf16[3,64,256]{2,1,0:T(8,128)(2,1)S(1)}, bf16[3,64,256]{2,1,0:T(8,128)(2,1)S(1)}, u32[]{:S(2)}, u32[]{:S(2)}) collective-permute-start(bf16[3,64,256]{2,1,0:T(8,128)(2,1)S(1)} %get-tuple-element.61), channel_id=1, source_target_pairs={{0,1},{1,0},{4,5},{5,4},{8,9},{9,8},{12,13},{13,12},{2,3},{3,2},{6... | collective-permute-start | bytes 294920 | tf_op jit(solution)/shard_map/ppermute | solution.py:472
  108.6 8.2 %collective-permute-start.26 = (bf16[3,64,256]{2,1,0:T(8,128)(2,1)S(1)}, bf16[3,64,256]{2,1,0:T(8,128)(2,1)S(1)}, u32[]{:S(2)}, u32[]{:S(2)}) collective-permute-start(bf16[3,64,256]{2,1,0:T(8,128)(2,1)S(1)} %get-tuple-element.62), channel_id=1, source_target_pairs={{0,5},{1,4},{4,9},{5,8},{8,13},{9,12},{12,1},{13,0},{2,7},{3,6},{6... | collective-permute-start | bytes 294920 | tf_op jit(solution)/shard_map/ppermute | solution.py:472
  108.6 9.3 %collective-permute-start.27 = (bf16[3,64,256]{2,1,0:T(8,128)(2,1)S(1)}, bf16[3,64,256]{2,1,0:T(8,128)(2,1)S(1)}, u32[]{:S(2)}, u32[]{:S(2)}) collective-permute-start(bf16[3,64,256]{2,1,0:T(8,128)(2,1)S(1)} %get-tuple-element.63), channel_id=1, source_target_pairs={{0,9},{1,8},{4,13},{5,12},{8,1},{9,0},{12,5},{13,4},{2,11},{3,10},... | collective-permute-start | bytes 294920 | tf_op jit(solution)/shard_map/ppermute | solution.py:472
  110.6 7.3 %collective-permute-start.28 = (bf16[3,64,256]{2,1,0:T(8,128)(2,1)S(1)}, bf16[3,64,256]{2,1,0:T(8,128)(2,1)S(1)}, u32[]{:S(2)}, u32[]{:S(2)}) collective-permute-start(bf16[3,64,256]{2,1,0:T(8,128)(2,1)S(1)} %get-tuple-element.64), channel_id=1, source_target_pairs={{0,13},{1,12},{4,1},{5,0},{8,5},{9,4},{12,9},{13,8},{2,15},{3,14},... | collective-permute-start | bytes 294920 | tf_op jit(solution)/shard_map/ppermute | solution.py:472
  116.7 11.7 %copy-start.11 = (s32[16,1]{0,1:T(1,128)S(1)}, s32[16,1]{0,1:T(1,128)}, u32[]{:S(2)}) copy-start(s32[16,1]{0,1:T(1,128)} %param.15) | copy-start | bytes 196
  120.1 5.5 %collective-permute-start.29 = (f32[16,4,6]{0,1,2:T(4,128)S(1)}, f32[16,4,6]{0,1,2:T(4,128)S(1)}, u32[]{:S(2)}, u32[]{:S(2)}) collective-permute-start(f32[16,4,6]{0,1,2:T(4,128)S(1)} %bitcast.74), channel_id=1, source_target_pairs={{0,1},{1,2},{2,3},{3,0},{4,5},{5,6},{6,7},{7,4},{8,9},{9,10},{10,1... | collective-permute-start | bytes 4616 | tf_op jit(solution)/shard_map/ppermute | solution.py:63
  123.1 3.7 %collective-permute-start.30 = (f32[16,4,6]{0,1,2:T(4,128)S(1)}, f32[16,4,6]{0,1,2:T(4,128)S(1)}, u32[]{:S(2)}, u32[]{:S(2)}) collective-permute-start(f32[16,4,6]{0,1,2:T(4,128)S(1)} %bitcast.75), channel_id=1, source_target_pairs={{0,2},{1,3},{2,0},{3,1},{4,6},{5,7},{6,4},{7,5},{8,10},{9,11},{10,... | collective-permute-start | bytes 4616 | tf_op jit(solution)/shard_map/ppermute | solution.py:63
  124.6 2.2 %collective-permute-start.31 = (f32[16,4,6]{0,1,2:T(4,128)S(1)}, f32[16,4,6]{0,1,2:T(4,128)S(1)}, u32[]{:S(2)}, u32[]{:S(2)}) collective-permute-start(f32[16,4,6]{0,1,2:T(4,128)S(1)} %bitcast.76), channel_id=1, source_target_pairs={{0,3},{1,0},{2,1},{3,2},{4,7},{5,4},{6,5},{7,6},{8,11},{9,8},{10,9... | collective-permute-start | bytes 4616 | tf_op jit(solution)/shard_map/ppermute | solution.py:63
  127.0 4.6 %collective-permute-start.32 = (f32[16,2,6]{0,1,2:T(2,128)S(1)}, f32[16,2,6]{0,1,2:T(2,128)S(1)}, u32[]{:S(2)}, u32[]{:S(2)}) collective-permute-start(f32[16,2,6]{0,1,2:T(2,128)S(1)} %fusion.6), channel_id=1, source_target_pairs={{0,8},{4,12},{8,0},{12,4},{1,9},{5,13},{9,1},{13,5},{2,10},{6,14},... | collective-permute-start | bytes 2312 | tf_op jit(solution)/shard_map/ppermute | solution.py:74
  131.6 4.1 %collective-permute-start.33 = (f32[16,1,6]{0,1,2:T(1,128)S(1)}, f32[16,1,6]{0,1,2:T(1,128)S(1)}, u32[]{:S(2)}, u32[]{:S(2)}) collective-permute-start(f32[16,1,6]{0,1,2:T(1,128)S(1)} %fusion.12), channel_id=1, source_target_pairs={{0,4},{4,0},{8,12},{12,8},{1,5},{5,1},{9,13},{13,9},{2,6},{6,2},{1... | collective-permute-start | bytes 1160 | tf_op jit(solution)/shard_map/ppermute | solution.py:74

commit v7 on v6

--- a/solution.py
+++ b/solution.py
@@ -423,7 +423,7 @@
     x3 = [hop(after(x, y), 3) for x, y in zip(x2, y1, strict=True)]
 
     g_other, a_other = lax.ppermute(grads, "rep", swap), lax.ppermute(acts, "rep", swap)
-    own_tokens = [after(x, *x2) for x in (grads, acts)]
+    own_tokens = [after(x, *x1) for x in (grads, acts)]
     t_out, t_in = load(*own_tokens)
     g_own, a_own = kernel(
         own_body, [shaped(rows, n_tok)] * 2, [pltpu.VMEM((n_tok, rows), FLOAT)], 2 * rows * n_tok * (d + ff)

time: 137 us -> 136 us (level)
  starting transfers between devices: 76.1 us -> 73.8 us
    ppermute x3, starting transfers between devices: 23.8 us -> 20.4 us  [rotate(): return (mine, lax.ppermute(after(theirs, *before), 'rep', swap))]
where the time goes in v7:
time: 136 us; the launch traced here: 135 us
  starting transfers between devices  73.8 us (54%)
  waiting for transfers between devices  37 us (27%)
  Pallas kernels  12.6 us (9%)
  local copies, waits for them, and re-layouts  8.99 us (7%)
  other arithmetic  2.31 us (2%)
    ppermute x3, starting transfers between devices, rotate(): return (mine, lax.ppermute(after(theirs, *before), 'rep', swap))  20.4 us
    ppermute x7, starting transfers between devices, send(): return lax.ppermute(x, ('wide', 'rep'), pairs)  19.4 us
    ppermute x6, starting transfers between devices, hop(): return lax.ppermute(x, ('wide', 'rep'), hop_pairs(k, n_wide))  13.2 us
    ppermute x1, waiting for transfers between devices, local_fast(): early = lax.ppermute(early, 'layer', swap)  7.62 us
    ppermute x8, starting transfers between devices, to_group(): lax.ppermute(x, ('groups', 'wide', 'rep'), swap_pairs(2 * n_wide, numbers...  7.18 us
    ppermute x6, waiting for transfers between devices, hop(): return lax.ppermute(x, ('wide', 'rep'), hop_pairs(k, n_wide))  6.18 us
    ppermute x1, waiting for transfers between devices, local_fast(): late = lax.ppermute(late, 'layer', swap)  5.45 us
    unnamed x24, local copies, waits for them, and re-layouts  5.41 us
  transfers between devices with their start and end apart: 34, of which 13 were waited for; matrix products, arithmetic and copies ran while one was open for 4% of the time, Pallas kernels for 7%

profile of v7, /device:TPU:0, one launch (start us, length us, event | category | flops | bytes accessed | tf_op | source)
XLA Modules:
  0.0 135.2 jit_solution(17255154108795130537)
XLA Ops:
  0.0 0.5 collective-permute-start.7
  0.5 1.2 dynamic-slice
  1.7 4.5 %collective-permute-start = (bf16[64,4736]{1,0:T(8,128)(2,1)S(1)}, bf16[64,4736]{1,0:T(8,128)(2,1)S(1)}, u32[]{:S(2)}, u32[]{:S(2)}) collective-permute-start(bf16[64,4736]{1,0:T(8,128)(2,1)S(1)} %dynamic-slice), channel_id=1, source_target_pairs={{0,4},{4,8},{8,12},{5,1},{9,5},{13,9},{2,6},{6,10},{10,14},{7,3},{... | collective-permute-start | bytes 1818632 | tf_op jit(solution)/shard_map/ppermute | solution.py:417
  6.3 1.0 constant_dynamic-slice_fusion.5
  7.3 1.0 constant_dynamic-slice_fusion.4
  8.4 3.5 %collective-permute-start.4 = (bf16[64,4736]{1,0:T(8,128)(2,1)S(1)}, bf16[64,4736]{1,0:T(8,128)(2,1)S(1)}, u32[]{:S(2)}, u32[]{:S(2)}) collective-permute-start(bf16[64,4736]{1,0:T(8,128)(2,1)S(1)} %pad_maximum_fusion), channel_id=1, source_target_pairs={{0,4},{4,8},{8,12},{5,1},{9,5},{13,9},{2,6},{6,10},{10,14},{7,3},{... | collective-permute-start | bytes 1818632 | tf_op jit(solution)/shard_map/ppermute | solution.py:417
  11.9 1.9 %collective-permute-done.refs_1_.refs_5_ = bf16[64,4736]{1,0:T(8,128)(2,1)S(1)} collective-permute-done((bf16[64,4736]{1,0:T(8,128)(2,1)S(1)}, bf16[64,4736]{1,0:T(8,128)(2,1)S(1)}, u32[]{:S(2)}, u32[]{:S(2)}) %collective-permute-start) | collective-permute-done | bytes 606240 | tf_op jit(solution)/shard_map/ppermute | solution.py:417
  13.8 0.7 collective-permute-start.2
  14.5 1.5 %collective-permute-start.1 = (bf16[64,4736]{1,0:T(8,128)(2,1)S(1)}, bf16[64,4736]{1,0:T(8,128)(2,1)}, u32[]{:S(2)}, u32[]{:S(2)}) collective-permute-start(bf16[64,4736]{1,0:T(8,128)(2,1)S(1)} %collective-permute-done.refs_1_.refs_5_), channel_id=1, source_target_pairs={{4,8},{8,12},{5,1},{9,5},{6,10},{10,14},{7,3},{11,7},{20,24},{24,2... | collective-permute-start | bytes 1818632 | tf_op jit(solution)/shard_map/ppermute | solution.py:417
  16.0 4.3 %collective-permute-done.4.refs_0_.refs_4_ = bf16[64,4736]{1,0:T(8,128)(2,1)S(1)} collective-permute-done((bf16[64,4736]{1,0:T(8,128)(2,1)S(1)}, bf16[64,4736]{1,0:T(8,128)(2,1)S(1)}, u32[]{:S(2)}, u32[]{:S(2)}) %collective-permute-start.4) | collective-permute-done | bytes 606240 | tf_op jit(solution)/shard_map/ppermute | solution.py:417
  20.3 1.6 %collective-permute-start.5 = (bf16[64,4736]{1,0:T(8,128)(2,1)S(1)}, bf16[64,4736]{1,0:T(8,128)(2,1)}, u32[]{:S(2)}, u32[]{:S(2)}) collective-permute-start(bf16[64,4736]{1,0:T(8,128)(2,1)S(1)} %collective-permute-done.4.refs_0_.refs_4_), channel_id=1, source_target_pairs={{1,17},{5,21},{8,24},{12,28},{17,1},{21,5},{24,8},{28,12},{3,19},{... | collective-permute-start | bytes 1818632 | tf_op jit(solution)/shard_map/ppermute | solution.py:414
  21.8 0.8 copy-done.6
  22.6 1.5 %collective-permute-start.9 = (bf16[64,4736]{1,0:T(8,128)(2,1)S(1)}, bf16[64,4736]{1,0:T(8,128)(2,1)}, u32[]{:S(2)}, u32[]{:S(2)}) collective-permute-start(bf16[64,4736]{1,0:T(8,128)(2,1)S(1)} %collective-permute-done.4.refs_0_.refs_4_), channel_id=1, source_target_pairs={{4,8},{8,12},{5,1},{9,5},{6,10},{10,14},{7,3},{11,7},{20,24},{24,2... | collective-permute-start | bytes 1818632 | tf_op jit(solution)/shard_map/ppermute | solution.py:417
  24.1 1.5 %collective-permute-start.11 = (bf16[64,4736]{1,0:T(8,128)(2,1)}, bf16[64,4736]{1,0:T(8,128)(2,1)}, u32[]{:S(2)}, u32[]{:S(2)}) collective-permute-start(bf16[64,4736]{1,0:T(8,128)(2,1)} %collective-permute-done.1.refs_1_), channel_id=1, source_target_pairs={{1,17},{5,21},{8,24},{12,28},{17,1},{21,5},{24,8},{28,12},{3,19},{... | collective-permute-start | bytes 1818632 | tf_op jit(solution)/shard_map/ppermute | solution.py:414
  25.6 1.3 copy-done.3
  26.8 1.5 %collective-permute-start.3 = (bf16[64,4736]{1,0:T(8,128)(2,1)}, bf16[64,4736]{1,0:T(8,128)(2,1)}, u32[]{:S(2)}, u32[]{:S(2)}) collective-permute-start(bf16[64,4736]{1,0:T(8,128)(2,1)} %collective-permute-done.1.refs_1_), channel_id=1, source_target_pairs={{8,12},{5,1},{10,14},{7,3},{24,28},{21,17},{26,30},{23,19}} | collective-permute-start | bytes 1818632 | tf_op jit(solution)/shard_map/ppermute | solution.py:417
  28.3 0.1 stack.51.at
  28.4 2.5 %copy-done = bf16[3,128,6912]{2,1,0:T(8,128)(2,1)S(1)} copy-done((bf16[3,128,6912]{2,1,0:T(8,128)(2,1)S(1)}, bf16[3,128,6912]{2,1,0:T(8,128)(2,1)}, u32[]{:S(2)}) %copy-start) | copy-done | bytes 5308440
  30.9 0.8 shard_map.82
  31.7 0.8 copy-done.4
  32.5 2.8 %shard_map.84 = (bf16[384,2560]{1,0:T(8,128)(2,1)S(1)}, bf16[384,6912]{1,0:T(8,128)(2,1)S(1)}) custom-call(bf16[384,2560]{1,0:T(8,128)(2,1)S(1)} %bitcast.72, bf16[384,6912]{1,0:T(8,128)(2,1)} %bitcast.12.y_ref), custom_call_target="tpu_custom_call" | custom-call | bytes 1024 | tf_op jit(solution)/shard_map/pallas_call | solution.py:404
  35.3 0.6 shard_map.85
  36.0 10.3 %collective-permute-start.8 = (f32[256,384]{1,0:T(8,128)S(1)}, f32[256,384]{1,0:T(8,128)S(1)}, u32[]{:S(2)}, u32[]{:S(2)}) collective-permute-start(f32[256,384]{1,0:T(8,128)S(1)} %get-tuple-element.46), channel_id=1, source_target_pairs={{0,1},{1,0},{2,3},{3,2},{4,5},{5,4},{6,7},{7,6},{8,9},{9,8},{10,11... | collective-permute-start | bytes 1179656 | tf_op jit(solution)/shard_map/ppermute | solution.py:441
  46.2 0.7 collective-permute-start.16
  46.9 0.7 collective-permute-start.13
  47.7 0.7 collective-permute-start.14
  48.4 0.7 collective-permute-start.10
  49.1 2.1 %shard_map.83 = (f32[128,384]{1,0:T(8,128)S(1)}, f32[128,384]{1,0:T(8,128)S(1)}) custom-call(bf16[128,2560]{1,0:T(8,128)(2,1)S(1)} %copy-done.5, bf16[128,6912]{1,0:T(8,128)(2,1)S(1)} %copy-done.1, bf16[384,2560]{1,0:T(8,128)(2,1)S(1)} %get-tuple-element.39.t_out.refs_4_.refs_8_, bf16[384,6912]{1,0:T(8,128)(2,1)S(1)} %get-tuple-element.40.t_in.refs_5_.refs_9_), custom_call_target="tpu_custom_call" | custom-call | flops 931135 | bytes 1024 | tf_op jit(solution)/shard_map/pallas_call | solution.py:428
  51.2 0.6 shard_map.86
  51.8 1.6 %collective-permute-start.12 = (bf16[512,384]{1,0:T(8,128)(2,1)S(1)}, bf16[512,384]{1,0:T(8,128)(2,1)S(1)}, u32[]{:S(2)}, u32[]{:S(2)}) collective-permute-start(bf16[512,384]{1,0:T(8,128)(2,1)S(1)} %shard_map.86), channel_id=1, source_target_pairs={{0,2},{2,0},{1,3},{3,1},{4,6},{6,4},{5,7},{7,5},{8,10},{10,8},{9,1... | collective-permute-start | bytes 1179656 | tf_op jit(solution)/shard_map/ppermute | solution.py:451
  53.4 0.7 collective-permute-start.18
  54.1 7.6 %collective-permute-done.12.early = bf16[512,384]{1,0:T(8,128)(2,1)S(1)} collective-permute-done((bf16[512,384]{1,0:T(8,128)(2,1)S(1)}, bf16[512,384]{1,0:T(8,128)(2,1)S(1)}, u32[]{:S(2)}, u32[]{:S(2)}) %collective-permute-start.12) | collective-permute-done | bytes 393248 | tf_op jit(solution)/shard_map/ppermute | solution.py:451
  61.7 0.7 collective-permute-start.17
  62.4 0.6 shard_map.87
  63.1 10.1 %collective-permute-start.15 = (f32[256,384]{1,0:T(8,128)S(1)}, f32[256,384]{1,0:T(8,128)S(1)}, u32[]{:S(2)}, u32[]{:S(2)}) collective-permute-start(f32[256,384]{1,0:T(8,128)S(1)} %get-tuple-element.51), channel_id=1, source_target_pairs={{0,1},{1,0},{2,3},{3,2},{4,5},{5,4},{6,7},{7,6},{8,9},{9,8},{10,11... | collective-permute-start | bytes 1179656 | tf_op jit(solution)/shard_map/ppermute | solution.py:441
  73.2 1.3 collective-permute-done.15.both_far
  74.5 0.6 shard_map.88
  75.1 1.6 %collective-permute-start.19 = (bf16[256,384]{1,0:T(8,128)(2,1)S(1)}, bf16[256,384]{1,0:T(8,128)(2,1)S(1)}, u32[]{:S(2)}, u32[]{:S(2)}) collective-permute-start(bf16[256,384]{1,0:T(8,128)(2,1)S(1)} %shard_map.88), channel_id=1, source_target_pairs={{0,2},{2,0},{1,3},{3,1},{4,6},{6,4},{5,7},{7,5},{8,10},{10,8},{9,1... | collective-permute-start | bytes 589832 | tf_op jit(solution)/shard_map/ppermute | solution.py:455
  76.7 0.8 shard_map.89
  77.5 4.9 %collective-permute-done.19.middle = bf16[256,384]{1,0:T(8,128)(2,1)S(1)} collective-permute-done((bf16[256,384]{1,0:T(8,128)(2,1)S(1)}, bf16[256,384]{1,0:T(8,128)(2,1)S(1)}, u32[]{:S(2)}, u32[]{:S(2)}) %collective-permute-start.19) | collective-permute-done | bytes 196640 | tf_op jit(solution)/shard_map/ppermute | solution.py:455
  82.4 1.7 %collective-permute-done.20.last_far = f32[256,384]{1,0:T(8,128)S(1)} collective-permute-done((f32[256,384]{1,0:T(8,128)S(1)}, f32[256,384]{1,0:T(8,128)S(1)}, u32[]{:S(2)}, u32[]{:S(2)}) %collective-permute-start.20) | collective-permute-done | bytes 393248 | tf_op jit(solution)/shard_map/ppermute | solution.py:441
  84.1 0.6 shard_map.90
  84.7 1.6 %collective-permute-start.21 = (bf16[256,384]{1,0:T(8,128)(2,1)S(1)}, bf16[256,384]{1,0:T(8,128)(2,1)S(1)}, u32[]{:S(2)}, u32[]{:S(2)}) collective-permute-start(bf16[256,384]{1,0:T(8,128)(2,1)S(1)} %shard_map.90), channel_id=1, source_target_pairs={{0,2},{2,0},{1,3},{3,1},{4,6},{6,4},{5,7},{7,5},{8,10},{10,8},{9,1... | collective-permute-start | bytes 589832 | tf_op jit(solution)/shard_map/ppermute | solution.py:458
  86.3 5.4 %collective-permute-done.21.late = bf16[256,384]{1,0:T(8,128)(2,1)S(1)} collective-permute-done((bf16[256,384]{1,0:T(8,128)(2,1)S(1)}, bf16[256,384]{1,0:T(8,128)(2,1)S(1)}, u32[]{:S(2)}, u32[]{:S(2)}) %collective-permute-start.21) | collective-permute-done | bytes 196640 | tf_op jit(solution)/shard_map/ppermute | solution.py:458
  91.7 1.1 shard_map.91
  92.9 7.6 %collective-permute-start.22 = (bf16[3,64,256]{2,1,0:T(8,128)(2,1)S(1)}, bf16[3,64,256]{2,1,0:T(8,128)(2,1)S(1)}, u32[]{:S(2)}, u32[]{:S(2)}) collective-permute-start(bf16[3,64,256]{2,1,0:T(8,128)(2,1)S(1)} %get-tuple-element.58), channel_id=1, source_target_pairs={{0,4},{1,5},{4,8},{5,9},{8,12},{9,13},{12,0},{13,1},{2,6},{3,7},{6... | collective-permute-start | bytes 294920 | tf_op jit(solution)/shard_map/ppermute | solution.py:472
  100.4 4.1 %collective-permute-start.23 = (bf16[3,64,256]{2,1,0:T(8,128)(2,1)S(1)}, bf16[3,64,256]{2,1,0:T(8,128)(2,1)S(1)}, u32[]{:S(2)}, u32[]{:S(2)}) collective-permute-start(bf16[3,64,256]{2,1,0:T(8,128)(2,1)S(1)} %get-tuple-element.59), channel_id=1, source_target_pairs={{0,8},{1,9},{4,12},{5,13},{8,0},{9,1},{12,4},{13,5},{2,10},{3,11},... | collective-permute-start | bytes 294920 | tf_op jit(solution)/shard_map/ppermute | solution.py:472
  104.5 2.8 %collective-permute-start.24 = (bf16[3,64,256]{2,1,0:T(8,128)(2,1)S(1)}, bf16[3,64,256]{2,1,0:T(8,128)(2,1)S(1)}, u32[]{:S(2)}, u32[]{:S(2)}) collective-permute-start(bf16[3,64,256]{2,1,0:T(8,128)(2,1)S(1)} %get-tuple-element.60), channel_id=1, source_target_pairs={{0,12},{1,13},{4,0},{5,1},{8,4},{9,5},{12,8},{13,9},{2,14},{3,15},... | collective-permute-start | bytes 294920 | tf_op jit(solution)/shard_map/ppermute | solution.py:472
  107.4 0.3 collective-permute-start.27
  107.7 1.7 %collective-permute-done.23.refs_2_ = bf16[3,64,256]{2,1,0:T(8,128)(2,1)S(1)} collective-permute-done((bf16[3,64,256]{2,1,0:T(8,128)(2,1)S(1)}, bf16[3,64,256]{2,1,0:T(8,128)(2,1)S(1)}, u32[]{:S(2)}, u32[]{:S(2)}) %collective-permute-start.23) | collective-permute-done | bytes 98336 | tf_op jit(solution)/shard_map/ppermute | solution.py:472
  109.4 4.6 %collective-permute-start.28 = (bf16[3,64,256]{2,1,0:T(8,128)(2,1)S(1)}, bf16[3,64,256]{2,1,0:T(8,128)(2,1)S(1)}, u32[]{:S(2)}, u32[]{:S(2)}) collective-permute-start(bf16[3,64,256]{2,1,0:T(8,128)(2,1)S(1)} %get-tuple-element.64), channel_id=1, source_target_pairs={{0,13},{1,12},{4,1},{5,0},{8,5},{9,4},{12,9},{13,8},{2,15},{3,14},... | collective-permute-start | bytes 294920 | tf_op jit(solution)/shard_map/ppermute | solution.py:472
  114.0 1.5 %fusion.weights = bf16[64,64,256]{2,1,0:T(8,128)(2,1)S(1)} fusion(bf16[64,64,256]{2,1,0:T(8,128)(2,1)S(1)} %copy-done.9, f32[64,256]{1,0:T(8,128)S(1)} %copy-done.10), kind=kLoop, calls=%fused_computation.1 | loop fusion | flops 3145728 | bytes 4259840 | tf_op jit(solution)/shard_map/transpose | solution.py:396
  115.6 1.1 collective-permute-done.27.refs_6_
  116.7 2.0 %shard_map.92 = f32[64,24]{1,0:T(8,128)S(1)} custom-call(s32[8]{0:T(128)S(1)} %stack.51.at, bf16[64,64,256]{2,1,0:T(8,128)(2,1)S(1)} %fusion.weights, bf16[3,64,256]{2,1,0:T(8,128)(2,1)S(1)} %get-tuple-element.57.refs_0_, bf16[3,64,256]{2,1,0:T(8,128)(2,1)S(1)} %collective-permute-done.22.refs_1_, bf16[3,64,256]{2,1,0:T(8,128)(2,1)S(1)} %collective-permute-done.23.refs_2_, ...), custom_call_target="tpu_custom_call" | custom-call | flops 50331 | bytes 1024 | tf_op jit(solution)/shard_map/pallas_call | solution.py:477
  118.8 0.1 reshape_reshape.3
  118.9 3.0 %collective-permute-start.29 = (f32[16,4,6]{0,1,2:T(4,128)S(1)}, f32[16,4,6]{0,1,2:T(4,128)S(1)}, u32[]{:S(2)}, u32[]{:S(2)}) collective-permute-start(f32[16,4,6]{0,1,2:T(4,128)S(1)} %bitcast.75), channel_id=1, source_target_pairs={{0,1},{1,2},{2,3},{3,0},{4,5},{5,6},{6,7},{7,4},{8,9},{9,10},{10,1... | collective-permute-start | bytes 4616 | tf_op jit(solution)/shard_map/ppermute | solution.py:63
  121.9 1.5 %collective-permute-start.30 = (f32[16,4,6]{0,1,2:T(4,128)S(1)}, f32[16,4,6]{0,1,2:T(4,128)S(1)}, u32[]{:S(2)}, u32[]{:S(2)}) collective-permute-start(f32[16,4,6]{0,1,2:T(4,128)S(1)} %bitcast.76), channel_id=1, source_target_pairs={{0,2},{1,3},{2,0},{3,1},{4,6},{5,7},{6,4},{7,5},{8,10},{9,11},{10,... | collective-permute-start | bytes 4616 | tf_op jit(solution)/shard_map/ppermute | solution.py:63
  123.4 1.0 collective-permute-done.29
  124.4 1.2 collective-permute-done.30
  125.8 1.4 %collective-permute-start.32 = (f32[16,2,6]{0,1,2:T(2,128)S(1)}, f32[16,2,6]{0,1,2:T(2,128)S(1)}, u32[]{:S(2)}, u32[]{:S(2)}) collective-permute-start(f32[16,2,6]{0,1,2:T(2,128)S(1)} %fusion.6), channel_id=1, source_target_pairs={{0,8},{4,12},{8,0},{12,4},{1,9},{5,13},{9,1},{13,5},{2,10},{6,14},... | collective-permute-start | bytes 2312 | tf_op jit(solution)/shard_map/ppermute | solution.py:74
  127.2 3.2 %collective-permute-done.32 = f32[16,2,6]{0,1,2:T(2,128)S(1)} collective-permute-done((f32[16,2,6]{0,1,2:T(2,128)S(1)}, f32[16,2,6]{0,1,2:T(2,128)S(1)}, u32[]{:S(2)}, u32[]{:S(2)}) %collective-permute-start.32) | collective-permute-done | bytes 800 | tf_op jit(solution)/shard_map/ppermute | solution.py:74
  130.4 2.6 %collective-permute-start.33 = (f32[16,1,6]{0,1,2:T(1,128)S(1)}, f32[16,1,6]{0,1,2:T(1,128)S(1)}, u32[]{:S(2)}, u32[]{:S(2)}) collective-permute-start(f32[16,1,6]{0,1,2:T(1,128)S(1)} %fusion.12), channel_id=1, source_target_pairs={{0,4},{4,0},{8,12},{12,8},{1,5},{5,1},{9,13},{13,9},{2,6},{6,2},{1... | collective-permute-start | bytes 1160 | tf_op jit(solution)/shard_map/ppermute | solution.py:74
  133.0 1.6 %collective-permute-done.33 = f32[16,1,6]{0,1,2:T(1,128)S(1)} collective-permute-done((f32[16,1,6]{0,1,2:T(1,128)S(1)}, f32[16,1,6]{0,1,2:T(1,128)S(1)}, u32[]{:S(2)}, u32[]{:S(2)}) %collective-permute-start.33) | collective-permute-done | bytes 416 | tf_op jit(solution)/shard_map/ppermute | solution.py:74
  134.5 0.7 bitcast_multiply_fusion
  (63 shorter events, 0.6 us)
Async XLA Ops:
  0.0 28.4 %copy-start.2 = (bf16[3,128,2560]{2,1,0:T(8,128)(2,1)S(1)}, bf16[3,128,2560]{2,1,0:T(8,128)(2,1)}, u32[]{:S(2)}) copy-start(bf16[3,128,2560]{2,1,0:T(8,128)(2,1)} %param.9) | copy-start | bytes 5898244
  0.0 31.7 %collective-permute-start.7 = (bf16[3,128,6912]{2,1,0:T(8,128)(2,1)}, bf16[3,128,6912]{2,1,0:T(8,128)(2,1)}, u32[]{:S(2)}, u32[]{:S(2)}) collective-permute-start(bf16[3,128,6912]{2,1,0:T(8,128)(2,1)} %param.8), channel_id=1, source_target_pairs={{0,1},{1,0},{2,3},{3,2},{4,5},{5,4},{6,7},{7,6},{8,9},{9,8},{10,11... | collective-permute-start | bytes 15925256 | tf_op jit(solution)/shard_map/ppermute | solution.py:425
  1.7 12.1 %collective-permute-start = (bf16[64,4736]{1,0:T(8,128)(2,1)S(1)}, bf16[64,4736]{1,0:T(8,128)(2,1)S(1)}, u32[]{:S(2)}, u32[]{:S(2)}) collective-permute-start(bf16[64,4736]{1,0:T(8,128)(2,1)S(1)} %dynamic-slice), channel_id=1, source_target_pairs={{0,4},{4,8},{8,12},{5,1},{9,5},{13,9},{2,6},{6,10},{10,14},{7,3},{... | collective-permute-start | bytes 1818632 | tf_op jit(solution)/shard_map/ppermute | solution.py:417
  6.2 19.3 %collective-permute-start.6 = (bf16[3,128,2560]{2,1,0:T(8,128)(2,1)}, bf16[3,128,2560]{2,1,0:T(8,128)(2,1)S(1)}, u32[]{:S(2)}, u32[]{:S(2)}) collective-permute-start(bf16[3,128,2560]{2,1,0:T(8,128)(2,1)} %param.9), channel_id=1, source_target_pairs={{0,1},{1,0},{2,3},{3,2},{4,5},{5,4},{6,7},{7,6},{8,9},{9,8},{10,11... | collective-permute-start | bytes 5898248 | tf_op jit(solution)/shard_map/ppermute | solution.py:425
  8.4 11.9 %collective-permute-start.4 = (bf16[64,4736]{1,0:T(8,128)(2,1)S(1)}, bf16[64,4736]{1,0:T(8,128)(2,1)S(1)}, u32[]{:S(2)}, u32[]{:S(2)}) collective-permute-start(bf16[64,4736]{1,0:T(8,128)(2,1)S(1)} %pad_maximum_fusion), channel_id=1, source_target_pairs={{0,4},{4,8},{8,12},{5,1},{9,5},{13,9},{2,6},{6,10},{10,14},{7,3},{... | collective-permute-start | bytes 1818632 | tf_op jit(solution)/shard_map/ppermute | solution.py:417
  13.8 8.0 %collective-permute-start.2 = (bf16[64,4736]{1,0:T(8,128)(2,1)S(1)}, bf16[64,4736]{1,0:T(8,128)(2,1)S(1)}, u32[]{:S(2)}, u32[]{:S(2)}) collective-permute-start(bf16[64,4736]{1,0:T(8,128)(2,1)S(1)} %collective-permute-done.refs_1_.refs_5_), channel_id=1, source_target_pairs={{1,17},{5,21},{8,24},{12,28},{17,1},{21,5},{24,8},{28,12},{3,19},{... | collective-permute-start | bytes 1818632 | tf_op jit(solution)/shard_map/ppermute | solution.py:414
  14.5 9.7 %collective-permute-start.1 = (bf16[64,4736]{1,0:T(8,128)(2,1)S(1)}, bf16[64,4736]{1,0:T(8,128)(2,1)}, u32[]{:S(2)}, u32[]{:S(2)}) collective-permute-start(bf16[64,4736]{1,0:T(8,128)(2,1)S(1)} %collective-permute-done.refs_1_.refs_5_), channel_id=1, source_target_pairs={{4,8},{8,12},{5,1},{9,5},{6,10},{10,14},{7,3},{11,7},{20,24},{24,2... | collective-permute-start | bytes 1818632 | tf_op jit(solution)/shard_map/ppermute | solution.py:417
  20.3 15.1 %collective-permute-start.5 = (bf16[64,4736]{1,0:T(8,128)(2,1)S(1)}, bf16[64,4736]{1,0:T(8,128)(2,1)}, u32[]{:S(2)}, u32[]{:S(2)}) collective-permute-start(bf16[64,4736]{1,0:T(8,128)(2,1)S(1)} %collective-permute-done.4.refs_0_.refs_4_), channel_id=1, source_target_pairs={{1,17},{5,21},{8,24},{12,28},{17,1},{21,5},{24,8},{28,12},{3,19},{... | collective-permute-start | bytes 1818632 | tf_op jit(solution)/shard_map/ppermute | solution.py:414
  21.8 0.8 copy-start.6
  22.6 23.6 %collective-permute-start.9 = (bf16[64,4736]{1,0:T(8,128)(2,1)S(1)}, bf16[64,4736]{1,0:T(8,128)(2,1)}, u32[]{:S(2)}, u32[]{:S(2)}) collective-permute-start(bf16[64,4736]{1,0:T(8,128)(2,1)S(1)} %collective-permute-done.4.refs_0_.refs_4_), channel_id=1, source_target_pairs={{4,8},{8,12},{5,1},{9,5},{6,10},{10,14},{7,3},{11,7},{20,24},{24,2... | collective-permute-start | bytes 1818632 | tf_op jit(solution)/shard_map/ppermute | solution.py:417
  24.1 23.5 %collective-permute-start.11 = (bf16[64,4736]{1,0:T(8,128)(2,1)}, bf16[64,4736]{1,0:T(8,128)(2,1)}, u32[]{:S(2)}, u32[]{:S(2)}) collective-permute-start(bf16[64,4736]{1,0:T(8,128)(2,1)} %collective-permute-done.1.refs_1_), channel_id=1, source_target_pairs={{1,17},{5,21},{8,24},{12,28},{17,1},{21,5},{24,8},{28,12},{3,19},{... | collective-permute-start | bytes 1818632 | tf_op jit(solution)/shard_map/ppermute | solution.py:414
  25.6 1.3 copy-start.3
  26.8 25.0 %collective-permute-start.3 = (bf16[64,4736]{1,0:T(8,128)(2,1)}, bf16[64,4736]{1,0:T(8,128)(2,1)}, u32[]{:S(2)}, u32[]{:S(2)}) collective-permute-start(bf16[64,4736]{1,0:T(8,128)(2,1)} %collective-permute-done.1.refs_1_), channel_id=1, source_target_pairs={{8,12},{5,1},{10,14},{7,3},{24,28},{21,17},{26,30},{23,19}} | collective-permute-start | bytes 1818632 | tf_op jit(solution)/shard_map/ppermute | solution.py:417
  28.4 2.5 %copy-start = (bf16[3,128,6912]{2,1,0:T(8,128)(2,1)S(1)}, bf16[3,128,6912]{2,1,0:T(8,128)(2,1)}, u32[]{:S(2)}) copy-start(bf16[3,128,6912]{2,1,0:T(8,128)(2,1)} %param.8) | copy-start | bytes 15925252
  30.9 1.5 %copy-start.4 = (bf16[3,128,2560]{2,1,0:T(8,128)(2,1)S(1)}, bf16[3,128,2560]{2,1,0:T(8,128)(2,1)}, u32[]{:S(2)}) copy-start(bf16[3,128,2560]{2,1,0:T(8,128)(2,1)} %copy-done.3) | copy-start | bytes 5898244
  32.5 2.8 %copy-start.7 = (bf16[64,4736]{1,0:T(8,128)(2,1)S(1)}, bf16[64,4736]{1,0:T(8,128)(2,1)}, u32[]{:S(2)}) copy-start(bf16[64,4736]{1,0:T(8,128)(2,1)} %copy-done.6) | copy-start | bytes 1818628
  35.3 13.8 %copy-start.1 = (bf16[128,6912]{1,0:T(8,128)(2,1)S(1)}, bf16[128,6912]{1,0:T(8,128)(2,1)}, u32[]{:S(2)}) copy-start(bf16[128,6912]{1,0:T(8,128)(2,1)} %b_in.1) | copy-start | bytes 5308420
  35.3 13.8 %copy-start.5 = (bf16[128,2560]{1,0:T(8,128)(2,1)S(1)}, bf16[128,2560]{1,0:T(8,128)(2,1)}, u32[]{:S(2)}) copy-start(bf16[128,2560]{1,0:T(8,128)(2,1)} %b_out.1) | copy-start | bytes 1966084
  36.0 12.4 %collective-permute-start.8 = (f32[256,384]{1,0:T(8,128)S(1)}, f32[256,384]{1,0:T(8,128)S(1)}, u32[]{:S(2)}, u32[]{:S(2)}) collective-permute-start(f32[256,384]{1,0:T(8,128)S(1)} %get-tuple-element.46), channel_id=1, source_target_pairs={{0,1},{1,0},{2,3},{3,2},{4,5},{5,4},{6,7},{7,6},{8,9},{9,8},{10,11... | collective-permute-start | bytes 1179656 | tf_op jit(solution)/shard_map/ppermute | solution.py:441
  46.2 7.1 %collective-permute-start.16 = (bf16[64,4736]{1,0:T(8,128)(2,1)}, bf16[64,4736]{1,0:T(8,128)(2,1)S(1)}, u32[]{:S(2)}, u32[]{:S(2)}) collective-permute-start(bf16[64,4736]{1,0:T(8,128)(2,1)} %collective-permute-done.9.refs_0_), channel_id=1, source_target_pairs={{8,12},{5,1},{10,14},{7,3},{24,28},{21,17},{26,30},{23,19}} | collective-permute-start | bytes 1818632 | tf_op jit(solution)/shard_map/ppermute | solution.py:417
  46.9 15.5 %collective-permute-start.13 = (bf16[64,4736]{1,0:T(8,128)(2,1)S(1)}, bf16[64,4736]{1,0:T(8,128)(2,1)S(1)}, u32[]{:S(2)}, u32[]{:S(2)}) collective-permute-start(bf16[64,4736]{1,0:T(8,128)(2,1)S(1)} %collective-permute-done.4.refs_0_.refs_4_), channel_id=1, source_target_pairs={{4,20},{9,25},{20,4},{25,9},{6,22},{11,27},{22,6},{27,11}} | collective-permute-start | bytes 1818632 | tf_op jit(solution)/shard_map/ppermute | solution.py:414
  47.7 14.8 %collective-permute-start.14 = (bf16[64,4736]{1,0:T(8,128)(2,1)S(1)}, bf16[64,4736]{1,0:T(8,128)(2,1)S(1)}, u32[]{:S(2)}, u32[]{:S(2)}) collective-permute-start(bf16[64,4736]{1,0:T(8,128)(2,1)S(1)} %collective-permute-done.refs_1_.refs_5_), channel_id=1, source_target_pairs={{4,20},{9,25},{20,4},{25,9},{6,22},{11,27},{22,6},{27,11}} | collective-permute-start | bytes 1818632 | tf_op jit(solution)/shard_map/ppermute | solution.py:414
  48.4 14.1 %collective-permute-start.10 = (bf16[64,4736]{1,0:T(8,128)(2,1)}, bf16[64,4736]{1,0:T(8,128)(2,1)S(1)}, u32[]{:S(2)}, u32[]{:S(2)}) collective-permute-start(bf16[64,4736]{1,0:T(8,128)(2,1)} %collective-permute-done.9.refs_0_), channel_id=1, source_target_pairs={{1,17},{5,21},{8,24},{12,28},{17,1},{21,5},{24,8},{28,12},{3,19},{... | collective-permute-start | bytes 1818632 | tf_op jit(solution)/shard_map/ppermute | solution.py:414
  51.8 9.9 %collective-permute-start.12 = (bf16[512,384]{1,0:T(8,128)(2,1)S(1)}, bf16[512,384]{1,0:T(8,128)(2,1)S(1)}, u32[]{:S(2)}, u32[]{:S(2)}) collective-permute-start(bf16[512,384]{1,0:T(8,128)(2,1)S(1)} %shard_map.86), channel_id=1, source_target_pairs={{0,2},{2,0},{1,3},{3,1},{4,6},{6,4},{5,7},{7,5},{8,10},{10,8},{9,1... | collective-permute-start | bytes 1179656 | tf_op jit(solution)/shard_map/ppermute | solution.py:451
  53.4 23.3 %collective-permute-start.18 = (bf16[64,4736]{1,0:T(8,128)(2,1)}, bf16[64,4736]{1,0:T(8,128)(2,1)S(1)}, u32[]{:S(2)}, u32[]{:S(2)}) collective-permute-start(bf16[64,4736]{1,0:T(8,128)(2,1)} %collective-permute-done.3.refs_1_), channel_id=1, source_target_pairs={{1,17},{12,28},{17,1},{28,12},{3,19},{14,30},{19,3},{30,14}} | collective-permute-start | bytes 1818632 | tf_op jit(solution)/shard_map/ppermute | solution.py:414
  61.7 15.0 %collective-permute-start.17 = (bf16[64,4736]{1,0:T(8,128)(2,1)S(1)}, bf16[64,4736]{1,0:T(8,128)(2,1)S(1)}, u32[]{:S(2)}, u32[]{:S(2)}) collective-permute-start(bf16[64,4736]{1,0:T(8,128)(2,1)S(1)} %collective-permute-done.16.refs_0_), channel_id=1, source_target_pairs={{1,17},{12,28},{17,1},{28,12},{3,19},{14,30},{19,3},{30,14}} | collective-permute-start | bytes 1818632 | tf_op jit(solution)/shard_map/ppermute | solution.py:414
  63.1 11.4 %collective-permute-start.15 = (f32[256,384]{1,0:T(8,128)S(1)}, f32[256,384]{1,0:T(8,128)S(1)}, u32[]{:S(2)}, u32[]{:S(2)}) collective-permute-start(f32[256,384]{1,0:T(8,128)S(1)} %get-tuple-element.51), channel_id=1, source_target_pairs={{0,1},{1,0},{2,3},{3,2},{4,5},{5,4},{6,7},{7,6},{8,9},{9,8},{10,11... | collective-permute-start | bytes 1179656 | tf_op jit(solution)/shard_map/ppermute | solution.py:441
  75.1 16.6 %copy-start.8 = (s32[3]{0:T(128)S(1)}, s32[3]{0:T(128)}, u32[]{:S(2)}) copy-start(s32[3]{0:T(128)} %counts.1) | copy-start | bytes 40
  75.1 7.2 %collective-permute-start.19 = (bf16[256,384]{1,0:T(8,128)(2,1)S(1)}, bf16[256,384]{1,0:T(8,128)(2,1)S(1)}, u32[]{:S(2)}, u32[]{:S(2)}) collective-permute-start(bf16[256,384]{1,0:T(8,128)(2,1)S(1)} %shard_map.88), channel_id=1, source_target_pairs={{0,2},{2,0},{1,3},{3,1},{4,6},{6,4},{5,7},{7,5},{8,10},{10,8},{9,1... | collective-permute-start | bytes 589832 | tf_op jit(solution)/shard_map/ppermute | solution.py:455
  82.4 1.7 %collective-permute-start.20 = (f32[256,384]{1,0:T(8,128)S(1)}, f32[256,384]{1,0:T(8,128)S(1)}, u32[]{:S(2)}, u32[]{:S(2)}) collective-permute-start(f32[256,384]{1,0:T(8,128)S(1)} %get-tuple-element.56), channel_id=1, source_target_pairs={{0,1},{1,0},{2,3},{3,2},{4,5},{5,4},{6,7},{7,6},{8,9},{9,8},{10,11... | collective-permute-start | bytes 1179656 | tf_op jit(solution)/shard_map/ppermute | solution.py:441
  84.7 29.3 %copy-start.9 = (bf16[64,64,256]{2,1,0:T(8,128)(2,1)S(1)}, bf16[64,64,256]{2,1,0:T(8,128)(2,1)}, u32[]{:S(2)}) copy-start(bf16[64,64,256]{2,1,0:T(8,128)(2,1)} %param.13) | copy-start | bytes 6291460
  84.7 29.3 %copy-start.10 = (f32[64,256]{1,0:T(8,128)S(1)}, f32[64,256]{1,0:T(8,128)}, u32[]{:S(2)}) copy-start(f32[64,256]{1,0:T(8,128)} %param.14) | copy-start | bytes 196612
  84.7 7.0 %collective-permute-start.21 = (bf16[256,384]{1,0:T(8,128)(2,1)S(1)}, bf16[256,384]{1,0:T(8,128)(2,1)S(1)}, u32[]{:S(2)}, u32[]{:S(2)}) collective-permute-start(bf16[256,384]{1,0:T(8,128)(2,1)S(1)} %shard_map.90), channel_id=1, source_target_pairs={{0,2},{2,0},{1,3},{3,1},{4,6},{6,4},{5,7},{7,5},{8,10},{10,8},{9,1... | collective-permute-start | bytes 589832 | tf_op jit(solution)/shard_map/ppermute | solution.py:458
  92.9 14.5 %collective-permute-start.22 = (bf16[3,64,256]{2,1,0:T(8,128)(2,1)S(1)}, bf16[3,64,256]{2,1,0:T(8,128)(2,1)S(1)}, u32[]{:S(2)}, u32[]{:S(2)}) collective-permute-start(bf16[3,64,256]{2,1,0:T(8,128)(2,1)S(1)} %get-tuple-element.58), channel_id=1, source_target_pairs={{0,4},{1,5},{4,8},{5,9},{8,12},{9,13},{12,0},{13,1},{2,6},{3,7},{6... | collective-permute-start | bytes 294920 | tf_op jit(solution)/shard_map/ppermute | solution.py:472
  100.4 8.9 %collective-permute-start.23 = (bf16[3,64,256]{2,1,0:T(8,128)(2,1)S(1)}, bf16[3,64,256]{2,1,0:T(8,128)(2,1)S(1)}, u32[]{:S(2)}, u32[]{:S(2)}) collective-permute-start(bf16[3,64,256]{2,1,0:T(8,128)(2,1)S(1)} %get-tuple-element.59), channel_id=1, source_target_pairs={{0,8},{1,9},{4,12},{5,13},{8,0},{9,1},{12,4},{13,5},{2,10},{3,11},... | collective-permute-start | bytes 294920 | tf_op jit(solution)/shard_map/ppermute | solution.py:472
  104.5 11.0 %collective-permute-start.24 = (bf16[3,64,256]{2,1,0:T(8,128)(2,1)S(1)}, bf16[3,64,256]{2,1,0:T(8,128)(2,1)S(1)}, u32[]{:S(2)}, u32[]{:S(2)}) collective-permute-start(bf16[3,64,256]{2,1,0:T(8,128)(2,1)S(1)} %get-tuple-element.60), channel_id=1, source_target_pairs={{0,12},{1,13},{4,0},{5,1},{8,4},{9,5},{12,8},{13,9},{2,14},{3,15},... | collective-permute-start | bytes 294920 | tf_op jit(solution)/shard_map/ppermute | solution.py:472
  107.4 8.2 %collective-permute-start.25 = (bf16[3,64,256]{2,1,0:T(8,128)(2,1)S(1)}, bf16[3,64,256]{2,1,0:T(8,128)(2,1)S(1)}, u32[]{:S(2)}, u32[]{:S(2)}) collective-permute-start(bf16[3,64,256]{2,1,0:T(8,128)(2,1)S(1)} %get-tuple-element.61), channel_id=1, source_target_pairs={{0,1},{1,0},{4,5},{5,4},{8,9},{9,8},{12,13},{13,12},{2,3},{3,2},{6... | collective-permute-start | bytes 294920 | tf_op jit(solution)/shard_map/ppermute | solution.py:472
  107.4 8.2 %collective-permute-start.26 = (bf16[3,64,256]{2,1,0:T(8,128)(2,1)S(1)}, bf16[3,64,256]{2,1,0:T(8,128)(2,1)S(1)}, u32[]{:S(2)}, u32[]{:S(2)}) collective-permute-start(bf16[3,64,256]{2,1,0:T(8,128)(2,1)S(1)} %get-tuple-element.62), channel_id=1, source_target_pairs={{0,5},{1,4},{4,9},{5,8},{8,13},{9,12},{12,1},{13,0},{2,7},{3,6},{6... | collective-permute-start | bytes 294920 | tf_op jit(solution)/shard_map/ppermute | solution.py:472
  107.4 9.3 %collective-permute-start.27 = (bf16[3,64,256]{2,1,0:T(8,128)(2,1)S(1)}, bf16[3,64,256]{2,1,0:T(8,128)(2,1)S(1)}, u32[]{:S(2)}, u32[]{:S(2)}) collective-permute-start(bf16[3,64,256]{2,1,0:T(8,128)(2,1)S(1)} %get-tuple-element.63), channel_id=1, source_target_pairs={{0,9},{1,8},{4,13},{5,12},{8,1},{9,0},{12,5},{13,4},{2,11},{3,10},... | collective-permute-start | bytes 294920 | tf_op jit(solution)/shard_map/ppermute | solution.py:472
  109.4 7.3 %collective-permute-start.28 = (bf16[3,64,256]{2,1,0:T(8,128)(2,1)S(1)}, bf16[3,64,256]{2,1,0:T(8,128)(2,1)S(1)}, u32[]{:S(2)}, u32[]{:S(2)}) collective-permute-start(bf16[3,64,256]{2,1,0:T(8,128)(2,1)S(1)} %get-tuple-element.64), channel_id=1, source_target_pairs={{0,13},{1,12},{4,1},{5,0},{8,5},{9,4},{12,9},{13,8},{2,15},{3,14},... | collective-permute-start | bytes 294920 | tf_op jit(solution)/shard_map/ppermute | solution.py:472
  115.5 11.7 %copy-start.11 = (s32[16,1]{0,1:T(1,128)S(1)}, s32[16,1]{0,1:T(1,128)}, u32[]{:S(2)}) copy-start(s32[16,1]{0,1:T(1,128)} %param.15) | copy-start | bytes 196
  118.9 5.5 %collective-permute-start.29 = (f32[16,4,6]{0,1,2:T(4,128)S(1)}, f32[16,4,6]{0,1,2:T(4,128)S(1)}, u32[]{:S(2)}, u32[]{:S(2)}) collective-permute-start(f32[16,4,6]{0,1,2:T(4,128)S(1)} %bitcast.75), channel_id=1, source_target_pairs={{0,1},{1,2},{2,3},{3,0},{4,5},{5,6},{6,7},{7,4},{8,9},{9,10},{10,1... | collective-permute-start | bytes 4616 | tf_op jit(solution)/shard_map/ppermute | solution.py:63
  121.9 3.7 %collective-permute-start.30 = (f32[16,4,6]{0,1,2:T(4,128)S(1)}, f32[16,4,6]{0,1,2:T(4,128)S(1)}, u32[]{:S(2)}, u32[]{:S(2)}) collective-permute-start(f32[16,4,6]{0,1,2:T(4,128)S(1)} %bitcast.76), channel_id=1, source_target_pairs={{0,2},{1,3},{2,0},{3,1},{4,6},{5,7},{6,4},{7,5},{8,10},{9,11},{10,... | collective-permute-start | bytes 4616 | tf_op jit(solution)/shard_map/ppermute | solution.py:63
  123.4 2.2 %collective-permute-start.31 = (f32[16,4,6]{0,1,2:T(4,128)S(1)}, f32[16,4,6]{0,1,2:T(4,128)S(1)}, u32[]{:S(2)}, u32[]{:S(2)}) collective-permute-start(f32[16,4,6]{0,1,2:T(4,128)S(1)} %bitcast.77), channel_id=1, source_target_pairs={{0,3},{1,0},{2,1},{3,2},{4,7},{5,4},{6,5},{7,6},{8,11},{9,8},{10,9... | collective-permute-start | bytes 4616 | tf_op jit(solution)/shard_map/ppermute | solution.py:63
  125.8 4.6 %collective-permute-start.32 = (f32[16,2,6]{0,1,2:T(2,128)S(1)}, f32[16,2,6]{0,1,2:T(2,128)S(1)}, u32[]{:S(2)}, u32[]{:S(2)}) collective-permute-start(f32[16,2,6]{0,1,2:T(2,128)S(1)} %fusion.6), channel_id=1, source_target_pairs={{0,8},{4,12},{8,0},{12,4},{1,9},{5,13},{9,1},{13,5},{2,10},{6,14},... | collective-permute-start | bytes 2312 | tf_op jit(solution)/shard_map/ppermute | solution.py:74
  130.4 4.1 %collective-permute-start.33 = (f32[16,1,6]{0,1,2:T(1,128)S(1)}, f32[16,1,6]{0,1,2:T(1,128)S(1)}, u32[]{:S(2)}, u32[]{:S(2)}) collective-permute-start(f32[16,1,6]{0,1,2:T(1,128)S(1)} %fusion.12), channel_id=1, source_target_pairs={{0,4},{4,0},{8,12},{12,8},{1,5},{5,1},{9,13},{13,9},{2,6},{6,2},{1... | collective-permute-start | bytes 1160 | tf_op jit(solution)/shard_map/ppermute | solution.py:74

commit v8 on v7

--- a/solution.py
+++ b/solution.py
@@ -176,7 +176,7 @@
         out_shape=out_shape,
         scratch_shapes=list(scratch),
         compiler_params=pltpu.CompilerParams(vmem_limit_bytes=grant * 1024 * 1024),
-        cost_estimate=pl.CostEstimate(flops=flops // 1000, bytes_accessed=1024, transcendentals=0),
+        cost_estimate=pl.CostEstimate(flops=flops, bytes_accessed=flops // 200, transcendentals=0),
     )
 
 

time: 136 us -> 133 us (0.978)
  local copies, waits for them, and re-layouts: 8.99 us -> 6.98 us
  starting transfers between devices: 73.8 us -> 72.1 us
    unnamed x24 -> x20, local copies, waits for them, and re-layouts: 5.41 us -> 3.4 us
    ppermute x7, starting transfers between devices: 19.4 us -> 17.7 us  [send(): return lax.ppermute(x, ('wide', 'rep'), pairs)]
where the time goes in v8:
time: 133 us
  starting transfers between devices  72.1 us (54%)
  waiting for transfers between devices  38 us (29%)
  Pallas kernels  13 us (10%)
  local copies, waits for them, and re-layouts  6.98 us (5%)
  other arithmetic  2.16 us (2%)
    ppermute x3, starting transfers between devices, rotate(): return (mine, lax.ppermute(after(theirs, *before), 'rep', swap))  21.2 us
    ppermute x7, starting transfers between devices, send(): return lax.ppermute(x, ('wide', 'rep'), pairs)  17.7 us
    ppermute x6, starting transfers between devices, hop(): return lax.ppermute(x, ('wide', 'rep'), hop_pairs(k, n_wide))  12.4 us
    ppermute x1, waiting for transfers between devices, local_fast(): early = lax.ppermute(early, 'layer', swap)  7.6 us
    ppermute x8, starting transfers between devices, to_group(): lax.ppermute(x, ('groups', 'wide', 'rep'), swap_pairs(2 * n_wide, numbers...  7.18 us
    ppermute x6, waiting for transfers between devices, hop(): return lax.ppermute(x, ('wide', 'rep'), hop_pairs(k, n_wide))  6.18 us
    ppermute x1, waiting for transfers between devices, local_fast(): late = lax.ppermute(late, 'layer', swap)  5.46 us
    ppermute x1, waiting for transfers between devices, local_fast(): middle_came = lax.ppermute(middle, 'layer', swap)  4.87 us
  transfers between devices with their start and end apart: 34, of which 13 were waited for; matrix products, arithmetic and copies ran while one was open for 4% of the time, Pallas kernels for 7%

profile of v8, /device:TPU:0, one launch (start us, length us, event | category | flops | bytes accessed | tf_op | source)
XLA Modules:
  0.0 132.8 jit_solution(1880466755375261386)
XLA Ops:
  0.0 0.5 collective-permute-start.7
  0.5 1.2 dynamic-slice
  1.7 4.5 %collective-permute-start = (bf16[64,4736]{1,0:T(8,128)(2,1)S(1)}, bf16[64,4736]{1,0:T(8,128)(2,1)S(1)}, u32[]{:S(2)}, u32[]{:S(2)}) collective-permute-start(bf16[64,4736]{1,0:T(8,128)(2,1)S(1)} %dynamic-slice), channel_id=1, source_target_pairs={{0,4},{4,8},{8,12},{5,1},{9,5},{13,9},{2,6},{6,10},{10,14},{7,3},{... | collective-permute-start | bytes 1818632 | tf_op jit(solution)/shard_map/ppermute | solution.py:417
  6.2 0.1 collective-permute-start.6
  6.3 1.0 constant_dynamic-slice_fusion.5
  7.3 1.0 constant_dynamic-slice_fusion.4
  8.4 3.5 %collective-permute-start.4 = (bf16[64,4736]{1,0:T(8,128)(2,1)S(1)}, bf16[64,4736]{1,0:T(8,128)(2,1)S(1)}, u32[]{:S(2)}, u32[]{:S(2)}) collective-permute-start(bf16[64,4736]{1,0:T(8,128)(2,1)S(1)} %pad_maximum_fusion), channel_id=1, source_target_pairs={{0,4},{4,8},{8,12},{5,1},{9,5},{13,9},{2,6},{6,10},{10,14},{7,3},{... | collective-permute-start | bytes 1818632 | tf_op jit(solution)/shard_map/ppermute | solution.py:417
  11.9 1.9 %collective-permute-done.refs_1_.refs_5_ = bf16[64,4736]{1,0:T(8,128)(2,1)S(1)} collective-permute-done((bf16[64,4736]{1,0:T(8,128)(2,1)S(1)}, bf16[64,4736]{1,0:T(8,128)(2,1)S(1)}, u32[]{:S(2)}, u32[]{:S(2)}) %collective-permute-start) | collective-permute-done | bytes 606240 | tf_op jit(solution)/shard_map/ppermute | solution.py:417
  13.8 0.7 collective-permute-start.2
  14.5 1.5 %collective-permute-start.1 = (bf16[64,4736]{1,0:T(8,128)(2,1)S(1)}, bf16[64,4736]{1,0:T(8,128)(2,1)}, u32[]{:S(2)}, u32[]{:S(2)}) collective-permute-start(bf16[64,4736]{1,0:T(8,128)(2,1)S(1)} %collective-permute-done.refs_1_.refs_5_), channel_id=1, source_target_pairs={{4,8},{8,12},{5,1},{9,5},{6,10},{10,14},{7,3},{11,7},{20,24},{24,2... | collective-permute-start | bytes 1818632 | tf_op jit(solution)/shard_map/ppermute | solution.py:417
  16.0 4.3 %collective-permute-done.4.refs_0_.refs_4_ = bf16[64,4736]{1,0:T(8,128)(2,1)S(1)} collective-permute-done((bf16[64,4736]{1,0:T(8,128)(2,1)S(1)}, bf16[64,4736]{1,0:T(8,128)(2,1)S(1)}, u32[]{:S(2)}, u32[]{:S(2)}) %collective-permute-start.4) | collective-permute-done | bytes 606240 | tf_op jit(solution)/shard_map/ppermute | solution.py:417
  20.3 1.6 %collective-permute-start.5 = (bf16[64,4736]{1,0:T(8,128)(2,1)S(1)}, bf16[64,4736]{1,0:T(8,128)(2,1)}, u32[]{:S(2)}, u32[]{:S(2)}) collective-permute-start(bf16[64,4736]{1,0:T(8,128)(2,1)S(1)} %collective-permute-done.4.refs_0_.refs_4_), channel_id=1, source_target_pairs={{1,17},{5,21},{8,24},{12,28},{17,1},{21,5},{24,8},{28,12},{3,19},{... | collective-permute-start | bytes 1818632 | tf_op jit(solution)/shard_map/ppermute | solution.py:414
  21.8 0.8 copy-done.4
  22.7 1.5 %collective-permute-start.9 = (bf16[64,4736]{1,0:T(8,128)(2,1)S(1)}, bf16[64,4736]{1,0:T(8,128)(2,1)}, u32[]{:S(2)}, u32[]{:S(2)}) collective-permute-start(bf16[64,4736]{1,0:T(8,128)(2,1)S(1)} %collective-permute-done.4.refs_0_.refs_4_), channel_id=1, source_target_pairs={{4,8},{8,12},{5,1},{9,5},{6,10},{10,14},{7,3},{11,7},{20,24},{24,2... | collective-permute-start | bytes 1818632 | tf_op jit(solution)/shard_map/ppermute | solution.py:417
  24.1 1.5 %collective-permute-start.11 = (bf16[64,4736]{1,0:T(8,128)(2,1)}, bf16[64,4736]{1,0:T(8,128)(2,1)}, u32[]{:S(2)}, u32[]{:S(2)}) collective-permute-start(bf16[64,4736]{1,0:T(8,128)(2,1)} %collective-permute-done.1.refs_1_), channel_id=1, source_target_pairs={{1,17},{5,21},{8,24},{12,28},{17,1},{21,5},{24,8},{28,12},{3,19},{... | collective-permute-start | bytes 1818632 | tf_op jit(solution)/shard_map/ppermute | solution.py:414
  25.6 0.1 stack.51.at
  25.7 2.5 %copy-done = bf16[3,128,6912]{2,1,0:T(8,128)(2,1)S(1)} copy-done((bf16[3,128,6912]{2,1,0:T(8,128)(2,1)S(1)}, bf16[3,128,6912]{2,1,0:T(8,128)(2,1)}, u32[]{:S(2)}) %copy-start) | copy-done | bytes 5308440
  28.2 0.8 shard_map.82
  29.0 0.7 collective-permute-start.3
  29.7 3.2 %shard_map.84 = (bf16[384,2560]{1,0:T(8,128)(2,1)S(1)}, bf16[384,6912]{1,0:T(8,128)(2,1)S(1)}) custom-call(bf16[384,2560]{1,0:T(8,128)(2,1)} %bitcast.11.x_ref, bf16[384,6912]{1,0:T(8,128)(2,1)} %bitcast.12.y_ref), custom_call_target="tpu_custom_call" | custom-call | tf_op jit(solution)/shard_map/pallas_call | solution.py:404
  32.9 0.6 shard_map.85
  33.6 11.0 %collective-permute-start.8 = (f32[256,384]{1,0:T(8,128)S(1)}, f32[256,384]{1,0:T(8,128)S(1)}, u32[]{:S(2)}, u32[]{:S(2)}) collective-permute-start(f32[256,384]{1,0:T(8,128)S(1)} %get-tuple-element.46), channel_id=1, source_target_pairs={{0,1},{1,0},{2,3},{3,2},{4,5},{5,4},{6,7},{7,6},{8,9},{9,8},{10,11... | collective-permute-start | bytes 1179656 | tf_op jit(solution)/shard_map/ppermute | solution.py:441
  44.6 0.7 collective-permute-start.16
  45.3 0.7 collective-permute-start.13
  46.0 0.7 collective-permute-start.14
  46.7 0.7 collective-permute-start.10
  47.4 2.1 %shard_map.83 = (f32[128,384]{1,0:T(8,128)S(1)}, f32[128,384]{1,0:T(8,128)S(1)}) custom-call(bf16[128,2560]{1,0:T(8,128)(2,1)S(1)} %copy-done.3, bf16[128,6912]{1,0:T(8,128)(2,1)S(1)} %copy-done.1, bf16[384,2560]{1,0:T(8,128)(2,1)S(1)} %get-tuple-element.39.t_out.refs_4_.refs_8_, bf16[384,6912]{1,0:T(8,128)(2,1)S(1)} %get-tuple-element.40.t_in.refs_5_.refs_9_), custom_call_target="tpu_custom_call" | custom-call | flops 931135488 | bytes 4655677 | tf_op jit(solution)/shard_map/pallas_call | solution.py:428
  49.6 0.6 shard_map.86
  50.2 1.6 %collective-permute-start.12 = (bf16[512,384]{1,0:T(8,128)(2,1)S(1)}, bf16[512,384]{1,0:T(8,128)(2,1)S(1)}, u32[]{:S(2)}, u32[]{:S(2)}) collective-permute-start(bf16[512,384]{1,0:T(8,128)(2,1)S(1)} %shard_map.86), channel_id=1, source_target_pairs={{0,2},{2,0},{1,3},{3,1},{4,6},{6,4},{5,7},{7,5},{8,10},{10,8},{9,1... | collective-permute-start | bytes 1179656 | tf_op jit(solution)/shard_map/ppermute | solution.py:451
  51.7 0.7 collective-permute-start.18
  52.4 7.6 %collective-permute-done.12.early = bf16[512,384]{1,0:T(8,128)(2,1)S(1)} collective-permute-done((bf16[512,384]{1,0:T(8,128)(2,1)S(1)}, bf16[512,384]{1,0:T(8,128)(2,1)S(1)}, u32[]{:S(2)}, u32[]{:S(2)}) %collective-permute-start.12) | collective-permute-done | bytes 393248 | tf_op jit(solution)/shard_map/ppermute | solution.py:451
  60.0 0.7 collective-permute-start.17
  60.8 0.6 shard_map.87
  61.4 10.1 %collective-permute-start.15 = (f32[256,384]{1,0:T(8,128)S(1)}, f32[256,384]{1,0:T(8,128)S(1)}, u32[]{:S(2)}, u32[]{:S(2)}) collective-permute-start(f32[256,384]{1,0:T(8,128)S(1)} %get-tuple-element.51), channel_id=1, source_target_pairs={{0,1},{1,0},{2,3},{3,2},{4,5},{5,4},{6,7},{7,6},{8,9},{9,8},{10,11... | collective-permute-start | bytes 1179656 | tf_op jit(solution)/shard_map/ppermute | solution.py:441
  71.5 1.3 %collective-permute-done.15.both_far = f32[256,384]{1,0:T(8,128)S(1)} collective-permute-done((f32[256,384]{1,0:T(8,128)S(1)}, f32[256,384]{1,0:T(8,128)S(1)}, u32[]{:S(2)}, u32[]{:S(2)}) %collective-permute-start.15) | collective-permute-done | bytes 393248 | tf_op jit(solution)/shard_map/ppermute | solution.py:441
  72.9 0.6 shard_map.88
  73.5 1.6 %collective-permute-start.19 = (bf16[256,384]{1,0:T(8,128)(2,1)S(1)}, bf16[256,384]{1,0:T(8,128)(2,1)S(1)}, u32[]{:S(2)}, u32[]{:S(2)}) collective-permute-start(bf16[256,384]{1,0:T(8,128)(2,1)S(1)} %shard_map.88), channel_id=1, source_target_pairs={{0,2},{2,0},{1,3},{3,1},{4,6},{6,4},{5,7},{7,5},{8,10},{10,8},{9,1... | collective-permute-start | bytes 589832 | tf_op jit(solution)/shard_map/ppermute | solution.py:455
  75.0 0.8 shard_map.89
  75.8 4.9 %collective-permute-done.19.middle = bf16[256,384]{1,0:T(8,128)(2,1)S(1)} collective-permute-done((bf16[256,384]{1,0:T(8,128)(2,1)S(1)}, bf16[256,384]{1,0:T(8,128)(2,1)S(1)}, u32[]{:S(2)}, u32[]{:S(2)}) %collective-permute-start.19) | collective-permute-done | bytes 196640 | tf_op jit(solution)/shard_map/ppermute | solution.py:455
  80.7 0.1 collective-permute-start.20
  80.8 1.6 %collective-permute-done.20.last_far = f32[256,384]{1,0:T(8,128)S(1)} collective-permute-done((f32[256,384]{1,0:T(8,128)S(1)}, f32[256,384]{1,0:T(8,128)S(1)}, u32[]{:S(2)}, u32[]{:S(2)}) %collective-permute-start.20) | collective-permute-done | bytes 393248 | tf_op jit(solution)/shard_map/ppermute | solution.py:441
  82.4 0.6 shard_map.90
  83.0 1.5 %collective-permute-start.21 = (bf16[256,384]{1,0:T(8,128)(2,1)S(1)}, bf16[256,384]{1,0:T(8,128)(2,1)S(1)}, u32[]{:S(2)}, u32[]{:S(2)}) collective-permute-start(bf16[256,384]{1,0:T(8,128)(2,1)S(1)} %shard_map.90), channel_id=1, source_target_pairs={{0,2},{2,0},{1,3},{3,1},{4,6},{6,4},{5,7},{7,5},{8,10},{10,8},{9,1... | collective-permute-start | bytes 589832 | tf_op jit(solution)/shard_map/ppermute | solution.py:458
  84.6 5.5 %collective-permute-done.21.late = bf16[256,384]{1,0:T(8,128)(2,1)S(1)} collective-permute-done((bf16[256,384]{1,0:T(8,128)(2,1)S(1)}, bf16[256,384]{1,0:T(8,128)(2,1)S(1)}, u32[]{:S(2)}, u32[]{:S(2)}) %collective-permute-start.21) | collective-permute-done | bytes 196640 | tf_op jit(solution)/shard_map/ppermute | solution.py:458
  90.1 1.1 shard_map.91
  91.2 6.8 %collective-permute-start.22 = (bf16[3,64,256]{2,1,0:T(8,128)(2,1)S(1)}, bf16[3,64,256]{2,1,0:T(8,128)(2,1)S(1)}, u32[]{:S(2)}, u32[]{:S(2)}) collective-permute-start(bf16[3,64,256]{2,1,0:T(8,128)(2,1)S(1)} %get-tuple-element.58), channel_id=1, source_target_pairs={{0,4},{1,5},{4,8},{5,9},{8,12},{9,13},{12,0},{13,1},{2,6},{3,7},{6... | collective-permute-start | bytes 294920 | tf_op jit(solution)/shard_map/ppermute | solution.py:472
  98.0 4.1 %collective-permute-start.23 = (bf16[3,64,256]{2,1,0:T(8,128)(2,1)S(1)}, bf16[3,64,256]{2,1,0:T(8,128)(2,1)S(1)}, u32[]{:S(2)}, u32[]{:S(2)}) collective-permute-start(bf16[3,64,256]{2,1,0:T(8,128)(2,1)S(1)} %get-tuple-element.59), channel_id=1, source_target_pairs={{0,8},{1,9},{4,12},{5,13},{8,0},{9,1},{12,4},{13,5},{2,10},{3,11},... | collective-permute-start | bytes 294920 | tf_op jit(solution)/shard_map/ppermute | solution.py:472
  102.1 2.8 %collective-permute-start.24 = (bf16[3,64,256]{2,1,0:T(8,128)(2,1)S(1)}, bf16[3,64,256]{2,1,0:T(8,128)(2,1)S(1)}, u32[]{:S(2)}, u32[]{:S(2)}) collective-permute-start(bf16[3,64,256]{2,1,0:T(8,128)(2,1)S(1)} %get-tuple-element.60), channel_id=1, source_target_pairs={{0,12},{1,13},{4,0},{5,1},{8,4},{9,5},{12,8},{13,9},{2,14},{3,15},... | collective-permute-start | bytes 294920 | tf_op jit(solution)/shard_map/ppermute | solution.py:472
  105.0 0.3 collective-permute-start.27
  105.2 2.6 %collective-permute-done.23.refs_2_ = bf16[3,64,256]{2,1,0:T(8,128)(2,1)S(1)} collective-permute-done((bf16[3,64,256]{2,1,0:T(8,128)(2,1)S(1)}, bf16[3,64,256]{2,1,0:T(8,128)(2,1)S(1)}, u32[]{:S(2)}, u32[]{:S(2)}) %collective-permute-start.23) | collective-permute-done | bytes 98336 | tf_op jit(solution)/shard_map/ppermute | solution.py:472
  107.8 3.6 %collective-permute-start.28 = (bf16[3,64,256]{2,1,0:T(8,128)(2,1)S(1)}, bf16[3,64,256]{2,1,0:T(8,128)(2,1)S(1)}, u32[]{:S(2)}, u32[]{:S(2)}) collective-permute-start(bf16[3,64,256]{2,1,0:T(8,128)(2,1)S(1)} %get-tuple-element.64), channel_id=1, source_target_pairs={{0,13},{1,12},{4,1},{5,0},{8,5},{9,4},{12,9},{13,8},{2,15},{3,14},... | collective-permute-start | bytes 294920 | tf_op jit(solution)/shard_map/ppermute | solution.py:472
  111.5 1.4 %fusion.weights = bf16[64,64,256]{2,1,0:T(8,128)(2,1)S(1)} fusion(bf16[64,64,256]{2,1,0:T(8,128)(2,1)S(1)} %copy-done.7, f32[64,256]{1,0:T(8,128)S(1)} %copy-done.8), kind=kLoop, calls=%fused_computation.1 | loop fusion | flops 3145728 | bytes 4259840 | tf_op jit(solution)/shard_map/transpose | solution.py:396
  113.0 1.3 collective-permute-done.27.refs_6_
  114.2 2.0 %shard_map.92 = f32[64,24]{1,0:T(8,128)S(1)} custom-call(s32[8]{0:T(128)S(1)} %stack.51.at, bf16[64,64,256]{2,1,0:T(8,128)(2,1)S(1)} %fusion.weights, bf16[3,64,256]{2,1,0:T(8,128)(2,1)S(1)} %get-tuple-element.57.refs_0_, bf16[3,64,256]{2,1,0:T(8,128)(2,1)S(1)} %collective-permute-done.22.refs_1_, bf16[3,64,256]{2,1,0:T(8,128)(2,1)S(1)} %collective-permute-done.23.refs_2_, ...), custom_call_target="tpu_custom_call" | custom-call | flops 50331648 | bytes 251658 | tf_op jit(solution)/shard_map/pallas_call | solution.py:477
  116.3 0.1 reshape_reshape.3
  116.5 3.0 %collective-permute-start.29 = (f32[16,4,6]{0,1,2:T(4,128)S(1)}, f32[16,4,6]{0,1,2:T(4,128)S(1)}, u32[]{:S(2)}, u32[]{:S(2)}) collective-permute-start(f32[16,4,6]{0,1,2:T(4,128)S(1)} %bitcast.74), channel_id=1, source_target_pairs={{0,1},{1,2},{2,3},{3,0},{4,5},{5,6},{6,7},{7,4},{8,9},{9,10},{10,1... | collective-permute-start | bytes 4616 | tf_op jit(solution)/shard_map/ppermute | solution.py:63
  119.5 1.5 %collective-permute-start.30 = (f32[16,4,6]{0,1,2:T(4,128)S(1)}, f32[16,4,6]{0,1,2:T(4,128)S(1)}, u32[]{:S(2)}, u32[]{:S(2)}) collective-permute-start(f32[16,4,6]{0,1,2:T(4,128)S(1)} %bitcast.75), channel_id=1, source_target_pairs={{0,2},{1,3},{2,0},{3,1},{4,6},{5,7},{6,4},{7,5},{8,10},{9,11},{10,... | collective-permute-start | bytes 4616 | tf_op jit(solution)/shard_map/ppermute | solution.py:63
  121.0 1.0 collective-permute-done.29
  122.0 1.2 collective-permute-done.30
  123.3 1.4 %collective-permute-start.32 = (f32[16,2,6]{0,1,2:T(2,128)S(1)}, f32[16,2,6]{0,1,2:T(2,128)S(1)}, u32[]{:S(2)}, u32[]{:S(2)}) collective-permute-start(f32[16,2,6]{0,1,2:T(2,128)S(1)} %fusion.6), channel_id=1, source_target_pairs={{0,8},{4,12},{8,0},{12,4},{1,9},{5,13},{9,1},{13,5},{2,10},{6,14},... | collective-permute-start | bytes 2312 | tf_op jit(solution)/shard_map/ppermute | solution.py:74
  124.7 3.2 %collective-permute-done.32 = f32[16,2,6]{0,1,2:T(2,128)S(1)} collective-permute-done((f32[16,2,6]{0,1,2:T(2,128)S(1)}, f32[16,2,6]{0,1,2:T(2,128)S(1)}, u32[]{:S(2)}, u32[]{:S(2)}) %collective-permute-start.32) | collective-permute-done | bytes 800 | tf_op jit(solution)/shard_map/ppermute | solution.py:74
  127.9 2.6 %collective-permute-start.33 = (f32[16,1,6]{0,1,2:T(1,128)S(1)}, f32[16,1,6]{0,1,2:T(1,128)S(1)}, u32[]{:S(2)}, u32[]{:S(2)}) collective-permute-start(f32[16,1,6]{0,1,2:T(1,128)S(1)} %fusion.12), channel_id=1, source_target_pairs={{0,4},{4,0},{8,12},{12,8},{1,5},{5,1},{9,13},{13,9},{2,6},{6,2},{1... | collective-permute-start | bytes 1160 | tf_op jit(solution)/shard_map/ppermute | solution.py:74
  130.5 1.6 %collective-permute-done.33 = f32[16,1,6]{0,1,2:T(1,128)S(1)} collective-permute-done((f32[16,1,6]{0,1,2:T(1,128)S(1)}, f32[16,1,6]{0,1,2:T(1,128)S(1)}, u32[]{:S(2)}, u32[]{:S(2)}) %collective-permute-start.33) | collective-permute-done | bytes 416 | tf_op jit(solution)/shard_map/ppermute | solution.py:74
  132.1 0.7 bitcast_multiply_fusion
  (59 shorter events, 0.4 us)
Async XLA Ops:
  0.0 25.7 %copy-start.2 = (bf16[3,128,2560]{2,1,0:T(8,128)(2,1)S(1)}, bf16[3,128,2560]{2,1,0:T(8,128)(2,1)}, u32[]{:S(2)}) copy-start(bf16[3,128,2560]{2,1,0:T(8,128)(2,1)} %param.9) | copy-start | bytes 5898244
  0.0 29.7 %collective-permute-start.7 = (bf16[3,128,6912]{2,1,0:T(8,128)(2,1)}, bf16[3,128,6912]{2,1,0:T(8,128)(2,1)}, u32[]{:S(2)}, u32[]{:S(2)}) collective-permute-start(bf16[3,128,6912]{2,1,0:T(8,128)(2,1)} %param.8), channel_id=1, source_target_pairs={{0,1},{1,0},{2,3},{3,2},{4,5},{5,4},{6,7},{7,6},{8,9},{9,8},{10,11... | collective-permute-start | bytes 15925256 | tf_op jit(solution)/shard_map/ppermute | solution.py:425
  1.7 12.1 %collective-permute-start = (bf16[64,4736]{1,0:T(8,128)(2,1)S(1)}, bf16[64,4736]{1,0:T(8,128)(2,1)S(1)}, u32[]{:S(2)}, u32[]{:S(2)}) collective-permute-start(bf16[64,4736]{1,0:T(8,128)(2,1)S(1)} %dynamic-slice), channel_id=1, source_target_pairs={{0,4},{4,8},{8,12},{5,1},{9,5},{13,9},{2,6},{6,10},{10,14},{7,3},{... | collective-permute-start | bytes 1818632 | tf_op jit(solution)/shard_map/ppermute | solution.py:417
  6.2 22.7 %collective-permute-start.6 = (bf16[3,128,2560]{2,1,0:T(8,128)(2,1)}, bf16[3,128,2560]{2,1,0:T(8,128)(2,1)}, u32[]{:S(2)}, u32[]{:S(2)}) collective-permute-start(bf16[3,128,2560]{2,1,0:T(8,128)(2,1)} %param.9), channel_id=1, source_target_pairs={{0,1},{1,0},{2,3},{3,2},{4,5},{5,4},{6,7},{7,6},{8,9},{9,8},{10,11... | collective-permute-start | bytes 5898248 | tf_op jit(solution)/shard_map/ppermute | solution.py:425
  8.4 11.9 %collective-permute-start.4 = (bf16[64,4736]{1,0:T(8,128)(2,1)S(1)}, bf16[64,4736]{1,0:T(8,128)(2,1)S(1)}, u32[]{:S(2)}, u32[]{:S(2)}) collective-permute-start(bf16[64,4736]{1,0:T(8,128)(2,1)S(1)} %pad_maximum_fusion), channel_id=1, source_target_pairs={{0,4},{4,8},{8,12},{5,1},{9,5},{13,9},{2,6},{6,10},{10,14},{7,3},{... | collective-permute-start | bytes 1818632 | tf_op jit(solution)/shard_map/ppermute | solution.py:417
  13.8 8.1 %collective-permute-start.2 = (bf16[64,4736]{1,0:T(8,128)(2,1)S(1)}, bf16[64,4736]{1,0:T(8,128)(2,1)S(1)}, u32[]{:S(2)}, u32[]{:S(2)}) collective-permute-start(bf16[64,4736]{1,0:T(8,128)(2,1)S(1)} %collective-permute-done.refs_1_.refs_5_), channel_id=1, source_target_pairs={{1,17},{5,21},{8,24},{12,28},{17,1},{21,5},{24,8},{28,12},{3,19},{... | collective-permute-start | bytes 1818632 | tf_op jit(solution)/shard_map/ppermute | solution.py:414
  14.5 9.7 %collective-permute-start.1 = (bf16[64,4736]{1,0:T(8,128)(2,1)S(1)}, bf16[64,4736]{1,0:T(8,128)(2,1)}, u32[]{:S(2)}, u32[]{:S(2)}) collective-permute-start(bf16[64,4736]{1,0:T(8,128)(2,1)S(1)} %collective-permute-done.refs_1_.refs_5_), channel_id=1, source_target_pairs={{4,8},{8,12},{5,1},{9,5},{6,10},{10,14},{7,3},{11,7},{20,24},{24,2... | collective-permute-start | bytes 1818632 | tf_op jit(solution)/shard_map/ppermute | solution.py:417
  20.3 12.6 %collective-permute-start.5 = (bf16[64,4736]{1,0:T(8,128)(2,1)S(1)}, bf16[64,4736]{1,0:T(8,128)(2,1)}, u32[]{:S(2)}, u32[]{:S(2)}) collective-permute-start(bf16[64,4736]{1,0:T(8,128)(2,1)S(1)} %collective-permute-done.4.refs_0_.refs_4_), channel_id=1, source_target_pairs={{1,17},{5,21},{8,24},{12,28},{17,1},{21,5},{24,8},{28,12},{3,19},{... | collective-permute-start | bytes 1818632 | tf_op jit(solution)/shard_map/ppermute | solution.py:414
  21.8 0.8 copy-start.4
  22.7 21.9 %collective-permute-start.9 = (bf16[64,4736]{1,0:T(8,128)(2,1)S(1)}, bf16[64,4736]{1,0:T(8,128)(2,1)}, u32[]{:S(2)}, u32[]{:S(2)}) collective-permute-start(bf16[64,4736]{1,0:T(8,128)(2,1)S(1)} %collective-permute-done.4.refs_0_.refs_4_), channel_id=1, source_target_pairs={{4,8},{8,12},{5,1},{9,5},{6,10},{10,14},{7,3},{11,7},{20,24},{24,2... | collective-permute-start | bytes 1818632 | tf_op jit(solution)/shard_map/ppermute | solution.py:417
  24.1 21.9 %collective-permute-start.11 = (bf16[64,4736]{1,0:T(8,128)(2,1)}, bf16[64,4736]{1,0:T(8,128)(2,1)}, u32[]{:S(2)}, u32[]{:S(2)}) collective-permute-start(bf16[64,4736]{1,0:T(8,128)(2,1)} %collective-permute-done.1.refs_1_), channel_id=1, source_target_pairs={{1,17},{5,21},{8,24},{12,28},{17,1},{21,5},{24,8},{28,12},{3,19},{... | collective-permute-start | bytes 1818632 | tf_op jit(solution)/shard_map/ppermute | solution.py:414
  25.7 2.5 %copy-start = (bf16[3,128,6912]{2,1,0:T(8,128)(2,1)S(1)}, bf16[3,128,6912]{2,1,0:T(8,128)(2,1)}, u32[]{:S(2)}) copy-start(bf16[3,128,6912]{2,1,0:T(8,128)(2,1)} %param.8) | copy-start | bytes 15925252
  29.0 21.2 %collective-permute-start.3 = (bf16[64,4736]{1,0:T(8,128)(2,1)}, bf16[64,4736]{1,0:T(8,128)(2,1)S(1)}, u32[]{:S(2)}, u32[]{:S(2)}) collective-permute-start(bf16[64,4736]{1,0:T(8,128)(2,1)} %collective-permute-done.1.refs_1_), channel_id=1, source_target_pairs={{8,12},{5,1},{10,14},{7,3},{24,28},{21,17},{26,30},{23,19}} | collective-permute-start | bytes 1818632 | tf_op jit(solution)/shard_map/ppermute | solution.py:417
  29.7 3.2 %copy-start.5 = (bf16[64,4736]{1,0:T(8,128)(2,1)S(1)}, bf16[64,4736]{1,0:T(8,128)(2,1)}, u32[]{:S(2)}) copy-start(bf16[64,4736]{1,0:T(8,128)(2,1)} %copy-done.4) | copy-start | bytes 1818628
  32.9 14.5 %copy-start.1 = (bf16[128,6912]{1,0:T(8,128)(2,1)S(1)}, bf16[128,6912]{1,0:T(8,128)(2,1)}, u32[]{:S(2)}) copy-start(bf16[128,6912]{1,0:T(8,128)(2,1)} %b_in.1) | copy-start | bytes 5308420
  32.9 14.5 %copy-start.3 = (bf16[128,2560]{1,0:T(8,128)(2,1)S(1)}, bf16[128,2560]{1,0:T(8,128)(2,1)}, u32[]{:S(2)}) copy-start(bf16[128,2560]{1,0:T(8,128)(2,1)} %b_out.1) | copy-start | bytes 1966084
  33.6 13.2 %collective-permute-start.8 = (f32[256,384]{1,0:T(8,128)S(1)}, f32[256,384]{1,0:T(8,128)S(1)}, u32[]{:S(2)}, u32[]{:S(2)}) collective-permute-start(f32[256,384]{1,0:T(8,128)S(1)} %get-tuple-element.46), channel_id=1, source_target_pairs={{0,1},{1,0},{2,3},{3,2},{4,5},{5,4},{6,7},{7,6},{8,9},{9,8},{10,11... | collective-permute-start | bytes 1179656 | tf_op jit(solution)/shard_map/ppermute | solution.py:441
  44.6 7.2 %collective-permute-start.16 = (bf16[64,4736]{1,0:T(8,128)(2,1)}, bf16[64,4736]{1,0:T(8,128)(2,1)S(1)}, u32[]{:S(2)}, u32[]{:S(2)}) collective-permute-start(bf16[64,4736]{1,0:T(8,128)(2,1)} %collective-permute-done.9.refs_0_), channel_id=1, source_target_pairs={{8,12},{5,1},{10,14},{7,3},{24,28},{21,17},{26,30},{23,19}} | collective-permute-start | bytes 1818632 | tf_op jit(solution)/shard_map/ppermute | solution.py:417
  45.3 15.5 %collective-permute-start.13 = (bf16[64,4736]{1,0:T(8,128)(2,1)S(1)}, bf16[64,4736]{1,0:T(8,128)(2,1)S(1)}, u32[]{:S(2)}, u32[]{:S(2)}) collective-permute-start(bf16[64,4736]{1,0:T(8,128)(2,1)S(1)} %collective-permute-done.4.refs_0_.refs_4_), channel_id=1, source_target_pairs={{4,20},{9,25},{20,4},{25,9},{6,22},{11,27},{22,6},{27,11}} | collective-permute-start | bytes 1818632 | tf_op jit(solution)/shard_map/ppermute | solution.py:414
  46.0 14.7 %collective-permute-start.14 = (bf16[64,4736]{1,0:T(8,128)(2,1)S(1)}, bf16[64,4736]{1,0:T(8,128)(2,1)S(1)}, u32[]{:S(2)}, u32[]{:S(2)}) collective-permute-start(bf16[64,4736]{1,0:T(8,128)(2,1)S(1)} %collective-permute-done.refs_1_.refs_5_), channel_id=1, source_target_pairs={{4,20},{9,25},{20,4},{25,9},{6,22},{11,27},{22,6},{27,11}} | collective-permute-start | bytes 1818632 | tf_op jit(solution)/shard_map/ppermute | solution.py:414
  46.7 14.0 %collective-permute-start.10 = (bf16[64,4736]{1,0:T(8,128)(2,1)}, bf16[64,4736]{1,0:T(8,128)(2,1)S(1)}, u32[]{:S(2)}, u32[]{:S(2)}) collective-permute-start(bf16[64,4736]{1,0:T(8,128)(2,1)} %collective-permute-done.9.refs_0_), channel_id=1, source_target_pairs={{1,17},{5,21},{8,24},{12,28},{17,1},{21,5},{24,8},{28,12},{3,19},{... | collective-permute-start | bytes 1818632 | tf_op jit(solution)/shard_map/ppermute | solution.py:414
  50.2 9.9 %collective-permute-start.12 = (bf16[512,384]{1,0:T(8,128)(2,1)S(1)}, bf16[512,384]{1,0:T(8,128)(2,1)S(1)}, u32[]{:S(2)}, u32[]{:S(2)}) collective-permute-start(bf16[512,384]{1,0:T(8,128)(2,1)S(1)} %shard_map.86), channel_id=1, source_target_pairs={{0,2},{2,0},{1,3},{3,1},{4,6},{6,4},{5,7},{7,5},{8,10},{10,8},{9,1... | collective-permute-start | bytes 1179656 | tf_op jit(solution)/shard_map/ppermute | solution.py:451
  51.7 23.3 %collective-permute-start.18 = (bf16[64,4736]{1,0:T(8,128)(2,1)S(1)}, bf16[64,4736]{1,0:T(8,128)(2,1)S(1)}, u32[]{:S(2)}, u32[]{:S(2)}) collective-permute-start(bf16[64,4736]{1,0:T(8,128)(2,1)S(1)} %collective-permute-done.3.refs_1_), channel_id=1, source_target_pairs={{1,17},{12,28},{17,1},{28,12},{3,19},{14,30},{19,3},{30,14}} | collective-permute-start | bytes 1818632 | tf_op jit(solution)/shard_map/ppermute | solution.py:414
  60.0 15.0 %collective-permute-start.17 = (bf16[64,4736]{1,0:T(8,128)(2,1)S(1)}, bf16[64,4736]{1,0:T(8,128)(2,1)S(1)}, u32[]{:S(2)}, u32[]{:S(2)}) collective-permute-start(bf16[64,4736]{1,0:T(8,128)(2,1)S(1)} %collective-permute-done.16.refs_0_), channel_id=1, source_target_pairs={{1,17},{12,28},{17,1},{28,12},{3,19},{14,30},{19,3},{30,14}} | collective-permute-start | bytes 1818632 | tf_op jit(solution)/shard_map/ppermute | solution.py:414
  61.4 11.5 %collective-permute-start.15 = (f32[256,384]{1,0:T(8,128)S(1)}, f32[256,384]{1,0:T(8,128)S(1)}, u32[]{:S(2)}, u32[]{:S(2)}) collective-permute-start(f32[256,384]{1,0:T(8,128)S(1)} %get-tuple-element.51), channel_id=1, source_target_pairs={{0,1},{1,0},{2,3},{3,2},{4,5},{5,4},{6,7},{7,6},{8,9},{9,8},{10,11... | collective-permute-start | bytes 1179656 | tf_op jit(solution)/shard_map/ppermute | solution.py:441
  73.5 16.6 %copy-start.6 = (s32[3]{0:T(128)S(1)}, s32[3]{0:T(128)}, u32[]{:S(2)}) copy-start(s32[3]{0:T(128)} %counts.1) | copy-start | bytes 40
  73.5 7.2 %collective-permute-start.19 = (bf16[256,384]{1,0:T(8,128)(2,1)S(1)}, bf16[256,384]{1,0:T(8,128)(2,1)S(1)}, u32[]{:S(2)}, u32[]{:S(2)}) collective-permute-start(bf16[256,384]{1,0:T(8,128)(2,1)S(1)} %shard_map.88), channel_id=1, source_target_pairs={{0,2},{2,0},{1,3},{3,1},{4,6},{6,4},{5,7},{7,5},{8,10},{10,8},{9,1... | collective-permute-start | bytes 589832 | tf_op jit(solution)/shard_map/ppermute | solution.py:455
  80.7 1.7 %collective-permute-start.20 = (f32[256,384]{1,0:T(8,128)S(1)}, f32[256,384]{1,0:T(8,128)S(1)}, u32[]{:S(2)}, u32[]{:S(2)}) collective-permute-start(f32[256,384]{1,0:T(8,128)S(1)} %get-tuple-element.56), channel_id=1, source_target_pairs={{0,1},{1,0},{2,3},{3,2},{4,5},{5,4},{6,7},{7,6},{8,9},{9,8},{10,11... | collective-permute-start | bytes 1179656 | tf_op jit(solution)/shard_map/ppermute | solution.py:441
  83.0 28.5 %copy-start.7 = (bf16[64,64,256]{2,1,0:T(8,128)(2,1)S(1)}, bf16[64,64,256]{2,1,0:T(8,128)(2,1)}, u32[]{:S(2)}) copy-start(bf16[64,64,256]{2,1,0:T(8,128)(2,1)} %param.13) | copy-start | bytes 6291460
  83.0 28.5 %copy-start.8 = (f32[64,256]{1,0:T(8,128)S(1)}, f32[64,256]{1,0:T(8,128)}, u32[]{:S(2)}) copy-start(f32[64,256]{1,0:T(8,128)} %param.14) | copy-start | bytes 196612
  83.0 7.0 %collective-permute-start.21 = (bf16[256,384]{1,0:T(8,128)(2,1)S(1)}, bf16[256,384]{1,0:T(8,128)(2,1)S(1)}, u32[]{:S(2)}, u32[]{:S(2)}) collective-permute-start(bf16[256,384]{1,0:T(8,128)(2,1)S(1)} %shard_map.90), channel_id=1, source_target_pairs={{0,2},{2,0},{1,3},{3,1},{4,6},{6,4},{5,7},{7,5},{8,10},{10,8},{9,1... | collective-permute-start | bytes 589832 | tf_op jit(solution)/shard_map/ppermute | solution.py:458
  91.2 13.7 %collective-permute-start.22 = (bf16[3,64,256]{2,1,0:T(8,128)(2,1)S(1)}, bf16[3,64,256]{2,1,0:T(8,128)(2,1)S(1)}, u32[]{:S(2)}, u32[]{:S(2)}) collective-permute-start(bf16[3,64,256]{2,1,0:T(8,128)(2,1)S(1)} %get-tuple-element.58), channel_id=1, source_target_pairs={{0,4},{1,5},{4,8},{5,9},{8,12},{9,13},{12,0},{13,1},{2,6},{3,7},{6... | collective-permute-start | bytes 294920 | tf_op jit(solution)/shard_map/ppermute | solution.py:472
  98.0 9.8 %collective-permute-start.23 = (bf16[3,64,256]{2,1,0:T(8,128)(2,1)S(1)}, bf16[3,64,256]{2,1,0:T(8,128)(2,1)S(1)}, u32[]{:S(2)}, u32[]{:S(2)}) collective-permute-start(bf16[3,64,256]{2,1,0:T(8,128)(2,1)S(1)} %get-tuple-element.59), channel_id=1, source_target_pairs={{0,8},{1,9},{4,12},{5,13},{8,0},{9,1},{12,4},{13,5},{2,10},{3,11},... | collective-permute-start | bytes 294920 | tf_op jit(solution)/shard_map/ppermute | solution.py:472
  102.1 10.8 %collective-permute-start.24 = (bf16[3,64,256]{2,1,0:T(8,128)(2,1)S(1)}, bf16[3,64,256]{2,1,0:T(8,128)(2,1)S(1)}, u32[]{:S(2)}, u32[]{:S(2)}) collective-permute-start(bf16[3,64,256]{2,1,0:T(8,128)(2,1)S(1)} %get-tuple-element.60), channel_id=1, source_target_pairs={{0,12},{1,13},{4,0},{5,1},{8,4},{9,5},{12,8},{13,9},{2,14},{3,15},... | collective-permute-start | bytes 294920 | tf_op jit(solution)/shard_map/ppermute | solution.py:472
  104.9 8.0 %collective-permute-start.25 = (bf16[3,64,256]{2,1,0:T(8,128)(2,1)S(1)}, bf16[3,64,256]{2,1,0:T(8,128)(2,1)S(1)}, u32[]{:S(2)}, u32[]{:S(2)}) collective-permute-start(bf16[3,64,256]{2,1,0:T(8,128)(2,1)S(1)} %get-tuple-element.61), channel_id=1, source_target_pairs={{0,1},{1,0},{4,5},{5,4},{8,9},{9,8},{12,13},{13,12},{2,3},{3,2},{6... | collective-permute-start | bytes 294920 | tf_op jit(solution)/shard_map/ppermute | solution.py:472
  104.9 8.0 %collective-permute-start.26 = (bf16[3,64,256]{2,1,0:T(8,128)(2,1)S(1)}, bf16[3,64,256]{2,1,0:T(8,128)(2,1)S(1)}, u32[]{:S(2)}, u32[]{:S(2)}) collective-permute-start(bf16[3,64,256]{2,1,0:T(8,128)(2,1)S(1)} %get-tuple-element.62), channel_id=1, source_target_pairs={{0,5},{1,4},{4,9},{5,8},{8,13},{9,12},{12,1},{13,0},{2,7},{3,6},{6... | collective-permute-start | bytes 294920 | tf_op jit(solution)/shard_map/ppermute | solution.py:472
  105.0 9.3 %collective-permute-start.27 = (bf16[3,64,256]{2,1,0:T(8,128)(2,1)S(1)}, bf16[3,64,256]{2,1,0:T(8,128)(2,1)S(1)}, u32[]{:S(2)}, u32[]{:S(2)}) collective-permute-start(bf16[3,64,256]{2,1,0:T(8,128)(2,1)S(1)} %get-tuple-element.63), channel_id=1, source_target_pairs={{0,9},{1,8},{4,13},{5,12},{8,1},{9,0},{12,5},{13,4},{2,11},{3,10},... | collective-permute-start | bytes 294920 | tf_op jit(solution)/shard_map/ppermute | solution.py:472
  107.8 6.4 %collective-permute-start.28 = (bf16[3,64,256]{2,1,0:T(8,128)(2,1)S(1)}, bf16[3,64,256]{2,1,0:T(8,128)(2,1)S(1)}, u32[]{:S(2)}, u32[]{:S(2)}) collective-permute-start(bf16[3,64,256]{2,1,0:T(8,128)(2,1)S(1)} %get-tuple-element.64), channel_id=1, source_target_pairs={{0,13},{1,12},{4,1},{5,0},{8,5},{9,4},{12,9},{13,8},{2,15},{3,14},... | collective-permute-start | bytes 294920 | tf_op jit(solution)/shard_map/ppermute | solution.py:472
  112.9 11.8 %copy-start.9 = (s32[16,1]{0,1:T(1,128)S(1)}, s32[16,1]{0,1:T(1,128)}, u32[]{:S(2)}) copy-start(s32[16,1]{0,1:T(1,128)} %param.15) | copy-start | bytes 196
  116.5 5.5 %collective-permute-start.29 = (f32[16,4,6]{0,1,2:T(4,128)S(1)}, f32[16,4,6]{0,1,2:T(4,128)S(1)}, u32[]{:S(2)}, u32[]{:S(2)}) collective-permute-start(f32[16,4,6]{0,1,2:T(4,128)S(1)} %bitcast.74), channel_id=1, source_target_pairs={{0,1},{1,2},{2,3},{3,0},{4,5},{5,6},{6,7},{7,4},{8,9},{9,10},{10,1... | collective-permute-start | bytes 4616 | tf_op jit(solution)/shard_map/ppermute | solution.py:63
  119.5 3.7 %collective-permute-start.30 = (f32[16,4,6]{0,1,2:T(4,128)S(1)}, f32[16,4,6]{0,1,2:T(4,128)S(1)}, u32[]{:S(2)}, u32[]{:S(2)}) collective-permute-start(f32[16,4,6]{0,1,2:T(4,128)S(1)} %bitcast.75), channel_id=1, source_target_pairs={{0,2},{1,3},{2,0},{3,1},{4,6},{5,7},{6,4},{7,5},{8,10},{9,11},{10,... | collective-permute-start | bytes 4616 | tf_op jit(solution)/shard_map/ppermute | solution.py:63
  121.0 2.2 %collective-permute-start.31 = (f32[16,4,6]{0,1,2:T(4,128)S(1)}, f32[16,4,6]{0,1,2:T(4,128)S(1)}, u32[]{:S(2)}, u32[]{:S(2)}) collective-permute-start(f32[16,4,6]{0,1,2:T(4,128)S(1)} %bitcast.76), channel_id=1, source_target_pairs={{0,3},{1,0},{2,1},{3,2},{4,7},{5,4},{6,5},{7,6},{8,11},{9,8},{10,9... | collective-permute-start | bytes 4616 | tf_op jit(solution)/shard_map/ppermute | solution.py:63
  123.3 4.6 %collective-permute-start.32 = (f32[16,2,6]{0,1,2:T(2,128)S(1)}, f32[16,2,6]{0,1,2:T(2,128)S(1)}, u32[]{:S(2)}, u32[]{:S(2)}) collective-permute-start(f32[16,2,6]{0,1,2:T(2,128)S(1)} %fusion.6), channel_id=1, source_target_pairs={{0,8},{4,12},{8,0},{12,4},{1,9},{5,13},{9,1},{13,5},{2,10},{6,14},... | collective-permute-start | bytes 2312 | tf_op jit(solution)/shard_map/ppermute | solution.py:74
  127.9 4.1 %collective-permute-start.33 = (f32[16,1,6]{0,1,2:T(1,128)S(1)}, f32[16,1,6]{0,1,2:T(1,128)S(1)}, u32[]{:S(2)}, u32[]{:S(2)}) collective-permute-start(f32[16,1,6]{0,1,2:T(1,128)S(1)} %fusion.12), channel_id=1, source_target_pairs={{0,4},{4,0},{8,12},{12,8},{1,5},{5,1},{9,13},{13,9},{2,6},{6,2},{1... | collective-permute-start | bytes 1160 | tf_op jit(solution)/shard_map/ppermute | solution.py:74

commit v9 on v8

--- a/solution.py
+++ b/solution.py
@@ -449,11 +449,11 @@
         at, g_own, a_own, *near_done
     )
     early = lax.ppermute(early, "layer", swap)
-    both_done = rotate([4, 5], *x2, y2[0], after(y2[1], early), *x1, *y1_inner)
+    both_done = rotate([4, 5], *x2, y2[0], after(y2[1], near_done[0]), *x1, *y1_inner)
     pair = shaped(2 * rows, n_tok, kind=HALF)
     middle = kernel(middle_body, pair)(in_specs=[SMEM] + [VMEM] * 2, out_specs=VMEM)(at, *both_done)
     middle_came = lax.ppermute(middle, "layer", swap)
-    last_done = rotate([6], *x3, y3[0], after(y3[1], middle), before=(middle_came,))
+    last_done = rotate([6], *x3, y3[0], after(y3[1], middle), before=(middle_came, early))
     late = kernel(last_body, pair)(in_specs=[SMEM] + [VMEM] * 4, out_specs=VMEM)(at, *both_done, *last_done)
     late = lax.ppermute(late, "layer", swap)
 

time: 133 us -> 147 us (1.11)
  starting transfers between devices: 72.1 us -> 80.6 us
  waiting for transfers between devices: 38 us -> 40.1 us
  local copies, waits for them, and re-layouts: 6.98 us -> 9.06 us
    ppermute x1, waiting for transfers between devices: 7.6 us -> 0.01 us  [local_fast(): early = lax.ppermute(early, 'layer', swap)]
    ppermute x3, starting transfers between devices: 21.2 us -> 28.7 us  [rotate(): return (mine, lax.ppermute(after(theirs, *before), 'rep', swap))]
    ppermute x1, waiting for transfers between devices: 4.87 us -> 11.8 us  [local_fast(): middle_came = lax.ppermute(middle, 'layer', swap)]
    ppermute x6, waiting for transfers between devices: 6.18 us -> 9.98 us  [hop(): return lax.ppermute(x, ('wide', 'rep'), hop_pairs(k, n_wide))]
    unnamed x20 -> x28, local copies, waits for them, and re-layouts: 3.4 us -> 6.65 us
    ppermute x6, starting transfers between devices: 12.4 us -> 14.5 us  [hop(): return lax.ppermute(x, ('wide', 'rep'), hop_pairs(k, n_wide))]
  transfers between devices with their start and end apart: 34 -> 34, of which waited for: 13 -> 11; matrix products, arithmetic and copies ran while one was open for 4% -> 3% of each run, Pallas kernels for 7% -> 6%
where the time goes in v9:
time: 147 us; the launch traced here: 146 us
  starting transfers between devices  80.6 us (55%)
  waiting for transfers between devices  40.1 us (27%)
  Pallas kernels  13 us (9%)
  local copies, waits for them, and re-layouts  9.06 us (6%)
  other arithmetic  3.03 us (2%)
    ppermute x3, starting transfers between devices, rotate(): return (mine, lax.ppermute(after(theirs, *before), 'rep', swap))  28.7 us
    ppermute x7, starting transfers between devices, send(): return lax.ppermute(x, ('wide', 'rep'), pairs)  17 us
    ppermute x6, starting transfers between devices, hop(): return lax.ppermute(x, ('wide', 'rep'), hop_pairs(k, n_wide))  14.5 us
    ppermute x1, waiting for transfers between devices, local_fast(): middle_came = lax.ppermute(middle, 'layer', swap)  11.8 us
    ppermute x6, waiting for transfers between devices, hop(): return lax.ppermute(x, ('wide', 'rep'), hop_pairs(k, n_wide))  9.98 us
    ppermute x8, starting transfers between devices, to_group(): lax.ppermute(x, ('groups', 'wide', 'rep'), swap_pairs(2 * n_wide, numbers...  8 us
    unnamed x28, local copies, waits for them, and re-layouts  6.65 us
    ppermute x1, waiting for transfers between devices, local_fast(): late = lax.ppermute(late, 'layer', swap)  5.45 us
  transfers between devices with their start and end apart: 34, of which 11 were waited for; matrix products, arithmetic and copies ran while one was open for 3% of the time, Pallas kernels for 6%

profile of v9, /device:TPU:0, one launch (start us, length us, event | category | flops | bytes accessed | tf_op | source)
XLA Modules:
  0.0 146.3 jit_solution(15120795995834340066)
XLA Ops:
  0.0 0.5 collective-permute-start.7
  0.5 1.0 constant_dynamic-slice_fusion.4
  1.5 1.0 constant_dynamic-slice_fusion.5
  2.5 0.9 pad_maximum_fusion
  3.4 4.9 %collective-permute-start.4 = (bf16[64,4736]{1,0:T(8,128)(2,1)}, bf16[64,4736]{1,0:T(8,128)(2,1)S(1)}, u32[]{:S(2)}, u32[]{:S(2)}) collective-permute-start(bf16[64,4736]{1,0:T(8,128)(2,1)} %pad_maximum_fusion), channel_id=1, source_target_pairs={{0,4},{4,8},{8,12},{5,1},{9,5},{13,9},{2,6},{6,10},{10,14},{7,3},{... | collective-permute-start | bytes 1818632 | tf_op jit(solution)/shard_map/ppermute | solution.py:417
  8.5 3.5 %collective-permute-start = (bf16[64,4736]{1,0:T(8,128)(2,1)S(1)}, bf16[64,4736]{1,0:T(8,128)(2,1)S(1)}, u32[]{:S(2)}, u32[]{:S(2)}) collective-permute-start(bf16[64,4736]{1,0:T(8,128)(2,1)S(1)} %dynamic-slice), channel_id=1, source_target_pairs={{0,4},{4,8},{8,12},{5,1},{9,5},{13,9},{2,6},{6,10},{10,14},{7,3},{... | collective-permute-start | bytes 1818632 | tf_op jit(solution)/shard_map/ppermute | solution.py:417
  12.0 4.3 %collective-permute-done.4.refs_0_.refs_4_ = bf16[64,4736]{1,0:T(8,128)(2,1)S(1)} collective-permute-done((bf16[64,4736]{1,0:T(8,128)(2,1)}, bf16[64,4736]{1,0:T(8,128)(2,1)S(1)}, u32[]{:S(2)}, u32[]{:S(2)}) %collective-permute-start.4) | collective-permute-done | bytes 606240 | tf_op jit(solution)/shard_map/ppermute | solution.py:417
  16.2 0.7 collective-permute-start.5
  16.9 5.7 %collective-permute-done.refs_1_.refs_5_ = bf16[64,4736]{1,0:T(8,128)(2,1)S(1)} collective-permute-done((bf16[64,4736]{1,0:T(8,128)(2,1)S(1)}, bf16[64,4736]{1,0:T(8,128)(2,1)S(1)}, u32[]{:S(2)}, u32[]{:S(2)}) %collective-permute-start) | collective-permute-done | bytes 606240 | tf_op jit(solution)/shard_map/ppermute | solution.py:417
  22.6 1.5 %collective-permute-start.1 = (bf16[64,4736]{1,0:T(8,128)(2,1)S(1)}, bf16[64,4736]{1,0:T(8,128)(2,1)}, u32[]{:S(2)}, u32[]{:S(2)}) collective-permute-start(bf16[64,4736]{1,0:T(8,128)(2,1)S(1)} %collective-permute-done.refs_1_.refs_5_), channel_id=1, source_target_pairs={{4,8},{8,12},{5,1},{9,5},{6,10},{10,14},{7,3},{11,7},{20,24},{24,2... | collective-permute-start | bytes 1818632 | tf_op jit(solution)/shard_map/ppermute | solution.py:417
  24.2 0.7 collective-permute-start.2
  24.9 0.8 copy-done.4
  25.7 1.5 %collective-permute-start.9 = (bf16[64,4736]{1,0:T(8,128)(2,1)S(1)}, bf16[64,4736]{1,0:T(8,128)(2,1)}, u32[]{:S(2)}, u32[]{:S(2)}) collective-permute-start(bf16[64,4736]{1,0:T(8,128)(2,1)S(1)} %collective-permute-done.4.refs_0_.refs_4_), channel_id=1, source_target_pairs={{4,8},{8,12},{5,1},{9,5},{6,10},{10,14},{7,3},{11,7},{20,24},{24,2... | collective-permute-start | bytes 1818632 | tf_op jit(solution)/shard_map/ppermute | solution.py:417
  27.2 0.7 collective-permute-start.11
  27.9 0.8 copy-done.6
  28.7 1.5 %collective-permute-start.12 = (bf16[64,4736]{1,0:T(8,128)(2,1)S(1)}, bf16[64,4736]{1,0:T(8,128)(2,1)}, u32[]{:S(2)}, u32[]{:S(2)}) collective-permute-start(bf16[64,4736]{1,0:T(8,128)(2,1)S(1)} %collective-permute-done.4.refs_0_.refs_4_), channel_id=1, source_target_pairs={{4,20},{9,25},{20,4},{25,9},{6,22},{11,27},{22,6},{27,11}} | collective-permute-start | bytes 1818632 | tf_op jit(solution)/shard_map/ppermute | solution.py:414
  30.2 1.6 %collective-permute-start.3 = (bf16[64,4736]{1,0:T(8,128)(2,1)}, bf16[64,4736]{1,0:T(8,128)(2,1)}, u32[]{:S(2)}, u32[]{:S(2)}) collective-permute-start(bf16[64,4736]{1,0:T(8,128)(2,1)} %collective-permute-done.1.refs_1_), channel_id=1, source_target_pairs={{8,12},{5,1},{10,14},{7,3},{24,28},{21,17},{26,30},{23,19}} | collective-permute-start | bytes 1818632 | tf_op jit(solution)/shard_map/ppermute | solution.py:417
  31.8 0.8 copy-done.8
  32.6 1.5 collective-permute-start.15
  34.0 1.5 %collective-permute-start.13 = (bf16[64,4736]{1,0:T(8,128)(2,1)S(1)}, bf16[64,4736]{1,0:T(8,128)(2,1)}, u32[]{:S(2)}, u32[]{:S(2)}) collective-permute-start(bf16[64,4736]{1,0:T(8,128)(2,1)S(1)} %collective-permute-done.refs_1_.refs_5_), channel_id=1, source_target_pairs={{4,20},{9,25},{20,4},{25,9},{6,22},{11,27},{22,6},{27,11}} | collective-permute-start | bytes 1818632 | tf_op jit(solution)/shard_map/ppermute | solution.py:414
  35.6 1.5 %collective-permute-start.10 = (bf16[64,4736]{1,0:T(8,128)(2,1)}, bf16[64,4736]{1,0:T(8,128)(2,1)}, u32[]{:S(2)}, u32[]{:S(2)}) collective-permute-start(bf16[64,4736]{1,0:T(8,128)(2,1)} %collective-permute-done.9.refs_0_), channel_id=1, source_target_pairs={{1,17},{5,21},{8,24},{12,28},{17,1},{21,5},{24,8},{28,12},{3,19},{... | collective-permute-start | bytes 1818632 | tf_op jit(solution)/shard_map/ppermute | solution.py:414
  37.1 0.1 stack.51.at
  37.2 2.5 %copy-done = bf16[3,128,6912]{2,1,0:T(8,128)(2,1)S(1)} copy-done((bf16[3,128,6912]{2,1,0:T(8,128)(2,1)S(1)}, bf16[3,128,6912]{2,1,0:T(8,128)(2,1)}, u32[]{:S(2)}) %copy-start) | copy-done | bytes 5308440
  39.7 1.5 %copy-done.2 = bf16[3,128,2560]{2,1,0:T(8,128)(2,1)S(1)} copy-done((bf16[3,128,2560]{2,1,0:T(8,128)(2,1)S(1)}, bf16[3,128,2560]{2,1,0:T(8,128)(2,1)}, u32[]{:S(2)}) %copy-start.2) | copy-done | bytes 1966104
  41.2 0.8 shard_map.82
  42.0 3.2 %shard_map.84 = (bf16[384,2560]{1,0:T(8,128)(2,1)S(1)}, bf16[384,6912]{1,0:T(8,128)(2,1)S(1)}) custom-call(bf16[384,2560]{1,0:T(8,128)(2,1)} %bitcast.11.x_ref, bf16[384,6912]{1,0:T(8,128)(2,1)} %bitcast.12.y_ref), custom_call_target="tpu_custom_call" | custom-call | tf_op jit(solution)/shard_map/pallas_call | solution.py:404
  45.2 0.1 copy-done.7
  45.4 0.6 shard_map.85
  46.0 19.1 %collective-permute-start.8 = (f32[256,384]{1,0:T(8,128)S(1)}, f32[256,384]{1,0:T(8,128)S(1)}, u32[]{:S(2)}, u32[]{:S(2)}) collective-permute-start(f32[256,384]{1,0:T(8,128)S(1)} %get-tuple-element.46), channel_id=1, source_target_pairs={{0,1},{1,0},{2,3},{3,2},{4,5},{5,4},{6,7},{7,6},{8,9},{9,8},{10,11... | collective-permute-start | bytes 1179656 | tf_op jit(solution)/shard_map/ppermute | solution.py:441
  65.1 0.7 collective-permute-start.17
  65.8 0.7 collective-permute-start.16
  66.5 0.6 shard_map.86
  67.2 9.7 %collective-permute-start.14 = (f32[256,384]{1,0:T(8,128)S(1)}, f32[256,384]{1,0:T(8,128)S(1)}, u32[]{:S(2)}, u32[]{:S(2)}) collective-permute-start(f32[256,384]{1,0:T(8,128)S(1)} %get-tuple-element.51), channel_id=1, source_target_pairs={{0,1},{1,0},{2,3},{3,2},{4,5},{5,4},{6,7},{7,6},{8,9},{9,8},{10,11... | collective-permute-start | bytes 1179656 | tf_op jit(solution)/shard_map/ppermute | solution.py:441
  76.8 2.1 %shard_map.83 = (f32[128,384]{1,0:T(8,128)S(1)}, f32[128,384]{1,0:T(8,128)S(1)}) custom-call(bf16[128,2560]{1,0:T(8,128)(2,1)S(1)} %copy-done.3, bf16[128,6912]{1,0:T(8,128)(2,1)S(1)} %copy-done.1, bf16[384,2560]{1,0:T(8,128)(2,1)S(1)} %get-tuple-element.39.t_out.refs_4_.refs_8_, bf16[384,6912]{1,0:T(8,128)(2,1)S(1)} %get-tuple-element.40.t_in.refs_5_.refs_9_), custom_call_target="tpu_custom_call" | custom-call | flops 931135488 | bytes 4655677 | tf_op jit(solution)/shard_map/pallas_call | solution.py:428
  78.9 0.6 shard_map.89
  79.5 1.6 %collective-permute-start.19 = (bf16[512,384]{1,0:T(8,128)(2,1)S(1)}, bf16[512,384]{1,0:T(8,128)(2,1)S(1)}, u32[]{:S(2)}, u32[]{:S(2)}) collective-permute-start(bf16[512,384]{1,0:T(8,128)(2,1)S(1)} %shard_map.89), channel_id=1, source_target_pairs={{0,2},{2,0},{1,3},{3,1},{4,6},{6,4},{5,7},{7,5},{8,10},{10,8},{9,1... | collective-permute-start | bytes 1179656 | tf_op jit(solution)/shard_map/ppermute | solution.py:451
  81.1 0.6 shard_map.87
  81.7 0.6 collective-permute-start.18
  82.3 0.8 shard_map.88
  83.1 11.8 %collective-permute-done.18.middle = bf16[256,384]{1,0:T(8,128)(2,1)S(1)} collective-permute-done((bf16[256,384]{1,0:T(8,128)(2,1)S(1)}, bf16[256,384]{1,0:T(8,128)(2,1)S(1)}, u32[]{:S(2)}, u32[]{:S(2)}) %collective-permute-start.18) | collective-permute-done | bytes 196640 | tf_op jit(solution)/shard_map/ppermute | solution.py:455
  94.9 1.7 %collective-permute-done.20.last_far = f32[256,384]{1,0:T(8,128)S(1)} collective-permute-done((f32[256,384]{1,0:T(8,128)S(1)}, f32[256,384]{1,0:T(8,128)S(1)}, u32[]{:S(2)}, u32[]{:S(2)}) %collective-permute-start.20) | collective-permute-done | bytes 393248 | tf_op jit(solution)/shard_map/ppermute | solution.py:441
  96.6 0.6 shard_map.90
  97.2 1.6 %collective-permute-start.21 = (bf16[256,384]{1,0:T(8,128)(2,1)S(1)}, bf16[256,384]{1,0:T(8,128)(2,1)S(1)}, u32[]{:S(2)}, u32[]{:S(2)}) collective-permute-start(bf16[256,384]{1,0:T(8,128)(2,1)S(1)} %shard_map.90), channel_id=1, source_target_pairs={{0,2},{2,0},{1,3},{3,1},{4,6},{6,4},{5,7},{7,5},{8,10},{10,8},{9,1... | collective-permute-start | bytes 589832 | tf_op jit(solution)/shard_map/ppermute | solution.py:458
  98.8 5.4 %collective-permute-done.21.late = bf16[256,384]{1,0:T(8,128)(2,1)S(1)} collective-permute-done((bf16[256,384]{1,0:T(8,128)(2,1)S(1)}, bf16[256,384]{1,0:T(8,128)(2,1)S(1)}, u32[]{:S(2)}, u32[]{:S(2)}) %collective-permute-start.21) | collective-permute-done | bytes 196640 | tf_op jit(solution)/shard_map/ppermute | solution.py:458
  104.2 1.2 shard_map.91
  105.4 2.7 %collective-permute-start.22 = (bf16[3,64,256]{2,1,0:T(8,128)(2,1)S(1)}, bf16[3,64,256]{2,1,0:T(8,128)(2,1)S(1)}, u32[]{:S(2)}, u32[]{:S(2)}) collective-permute-start(bf16[3,64,256]{2,1,0:T(8,128)(2,1)S(1)} %get-tuple-element.58), channel_id=1, source_target_pairs={{0,4},{1,5},{4,8},{5,9},{8,12},{9,13},{12,0},{13,1},{2,6},{3,7},{6... | collective-permute-start | bytes 294920 | tf_op jit(solution)/shard_map/ppermute | solution.py:472
  108.0 7.6 %collective-permute-start.23 = (bf16[3,64,256]{2,1,0:T(8,128)(2,1)S(1)}, bf16[3,64,256]{2,1,0:T(8,128)(2,1)S(1)}, u32[]{:S(2)}, u32[]{:S(2)}) collective-permute-start(bf16[3,64,256]{2,1,0:T(8,128)(2,1)S(1)} %get-tuple-element.59), channel_id=1, source_target_pairs={{0,8},{1,9},{4,12},{5,13},{8,0},{9,1},{12,4},{13,5},{2,10},{3,11},... | collective-permute-start | bytes 294920 | tf_op jit(solution)/shard_map/ppermute | solution.py:472
  115.6 2.8 %collective-permute-start.24 = (bf16[3,64,256]{2,1,0:T(8,128)(2,1)S(1)}, bf16[3,64,256]{2,1,0:T(8,128)(2,1)S(1)}, u32[]{:S(2)}, u32[]{:S(2)}) collective-permute-start(bf16[3,64,256]{2,1,0:T(8,128)(2,1)S(1)} %get-tuple-element.60), channel_id=1, source_target_pairs={{0,12},{1,13},{4,0},{5,1},{8,4},{9,5},{12,8},{13,9},{2,14},{3,15},... | collective-permute-start | bytes 294920 | tf_op jit(solution)/shard_map/ppermute | solution.py:472
  118.5 0.3 collective-permute-start.27
  118.8 2.7 %collective-permute-done.23.refs_2_ = bf16[3,64,256]{2,1,0:T(8,128)(2,1)S(1)} collective-permute-done((bf16[3,64,256]{2,1,0:T(8,128)(2,1)S(1)}, bf16[3,64,256]{2,1,0:T(8,128)(2,1)S(1)}, u32[]{:S(2)}, u32[]{:S(2)}) %collective-permute-start.23) | collective-permute-done | bytes 98336 | tf_op jit(solution)/shard_map/ppermute | solution.py:472
  121.4 3.6 %collective-permute-start.28 = (bf16[3,64,256]{2,1,0:T(8,128)(2,1)S(1)}, bf16[3,64,256]{2,1,0:T(8,128)(2,1)S(1)}, u32[]{:S(2)}, u32[]{:S(2)}) collective-permute-start(bf16[3,64,256]{2,1,0:T(8,128)(2,1)S(1)} %get-tuple-element.64), channel_id=1, source_target_pairs={{0,13},{1,12},{4,1},{5,0},{8,5},{9,4},{12,9},{13,8},{2,15},{3,14},... | collective-permute-start | bytes 294920 | tf_op jit(solution)/shard_map/ppermute | solution.py:472
  125.0 1.4 fusion.weights
  126.5 1.5 %collective-permute-done.27.refs_6_ = bf16[3,64,256]{2,1,0:T(8,128)(2,1)S(1)} collective-permute-done((bf16[3,64,256]{2,1,0:T(8,128)(2,1)S(1)}, bf16[3,64,256]{2,1,0:T(8,128)(2,1)S(1)}, u32[]{:S(2)}, u32[]{:S(2)}) %collective-permute-start.27) | collective-permute-done | bytes 98336 | tf_op jit(solution)/shard_map/ppermute | solution.py:472
  128.0 2.0 %shard_map.92 = f32[64,24]{1,0:T(8,128)S(1)} custom-call(s32[8]{0:T(128)S(1)} %stack.51.at, bf16[64,64,256]{2,1,0:T(8,128)(2,1)S(1)} %fusion.weights, bf16[3,64,256]{2,1,0:T(8,128)(2,1)S(1)} %get-tuple-element.57.refs_0_, bf16[3,64,256]{2,1,0:T(8,128)(2,1)S(1)} %collective-permute-done.22.refs_1_, bf16[3,64,256]{2,1,0:T(8,128)(2,1)S(1)} %collective-permute-done.23.refs_2_, ...), custom_call_target="tpu_custom_call" | custom-call | flops 50331648 | bytes 251658 | tf_op jit(solution)/shard_map/pallas_call | solution.py:477
  130.1 0.1 reshape_reshape.3
  130.3 2.8 %collective-permute-start.29 = (f32[16,4,6]{0,1,2:T(4,128)S(1)}, f32[16,4,6]{0,1,2:T(4,128)S(1)}, u32[]{:S(2)}, u32[]{:S(2)}) collective-permute-start(f32[16,4,6]{0,1,2:T(4,128)S(1)} %bitcast.74), channel_id=1, source_target_pairs={{0,1},{1,2},{2,3},{3,0},{4,5},{5,6},{6,7},{7,4},{8,9},{9,10},{10,1... | collective-permute-start | bytes 4616 | tf_op jit(solution)/shard_map/ppermute | solution.py:63
  133.0 1.5 %collective-permute-start.30 = (f32[16,4,6]{0,1,2:T(4,128)S(1)}, f32[16,4,6]{0,1,2:T(4,128)S(1)}, u32[]{:S(2)}, u32[]{:S(2)}) collective-permute-start(f32[16,4,6]{0,1,2:T(4,128)S(1)} %bitcast.75), channel_id=1, source_target_pairs={{0,2},{1,3},{2,0},{3,1},{4,6},{5,7},{6,4},{7,5},{8,10},{9,11},{10,... | collective-permute-start | bytes 4616 | tf_op jit(solution)/shard_map/ppermute | solution.py:63
  134.5 1.0 collective-permute-done.29
  135.5 1.2 collective-permute-done.30
  136.9 1.4 collective-permute-start.32
  138.2 3.2 %collective-permute-done.32 = f32[16,2,6]{0,1,2:T(2,128)S(1)} collective-permute-done((f32[16,2,6]{0,1,2:T(2,128)S(1)}, f32[16,2,6]{0,1,2:T(2,128)S(1)}, u32[]{:S(2)}, u32[]{:S(2)}) %collective-permute-start.32) | collective-permute-done | bytes 800 | tf_op jit(solution)/shard_map/ppermute | solution.py:74
  141.5 2.6 %collective-permute-start.33 = (f32[16,1,6]{0,1,2:T(1,128)S(1)}, f32[16,1,6]{0,1,2:T(1,128)S(1)}, u32[]{:S(2)}, u32[]{:S(2)}) collective-permute-start(f32[16,1,6]{0,1,2:T(1,128)S(1)} %fusion.12), channel_id=1, source_target_pairs={{0,4},{4,0},{8,12},{12,8},{1,5},{5,1},{9,13},{13,9},{2,6},{6,2},{1... | collective-permute-start | bytes 1160 | tf_op jit(solution)/shard_map/ppermute | solution.py:74
  144.1 1.6 %collective-permute-done.33 = f32[16,1,6]{0,1,2:T(1,128)S(1)} collective-permute-done((f32[16,1,6]{0,1,2:T(1,128)S(1)}, f32[16,1,6]{0,1,2:T(1,128)S(1)}, u32[]{:S(2)}, u32[]{:S(2)}) %collective-permute-start.33) | collective-permute-done | bytes 416 | tf_op jit(solution)/shard_map/ppermute | solution.py:74
  145.6 0.7 bitcast_multiply_fusion
  (67 shorter events, 0.5 us)
Async XLA Ops:
  0.0 8.4 %copy-start.1 = (bf16[128,6912]{1,0:T(8,128)(2,1)S(1)}, bf16[128,6912]{1,0:T(8,128)(2,1)}, u32[]{:S(2)}) copy-start(bf16[128,6912]{1,0:T(8,128)(2,1)} %b_in.1) | copy-start | bytes 5308420
  0.0 35.6 %collective-permute-start.7 = (bf16[3,128,6912]{2,1,0:T(8,128)(2,1)}, bf16[3,128,6912]{2,1,0:T(8,128)(2,1)}, u32[]{:S(2)}, u32[]{:S(2)}) collective-permute-start(bf16[3,128,6912]{2,1,0:T(8,128)(2,1)} %param.8), channel_id=1, source_target_pairs={{0,1},{1,0},{2,3},{3,2},{4,5},{5,4},{6,7},{7,6},{8,9},{9,8},{10,11... | collective-permute-start | bytes 15925256 | tf_op jit(solution)/shard_map/ppermute | solution.py:425
  0.5 33.6 %collective-permute-start.6 = (bf16[3,128,2560]{2,1,0:T(8,128)(2,1)}, bf16[3,128,2560]{2,1,0:T(8,128)(2,1)}, u32[]{:S(2)}, u32[]{:S(2)}) collective-permute-start(bf16[3,128,2560]{2,1,0:T(8,128)(2,1)} %param.9), channel_id=1, source_target_pairs={{0,1},{1,0},{2,3},{3,2},{4,5},{5,4},{6,7},{7,6},{8,9},{9,8},{10,11... | collective-permute-start | bytes 5898248 | tf_op jit(solution)/shard_map/ppermute | solution.py:425
  3.4 12.8 %collective-permute-start.4 = (bf16[64,4736]{1,0:T(8,128)(2,1)}, bf16[64,4736]{1,0:T(8,128)(2,1)S(1)}, u32[]{:S(2)}, u32[]{:S(2)}) collective-permute-start(bf16[64,4736]{1,0:T(8,128)(2,1)} %pad_maximum_fusion), channel_id=1, source_target_pairs={{0,4},{4,8},{8,12},{5,1},{9,5},{13,9},{2,6},{6,10},{10,14},{7,3},{... | collective-permute-start | bytes 1818632 | tf_op jit(solution)/shard_map/ppermute | solution.py:417
  8.5 14.2 %collective-permute-start = (bf16[64,4736]{1,0:T(8,128)(2,1)S(1)}, bf16[64,4736]{1,0:T(8,128)(2,1)S(1)}, u32[]{:S(2)}, u32[]{:S(2)}) collective-permute-start(bf16[64,4736]{1,0:T(8,128)(2,1)S(1)} %dynamic-slice), channel_id=1, source_target_pairs={{0,4},{4,8},{8,12},{5,1},{9,5},{13,9},{2,6},{6,10},{10,14},{7,3},{... | collective-permute-start | bytes 1818632 | tf_op jit(solution)/shard_map/ppermute | solution.py:417
  16.2 8.6 %collective-permute-start.5 = (bf16[64,4736]{1,0:T(8,128)(2,1)S(1)}, bf16[64,4736]{1,0:T(8,128)(2,1)S(1)}, u32[]{:S(2)}, u32[]{:S(2)}) collective-permute-start(bf16[64,4736]{1,0:T(8,128)(2,1)S(1)} %collective-permute-done.4.refs_0_.refs_4_), channel_id=1, source_target_pairs={{1,17},{5,21},{8,24},{12,28},{17,1},{21,5},{24,8},{28,12},{3,19},{... | collective-permute-start | bytes 1818632 | tf_op jit(solution)/shard_map/ppermute | solution.py:414
  22.6 4.5 %collective-permute-start.1 = (bf16[64,4736]{1,0:T(8,128)(2,1)S(1)}, bf16[64,4736]{1,0:T(8,128)(2,1)}, u32[]{:S(2)}, u32[]{:S(2)}) collective-permute-start(bf16[64,4736]{1,0:T(8,128)(2,1)S(1)} %collective-permute-done.refs_1_.refs_5_), channel_id=1, source_target_pairs={{4,8},{8,12},{5,1},{9,5},{6,10},{10,14},{7,3},{11,7},{20,24},{24,2... | collective-permute-start | bytes 1818632 | tf_op jit(solution)/shard_map/ppermute | solution.py:417
  24.2 3.7 %collective-permute-start.2 = (bf16[64,4736]{1,0:T(8,128)(2,1)S(1)}, bf16[64,4736]{1,0:T(8,128)(2,1)S(1)}, u32[]{:S(2)}, u32[]{:S(2)}) collective-permute-start(bf16[64,4736]{1,0:T(8,128)(2,1)S(1)} %collective-permute-done.refs_1_.refs_5_), channel_id=1, source_target_pairs={{1,17},{5,21},{8,24},{12,28},{17,1},{21,5},{24,8},{28,12},{3,19},{... | collective-permute-start | bytes 1818632 | tf_op jit(solution)/shard_map/ppermute | solution.py:414
  24.9 0.8 copy-start.4
  25.7 4.5 %collective-permute-start.9 = (bf16[64,4736]{1,0:T(8,128)(2,1)S(1)}, bf16[64,4736]{1,0:T(8,128)(2,1)}, u32[]{:S(2)}, u32[]{:S(2)}) collective-permute-start(bf16[64,4736]{1,0:T(8,128)(2,1)S(1)} %collective-permute-done.4.refs_0_.refs_4_), channel_id=1, source_target_pairs={{4,8},{8,12},{5,1},{9,5},{6,10},{10,14},{7,3},{11,7},{20,24},{24,2... | collective-permute-start | bytes 1818632 | tf_op jit(solution)/shard_map/ppermute | solution.py:417
  27.2 4.6 %collective-permute-start.11 = (bf16[64,4736]{1,0:T(8,128)(2,1)}, bf16[64,4736]{1,0:T(8,128)(2,1)S(1)}, u32[]{:S(2)}, u32[]{:S(2)}) collective-permute-start(bf16[64,4736]{1,0:T(8,128)(2,1)} %collective-permute-done.1.refs_1_), channel_id=1, source_target_pairs={{1,17},{5,21},{8,24},{12,28},{17,1},{21,5},{24,8},{28,12},{3,19},{... | collective-permute-start | bytes 1818632 | tf_op jit(solution)/shard_map/ppermute | solution.py:414
  27.9 0.8 copy-start.6
  28.7 17.3 %collective-permute-start.12 = (bf16[64,4736]{1,0:T(8,128)(2,1)S(1)}, bf16[64,4736]{1,0:T(8,128)(2,1)}, u32[]{:S(2)}, u32[]{:S(2)}) collective-permute-start(bf16[64,4736]{1,0:T(8,128)(2,1)S(1)} %collective-permute-done.4.refs_0_.refs_4_), channel_id=1, source_target_pairs={{4,20},{9,25},{20,4},{25,9},{6,22},{11,27},{22,6},{27,11}} | collective-permute-start | bytes 1818632 | tf_op jit(solution)/shard_map/ppermute | solution.py:414
  30.2 34.9 %collective-permute-start.3 = (bf16[64,4736]{1,0:T(8,128)(2,1)}, bf16[64,4736]{1,0:T(8,128)(2,1)}, u32[]{:S(2)}, u32[]{:S(2)}) collective-permute-start(bf16[64,4736]{1,0:T(8,128)(2,1)} %collective-permute-done.1.refs_1_), channel_id=1, source_target_pairs={{8,12},{5,1},{10,14},{7,3},{24,28},{21,17},{26,30},{23,19}} | collective-permute-start | bytes 1818632 | tf_op jit(solution)/shard_map/ppermute | solution.py:417
  31.8 0.8 copy-start.8
  32.6 33.2 %collective-permute-start.15 = (bf16[64,4736]{1,0:T(8,128)(2,1)}, bf16[64,4736]{1,0:T(8,128)(2,1)}, u32[]{:S(2)}, u32[]{:S(2)}) collective-permute-start(bf16[64,4736]{1,0:T(8,128)(2,1)} %collective-permute-done.9.refs_0_), channel_id=1, source_target_pairs={{8,12},{5,1},{10,14},{7,3},{24,28},{21,17},{26,30},{23,19}} | collective-permute-start | bytes 1818632 | tf_op jit(solution)/shard_map/ppermute | solution.py:417
  34.0 32.5 %collective-permute-start.13 = (bf16[64,4736]{1,0:T(8,128)(2,1)S(1)}, bf16[64,4736]{1,0:T(8,128)(2,1)}, u32[]{:S(2)}, u32[]{:S(2)}) collective-permute-start(bf16[64,4736]{1,0:T(8,128)(2,1)S(1)} %collective-permute-done.refs_1_.refs_5_), channel_id=1, source_target_pairs={{4,20},{9,25},{20,4},{25,9},{6,22},{11,27},{22,6},{27,11}} | collective-permute-start | bytes 1818632 | tf_op jit(solution)/shard_map/ppermute | solution.py:414
  35.6 30.9 %collective-permute-start.10 = (bf16[64,4736]{1,0:T(8,128)(2,1)}, bf16[64,4736]{1,0:T(8,128)(2,1)}, u32[]{:S(2)}, u32[]{:S(2)}) collective-permute-start(bf16[64,4736]{1,0:T(8,128)(2,1)} %collective-permute-done.9.refs_0_), channel_id=1, source_target_pairs={{1,17},{5,21},{8,24},{12,28},{17,1},{21,5},{24,8},{28,12},{3,19},{... | collective-permute-start | bytes 1818632 | tf_op jit(solution)/shard_map/ppermute | solution.py:414
  37.2 2.5 %copy-start = (bf16[3,128,6912]{2,1,0:T(8,128)(2,1)S(1)}, bf16[3,128,6912]{2,1,0:T(8,128)(2,1)}, u32[]{:S(2)}) copy-start(bf16[3,128,6912]{2,1,0:T(8,128)(2,1)} %param.8) | copy-start | bytes 15925252
  39.7 1.5 %copy-start.2 = (bf16[3,128,2560]{2,1,0:T(8,128)(2,1)S(1)}, bf16[3,128,2560]{2,1,0:T(8,128)(2,1)}, u32[]{:S(2)}) copy-start(bf16[3,128,2560]{2,1,0:T(8,128)(2,1)} %param.9) | copy-start | bytes 5898244
  42.0 3.2 %copy-start.5 = (bf16[64,4736]{1,0:T(8,128)(2,1)S(1)}, bf16[64,4736]{1,0:T(8,128)(2,1)}, u32[]{:S(2)}) copy-start(bf16[64,4736]{1,0:T(8,128)(2,1)} %copy-done.4) | copy-start | bytes 1818628
  42.0 3.3 %copy-start.7 = (bf16[64,4736]{1,0:T(8,128)(2,1)S(1)}, bf16[64,4736]{1,0:T(8,128)(2,1)}, u32[]{:S(2)}) copy-start(bf16[64,4736]{1,0:T(8,128)(2,1)} %copy-done.6) | copy-start | bytes 1818628
  45.4 21.2 %copy-start.9 = (bf16[64,4736]{1,0:T(8,128)(2,1)S(1)}, bf16[64,4736]{1,0:T(8,128)(2,1)}, u32[]{:S(2)}) copy-start(bf16[64,4736]{1,0:T(8,128)(2,1)} %copy-done.8) | copy-start | bytes 1818628
  46.0 33.0 %collective-permute-start.8 = (f32[256,384]{1,0:T(8,128)S(1)}, f32[256,384]{1,0:T(8,128)S(1)}, u32[]{:S(2)}, u32[]{:S(2)}) collective-permute-start(f32[256,384]{1,0:T(8,128)S(1)} %get-tuple-element.46), channel_id=1, source_target_pairs={{0,1},{1,0},{2,3},{3,2},{4,5},{5,4},{6,7},{7,6},{8,9},{9,8},{10,11... | collective-permute-start | bytes 1179656 | tf_op jit(solution)/shard_map/ppermute | solution.py:441
  65.1 17.2 %collective-permute-start.17 = (bf16[64,4736]{1,0:T(8,128)(2,1)}, bf16[64,4736]{1,0:T(8,128)(2,1)S(1)}, u32[]{:S(2)}, u32[]{:S(2)}) collective-permute-start(bf16[64,4736]{1,0:T(8,128)(2,1)} %collective-permute-done.3.refs_1_), channel_id=1, source_target_pairs={{1,17},{12,28},{17,1},{28,12},{3,19},{14,30},{19,3},{30,14}} | collective-permute-start | bytes 1818632 | tf_op jit(solution)/shard_map/ppermute | solution.py:414
  65.8 16.5 %collective-permute-start.16 = (bf16[64,4736]{1,0:T(8,128)(2,1)}, bf16[64,4736]{1,0:T(8,128)(2,1)S(1)}, u32[]{:S(2)}, u32[]{:S(2)}) collective-permute-start(bf16[64,4736]{1,0:T(8,128)(2,1)} %collective-permute-done.15.refs_0_), channel_id=1, source_target_pairs={{1,17},{12,28},{17,1},{28,12},{3,19},{14,30},{19,3},{30,14}} | collective-permute-start | bytes 1818632 | tf_op jit(solution)/shard_map/ppermute | solution.py:414
  66.5 10.3 %copy-start.3 = (bf16[128,2560]{1,0:T(8,128)(2,1)S(1)}, bf16[128,2560]{1,0:T(8,128)(2,1)}, u32[]{:S(2)}) copy-start(bf16[128,2560]{1,0:T(8,128)(2,1)} %b_out.1) | copy-start | bytes 1966084
  67.2 13.9 %collective-permute-start.14 = (f32[256,384]{1,0:T(8,128)S(1)}, f32[256,384]{1,0:T(8,128)S(1)}, u32[]{:S(2)}, u32[]{:S(2)}) collective-permute-start(f32[256,384]{1,0:T(8,128)S(1)} %get-tuple-element.51), channel_id=1, source_target_pairs={{0,1},{1,0},{2,3},{3,2},{4,5},{5,4},{6,7},{7,6},{8,9},{9,8},{10,11... | collective-permute-start | bytes 1179656 | tf_op jit(solution)/shard_map/ppermute | solution.py:441
  79.5 15.3 %collective-permute-start.19 = (bf16[512,384]{1,0:T(8,128)(2,1)S(1)}, bf16[512,384]{1,0:T(8,128)(2,1)S(1)}, u32[]{:S(2)}, u32[]{:S(2)}) collective-permute-start(bf16[512,384]{1,0:T(8,128)(2,1)S(1)} %shard_map.89), channel_id=1, source_target_pairs={{0,2},{2,0},{1,3},{3,1},{4,6},{6,4},{5,7},{7,5},{8,10},{10,8},{9,1... | collective-permute-start | bytes 1179656 | tf_op jit(solution)/shard_map/ppermute | solution.py:451
  81.7 22.5 %copy-start.10 = (s32[3]{0:T(128)S(1)}, s32[3]{0:T(128)}, u32[]{:S(2)}) copy-start(s32[3]{0:T(128)} %counts.1) | copy-start | bytes 40
  81.7 13.2 %collective-permute-start.18 = (bf16[256,384]{1,0:T(8,128)(2,1)S(1)}, bf16[256,384]{1,0:T(8,128)(2,1)S(1)}, u32[]{:S(2)}, u32[]{:S(2)}) collective-permute-start(bf16[256,384]{1,0:T(8,128)(2,1)S(1)} %shard_map.87), channel_id=1, source_target_pairs={{0,2},{2,0},{1,3},{3,1},{4,6},{6,4},{5,7},{7,5},{8,10},{10,8},{9,1... | collective-permute-start | bytes 589832 | tf_op jit(solution)/shard_map/ppermute | solution.py:455
  94.9 1.7 %collective-permute-start.20 = (f32[256,384]{1,0:T(8,128)S(1)}, f32[256,384]{1,0:T(8,128)S(1)}, u32[]{:S(2)}, u32[]{:S(2)}) collective-permute-start(f32[256,384]{1,0:T(8,128)S(1)} %get-tuple-element.56), channel_id=1, source_target_pairs={{0,1},{1,0},{2,3},{3,2},{4,5},{5,4},{6,7},{7,6},{8,9},{9,8},{10,11... | collective-permute-start | bytes 1179656 | tf_op jit(solution)/shard_map/ppermute | solution.py:441
  97.2 27.8 %copy-start.11 = (bf16[64,64,256]{2,1,0:T(8,128)(2,1)S(1)}, bf16[64,64,256]{2,1,0:T(8,128)(2,1)}, u32[]{:S(2)}) copy-start(bf16[64,64,256]{2,1,0:T(8,128)(2,1)} %param.13) | copy-start | bytes 6291460
  97.2 27.8 %copy-start.12 = (f32[64,256]{1,0:T(8,128)S(1)}, f32[64,256]{1,0:T(8,128)}, u32[]{:S(2)}) copy-start(f32[64,256]{1,0:T(8,128)} %param.14) | copy-start | bytes 196612
  97.2 7.0 %collective-permute-start.21 = (bf16[256,384]{1,0:T(8,128)(2,1)S(1)}, bf16[256,384]{1,0:T(8,128)(2,1)S(1)}, u32[]{:S(2)}, u32[]{:S(2)}) collective-permute-start(bf16[256,384]{1,0:T(8,128)(2,1)S(1)} %shard_map.90), channel_id=1, source_target_pairs={{0,2},{2,0},{1,3},{3,1},{4,6},{6,4},{5,7},{7,5},{8,10},{10,8},{9,1... | collective-permute-start | bytes 589832 | tf_op jit(solution)/shard_map/ppermute | solution.py:458
  105.4 13.1 %collective-permute-start.22 = (bf16[3,64,256]{2,1,0:T(8,128)(2,1)S(1)}, bf16[3,64,256]{2,1,0:T(8,128)(2,1)S(1)}, u32[]{:S(2)}, u32[]{:S(2)}) collective-permute-start(bf16[3,64,256]{2,1,0:T(8,128)(2,1)S(1)} %get-tuple-element.58), channel_id=1, source_target_pairs={{0,4},{1,5},{4,8},{5,9},{8,12},{9,13},{12,0},{13,1},{2,6},{3,7},{6... | collective-permute-start | bytes 294920 | tf_op jit(solution)/shard_map/ppermute | solution.py:472
  108.0 13.4 %collective-permute-start.23 = (bf16[3,64,256]{2,1,0:T(8,128)(2,1)S(1)}, bf16[3,64,256]{2,1,0:T(8,128)(2,1)S(1)}, u32[]{:S(2)}, u32[]{:S(2)}) collective-permute-start(bf16[3,64,256]{2,1,0:T(8,128)(2,1)S(1)} %get-tuple-element.59), channel_id=1, source_target_pairs={{0,8},{1,9},{4,12},{5,13},{8,0},{9,1},{12,4},{13,5},{2,10},{3,11},... | collective-permute-start | bytes 294920 | tf_op jit(solution)/shard_map/ppermute | solution.py:472
  115.6 10.9 %collective-permute-start.24 = (bf16[3,64,256]{2,1,0:T(8,128)(2,1)S(1)}, bf16[3,64,256]{2,1,0:T(8,128)(2,1)S(1)}, u32[]{:S(2)}, u32[]{:S(2)}) collective-permute-start(bf16[3,64,256]{2,1,0:T(8,128)(2,1)S(1)} %get-tuple-element.60), channel_id=1, source_target_pairs={{0,12},{1,13},{4,0},{5,1},{8,4},{9,5},{12,8},{13,9},{2,14},{3,15},... | collective-permute-start | bytes 294920 | tf_op jit(solution)/shard_map/ppermute | solution.py:472
  118.5 8.0 %collective-permute-start.25 = (bf16[3,64,256]{2,1,0:T(8,128)(2,1)S(1)}, bf16[3,64,256]{2,1,0:T(8,128)(2,1)S(1)}, u32[]{:S(2)}, u32[]{:S(2)}) collective-permute-start(bf16[3,64,256]{2,1,0:T(8,128)(2,1)S(1)} %get-tuple-element.61), channel_id=1, source_target_pairs={{0,1},{1,0},{4,5},{5,4},{8,9},{9,8},{12,13},{13,12},{2,3},{3,2},{6... | collective-permute-start | bytes 294920 | tf_op jit(solution)/shard_map/ppermute | solution.py:472
  118.5 8.0 %collective-permute-start.26 = (bf16[3,64,256]{2,1,0:T(8,128)(2,1)S(1)}, bf16[3,64,256]{2,1,0:T(8,128)(2,1)S(1)}, u32[]{:S(2)}, u32[]{:S(2)}) collective-permute-start(bf16[3,64,256]{2,1,0:T(8,128)(2,1)S(1)} %get-tuple-element.62), channel_id=1, source_target_pairs={{0,5},{1,4},{4,9},{5,8},{8,13},{9,12},{12,1},{13,0},{2,7},{3,6},{6... | collective-permute-start | bytes 294920 | tf_op jit(solution)/shard_map/ppermute | solution.py:472
  118.5 9.5 %collective-permute-start.27 = (bf16[3,64,256]{2,1,0:T(8,128)(2,1)S(1)}, bf16[3,64,256]{2,1,0:T(8,128)(2,1)S(1)}, u32[]{:S(2)}, u32[]{:S(2)}) collective-permute-start(bf16[3,64,256]{2,1,0:T(8,128)(2,1)S(1)} %get-tuple-element.63), channel_id=1, source_target_pairs={{0,9},{1,8},{4,13},{5,12},{8,1},{9,0},{12,5},{13,4},{2,11},{3,10},... | collective-permute-start | bytes 294920 | tf_op jit(solution)/shard_map/ppermute | solution.py:472
  121.4 6.6 %collective-permute-start.28 = (bf16[3,64,256]{2,1,0:T(8,128)(2,1)S(1)}, bf16[3,64,256]{2,1,0:T(8,128)(2,1)S(1)}, u32[]{:S(2)}, u32[]{:S(2)}) collective-permute-start(bf16[3,64,256]{2,1,0:T(8,128)(2,1)S(1)} %get-tuple-element.64), channel_id=1, source_target_pairs={{0,13},{1,12},{4,1},{5,0},{8,5},{9,4},{12,9},{13,8},{2,15},{3,14},... | collective-permute-start | bytes 294920 | tf_op jit(solution)/shard_map/ppermute | solution.py:472
  126.4 11.8 %copy-start.13 = (s32[16,1]{0,1:T(1,128)S(1)}, s32[16,1]{0,1:T(1,128)}, u32[]{:S(2)}) copy-start(s32[16,1]{0,1:T(1,128)} %param.15) | copy-start | bytes 196
  130.3 5.2 %collective-permute-start.29 = (f32[16,4,6]{0,1,2:T(4,128)S(1)}, f32[16,4,6]{0,1,2:T(4,128)S(1)}, u32[]{:S(2)}, u32[]{:S(2)}) collective-permute-start(f32[16,4,6]{0,1,2:T(4,128)S(1)} %bitcast.74), channel_id=1, source_target_pairs={{0,1},{1,2},{2,3},{3,0},{4,5},{5,6},{6,7},{7,4},{8,9},{9,10},{10,1... | collective-permute-start | bytes 4616 | tf_op jit(solution)/shard_map/ppermute | solution.py:63
  133.0 3.7 %collective-permute-start.30 = (f32[16,4,6]{0,1,2:T(4,128)S(1)}, f32[16,4,6]{0,1,2:T(4,128)S(1)}, u32[]{:S(2)}, u32[]{:S(2)}) collective-permute-start(f32[16,4,6]{0,1,2:T(4,128)S(1)} %bitcast.75), channel_id=1, source_target_pairs={{0,2},{1,3},{2,0},{3,1},{4,6},{5,7},{6,4},{7,5},{8,10},{9,11},{10,... | collective-permute-start | bytes 4616 | tf_op jit(solution)/shard_map/ppermute | solution.py:63
  134.5 2.2 %collective-permute-start.31 = (f32[16,4,6]{0,1,2:T(4,128)S(1)}, f32[16,4,6]{0,1,2:T(4,128)S(1)}, u32[]{:S(2)}, u32[]{:S(2)}) collective-permute-start(f32[16,4,6]{0,1,2:T(4,128)S(1)} %bitcast.76), channel_id=1, source_target_pairs={{0,3},{1,0},{2,1},{3,2},{4,7},{5,4},{6,5},{7,6},{8,11},{9,8},{10,9... | collective-permute-start | bytes 4616 | tf_op jit(solution)/shard_map/ppermute | solution.py:63
  136.9 4.6 %collective-permute-start.32 = (f32[16,2,6]{0,1,2:T(2,128)S(1)}, f32[16,2,6]{0,1,2:T(2,128)S(1)}, u32[]{:S(2)}, u32[]{:S(2)}) collective-permute-start(f32[16,2,6]{0,1,2:T(2,128)S(1)} %fusion.6), channel_id=1, source_target_pairs={{0,8},{4,12},{8,0},{12,4},{1,9},{5,13},{9,1},{13,5},{2,10},{6,14},... | collective-permute-start | bytes 2312 | tf_op jit(solution)/shard_map/ppermute | solution.py:74
  141.5 4.1 %collective-permute-start.33 = (f32[16,1,6]{0,1,2:T(1,128)S(1)}, f32[16,1,6]{0,1,2:T(1,128)S(1)}, u32[]{:S(2)}, u32[]{:S(2)}) collective-permute-start(f32[16,1,6]{0,1,2:T(1,128)S(1)} %fusion.12), channel_id=1, source_target_pairs={{0,4},{4,0},{8,12},{12,8},{1,5},{5,1},{9,13},{13,9},{2,6},{6,2},{1... | collective-permute-start | bytes 1160 | tf_op jit(solution)/shard_map/ppermute | solution.py:74
